TPU v7x, 32 devices: a whole 2x2x4 slice. The times are simulated.
32 devices in a mesh: dom: 8 (over y, x, core), edge: 4 (over z).
Axes of the slice: x: 2, y: 2, z: 4, core: 2. Of those that a mesh axis runs over, the one named last changes fastest.
Arguments:
- edges: bfloat16 [32768, 512], P(('dom', 'edge')), may hold values from -6 to 6
- atoms: bfloat16 [1024, 256], P(('dom', 'edge')), may hold values from -6 to 6
- reverse: int32 [32768], P(('dom', 'edge')), may hold values from 0 to 32767, as said below
- atom_index: int32 [2, 32768], P(None, ('dom', 'edge')), may hold values from 0 to 127
- tile_source: int32 [512, 2], P(('dom', 'edge')), may hold values from 0 to 63
- tiles: bfloat16 [512, 64, 128], P(('dom', 'edge')), may hold values from -1 to 1
- weight_edge: bfloat16 [512, 512], replicated, may hold values from -0.25 to 0.25
- weight_down: bfloat16 [64, 512], replicated, may hold values from -0.25 to 0.25
- weight_up: bfloat16 [2, 64, 512], replicated, may hold values from -0.75 to 0.75
- weight_residual: bfloat16 [1, 2, 512, 512], replicated, may hold values from -0.25 to 0.25
- weight_message: bfloat16 [512, 256], replicated, may hold values from -0.25 to 0.25
- weight_atom: bfloat16 [2, 256, 256], replicated, may hold values from -0.375 to 0.375
- weight_join: bfloat16 [1024, 512], replicated, may hold values from -0.1875 to 0.1875
Outputs:
- new_edges: bfloat16 [32768, 512], P(('dom', 'edge'))
- new_atoms: bfloat16 [1024, 256], P(('dom', 'edge'))
Inputs may be any that keep to these rules, and one draw needn't show every extreme that they name: reverse is an involution without fixed points. The reverse of a row lies on a device of the same edge index. Besides its own partition, the rows of each partition have their reverses in exactly 4 other partitions; at most 128 rows of one device have their reverses in any one other partition, and some device reaches 128.
All inputs are finite; a program needn't handle non-finite values.
Results may differ from a plain program's by a relative error of at most 0.015.
Values may be sent and summed in bfloat16 or wider, within the bound.
No kernel may reach another device: no remote copies, remote signals or barrier semaphores. Data moves between devices by JAX's collectives and lax.ppermute only.
A program may use at most 64 MiB of HBM per device.

v0:
```python
import jax
import jax.numpy as jnp
from jax import lax
from jax.sharding import PartitionSpec as P

EPA = 32


root_half = 0.7071067811865476


def product(operand, weights):
    return jnp.dot(operand, weights, preferred_element_type=jnp.float32)


def contract_first(operand, weights):
    return lax.dot_general(
        operand, weights, (((0,), (0,)), ((), ())), preferred_element_type=jnp.float32
    )


def update_atoms(summed, atom_rows, weight_atom):
    scaled = (summed * EPA ** (-0.5)).astype(jnp.bfloat16)
    middle = jax.nn.silu(product(scaled, weight_atom[0])).astype(jnp.bfloat16)
    return (atom_rows.astype(jnp.float32) + product(middle, weight_atom[1])).astype(jnp.bfloat16)


def tile_terms(tile_source, tiles, channels):
    blocks, block_len, tile_width = tiles.shape
    tile_count = tile_width // block_len
    shaped = tiles.reshape(blocks, block_len, tile_count, block_len)
    offsets = jnp.arange(block_len, dtype=jnp.int32)

    def accumulate(running, shard_piece, start_at):
        piece_len = shard_piece.shape[1]
        relative = tile_source * block_len
        columns = relative[:, :, None] + offsets[None, None, :]
        inside = (columns >= 0) & (columns < piece_len)
        picked = jnp.take(shard_piece, jnp.clip(columns, 0, piece_len - 1).reshape(-1), axis=1)
        picked = picked.reshape(channels, blocks, tile_count, block_len)
        picked = jnp.where(inside[None], picked, jnp.zeros((), shard_piece.dtype))
        return jnp.einsum("tbkj,bekj->bte", picked, shaped, preferred_element_type=jnp.float32)

    initial = jnp.zeros((blocks, channels, block_len), jnp.float32)
    return (accumulate, initial)


def body(
    edges,
    atoms,
    reverse,
    atom_index,
    tile_source,
    tiles,
    weight_edge,
    weight_down,
    weight_up,
    weight_residual,
    weight_message,
    weight_atom,
    weight_join,
):
    edge_rows = edges.shape[0]
    channels = weight_down.shape[0]
    domain_count = lax.axis_size("dom")
    shard_count = lax.axis_size("edge")
    own_domain = lax.axis_index("dom")
    capacity = edge_rows // domain_count
    hidden = jax.nn.silu(product(edges, weight_edge)).astype(jnp.bfloat16)
    narrow = jax.nn.silu(
        lax.dot_general(
            weight_down, hidden, (((1,), (1,)), ((), ())), preferred_element_type=jnp.float32
        )
    ).astype(jnp.bfloat16)
    accumulate, initial = tile_terms(tile_source, tiles, channels)
    mixed = accumulate(initial, lax.all_gather(narrow, "edge", axis=1, tiled=True), jnp.int32(0))
    trip_out = mixed.transpose(1, 0, 2).reshape(channels, edge_rows).astype(jnp.bfloat16)
    holder = reverse // (edge_rows * shard_count)
    source_row = reverse % edge_rows
    is_local = holder == own_domain
    positions = jnp.arange(edge_rows, dtype=jnp.int32)
    matching = holder[:, None] == holder[None, :]
    send_slot = jnp.sum(matching & (positions[None, :] < positions[:, None]), axis=1)
    receive_slot = jnp.sum(matching & (source_row[None, :] < source_row[:, None]), axis=1)
    target_slot = jnp.where(is_local, domain_count * capacity, holder * capacity + send_slot)
    send_index = jnp.full((domain_count * capacity,), edge_rows, jnp.int32)
    send_index = send_index.at[target_slot].set(positions, mode="drop")
    filled = send_index < edge_rows
    safe_index = jnp.minimum(send_index, edge_rows - 1)
    fetch_index = jnp.where(is_local, 0, holder * capacity + receive_slot)
    zero_value = jnp.zeros((), jnp.bfloat16)
    outgoing = jnp.where(filled[None, :], jnp.take(trip_out, safe_index, axis=1), zero_value)
    outgoing = outgoing.reshape(channels, domain_count, capacity)
    arrived = lax.all_to_all(outgoing, "dom", split_axis=1, concat_axis=1, tiled=True).reshape(
        channels, domain_count * capacity
    )
    inputs = jnp.where(
        is_local[None, :],
        jnp.take(trip_out, source_row, axis=1),
        jnp.take(arrived, fetch_index, axis=1),
    )
    mirrored = contract_first(inputs, weight_up[1]).astype(jnp.bfloat16)
    direct = contract_first(trip_out, weight_up[0])
    joined = (direct + mirrored.astype(jnp.float32)) * root_half
    edge_state = (edges.astype(jnp.float32) + joined).astype(jnp.bfloat16)
    middle = jax.nn.silu(product(edge_state, weight_residual[0, 0])).astype(jnp.bfloat16)
    branch = jax.nn.silu(product(middle, weight_residual[0, 1]))
    edge_state = ((edge_state.astype(jnp.float32) + branch) * root_half).astype(jnp.bfloat16)
    message = product(edge_state, weight_message).astype(jnp.bfloat16)
    atom_count = atoms.shape[0]
    part_atoms = atom_count * shard_count
    onehot = (atom_index[1][:, None] == jnp.arange(part_atoms, dtype=jnp.int32)[None, :]).astype(
        jnp.bfloat16
    )
    partial_value = contract_first(onehot, message)
    totals = lax.psum(partial_value.astype(jnp.bfloat16), "edge").astype(jnp.float32)
    everyone = lax.all_gather(atoms, "edge", axis=0, tiled=True)
    renewed = update_atoms(totals, everyone, weight_atom)
    own_atoms = lax.dynamic_slice_in_dim(
        renewed, lax.axis_index("edge") * atom_count, atom_count, 0
    )
    gathered = jnp.concatenate(
        [
            jnp.take(renewed, atom_index[0], axis=0),
            jnp.take(renewed, atom_index[1], axis=0),
            edge_state,
        ],
        axis=1,
    )
    update = jax.nn.silu(product(gathered, weight_join))
    new_edges = ((edge_state.astype(jnp.float32) + update) * root_half).astype(jnp.bfloat16)
    return (new_edges, own_atoms)


def solution(mesh):
    placed = (
        P(("dom", "edge"), None),
        P(("dom", "edge"), None),
        P(("dom", "edge")),
        P(None, ("dom", "edge")),
        P(("dom", "edge"), None),
        P(("dom", "edge"), None, None),
        P(),
        P(),
        P(),
        P(),
        P(),
        P(),
        P(),
    )
    return jax.shard_map(
        body,
        mesh=mesh,
        in_specs=placed,
        out_specs=(P(("dom", "edge"), None), P(("dom", "edge"), None)),
        check_vma=False,
    )
```

profile of v0, /device:TPU:0, one launch (start us, length us, event | category | flops | bytes accessed | tf_op | source)
XLA Modules:
  0.0 123.8 jit_solution(3083999997252820115)
XLA Ops:
  7.2 0.8 broadcast_compare_fusion.1
  8.0 2.3 %convert_reduce_fusion = (s32[1024]{0:T(1024)S(1)}, s32[1024]{0:T(1024)S(1)}) fusion(s32[1024]{0:T(1024)S(1)} %get-tuple-element.19, s32[1024]{0:T(1024)S(1)} %get-tuple-element.7), kind=kLoop, calls=%fused_computation.9 | loop fusion | flops 9435136 | bytes 16384 | tf_op jit(solution)/shard_map/reduce_sum | solution.py:84
  10.3 4.3 %scatter_custom_fusion = s32[1024]{0:T(1024)S(1)} fusion(s32[1024]{0:T(1024)S(1)} %get-tuple-element.15, s32[1024]{0:T(1024)S(1)} %iota.19, s32[]{:T(128)} %constant.97.clone.1), kind=kCustom, calls=%fused_computation.106 | custom fusion | bytes 4100 | tf_op jit(solution)/shard_map/scatter | solution.py:87
  14.6 0.7 broadcast_multiply_fusion
  15.7 2.6 %multiply_convert_fusion.8 = bf16[64,1024]{1,0:T(8,128)(2,1)S(1)} fusion(bf16[64,512]{1,0:T(8,128)(2,1)} %param.24, bf16[1024,512]{1,0:T(8,128)(2,1)} %param.17, bf16[512,512]{1,0:T(8,128)(2,1)} %param.23), kind=kOutput, calls=%fused_computation.55 | convolution fusion | flops 606928896 | bytes 1769472 | tf_op jit(solution)/shard_map/dot_general | solution.py:71
  18.4 17.4 %all_gather.6 = bf16[64,4096]{1,0:T(8,128)(2,1)S(1)} all-gather(bf16[64,1024]{1,0:T(8,128)(2,1)S(1)} %multiply_convert_fusion.8), channel_id=1, replica_groups=mesh['dom'=8,'edge'=4] {'edge'}, dimensions={1}, use_global_device_ids=true | all-gather | bytes 655360 | tf_op jit(solution)/shard_map/all_gather | solution.py:76
  35.7 0.5 copy.48
  36.2 6.2 %gather_fusion = bf16[2048,64]{1,0:T(8,128)(2,1)S(1)} fusion(bf16[64,4096]{0,1:T(8,128)(2,1)S(1)} %copy.48, s32[2048]{0:T(1024)S(1)} %broadcast_clamp_fusion), kind=kCustom, calls=%fused_computation.5 | custom fusion | bytes 532480 | tf_op jit(solution)/shard_map/jit(_take)/gather | solution.py:39
  42.4 0.3 copy.49
  42.7 0.7 copy-done.2
  43.6 0.3 fusion.8
  44.5 3.2 %gather_fusion.2 = bf16[1024,64]{1,0:T(8,128)(2,1)S(1)} fusion(bf16[64,1024]{0,1:T(8,128)(2,1)S(1)} %copy.52, s32[1024]{0:T(1024)S(1)} %fusion.62), kind=kCustom, calls=%fused_computation.2.clone | custom fusion | bytes 266240 | tf_op jit(solution)/shard_map/jit(_take)/gather | solution.py:92
  47.7 0.3 bitcast_select_fusion.2
  48.1 0.8 copy.54
  48.9 3.7 %all-to-all-start = ((bf16[64,8,128]{2,0,1:T(8,128)(2,1)}), bf16[64,8,128]{2,0,1:T(8,128)(2,1)S(1)}, u32[]{:S(2)}, u32[]{:S(2)}) async-start(bf16[64,8,128]{2,0,1:T(8,128)(2,1)} %copy.54), calls=%async_computation | async-start | bytes 262144 | tf_op jit(solution)/shard_map/all_to_all | solution.py:94
  52.7 3.2 %gather_fusion.1 = bf16[1024,64]{1,0:T(8,128)(2,1)S(1)} fusion(bf16[64,1024]{0,1:T(8,128)(2,1)S(1)} %copy.52, s32[1024]{0:T(1024)S(1)} %fusion.59), kind=kCustom, calls=%fused_computation.clone | custom fusion | bytes 266240 | tf_op jit(solution)/shard_map/jit(_take)/gather | solution.py:99
  55.9 2.2 %all-to-all-done = bf16[64,8,128]{2,0,1:T(8,128)(2,1)S(1)} async-done(((bf16[64,8,128]{2,0,1:T(8,128)(2,1)}), bf16[64,8,128]{2,0,1:T(8,128)(2,1)S(1)}, u32[]{:S(2)}, u32[]{:S(2)}) %all-to-all-start) | async-done | bytes 131104 | tf_op jit(solution)/shard_map/all_to_all | solution.py:94
  58.3 3.2 %gather_fusion.3 = bf16[1024,64]{1,0:T(8,128)(2,1)S(1)} fusion(bf16[64,1024]{0,1:T(8,128)(2,1)S(1)} %bitcast.66, s32[1024]{0:T(1024)S(1)} %get-tuple-element.14), kind=kCustom, calls=%fused_computation.3.clone | custom fusion | bytes 266240 | tf_op jit(solution)/shard_map/jit(_take)/gather | solution.py:100
  61.5 1.1 convolution_convert_fusion
  62.7 0.6 add_convert_fusion
  63.3 0.6 copy-done.6
  64.0 2.7 %multiply_convert_fusion.1 = bf16[1024,512]{1,0:T(8,128)(2,1)} fusion(bf16[1024,512]{1,0:T(8,128)(2,1)S(1)} %add_convert_fusion, bf16[1,2,512,512]{3,2,1,0:T(8,128)(2,1)S(1)} %copy-done.6), kind=kOutput, calls=%fused_computation.19 | convolution fusion | flops 1080557568 | bytes 4194304 | tf_op jit(solution)/shard_map/dot_general | solution.py:13
  66.7 2.6 %fusion.9 = bf16[128,256]{1,0:T(8,128)(2,1)} fusion(bf16[1024,512]{1,0:T(8,128)(2,1)} %multiply_convert_fusion.1, bf16[512,256]{1,0:T(8,128)(2,1)} %param.27, s32[1024]{0:T(1024)S(1)} %bitcast.70), kind=kOutput, calls=%fused_computation.31 | convolution fusion | flops 335970304 | bytes 1380352 | tf_op jit(solution)/shard_map/dot_general | solution.py:17
  69.3 13.6 %all_gather.7 = bf16[128,256]{1,0:T(8,128)(2,1)S(1)} all-gather(bf16[32,256]{1,0:T(8,128)(2,1)S(1)} %copy-done.4), channel_id=1, replica_groups=mesh['dom'=8,'edge'=4] {'edge'}, dimensions={0}, use_global_device_ids=true | all-gather | bytes 81920 | tf_op jit(solution)/shard_map/all_gather | solution.py:117
  82.9 20.6 %all-reduce.2.cloned.1.call-done = bf16[128,256]{1,0:T(8,128)(2,1)} async-done(((bf16[128,256]{1,0:T(8,128)(2,1)}), bf16[128,256]{1,0:T(8,128)(2,1)}) %all-reduce.2.cloned.1.call-update) | async-done | bytes 65552 | tf_op jit(solution)/shard_map/psum | solution.py:116
  103.5 1.2 fusion.10
  104.7 0.6 constant_dynamic-slice_fusion
  105.3 3.9 %gather_fusion.5 = bf16[1024,256]{1,0:T(8,128)(2,1)S(1)} fusion(bf16[128,256]{1,0:T(8,128)(2,1)S(1)} %fusion.10, s32[1024]{0:T(1024)S(1)} %fusion.61), kind=kCustom, calls=%fused_computation.4.clone | custom fusion | bytes 1052672 | tf_op jit(solution)/shard_map/jit(_take)/gather | solution.py:125
  109.2 3.9 %gather_fusion.4 = bf16[1024,256]{1,0:T(8,128)(2,1)S(1)} fusion(bf16[128,256]{1,0:T(8,128)(2,1)S(1)} %fusion.10, s32[1024]{0:T(1024)S(1)} %fusion.60), kind=kCustom, calls=%fused_computation.1.clone | custom fusion | bytes 1052672 | tf_op jit(solution)/shard_map/jit(_take)/gather | solution.py:124
  113.2 0.7 broadcast_select_fusion
  113.9 0.5 copy-done.8
  114.4 2.6 %multiply_convert_fusion = bf16[1024,512]{1,0:T(8,128)(2,1)} fusion(bf16[1024,512]{1,0:T(8,128)(2,1)S(1)} %copy-done.8, bf16[1024,512]{1,0:T(8,128)(2,1)S(1)} %copy-done, bf16[1024,256]{1,0:T(8,128)(2,1)S(1)} %get-tuple-element.20, bf16[1024,256]{1,0:T(8,128)(2,1)S(1)} %get-tuple-element.21), kind=kOutput, calls=%fused_computation.18 | convolution fusion | flops 1084227584 | bytes 4194304 | tf_op jit(solution)/shard_map/dot_general | solution.py:13
  (39 shorter events, 1.7 us)
Async XLA Ops:
  7.2 106.8 %copy-start = (bf16[1024,512]{1,0:T(8,128)(2,1)S(1)}, bf16[1024,512]{1,0:T(8,128)(2,1)}, u32[]{:S(2)}) copy-start(bf16[1024,512]{1,0:T(8,128)(2,1)} %param.29) | copy-start | bytes 3145732
  42.4 1.0 copy-start.2
  44.5 8.2 %copy-start.5 = (s32[2,1024]{1,0:T(2,128)S(1)}, s32[2,1024]{1,0:T(2,128)}, u32[]{:S(2)}) copy-start(s32[2,1024]{1,0:T(2,128)} %param.20) | copy-start | bytes 24580
  48.9 9.2 %all-to-all-start = ((bf16[64,8,128]{2,0,1:T(8,128)(2,1)}), bf16[64,8,128]{2,0,1:T(8,128)(2,1)S(1)}, u32[]{:S(2)}, u32[]{:S(2)}) async-start(bf16[64,8,128]{2,0,1:T(8,128)(2,1)} %copy.54), calls=%async_computation | async-start | bytes 262144 | tf_op jit(solution)/shard_map/all_to_all | solution.py:94
  52.6 50.9 %all-reduce.2.cloned.1.call-start = ((), (), s32[]{:S(2)}) async-start(), calls=%async_computation.1 | async-start | bytes 131072 | tf_op jit(solution)/shard_map/psum | solution.py:116
  55.9 5.6 %copy-start.3 = (bf16[2,64,512]{2,1,0:T(8,128)(2,1)S(1)}, bf16[2,64,512]{2,1,0:T(8,128)(2,1)}, u32[]{:S(2)}) copy-start(bf16[2,64,512]{2,1,0:T(8,128)(2,1)} %param.25) | copy-start | bytes 393220
  61.5 1.2 copy-start.1
  62.7 1.2 copy-start.6
  66.7 2.7 %copy-start.4 = (bf16[32,256]{1,0:T(8,128)(2,1)S(1)}, bf16[32,256]{1,0:T(8,128)(2,1)}, u32[]{:S(2)}) copy-start(bf16[32,256]{1,0:T(8,128)(2,1)} %param.18) | copy-start | bytes 49156
  66.7 36.8 %copy-start.7 = (bf16[2,256,256]{2,1,0:T(8,128)(2,1)S(1)}, bf16[2,256,256]{2,1,0:T(8,128)(2,1)}, u32[]{:S(2)}) copy-start(bf16[2,256,256]{2,1,0:T(8,128)(2,1)} %param.28) | copy-start | bytes 786436
  113.2 1.2 copy-start.8
Sparse Core Ops, SparseCore 0:
  69.4 34.0 all-reduce.1
where the time goes:
time: 124 us
  local copies, waits for them, and re-layouts  33.2 us (27%)
  blocking collectives  31 us (25%)
  waiting for transfers between devices  22.7 us (18%)
  between operations  14.4 us (12%)
  matrix products  13.6 us (11%)
  other arithmetic  5.11 us (4%)
  starting transfers between devices  3.74 us (3%)
    psum x1, waiting for transfers between devices, body(): lax.psum(partial_value.astype(jnp.bfloat16), 'edge').astype(jnp.float32)  20.6 us
    all_gather x1, blocking collectives, body(): lax.all_gather(narrow, 'edge', axis=1, tiled=True)  17.4 us
    all_gather x1, blocking collectives, body(): everyone = lax.all_gather(atoms, 'edge', axis=0, tiled=True)  13.6 us
    gather x2, local copies, waits for them, and re-layouts, accumulate(): jnp.take(shard_piece, jnp.clip(columns, 0, piece_len - 1).reshape(-1), ax...  6.46 us
    dot_general x3, matrix products, product(): return jnp.dot(operand, weights, preferred_element_type=jnp.float32)  6.42 us
    scatter x1, local copies, waits for them, and re-layouts, body(): send_index = send_index.at[target_slot].set(positions, mode='drop')  4.31 us
    dot_general x3, matrix products, contract_first(): lax.dot_general(operand, weights, (((0,), (0,)), ((), ())), preferred_ele...  4.25 us
    gather x1, local copies, waits for them, and re-layouts, body(): jnp.take(renewed, atom_index[0], axis=0)  3.94 us
  transfers between devices with their start and end apart: 2, of which 2 were waited for; matrix products, arithmetic and copies ran while one was open for 3% of the time, Pallas kernels for 0%

commit v1 on v0

v1 whole, which is shorter than its diff:
```python
import functools

import jax
import jax.numpy as jnp
from jax import lax
from jax.experimental import pallas as pl
from jax.experimental.pallas import tpu as pltpu
from jax.sharding import PartitionSpec as P

root_half = 0.7071067811865476
MIB = 1 << 20
CHUNK = 256


def product(operand, weights):
    return jnp.dot(operand, weights, preferred_element_type=jnp.float32)


def silu(value):
    halved = 0.5 * value
    return halved + halved * jnp.tanh(halved)


def as_column(row):
    wide = jnp.broadcast_to(row.astype(jnp.float32), (8, row.shape[1]))
    return jnp.transpose(wide)[:, :1].astype(jnp.int32)


def row_chunks(rows):
    step = min(CHUNK, rows)
    return [slice(at, at + step) for at in range(0, rows, step)]


def call(kernel, outs, args, *, smem=(), scratch=(), flops=0, nbytes=0, limit=24):
    in_specs = [
        pl.BlockSpec(memory_space=pltpu.SMEM if at in smem else pltpu.VMEM)
        for at in range(len(args))
    ]
    return pl.pallas_call(
        kernel,
        out_shape=outs,
        in_specs=in_specs,
        out_specs=jax.tree.map(lambda _: pl.BlockSpec(memory_space=pltpu.VMEM), outs),
        scratch_shapes=list(scratch),
        compiler_params=pltpu.CompilerParams(vmem_limit_bytes=limit * MIB),
        cost_estimate=pl.CostEstimate(flops=flops, bytes_accessed=nbytes, transcendentals=0),
    )(*args)


def shaped(shape, dtype=jnp.bfloat16):
    return jax.ShapeDtypeStruct(shape, dtype)


def narrow_kernel(edges_ref, weight_ref, down_ref, out_ref):
    half = edges_ref.shape[0] // 2
    for rows in row_chunks(half):
        pieces = []
        for base in (0, half):
            piece = edges_ref[base + rows.start : base + rows.stop, :]
            hidden = silu(product(piece, weight_ref[...])).astype(jnp.bfloat16)
            pieces.append(
                silu(
                    lax.dot_general(
                        hidden,
                        down_ref[...],
                        (((1,), (1,)), ((), ())),
                        preferred_element_type=jnp.float32,
                    )
                )
            )
        out_ref[rows, :] = jnp.concatenate(pieces, axis=1).astype(jnp.bfloat16)


def index_kernel(domains, shards, reverse_ref, send_ref, fetch_ref, local_ref):
    rows = reverse_ref.shape[1]
    capacity = rows // domains
    half = capacity // 2
    slots = (domains - 1) * capacity
    own = lax.axis_index("dom")
    reverse = reverse_ref[...]
    holder = reverse // (rows * shards)
    source_row = lax.rem(reverse, rows)
    partner = holder ^ own
    source_column = as_column(source_row)
    member = (lax.broadcasted_iota(jnp.int32, (domains, rows), 0) == partner).astype(jnp.bfloat16)
    before = (
        lax.broadcasted_iota(jnp.int32, (rows, rows), 0)
        < lax.broadcasted_iota(jnp.int32, (rows, rows), 1)
    ).astype(jnp.bfloat16)
    place = jnp.sum(
        product(member, before) * member.astype(jnp.float32), axis=0, keepdims=True
    ).astype(jnp.int32)
    earlier = (source_column < source_row).astype(jnp.bfloat16)
    far_place = jnp.sum(
        product(member, earlier) * member.astype(jnp.float32), axis=0, keepdims=True
    ).astype(jnp.int32)

    def slot_of(at):
        part = (at >= half).astype(jnp.int32)
        slot = part * (slots // 2) + (partner - 1) * half + at - part * half
        return jnp.where(partner == 0, -1, slot)

    send_slot = slot_of(place)
    send_ref[...] = (
        lax.broadcasted_iota(jnp.int32, (slots, rows), 0) == send_slot
    ).astype(jnp.bfloat16)
    fetch_column = as_column(slot_of(far_place))
    fetch_ref[...] = (
        lax.broadcasted_iota(jnp.int32, (rows, slots), 1) == fetch_column
    ).astype(jnp.bfloat16)
    local_column = as_column(jnp.where(partner == 0, source_row, -1))
    local_ref[...] = (
        lax.broadcasted_iota(jnp.int32, (rows, rows), 1) == local_column
    ).astype(jnp.bfloat16)


def mix_kernel(shards, *refs):
    source_ref, tiles_ref = refs[:2]
    parts = refs[2 : 2 + shards]
    send_ref, trip_ref = refs[2 + shards : 4 + shards]
    out_refs = refs[4 + shards : -1]
    held_ref = refs[-1]
    blocks, block_len, width = tiles_ref.shape
    count = width // block_len
    lines = parts[0].shape[0]
    me = lax.axis_index("edge")
    for at in range(shards):
        held_ref[at * lines : (at + 1) * lines, :] = parts[at][...]
    half_blocks = blocks // 2
    channels = trip_ref.shape[1]
    for block in range(blocks):
        picks = []
        for tile in range(count):
            source = source_ref[block, tile]
            shard = source // blocks
            within = source - shard * blocks
            upper = within // half_blocks
            near = lax.rem(shard - me + shards, shards)
            start = near * lines + (within - upper * half_blocks) * block_len
            rows = held_ref[pl.ds(pl.multiple_of(start, block_len), block_len), :]
            picks.append(jnp.where(upper == 1, rows[:, channels:], rows[:, :channels]))
        mixed = product(tiles_ref[block], jnp.concatenate(picks, axis=0))
        trip_ref[block * block_len : (block + 1) * block_len, :] = mixed.astype(jnp.bfloat16)
    half_slots = send_ref.shape[0] // 2
    low = product(send_ref[:half_slots, :], trip_ref[...])
    high = product(send_ref[half_slots:, :], trip_ref[...])
    packed = jnp.concatenate([low, high], axis=1).astype(jnp.bfloat16)
    each = half_slots // len(out_refs)
    for at, out_ref in enumerate(out_refs):
        out_ref[...] = packed[at * each : (at + 1) * each, :]


def base_kernel(edges_ref, trip_ref, local_ref, up_ref, out_ref):
    channels = trip_ref.shape[1]
    for rows in row_chunks(edges_ref.shape[0]):
        picked = product(local_ref[rows, :], trip_ref[...]).astype(jnp.bfloat16)
        joined = product(trip_ref[rows, :], up_ref[0]) + product(picked, up_ref[1])
        out_ref[rows, :] = edges_ref[rows, :].astype(jnp.float32) + joined * root_half


def state_kernel(partners, *refs):
    base_ref, fetch_ref, up_ref, residual_ref, message_ref, index_ref = refs[:6]
    arrived = refs[6 : 6 + partners]
    state_ref, sums_ref, slots_ref = refs[6 + partners :]
    channels = up_ref.shape[1]
    each = arrived[0].shape[0]
    for at in range(partners):
        piece = arrived[at][...]
        slots_ref[at * each : (at + 1) * each, :] = piece[:, :channels]
        slots_ref[(partners + at) * each : (partners + at + 1) * each, :] = piece[:, channels:]
    for rows in row_chunks(base_ref.shape[0]):
        picked = product(fetch_ref[rows, :], slots_ref[...]).astype(jnp.bfloat16)
        state = (base_ref[rows, :] + product(picked, up_ref[1]) * root_half).astype(jnp.bfloat16)
        for layer in range(residual_ref.shape[0]):
            middle = silu(product(state, residual_ref[layer, 0])).astype(jnp.bfloat16)
            branch = silu(product(middle, residual_ref[layer, 1]))
            state = ((state.astype(jnp.float32) + branch) * root_half).astype(jnp.bfloat16)
        state_ref[rows, :] = state
    part_atoms = sums_ref.shape[0]
    shards = lax.axis_size("edge")
    near = near_atoms(index_ref[1:2, :], part_atoms, shards)
    chosen = (
        lax.broadcasted_iota(jnp.int32, (part_atoms, near.shape[1]), 0) == near
    ).astype(jnp.bfloat16)
    gathered = product(chosen, state_ref[...]).astype(jnp.bfloat16)
    sums_ref[...] = product(gathered, message_ref[...]).astype(jnp.bfloat16)


def near_atoms(index, part_atoms, shards):
    first = lax.axis_index("edge") * (part_atoms // shards)
    shifted = index - first
    return jnp.where(shifted < 0, shifted + part_atoms, shifted)


def side_kernel(shards, part_atoms, state_ref, join_ref, index_ref, out_ref, chosen_ref):
    width = join_ref.shape[0] - state_ref.shape[1]
    for rows in row_chunks(state_ref.shape[0]):
        out_ref[rows, :] = product(state_ref[rows, :], join_ref[width:, :])
    index = near_atoms(index_ref[...], part_atoms, shards)
    for end in range(2):
        column = as_column(index[end : end + 1, :])
        chosen_ref[:, end * part_atoms : (end + 1) * part_atoms] = (
            lax.broadcasted_iota(jnp.int32, (column.shape[0], part_atoms), 1) == column
        ).astype(jnp.bfloat16)


def final_kernel(shards, scale, *refs):
    sums = refs[:shards]
    atoms = refs[shards : 2 * shards]
    weight_ref, join_ref, state_ref, side_ref, chosen_ref = refs[2 * shards : 2 * shards + 5]
    edges_ref, own_ref, table_ref = refs[2 * shards + 5 :]
    count = atoms[0].shape[0]
    part_atoms = count * shards
    total = sums[0][...].astype(jnp.float32)
    for at in range(1, shards):
        piece = sums[at][...].astype(jnp.float32)
        cut = part_atoms - at * count
        total = total + jnp.concatenate([piece[cut:], piece[:cut]], axis=0)
    everyone = jnp.concatenate([ref[...].astype(jnp.float32) for ref in atoms], axis=0)
    scaled = (total * scale).astype(jnp.bfloat16)
    middle = silu(product(scaled, weight_ref[0])).astype(jnp.bfloat16)
    renewed = (everyone + product(middle, weight_ref[1])).astype(jnp.bfloat16)
    own_ref[...] = renewed[:count, :]
    width = renewed.shape[1]
    for end in range(2):
        table_ref[end * part_atoms : (end + 1) * part_atoms, :] = product(
            renewed, join_ref[end * width : (end + 1) * width, :]
        ).astype(jnp.bfloat16)
    for rows in row_chunks(state_ref.shape[0]):
        update = silu(product(chosen_ref[rows, :], table_ref[...]) + side_ref[rows, :])
        state = state_ref[rows, :].astype(jnp.float32)
        edges_ref[rows, :] = ((state + update) * root_half).astype(jnp.bfloat16)


def from_next(value, shards):
    return [
        lax.ppermute(value, "edge", [((at + by) % shards, at) for at in range(shards)])
        for by in range(1, shards)
    ]


def body(
    edges,
    atoms,
    reverse,
    atom_index,
    tile_source,
    tiles,
    weight_edge,
    weight_down,
    weight_up,
    weight_residual,
    weight_message,
    weight_atom,
    weight_join,
):
    rows, wide = edges.shape
    channels = weight_down.shape[0]
    domains = lax.axis_size("dom")
    shards = lax.axis_size("edge")
    count, atom_wide = atoms.shape
    part_atoms = count * shards
    capacity = rows // domains
    partners = domains - 1
    slots = partners * capacity
    packed = (rows // 2, 2 * channels)

    atom_parts = [atoms] + from_next(atoms, shards)
    narrow = call(
        narrow_kernel,
        shaped(packed),
        (edges, weight_edge, weight_down),
        flops=2 * rows * wide * (wide + channels),
        nbytes=2 * (rows * wide + wide * wide),
    )
    narrow_parts = [narrow] + from_next(narrow, shards)
    send, fetch, local = call(
        functools.partial(index_kernel, domains, shards),
        (shaped((slots, rows)), shaped((rows, slots)), shaped((rows, rows))),
        (reverse.reshape(1, rows),),
        flops=40 * rows * rows,
        nbytes=6 * rows * rows,
    )
    trip_out, *outgoing = call(
        functools.partial(mix_kernel, shards),
        (shaped((rows, channels)),) + (shaped((capacity // 2, 2 * channels)),) * partners,
        (tile_source, tiles, *narrow_parts, send),
        smem=(0,),
        scratch=[pltpu.VMEM((shards * rows // 2, 2 * channels), jnp.bfloat16)],
        flops=2 * rows * rows * channels,
        nbytes=2 * rows * rows,
    )
    arrived = [
        lax.ppermute(outgoing[by - 1], "dom", [(at, at ^ by) for at in range(domains)])
        for by in range(1, domains)
    ]
    base = call(
        base_kernel,
        shaped((rows, wide), jnp.float32),
        (edges, trip_out, local, weight_up),
        flops=2 * rows * channels * (rows + 2 * wide),
        nbytes=2 * rows * rows + 6 * rows * wide,
    )
    state, sums = call(
        functools.partial(state_kernel, partners),
        (shaped((rows, wide)), shaped((part_atoms, atom_wide))),
        (base, fetch, weight_up, weight_residual, weight_message, atom_index, *arrived),
        scratch=[pltpu.VMEM((slots, channels), jnp.bfloat16)],
        flops=4 * rows * wide * wide,
        nbytes=8 * rows * wide,
    )
    sums_parts = [sums] + from_next(sums, shards)
    side, chosen = call(
        functools.partial(side_kernel, shards, part_atoms),
        (shaped((rows, wide), jnp.float32), shaped((rows, 2 * part_atoms))),
        (state, weight_join, atom_index),
        flops=2 * rows * wide * wide,
        nbytes=8 * rows * wide,
    )
    return call(
        functools.partial(final_kernel, shards, (rows // count) ** -0.5),
        (shaped((rows, wide)), shaped((count, atom_wide))),
        (*sums_parts, *atom_parts, weight_atom, weight_join, state, side, chosen),
        scratch=[pltpu.VMEM((2 * part_atoms, wide), jnp.bfloat16)],
        flops=4 * rows * part_atoms * wide,
        nbytes=8 * rows * wide,
    )


def solution(mesh):
    split = P(("dom", "edge"))
    placed = (
        P(("dom", "edge"), None),
        P(("dom", "edge"), None),
        split,
        P(None, ("dom", "edge")),
        P(("dom", "edge"), None),
        P(("dom", "edge"), None, None),
    ) + (P(),) * 7
    return jax.shard_map(
        body,
        mesh=mesh,
        in_specs=placed,
        out_specs=(P(("dom", "edge"), None), P(("dom", "edge"), None)),
        check_vma=False,
    )
```

time: 124 us -> 50.7 us (0.41)
  blocking collectives: 31 us -> 0 us
  local copies, waits for them, and re-layouts: 33.2 us -> 3.23 us
  starting transfers between devices: 3.74 us -> 21.2 us
  Pallas kernels: 0 us -> 14.5 us
  between operations: 14.4 us -> 0.79 us
  matrix products: 13.6 us -> 0 us
  waiting for transfers between devices: 22.7 us -> 10.7 us
  other arithmetic: 5.11 us -> 0 us
    all_gather x2 -> x0, blocking collectives: 31 us -> none  [the longest x1 17.4 us: body(): lax.all_gather(narrow, 'edge', axis=1, tiled=True)]
    gather x7 -> x0, local copies, waits for them, and re-layouts: 24 us -> none  [the longest x2 6.46 us: accumulate(): jnp.take(shard_piece, jnp.clip(columns, 0, piece_len - 1).reshape(-1), ax...]
    ppermute x0 -> x16, starting transfers between devices: none -> 21.2 us  [the longest x9 14.9 us: from_next(): lax.ppermute(value, 'edge', [((at + by) % shards, at) for at in range(sha...]
    psum x1 -> x0, waiting for transfers between devices: 20.6 us -> none  [body(): lax.psum(partial_value.astype(jnp.bfloat16), 'edge').astype(jnp.float32)]
    pallas_call x0 -> x7, Pallas kernels: none -> 14.5 us  [call(): pl.pallas_call(kernel, out_shape=outs, in_specs=in_specs, out_specs=jax.t...]
    dot_general x8 -> x0, matrix products: 13.6 us -> none  [the longest x3 6.42 us: product(): return jnp.dot(operand, weights, preferred_element_type=jnp.float32)]
    ppermute x0 -> x16, waiting for transfers between devices: none -> 10.7 us  [the longest x9 10.2 us: from_next(): lax.ppermute(value, 'edge', [((at + by) % shards, at) for at in range(sha...]
    scatter x1 -> x0, local copies, waits for them, and re-layouts: 4.31 us -> none  [body(): send_index = send_index.at[target_slot].set(positions, mode='drop')]
  transfers between devices with their start and end apart: 2 -> 16, of which waited for: 2 -> 5; matrix products, arithmetic and copies ran while one was open for 3% -> 0% of each run, Pallas kernels for 0% -> 17%
where the time goes in v1:
time: 50.7 us; the launch traced here: 50.4 us
  starting transfers between devices  21.2 us (42%)
  Pallas kernels  14.5 us (29%)
  waiting for transfers between devices  10.7 us (21%)
  local copies, waits for them, and re-layouts  3.23 us (6%)
  between operations  0.79 us (2%)
    ppermute x9, starting transfers between devices, from_next(): lax.ppermute(value, 'edge', [((at + by) % shards, at) for at in range(sha...  14.9 us
    pallas_call x7, Pallas kernels, call(): pl.pallas_call(kernel, out_shape=outs, in_specs=in_specs, out_specs=jax.t...  14.5 us
    ppermute x9, waiting for transfers between devices, from_next(): lax.ppermute(value, 'edge', [((at + by) % shards, at) for at in range(sha...  10.2 us
    ppermute x7, starting transfers between devices, body(): lax.ppermute(outgoing[by - 1], 'dom', [(at, at ^ by) for at in range(doma...  6.32 us
    unnamed x29, local copies, waits for them, and re-layouts  3.23 us
  transfers between devices with their start and end apart: 16, of which 5 were waited for; matrix products, arithmetic and copies ran while one was open for 0% of the time, Pallas kernels for 17%

profile of v1, /device:TPU:0, one launch (start us, length us, event | category | flops | bytes accessed | tf_op | source)
XLA Modules:
  0.0 50.4 jit_solution(9660933267978059012)
XLA Ops:
  0.6 1.2 %copy-done.1 = bf16[1024,512]{1,0:T(8,128)(2,1)S(1)} copy-done((bf16[1024,512]{1,0:T(8,128)(2,1)S(1)}, bf16[1024,512]{1,0:T(8,128)(2,1)}, u32[]{:S(2)}) %copy-start.1) | copy-done | bytes 1048600
  1.9 1.0 %copy-done.10 = bf16[512,512]{1,0:T(8,128)(2,1)S(1)} copy-done((bf16[512,512]{1,0:T(8,128)(2,1)S(1)}, bf16[512,512]{1,0:T(8,128)(2,1)}, u32[]{:S(2)}) %copy-start.10) | copy-done | bytes 524312
  2.9 0.8 %copy-done.11 = bf16[64,512]{1,0:T(8,128)(2,1)S(1)} copy-done((bf16[64,512]{1,0:T(8,128)(2,1)S(1)}, bf16[64,512]{1,0:T(8,128)(2,1)}, u32[]{:S(2)}) %copy-start.11) | copy-done | bytes 65560
  3.8 1.4 %shard_map.140.refs_2_ = bf16[512,128]{1,0:T(8,128)(2,1)S(1)} custom-call(bf16[1024,512]{1,0:T(8,128)(2,1)S(1)} %copy-done.1, bf16[512,512]{1,0:T(8,128)(2,1)S(1)} %copy-done.10, bf16[64,512]{1,0:T(8,128)(2,1)S(1)} %copy-done.11), custom_call_target="tpu_custom_call" | custom-call | flops 603979776 | bytes 1572864 | tf_op jit(solution)/shard_map/pallas_call | solution.py:39
  5.2 5.1 %collective-permute-start = (bf16[512,128]{1,0:T(8,128)(2,1)S(1)}, bf16[512,128]{1,0:T(8,128)(2,1)S(1)}, u32[]{:S(2)}, u32[]{:S(2)}) collective-permute-start(bf16[512,128]{1,0:T(8,128)(2,1)S(1)} %shard_map.140.refs_2_), channel_id=1, source_target_pairs={{1,0},{2,1},{3,2},{0,3},{5,4},{6,5},{7,6},{4,7},{9,8},{10,9},{11,1... | collective-permute-start | bytes 393224 | tf_op jit(solution)/shard_map/ppermute | solution.py:237
  10.3 1.0 %collective-permute-start.2 = (bf16[512,128]{1,0:T(8,128)(2,1)S(1)}, bf16[512,128]{1,0:T(8,128)(2,1)S(1)}, u32[]{:S(2)}, u32[]{:S(2)}) collective-permute-start(bf16[512,128]{1,0:T(8,128)(2,1)S(1)} %shard_map.140.refs_2_), channel_id=1, source_target_pairs={{3,0},{0,1},{1,2},{2,3},{7,4},{4,5},{5,6},{6,7},{11,8},{8,9},{9,10... | collective-permute-start | bytes 393224 | tf_op jit(solution)/shard_map/ppermute | solution.py:237
  11.3 0.1 copy.15.refs_0_
  11.4 2.6 %shard_map.141 = (bf16[896,1024]{1,0:T(8,128)(2,1)S(1)}, bf16[1024,896]{1,0:T(8,128)(2,1)S(1)}, bf16[1024,1024]{1,0:T(8,128)(2,1)S(1)}) custom-call(s32[1,1024]{1,0:T(1,128)S(1)} %bitcast.1), custom_call_target="tpu_custom_call" | custom-call | flops 41943040 | bytes 6291456 | tf_op jit(solution)/shard_map/pallas_call | solution.py:39
  14.0 0.2 collective-permute-done.refs_3_
  14.2 7.3 %collective-permute-done.1.refs_4_ = bf16[512,128]{1,0:T(8,128)(2,1)S(1)} collective-permute-done((bf16[512,128]{1,0:T(8,128)(2,1)S(1)}, bf16[512,128]{1,0:T(8,128)(2,1)S(1)}, u32[]{:S(2)}, u32[]{:S(2)}) %collective-permute-start.1) | collective-permute-done | bytes 131104 | tf_op jit(solution)/shard_map/ppermute | solution.py:237
  21.5 2.0 %shard_map.142 = (bf16[1024,64]{1,0:T(8,128)(2,1)S(1)}, bf16[64,128]{1,0:T(8,128)(2,1)S(1)}, bf16[64,128]{1,0:T(8,128)(2,1)S(1)}, bf16[64,128]{1,0:T(8,128)(2,1)...) custom-call(s32[16,2]{1,0:T(8,128)S(1)} %copy.15.refs_0_, ...), custom_call_target="tpu_custom_call" | custom-call | flops 134217728 | bytes 2097152 | tf_op jit(solution)/shard_map/pallas_call | solution.py:39
  23.5 0.1 collective-permute-start.3
  23.6 1.6 %collective-permute-start.4 = (bf16[64,128]{1,0:T(8,128)(2,1)S(1)}, bf16[64,128]{1,0:T(8,128)(2,1)S(1)}, u32[]{:S(2)}, u32[]{:S(2)}) collective-permute-start(bf16[64,128]{1,0:T(8,128)(2,1)S(1)} %get-tuple-element.22), channel_id=1, source_target_pairs={{0,8},{4,12},{8,0},{12,4},{16,24},{20,28},{24,16},{28,20},{1,9},{5... | collective-permute-start | bytes 49160 | tf_op jit(solution)/shard_map/ppermute | solution.py:294
  25.1 0.3 collective-permute-start.5
  25.4 1.5 %collective-permute-start.6 = (bf16[64,128]{1,0:T(8,128)(2,1)S(1)}, bf16[64,128]{1,0:T(8,128)(2,1)S(1)}, u32[]{:S(2)}, u32[]{:S(2)}) collective-permute-start(bf16[64,128]{1,0:T(8,128)(2,1)S(1)} %get-tuple-element.24), channel_id=1, source_target_pairs={{0,16},{4,20},{8,24},{12,28},{16,0},{20,4},{24,8},{28,12},{1,17},{... | collective-permute-start | bytes 49160 | tf_op jit(solution)/shard_map/ppermute | solution.py:294
  27.0 0.2 collective-permute-start.7
  27.1 2.5 %collective-permute-start.8 = (bf16[64,128]{1,0:T(8,128)(2,1)S(1)}, bf16[64,128]{1,0:T(8,128)(2,1)S(1)}, u32[]{:S(2)}, u32[]{:S(2)}) collective-permute-start(bf16[64,128]{1,0:T(8,128)(2,1)S(1)} %get-tuple-element.26), channel_id=1, source_target_pairs={{0,24},{4,28},{8,16},{12,20},{16,8},{20,12},{24,0},{28,4},{1,25},{... | collective-permute-start | bytes 49160 | tf_op jit(solution)/shard_map/ppermute | solution.py:294
  29.6 0.2 collective-permute-start.9
  29.8 0.0 copy-start.6
  29.9 1.6 %shard_map.143.refs_0_ = f32[1024,512]{1,0:T(8,128)S(1)} custom-call(bf16[1024,512]{1,0:T(8,128)(2,1)S(1)} %copy-done.2, bf16[1024,64]{1,0:T(8,128)(2,1)S(1)} %get-tuple-element.18.trip_ref, bf16[1024,1024]{1,0:T(8,128)(2,1)S(1)} %get-tuple-element.19.local_ref, bf16[2,64,512]{2,1,0:T(8,128)(2,1)S(1)} %copy-done.4), custom_call_target="tpu_custom_call" | custom-call | flops 268435456 | bytes 5242880 | tf_op jit(solution)/shard_map/pallas_call | solution.py:39
  31.5 1.7 %collective-permute-start.13 = (bf16[32,256]{1,0:T(8,128)(2,1)S(1)}, bf16[32,256]{1,0:T(8,128)(2,1)S(1)}, u32[]{:S(2)}, u32[]{:S(2)}) collective-permute-start(bf16[32,256]{1,0:T(8,128)(2,1)S(1)} %copy-done.9), channel_id=1, source_target_pairs={{1,0},{2,1},{3,2},{0,3},{5,4},{6,5},{7,6},{4,7},{9,8},{10,9},{11,1... | collective-permute-start | bytes 49160 | tf_op jit(solution)/shard_map/ppermute | solution.py:237
  33.2 0.5 collective-permute-done.9.refs_12_
  33.7 3.8 %shard_map.144 = (bf16[1024,512]{1,0:T(8,128)(2,1)S(1)}, bf16[128,256]{1,0:T(8,128)(2,1)S(1)}) custom-call(f32[1024,512]{1,0:T(8,128)S(1)} %shard_map.143.refs_0_, bf16[1024,896]{1,0:T(8,128)(2,1)S(1)} %get-tuple-element.20.refs_1_, bf16[2,64,512]{2,1,0:T(8,128)(2,1)S(1)} %copy-done.4, bf16[1,2,512,512]{3,2,1,0:T(8,128)(2,1)S(1)} %copy-done.3, ...), custom_call_target="tpu_custom_call" | custom-call | flops 1073741824 | bytes 4194304 | tf_op jit(solution)/shard_map/pallas_call | solution.py:39
  37.5 2.1 %collective-permute-start.10 = (bf16[128,256]{1,0:T(8,128)(2,1)S(1)}, bf16[128,256]{1,0:T(8,128)(2,1)S(1)}, u32[]{:S(2)}, u32[]{:S(2)}) collective-permute-start(bf16[128,256]{1,0:T(8,128)(2,1)S(1)} %get-tuple-element.28.refs_0_), channel_id=1, source_target_pairs={{1,0},{2,1},{3,2},{0,3},{5,4},{6,5},{7,6},{4,7},{9,8},{10,9},{11,1... | collective-permute-start | bytes 196616 | tf_op jit(solution)/shard_map/ppermute | solution.py:237
  39.5 0.7 %collective-permute-start.11 = (bf16[128,256]{1,0:T(8,128)(2,1)S(1)}, bf16[128,256]{1,0:T(8,128)(2,1)S(1)}, u32[]{:S(2)}, u32[]{:S(2)}) collective-permute-start(bf16[128,256]{1,0:T(8,128)(2,1)S(1)} %get-tuple-element.28.refs_0_), channel_id=1, source_target_pairs={{2,0},{3,1},{0,2},{1,3},{6,4},{7,5},{4,6},{5,7},{10,8},{11,9},{8,1... | collective-permute-start | bytes 196616 | tf_op jit(solution)/shard_map/ppermute | solution.py:237
  40.2 1.9 %collective-permute-start.12 = (bf16[128,256]{1,0:T(8,128)(2,1)S(1)}, bf16[128,256]{1,0:T(8,128)(2,1)S(1)}, u32[]{:S(2)}, u32[]{:S(2)}) collective-permute-start(bf16[128,256]{1,0:T(8,128)(2,1)S(1)} %get-tuple-element.28.refs_0_), channel_id=1, source_target_pairs={{3,0},{0,1},{1,2},{2,3},{7,4},{4,5},{5,6},{6,7},{11,8},{8,9},{9,10... | collective-permute-start | bytes 196616 | tf_op jit(solution)/shard_map/ppermute | solution.py:237
  42.2 0.3 collective-permute-start.14
  42.5 2.1 %collective-permute-start.15 = (bf16[32,256]{1,0:T(8,128)(2,1)S(1)}, bf16[32,256]{1,0:T(8,128)(2,1)S(1)}, u32[]{:S(2)}, u32[]{:S(2)}) collective-permute-start(bf16[32,256]{1,0:T(8,128)(2,1)S(1)} %copy-done.9), channel_id=1, source_target_pairs={{3,0},{0,1},{1,2},{2,3},{7,4},{4,5},{5,6},{6,7},{11,8},{8,9},{9,10... | collective-permute-start | bytes 49160 | tf_op jit(solution)/shard_map/ppermute | solution.py:237
  44.6 0.8 %shard_map.145 = (f32[1024,512]{1,0:T(8,128)S(1)}, bf16[1024,256]{1,0:T(8,128)(2,1)S(1)}) custom-call(bf16[1024,512]{1,0:T(8,128)(2,1)S(1)} %get-tuple-element.29.state_ref.refs_10_, bf16[1024,512]{1,0:T(8,128)(2,1)S(1)} %copy-done, s32[2,1024]{1,0:T(2,128)S(1)} %copy-done.8), custom_call_target="tpu_custom_call" | custom-call | flops 536870912 | bytes 4194304 | tf_op jit(solution)/shard_map/pallas_call | solution.py:39
  45.4 2.5 %collective-permute-done.14.refs_6_ = bf16[32,256]{1,0:T(8,128)(2,1)S(1)} collective-permute-done((bf16[32,256]{1,0:T(8,128)(2,1)S(1)}, bf16[32,256]{1,0:T(8,128)(2,1)S(1)}, u32[]{:S(2)}, u32[]{:S(2)}) %collective-permute-start.14) | collective-permute-done | bytes 16416 | tf_op jit(solution)/shard_map/ppermute | solution.py:237
  47.9 0.2 collective-permute-done.15.refs_7_
  48.1 2.3 %shard_map.146 = (bf16[1024,512]{1,0:T(8,128)(2,1)}, bf16[32,256]{1,0:T(8,128)(2,1)}) custom-call(bf16[128,256]{1,0:T(8,128)(2,1)S(1)} %get-tuple-element.28.refs_0_, bf16[128,256]{1,0:T(8,128)(2,1)S(1)} %collective-permute-done.10.refs_1_, bf16[128,256]{1,0:T(8,128)(2,1)S(1)} %collective-permute-done.11.refs_2_, ...), custom_call_target="tpu_custom_call" | custom-call | flops 268435456 | bytes 4194304 | tf_op jit(solution)/shard_map/pallas_call | solution.py:39
  (36 shorter events, 0.1 us)
Async XLA Ops:
  0.6 1.2 %copy-start.1 = (bf16[1024,512]{1,0:T(8,128)(2,1)S(1)}, bf16[1024,512]{1,0:T(8,128)(2,1)}, u32[]{:S(2)}) copy-start(bf16[1024,512]{1,0:T(8,128)(2,1)} %edges_ref.3) | copy-start | bytes 3145732
  1.9 1.0 %copy-start.10 = (bf16[512,512]{1,0:T(8,128)(2,1)S(1)}, bf16[512,512]{1,0:T(8,128)(2,1)}, u32[]{:S(2)}) copy-start(bf16[512,512]{1,0:T(8,128)(2,1)} %weight_ref.1) | copy-start | bytes 1572868
  2.9 0.8 %copy-start.11 = (bf16[64,512]{1,0:T(8,128)(2,1)S(1)}, bf16[64,512]{1,0:T(8,128)(2,1)}, u32[]{:S(2)}) copy-start(bf16[64,512]{1,0:T(8,128)(2,1)} %down_ref.1) | copy-start | bytes 196612
  3.7 7.6 %copy-start.13 = (s32[16,2]{0,1:T(2,128)S(1)}, s32[16,2]{0,1:T(2,128)}, u32[]{:S(2)}) copy-start(s32[16,2]{0,1:T(2,128)} %param.17) | copy-start | bytes 388
  3.7 7.6 %copy-start.12 = (s32[1024]{0:T(1024)S(1)}, s32[1024]{0:T(1024)}, u32[]{:S(2)}) copy-start(s32[1024]{0:T(1024)} %param.15) | copy-start | bytes 12292
  3.7 17.7 %copy-start.5 = (bf16[16,64,128]{2,1,0:T(8,128)(2,1)S(1)}, bf16[16,64,128]{2,1,0:T(8,128)(2,1)}, u32[]{:S(2)}) copy-start(bf16[16,64,128]{2,1,0:T(8,128)(2,1)} %refs_1_.1) | copy-start | bytes 786436
  3.7 26.1 %copy-start.2 = (bf16[1024,512]{1,0:T(8,128)(2,1)S(1)}, bf16[1024,512]{1,0:T(8,128)(2,1)}, u32[]{:S(2)}) copy-start(bf16[1024,512]{1,0:T(8,128)(2,1)} %edges_ref.3) | copy-start | bytes 3145732
  3.8 26.1 %copy-start.4 = (bf16[2,64,512]{2,1,0:T(8,128)(2,1)S(1)}, bf16[2,64,512]{2,1,0:T(8,128)(2,1)}, u32[]{:S(2)}) copy-start(bf16[2,64,512]{2,1,0:T(8,128)(2,1)} %refs_2_.1) | copy-start | bytes 393220
  5.2 9.0 %collective-permute-start = (bf16[512,128]{1,0:T(8,128)(2,1)S(1)}, bf16[512,128]{1,0:T(8,128)(2,1)S(1)}, u32[]{:S(2)}, u32[]{:S(2)}) collective-permute-start(bf16[512,128]{1,0:T(8,128)(2,1)S(1)} %shard_map.140.refs_2_), channel_id=1, source_target_pairs={{1,0},{2,1},{3,2},{0,3},{5,4},{6,5},{7,6},{4,7},{9,8},{10,9},{11,1... | collective-permute-start | bytes 393224 | tf_op jit(solution)/shard_map/ppermute | solution.py:237
  10.3 11.2 %collective-permute-start.1 = (bf16[512,128]{1,0:T(8,128)(2,1)S(1)}, bf16[512,128]{1,0:T(8,128)(2,1)S(1)}, u32[]{:S(2)}, u32[]{:S(2)}) collective-permute-start(bf16[512,128]{1,0:T(8,128)(2,1)S(1)} %shard_map.140.refs_2_), channel_id=1, source_target_pairs={{2,0},{3,1},{0,2},{1,3},{6,4},{7,5},{4,6},{5,7},{10,8},{11,9},{8,1... | collective-permute-start | bytes 393224 | tf_op jit(solution)/shard_map/ppermute | solution.py:237
  10.3 11.2 %collective-permute-start.2 = (bf16[512,128]{1,0:T(8,128)(2,1)S(1)}, bf16[512,128]{1,0:T(8,128)(2,1)S(1)}, u32[]{:S(2)}, u32[]{:S(2)}) collective-permute-start(bf16[512,128]{1,0:T(8,128)(2,1)S(1)} %shard_map.140.refs_2_), channel_id=1, source_target_pairs={{3,0},{0,1},{1,2},{2,3},{7,4},{4,5},{5,6},{6,7},{11,8},{8,9},{9,10... | collective-permute-start | bytes 393224 | tf_op jit(solution)/shard_map/ppermute | solution.py:237
  23.5 3.6 %collective-permute-start.3 = (bf16[64,128]{1,0:T(8,128)(2,1)S(1)}, bf16[64,128]{1,0:T(8,128)(2,1)S(1)}, u32[]{:S(2)}, u32[]{:S(2)}) collective-permute-start(bf16[64,128]{1,0:T(8,128)(2,1)S(1)} %get-tuple-element.21), channel_id=1, source_target_pairs={{0,4},{4,0},{8,12},{12,8},{16,20},{20,16},{24,28},{28,24},{1,5},{5... | collective-permute-start | bytes 49160 | tf_op jit(solution)/shard_map/ppermute | solution.py:294
  23.6 6.0 %collective-permute-start.4 = (bf16[64,128]{1,0:T(8,128)(2,1)S(1)}, bf16[64,128]{1,0:T(8,128)(2,1)S(1)}, u32[]{:S(2)}, u32[]{:S(2)}) collective-permute-start(bf16[64,128]{1,0:T(8,128)(2,1)S(1)} %get-tuple-element.22), channel_id=1, source_target_pairs={{0,8},{4,12},{8,0},{12,4},{16,24},{20,28},{24,16},{28,20},{1,9},{5... | collective-permute-start | bytes 49160 | tf_op jit(solution)/shard_map/ppermute | solution.py:294
  25.1 6.3 %collective-permute-start.5 = (bf16[64,128]{1,0:T(8,128)(2,1)S(1)}, bf16[64,128]{1,0:T(8,128)(2,1)S(1)}, u32[]{:S(2)}, u32[]{:S(2)}) collective-permute-start(bf16[64,128]{1,0:T(8,128)(2,1)S(1)} %get-tuple-element.23), channel_id=1, source_target_pairs={{0,12},{4,8},{8,4},{12,0},{16,28},{20,24},{24,20},{28,16},{1,13},{... | collective-permute-start | bytes 49160 | tf_op jit(solution)/shard_map/ppermute | solution.py:294
  25.4 7.7 %collective-permute-start.6 = (bf16[64,128]{1,0:T(8,128)(2,1)S(1)}, bf16[64,128]{1,0:T(8,128)(2,1)S(1)}, u32[]{:S(2)}, u32[]{:S(2)}) collective-permute-start(bf16[64,128]{1,0:T(8,128)(2,1)S(1)} %get-tuple-element.24), channel_id=1, source_target_pairs={{0,16},{4,20},{8,24},{12,28},{16,0},{20,4},{24,8},{28,12},{1,17},{... | collective-permute-start | bytes 49160 | tf_op jit(solution)/shard_map/ppermute | solution.py:294
  27.0 6.2 %collective-permute-start.7 = (bf16[64,128]{1,0:T(8,128)(2,1)S(1)}, bf16[64,128]{1,0:T(8,128)(2,1)S(1)}, u32[]{:S(2)}, u32[]{:S(2)}) collective-permute-start(bf16[64,128]{1,0:T(8,128)(2,1)S(1)} %get-tuple-element.25), channel_id=1, source_target_pairs={{0,20},{4,16},{8,28},{12,24},{16,4},{20,0},{24,12},{28,8},{1,21},{... | collective-permute-start | bytes 49160 | tf_op jit(solution)/shard_map/ppermute | solution.py:294
  27.1 6.0 %collective-permute-start.8 = (bf16[64,128]{1,0:T(8,128)(2,1)S(1)}, bf16[64,128]{1,0:T(8,128)(2,1)S(1)}, u32[]{:S(2)}, u32[]{:S(2)}) collective-permute-start(bf16[64,128]{1,0:T(8,128)(2,1)S(1)} %get-tuple-element.26), channel_id=1, source_target_pairs={{0,24},{4,28},{8,16},{12,20},{16,8},{20,12},{24,0},{28,4},{1,25},{... | collective-permute-start | bytes 49160 | tf_op jit(solution)/shard_map/ppermute | solution.py:294
  29.6 4.1 %collective-permute-start.9 = (bf16[64,128]{1,0:T(8,128)(2,1)S(1)}, bf16[64,128]{1,0:T(8,128)(2,1)S(1)}, u32[]{:S(2)}, u32[]{:S(2)}) collective-permute-start(bf16[64,128]{1,0:T(8,128)(2,1)S(1)} %get-tuple-element.27), channel_id=1, source_target_pairs={{0,28},{4,24},{8,20},{12,16},{16,12},{20,8},{24,4},{28,0},{1,29},{... | collective-permute-start | bytes 49160 | tf_op jit(solution)/shard_map/ppermute | solution.py:294
  29.8 1.6 %copy-start.9 = (bf16[32,256]{1,0:T(8,128)(2,1)S(1)}, bf16[32,256]{1,0:T(8,128)(2,1)}, u32[]{:S(2)}) copy-start(bf16[32,256]{1,0:T(8,128)(2,1)} %refs_4_.3) | copy-start | bytes 49156
  29.8 3.8 %copy-start.3 = (bf16[1,2,512,512]{3,2,1,0:T(8,128)(2,1)S(1)}, bf16[1,2,512,512]{3,2,1,0:T(8,128)(2,1)}, u32[]{:S(2)}) copy-start(bf16[1,2,512,512]{3,2,1,0:T(8,128)(2,1)} %refs_3_.1) | copy-start | bytes 3145732
  29.8 3.8 %copy-start.6 = (bf16[512,256]{1,0:T(8,128)(2,1)S(1)}, bf16[512,256]{1,0:T(8,128)(2,1)}, u32[]{:S(2)}) copy-start(bf16[512,256]{1,0:T(8,128)(2,1)} %refs_4_.2) | copy-start | bytes 786436
  29.9 3.8 %copy-start.8 = (s32[2,1024]{1,0:T(2,128)S(1)}, s32[2,1024]{1,0:T(2,128)}, u32[]{:S(2)}) copy-start(s32[2,1024]{1,0:T(2,128)} %index_ref.1) | copy-start | bytes 24580
  31.5 11.0 %collective-permute-start.13 = (bf16[32,256]{1,0:T(8,128)(2,1)S(1)}, bf16[32,256]{1,0:T(8,128)(2,1)S(1)}, u32[]{:S(2)}, u32[]{:S(2)}) collective-permute-start(bf16[32,256]{1,0:T(8,128)(2,1)S(1)} %copy-done.9), channel_id=1, source_target_pairs={{1,0},{2,1},{3,2},{0,3},{5,4},{6,5},{7,6},{4,7},{9,8},{10,9},{11,1... | collective-permute-start | bytes 49160 | tf_op jit(solution)/shard_map/ppermute | solution.py:237
  33.7 11.0 %copy-start = (bf16[1024,512]{1,0:T(8,128)(2,1)S(1)}, bf16[1024,512]{1,0:T(8,128)(2,1)}, u32[]{:S(2)}) copy-start(bf16[1024,512]{1,0:T(8,128)(2,1)} %refs_9_.1) | copy-start | bytes 3145732
  37.5 10.6 %copy-start.7 = (bf16[2,256,256]{2,1,0:T(8,128)(2,1)S(1)}, bf16[2,256,256]{2,1,0:T(8,128)(2,1)}, u32[]{:S(2)}) copy-start(bf16[2,256,256]{2,1,0:T(8,128)(2,1)} %refs_8_.1) | copy-start | bytes 786436
  37.5 10.6 %collective-permute-start.10 = (bf16[128,256]{1,0:T(8,128)(2,1)S(1)}, bf16[128,256]{1,0:T(8,128)(2,1)S(1)}, u32[]{:S(2)}, u32[]{:S(2)}) collective-permute-start(bf16[128,256]{1,0:T(8,128)(2,1)S(1)} %get-tuple-element.28.refs_0_), channel_id=1, source_target_pairs={{1,0},{2,1},{3,2},{0,3},{5,4},{6,5},{7,6},{4,7},{9,8},{10,9},{11,1... | collective-permute-start | bytes 196616 | tf_op jit(solution)/shard_map/ppermute | solution.py:237
  39.5 8.5 %collective-permute-start.11 = (bf16[128,256]{1,0:T(8,128)(2,1)S(1)}, bf16[128,256]{1,0:T(8,128)(2,1)S(1)}, u32[]{:S(2)}, u32[]{:S(2)}) collective-permute-start(bf16[128,256]{1,0:T(8,128)(2,1)S(1)} %get-tuple-element.28.refs_0_), channel_id=1, source_target_pairs={{2,0},{3,1},{0,2},{1,3},{6,4},{7,5},{4,6},{5,7},{10,8},{11,9},{8,1... | collective-permute-start | bytes 196616 | tf_op jit(solution)/shard_map/ppermute | solution.py:237
  40.2 7.9 %collective-permute-start.12 = (bf16[128,256]{1,0:T(8,128)(2,1)S(1)}, bf16[128,256]{1,0:T(8,128)(2,1)S(1)}, u32[]{:S(2)}, u32[]{:S(2)}) collective-permute-start(bf16[128,256]{1,0:T(8,128)(2,1)S(1)} %get-tuple-element.28.refs_0_), channel_id=1, source_target_pairs={{3,0},{0,1},{1,2},{2,3},{7,4},{4,5},{5,6},{6,7},{11,8},{8,9},{9,10... | collective-permute-start | bytes 196616 | tf_op jit(solution)/shard_map/ppermute | solution.py:237
  42.2 5.7 %collective-permute-start.14 = (bf16[32,256]{1,0:T(8,128)(2,1)S(1)}, bf16[32,256]{1,0:T(8,128)(2,1)S(1)}, u32[]{:S(2)}, u32[]{:S(2)}) collective-permute-start(bf16[32,256]{1,0:T(8,128)(2,1)S(1)} %copy-done.9), channel_id=1, source_target_pairs={{2,0},{3,1},{0,2},{1,3},{6,4},{7,5},{4,6},{5,7},{10,8},{11,9},{8,1... | collective-permute-start | bytes 49160 | tf_op jit(solution)/shard_map/ppermute | solution.py:237
  42.5 5.6 %collective-permute-start.15 = (bf16[32,256]{1,0:T(8,128)(2,1)S(1)}, bf16[32,256]{1,0:T(8,128)(2,1)S(1)}, u32[]{:S(2)}, u32[]{:S(2)}) collective-permute-start(bf16[32,256]{1,0:T(8,128)(2,1)S(1)} %copy-done.9), channel_id=1, source_target_pairs={{3,0},{0,1},{1,2},{2,3},{7,4},{4,5},{5,6},{6,7},{11,8},{8,9},{9,10... | collective-permute-start | bytes 49160 | tf_op jit(solution)/shard_map/ppermute | solution.py:237

commit v2 on v1

--- a/solution.py
+++ b/solution.py
@@ -31,10 +31,14 @@
     return [slice(at, at + step) for at in range(0, rows, step)]
 
 
-def call(kernel, outs, args, *, smem=(), scratch=(), flops=0, nbytes=0, limit=24):
-    in_specs = [
-        pl.BlockSpec(memory_space=pltpu.SMEM if at in smem else pltpu.VMEM)
-        for at in range(len(args))
+def call(kernel, outs, args, *, smem=(), hbm=(), scratch=(), flops=0, nbytes=0, limit=24):
+    def space(at):
+        return pltpu.SMEM if at in smem else pltpu.HBM if at in hbm else pltpu.VMEM
+
+    in_specs = [pl.BlockSpec(memory_space=space(at)) for at in range(len(args))]
+    args = [
+        pltpu.with_memory_space_constraint(arg, pltpu.HBM) if at in hbm else arg
+        for at, arg in enumerate(args)
     ]
     return pl.pallas_call(
         kernel,
@@ -51,38 +55,60 @@
     return jax.ShapeDtypeStruct(shape, dtype)
 
 
-def narrow_kernel(edges_ref, weight_ref, down_ref, out_ref):
-    half = edges_ref.shape[0] // 2
-    for rows in row_chunks(half):
-        pieces = []
-        for base in (0, half):
-            piece = edges_ref[base + rows.start : base + rows.stop, :]
-            hidden = silu(product(piece, weight_ref[...])).astype(jnp.bfloat16)
-            pieces.append(
+def narrow_kernel(
+    edges_hbm, weight_hbm, down_hbm, atoms_ref, out_ref, edges_ref, weight_ref, down_ref, sems
+):
+    half = edges_hbm.shape[0] // 2
+    pieces = [
+        slice(base + rows.start, base + rows.stop)
+        for rows in row_chunks(half)
+        for base in (0, half)
+    ]
+    copies = [
+        pltpu.make_async_copy(weight_hbm, weight_ref, sems.at[0]),
+        pltpu.make_async_copy(down_hbm, down_ref, sems.at[1]),
+    ] + [
+        pltpu.make_async_copy(edges_hbm.at[piece], edges_ref.at[piece], sems.at[2 + at])
+        for at, piece in enumerate(pieces)
+    ]
+    for copy in [copies[0], copies[2], copies[1]] + copies[3:]:
+        copy.start()
+    count, wide = atoms_ref.shape
+    for at in range(wide // 128):
+        out_ref[half + at * count : half + (at + 1) * count, :] = atoms_ref[
+            :, at * 128 : (at + 1) * 128
+        ]
+    copies[0].wait()
+    copies[1].wait()
+    for at, rows in enumerate(row_chunks(half)):
+        sides = []
+        for side in range(2):
+            copies[2 + 2 * at + side].wait()
+            hidden = silu(product(edges_ref[pieces[2 * at + side], :], weight_ref[...]))
+            sides.append(
                 silu(
                     lax.dot_general(
-                        hidden,
+                        hidden.astype(jnp.bfloat16),
                         down_ref[...],
                         (((1,), (1,)), ((), ())),
                         preferred_element_type=jnp.float32,
                     )
                 )
             )
-        out_ref[rows, :] = jnp.concatenate(pieces, axis=1).astype(jnp.bfloat16)
+        out_ref[rows, :] = jnp.concatenate(sides, axis=1).astype(jnp.bfloat16)
 
 
 def index_kernel(domains, shards, reverse_ref, send_ref, fetch_ref, local_ref):
     rows = reverse_ref.shape[1]
     capacity = rows // domains
     half = capacity // 2
-    slots = (domains - 1) * capacity
+    slots = domains * capacity
     own = lax.axis_index("dom")
     reverse = reverse_ref[...]
     holder = reverse // (rows * shards)
     source_row = lax.rem(reverse, rows)
-    partner = holder ^ own
     source_column = as_column(source_row)
-    member = (lax.broadcasted_iota(jnp.int32, (domains, rows), 0) == partner).astype(jnp.bfloat16)
+    member = (lax.broadcasted_iota(jnp.int32, (domains, rows), 0) == holder).astype(jnp.bfloat16)
     before = (
         lax.broadcasted_iota(jnp.int32, (rows, rows), 0)
         < lax.broadcasted_iota(jnp.int32, (rows, rows), 1)
@@ -97,8 +123,8 @@
 
     def slot_of(at):
         part = (at >= half).astype(jnp.int32)
-        slot = part * (slots // 2) + (partner - 1) * half + at - part * half
-        return jnp.where(partner == 0, -1, slot)
+        slot = part * (slots // 2) + holder * half + at - part * half
+        return jnp.where(holder == own, -1, slot)
 
     send_slot = slot_of(place)
     send_ref[...] = (
@@ -108,7 +134,7 @@
     fetch_ref[...] = (
         lax.broadcasted_iota(jnp.int32, (rows, slots), 1) == fetch_column
     ).astype(jnp.bfloat16)
-    local_column = as_column(jnp.where(partner == 0, source_row, -1))
+    local_column = as_column(jnp.where(holder == own, source_row, -1))
     local_ref[...] = (
         lax.broadcasted_iota(jnp.int32, (rows, rows), 1) == local_column
     ).astype(jnp.bfloat16)
@@ -117,15 +143,20 @@
 def mix_kernel(shards, *refs):
     source_ref, tiles_ref = refs[:2]
     parts = refs[2 : 2 + shards]
-    send_ref, trip_ref = refs[2 + shards : 4 + shards]
-    out_refs = refs[4 + shards : -1]
-    held_ref = refs[-1]
+    send_ref, trip_ref, out_ref, atoms_ref, held_ref = refs[2 + shards :]
     blocks, block_len, width = tiles_ref.shape
     count = width // block_len
-    lines = parts[0].shape[0]
+    lines = held_ref.shape[0] // shards
+    part_atoms, atom_wide = atoms_ref.shape
+    near_atoms = part_atoms // shards
     me = lax.axis_index("edge")
     for at in range(shards):
-        held_ref[at * lines : (at + 1) * lines, :] = parts[at][...]
+        held_ref[at * lines : (at + 1) * lines, :] = parts[at][:lines, :]
+        for piece in range(atom_wide // 128):
+            start = lines + piece * near_atoms
+            atoms_ref[
+                at * near_atoms : (at + 1) * near_atoms, piece * 128 : (piece + 1) * 128
+            ] = parts[at][start : start + near_atoms, :]
     half_blocks = blocks // 2
     channels = trip_ref.shape[1]
     for block in range(blocks):
@@ -144,10 +175,7 @@
     half_slots = send_ref.shape[0] // 2
     low = product(send_ref[:half_slots, :], trip_ref[...])
     high = product(send_ref[half_slots:, :], trip_ref[...])
-    packed = jnp.concatenate([low, high], axis=1).astype(jnp.bfloat16)
-    each = half_slots // len(out_refs)
-    for at, out_ref in enumerate(out_refs):
-        out_ref[...] = packed[at * each : (at + 1) * each, :]
+    out_ref[...] = jnp.concatenate([low, high], axis=1).astype(jnp.bfloat16)
 
 
 def base_kernel(edges_ref, trip_ref, local_ref, up_ref, out_ref):
@@ -158,16 +186,14 @@
         out_ref[rows, :] = edges_ref[rows, :].astype(jnp.float32) + joined * root_half
 
 
-def state_kernel(partners, *refs):
-    base_ref, fetch_ref, up_ref, residual_ref, message_ref, index_ref = refs[:6]
-    arrived = refs[6 : 6 + partners]
-    state_ref, sums_ref, slots_ref = refs[6 + partners :]
+def state_kernel(
+    base_ref, fetch_ref, up_ref, residual_ref, message_ref, index_ref, arrived_ref,
+    state_ref, sums_ref, slots_ref,
+):
     channels = up_ref.shape[1]
-    each = arrived[0].shape[0]
-    for at in range(partners):
-        piece = arrived[at][...]
-        slots_ref[at * each : (at + 1) * each, :] = piece[:, :channels]
-        slots_ref[(partners + at) * each : (partners + at + 1) * each, :] = piece[:, channels:]
+    half = arrived_ref.shape[0]
+    slots_ref[:half, :] = arrived_ref[:, :channels]
+    slots_ref[half:, :] = arrived_ref[:, channels:]
     for rows in row_chunks(base_ref.shape[0]):
         picked = product(fetch_ref[rows, :], slots_ref[...]).astype(jnp.bfloat16)
         state = (base_ref[rows, :] + product(picked, up_ref[1]) * root_half).astype(jnp.bfloat16)
@@ -206,20 +232,18 @@
 
 def final_kernel(shards, scale, *refs):
     sums = refs[:shards]
-    atoms = refs[shards : 2 * shards]
-    weight_ref, join_ref, state_ref, side_ref, chosen_ref = refs[2 * shards : 2 * shards + 5]
-    edges_ref, own_ref, table_ref = refs[2 * shards + 5 :]
-    count = atoms[0].shape[0]
-    part_atoms = count * shards
+    atoms_ref, weight_ref, join_ref, state_ref, side_ref, chosen_ref = refs[shards : shards + 6]
+    edges_ref, own_ref, table_ref = refs[shards + 6 :]
+    part_atoms = atoms_ref.shape[0]
+    count = part_atoms // shards
     total = sums[0][...].astype(jnp.float32)
     for at in range(1, shards):
         piece = sums[at][...].astype(jnp.float32)
         cut = part_atoms - at * count
         total = total + jnp.concatenate([piece[cut:], piece[:cut]], axis=0)
-    everyone = jnp.concatenate([ref[...].astype(jnp.float32) for ref in atoms], axis=0)
     scaled = (total * scale).astype(jnp.bfloat16)
     middle = silu(product(scaled, weight_ref[0])).astype(jnp.bfloat16)
-    renewed = (everyone + product(middle, weight_ref[1])).astype(jnp.bfloat16)
+    renewed = (atoms_ref[...].astype(jnp.float32) + product(middle, weight_ref[1])).astype(jnp.bfloat16)
     own_ref[...] = renewed[:count, :]
     width = renewed.shape[1]
     for end in range(2):
@@ -260,40 +284,45 @@
     shards = lax.axis_size("edge")
     count, atom_wide = atoms.shape
     part_atoms = count * shards
-    capacity = rows // domains
-    partners = domains - 1
-    slots = partners * capacity
-    packed = (rows // 2, 2 * channels)
-
-    atom_parts = [atoms] + from_next(atoms, shards)
+    lines = rows // 2
+    packed = 2 * channels
+
     narrow = call(
         narrow_kernel,
-        shaped(packed),
-        (edges, weight_edge, weight_down),
+        shaped((lines + count * atom_wide // packed, packed)),
+        (edges, weight_edge, weight_down, atoms),
+        hbm=(0, 1, 2),
+        scratch=[
+            pltpu.VMEM(edges.shape, jnp.bfloat16),
+            pltpu.VMEM(weight_edge.shape, jnp.bfloat16),
+            pltpu.VMEM(weight_down.shape, jnp.bfloat16),
+            pltpu.SemaphoreType.DMA((2 + 2 * len(row_chunks(lines)),)),
+        ],
         flops=2 * rows * wide * (wide + channels),
         nbytes=2 * (rows * wide + wide * wide),
     )
     narrow_parts = [narrow] + from_next(narrow, shards)
     send, fetch, local = call(
         functools.partial(index_kernel, domains, shards),
-        (shaped((slots, rows)), shaped((rows, slots)), shaped((rows, rows))),
+        (shaped((rows, rows)),) * 3,
         (reverse.reshape(1, rows),),
         flops=40 * rows * rows,
         nbytes=6 * rows * rows,
     )
-    trip_out, *outgoing = call(
+    trip_out, outgoing, all_atoms = call(
         functools.partial(mix_kernel, shards),
-        (shaped((rows, channels)),) + (shaped((capacity // 2, 2 * channels)),) * partners,
+        (
+            shaped((rows, channels)),
+            shaped((lines, packed)),
+            shaped((part_atoms, atom_wide)),
+        ),
         (tile_source, tiles, *narrow_parts, send),
         smem=(0,),
-        scratch=[pltpu.VMEM((shards * rows // 2, 2 * channels), jnp.bfloat16)],
+        scratch=[pltpu.VMEM((shards * lines, packed), jnp.bfloat16)],
         flops=2 * rows * rows * channels,
         nbytes=2 * rows * rows,
     )
-    arrived = [
-        lax.ppermute(outgoing[by - 1], "dom", [(at, at ^ by) for at in range(domains)])
-        for by in range(1, domains)
-    ]
+    arrived = lax.all_to_all(outgoing, "dom", split_axis=0, concat_axis=0, tiled=True)
     base = call(
         base_kernel,
         shaped((rows, wide), jnp.float32),
@@ -302,10 +331,10 @@
         nbytes=2 * rows * rows + 6 * rows * wide,
     )
     state, sums = call(
-        functools.partial(state_kernel, partners),
+        state_kernel,
         (shaped((rows, wide)), shaped((part_atoms, atom_wide))),
-        (base, fetch, weight_up, weight_residual, weight_message, atom_index, *arrived),
-        scratch=[pltpu.VMEM((slots, channels), jnp.bfloat16)],
+        (base, fetch, weight_up, weight_residual, weight_message, atom_index, arrived),
+        scratch=[pltpu.VMEM((rows, channels), jnp.bfloat16)],
         flops=4 * rows * wide * wide,
         nbytes=8 * rows * wide,
     )
@@ -320,7 +349,7 @@
     return call(
         functools.partial(final_kernel, shards, (rows // count) ** -0.5),
         (shaped((rows, wide)), shaped((count, atom_wide))),
-        (*sums_parts, *atom_parts, weight_atom, weight_join, state, side, chosen),
+        (*sums_parts, all_atoms, weight_atom, weight_join, state, side, chosen),
         scratch=[pltpu.VMEM((2 * part_atoms, wide), jnp.bfloat16)],
         flops=4 * rows * part_atoms * wide,
         nbytes=8 * rows * wide,

time: 50.7 us -> 53.8 us (1.061)
  local copies, waits for them, and re-layouts: 3.23 us -> 10.5 us
  starting transfers between devices: 21.2 us -> 16.9 us
  waiting for transfers between devices: 10.7 us -> 7.79 us
  Pallas kernels: 14.5 us -> 17.4 us
    unnamed x29 -> x35, local copies, waits for them, and re-layouts: 3.23 us -> 10.5 us
    ppermute x7 -> x0, starting transfers between devices: 6.32 us -> none  [body(): lax.ppermute(outgoing[by - 1], 'dom', [(at, at ^ by) for at in range(doma...]
    ppermute x9 -> x6, waiting for transfers between devices: 10.2 us -> 6.39 us  [from_next(): lax.ppermute(value, 'edge', [((at + by) % shards, at) for at in range(sha...]
    all_to_all x0 -> x1, starting transfers between devices: none -> 3.73 us  [body(): lax.all_to_all(outgoing, 'dom', split_axis=0, concat_axis=0, tiled=True)]
    pallas_call x7, Pallas kernels: 14.5 us -> 17.4 us  [call(): pl.pallas_call(kernel, out_shape=outs, in_specs=in_specs, out_specs=jax.t...]
    ppermute x9 -> x6, starting transfers between devices: 14.9 us -> 13.1 us  [from_next(): lax.ppermute(value, 'edge', [((at + by) % shards, at) for at in range(sha...]
    all_to_all x0 -> x1, waiting for transfers between devices: none -> 1.4 us  [body(): lax.all_to_all(outgoing, 'dom', split_axis=0, concat_axis=0, tiled=True)]
  transfers between devices with their start and end apart: 16 -> 7, of which waited for: 5 -> 5; matrix products, arithmetic and copies ran while one was open for 0% -> 0% of each run, Pallas kernels for 17% -> 9%
where the time goes in v2:
time: 53.8 us; the launch traced here: 53.4 us
  Pallas kernels  17.4 us (32%)
  starting transfers between devices  16.9 us (31%)
  local copies, waits for them, and re-layouts  10.5 us (20%)
  waiting for transfers between devices  7.79 us (14%)
  between operations  0.76 us (1%)
    pallas_call x7, Pallas kernels, call(): pl.pallas_call(kernel, out_shape=outs, in_specs=in_specs, out_specs=jax.t...  17.4 us
    ppermute x6, starting transfers between devices, from_next(): lax.ppermute(value, 'edge', [((at + by) % shards, at) for at in range(sha...  13.1 us
    unnamed x35, local copies, waits for them, and re-layouts  10.5 us
    ppermute x6, waiting for transfers between devices, from_next(): lax.ppermute(value, 'edge', [((at + by) % shards, at) for at in range(sha...  6.39 us
    all_to_all x1, starting transfers between devices, body(): lax.all_to_all(outgoing, 'dom', split_axis=0, concat_axis=0, tiled=True)  3.73 us
    all_to_all x1, waiting for transfers between devices, body(): lax.all_to_all(outgoing, 'dom', split_axis=0, concat_axis=0, tiled=True)  1.4 us
  transfers between devices with their start and end apart: 7, of which 5 were waited for; matrix products, arithmetic and copies ran while one was open for 0% of the time, Pallas kernels for 9%

profile of v2, /device:TPU:0, one launch (start us, length us, event | category | flops | bytes accessed | tf_op | source)
XLA Modules:
  0.0 53.4 jit_solution(11667899420855331000)
XLA Ops:
  0.7 0.8 %copy-done.14 = bf16[32,256]{1,0:T(8,128)(2,1)S(1)} copy-done((bf16[32,256]{1,0:T(8,128)(2,1)S(1)}, bf16[32,256]{1,0:T(8,128)(2,1)}, u32[]{:S(2)}) %copy-start.14) | copy-done | bytes 16408
  1.4 3.5 %shard_map.140.refs_2_ = bf16[576,128]{1,0:T(8,128)(2,1)S(1)} custom-call(bf16[1024,512]{1,0:T(8,128)(2,1)} %edges_ref.1, bf16[512,512]{1,0:T(8,128)(2,1)} %weight_hbm.1, bf16[64,512]{1,0:T(8,128)(2,1)} %down_hbm.1, bf16[32,256]{1,0:T(8,128)(2,1)S(1)} %copy-done.14), custom_call_target="tpu_custom_call" | custom-call | flops 603979776 | bytes 1572864 | tf_op jit(solution)/shard_map/pallas_call | solution.py:43
  4.9 0.0 copy-start.5
  4.9 0.0 copy-start.7
  4.9 3.1 %collective-permute-start.2 = (bf16[576,128]{1,0:T(8,128)(2,1)S(1)}, bf16[576,128]{1,0:T(8,128)(2,1)S(1)}, u32[]{:S(2)}, u32[]{:S(2)}) collective-permute-start(bf16[576,128]{1,0:T(8,128)(2,1)S(1)} %shard_map.140.refs_2_), channel_id=1, source_target_pairs={{3,0},{0,1},{1,2},{2,3},{7,4},{4,5},{5,6},{6,7},{11,8},{8,9},{9,10... | collective-permute-start | bytes 442376 | tf_op jit(solution)/shard_map/ppermute | solution.py:261
  8.0 2.6 %collective-permute-start.1 = (bf16[576,128]{1,0:T(8,128)(2,1)S(1)}, bf16[576,128]{1,0:T(8,128)(2,1)S(1)}, u32[]{:S(2)}, u32[]{:S(2)}) collective-permute-start(bf16[576,128]{1,0:T(8,128)(2,1)S(1)} %shard_map.140.refs_2_), channel_id=1, source_target_pairs={{2,0},{3,1},{0,2},{1,3},{6,4},{7,5},{4,6},{5,7},{10,8},{11,9},{8,1... | collective-permute-start | bytes 442376 | tf_op jit(solution)/shard_map/ppermute | solution.py:261
  10.6 1.3 %collective-permute-start = (bf16[576,128]{1,0:T(8,128)(2,1)S(1)}, bf16[576,128]{1,0:T(8,128)(2,1)S(1)}, u32[]{:S(2)}, u32[]{:S(2)}) collective-permute-start(bf16[576,128]{1,0:T(8,128)(2,1)S(1)} %shard_map.140.refs_2_), channel_id=1, source_target_pairs={{1,0},{2,1},{3,2},{0,3},{5,4},{6,5},{7,6},{4,7},{9,8},{10,9},{11,1... | collective-permute-start | bytes 442376 | tf_op jit(solution)/shard_map/ppermute | solution.py:261
  11.9 0.1 copy.15.refs_0_
  12.0 2.7 %shard_map.141 = (bf16[1024,1024]{1,0:T(8,128)(2,1)S(1)}, bf16[1024,1024]{1,0:T(8,128)(2,1)S(1)}, bf16[1024,1024]{1,0:T(8,128)(2,1)S(1)}) custom-call(s32[1,1024]{1,0:T(1,128)S(1)} %bitcast.4), custom_call_target="tpu_custom_call" | custom-call | flops 41943040 | bytes 6291456 | tf_op jit(solution)/shard_map/pallas_call | solution.py:43
  14.8 1.3 %copy-done.1 = bf16[1024,1024]{1,0:T(8,128)(2,1)} copy-done((bf16[1024,1024]{1,0:T(8,128)(2,1)}, bf16[1024,1024]{1,0:T(8,128)(2,1)S(1)}, u32[]{:S(2)}) %copy-start.1) | copy-done | bytes 2097176
  16.1 1.3 %copy-done.3 = bf16[1024,1024]{1,0:T(8,128)(2,1)} copy-done((bf16[1024,1024]{1,0:T(8,128)(2,1)}, bf16[1024,1024]{1,0:T(8,128)(2,1)S(1)}, u32[]{:S(2)}) %copy-start.3) | copy-done | bytes 2097176
  17.4 2.9 %collective-permute-done.1.refs_4_ = bf16[576,128]{1,0:T(8,128)(2,1)S(1)} collective-permute-done((bf16[576,128]{1,0:T(8,128)(2,1)S(1)}, bf16[576,128]{1,0:T(8,128)(2,1)S(1)}, u32[]{:S(2)}, u32[]{:S(2)}) %collective-permute-start.1) | collective-permute-done | bytes 147488 | tf_op jit(solution)/shard_map/ppermute | solution.py:261
  20.3 2.7 %shard_map.142 = (bf16[1024,64]{1,0:T(8,128)(2,1)S(1)}, bf16[512,128]{1,0:T(8,128)(2,1)}, bf16[128,256]{1,0:T(8,128)(2,1)S(1)}) custom-call(s32[16,2]{1,0:T(8,128)S(1)} %copy.15.refs_0_, bf16[16,64,128]{2,1,0:T(8,128)(2,1)S(1)} %copy-done.8, bf16[576,128]{1,0:T(8,128)(2,1)S(1)} %shard_map.140.refs_2_, bf16[576,128]{1,0:T(8,128)(2,1)S(1)} %collective-permute-done.refs_3_, ...), custom_call_target="tpu_custom_call" | custom-call | flops 134217728 | bytes 2097152 | tf_op jit(solution)/shard_map/pallas_call | solution.py:43
  23.0 0.7 %copy-done.10 = bf16[1024,64]{1,0:T(8,128)(2,1)} copy-done((bf16[1024,64]{1,0:T(8,128)(2,1)}, bf16[1024,64]{1,0:T(8,128)(2,1)S(1)}, u32[]{:S(2)}) %copy-start.10) | copy-done | bytes 131096
  23.7 3.7 %all-to-all-start = ((bf16[8,64,128]{2,1,0:T(8,128)(2,1)}), bf16[8,64,128]{2,1,0:T(8,128)(2,1)S(1)}, u32[]{:S(2)}, u32[]{:S(2)}) async-start(bf16[8,64,128]{2,1,0:T(8,128)(2,1)} %bitcast.1), calls=%async_computation | async-start | bytes 262144 | tf_op jit(solution)/shard_map/all_to_all | solution.py:325
  27.5 1.6 %copy-done.4 = bf16[1024,1024]{1,0:T(8,128)(2,1)S(1)} copy-done((bf16[1024,1024]{1,0:T(8,128)(2,1)S(1)}, bf16[1024,1024]{1,0:T(8,128)(2,1)}, u32[]{:S(2)}) %copy-start.4) | copy-done | bytes 2097176
  29.0 0.9 %copy-done.11 = bf16[1024,64]{1,0:T(8,128)(2,1)S(1)} copy-done((bf16[1024,64]{1,0:T(8,128)(2,1)S(1)}, bf16[1024,64]{1,0:T(8,128)(2,1)}, u32[]{:S(2)}) %copy-start.11) | copy-done | bytes 131096
  30.0 1.6 %shard_map.143.base_ref = f32[1024,512]{1,0:T(8,128)S(1)} custom-call(bf16[1024,512]{1,0:T(8,128)(2,1)S(1)} %copy-done.5, bf16[1024,64]{1,0:T(8,128)(2,1)S(1)} %copy-done.11, bf16[1024,1024]{1,0:T(8,128)(2,1)S(1)} %copy-done.4, bf16[2,64,512]{2,1,0:T(8,128)(2,1)S(1)} %copy-done.7), custom_call_target="tpu_custom_call" | custom-call | flops 268435456 | bytes 5242880 | tf_op jit(solution)/shard_map/pallas_call | solution.py:43
  31.6 1.4 %all-to-all-done = bf16[8,64,128]{2,1,0:T(8,128)(2,1)S(1)} async-done(((bf16[8,64,128]{2,1,0:T(8,128)(2,1)}), bf16[8,64,128]{2,1,0:T(8,128)(2,1)S(1)}, u32[]{:S(2)}, u32[]{:S(2)}) %all-to-all-start) | async-done | bytes 131104 | tf_op jit(solution)/shard_map/all_to_all | solution.py:325
  33.0 1.6 %copy-done.2 = bf16[1024,1024]{1,0:T(8,128)(2,1)S(1)} copy-done((bf16[1024,1024]{1,0:T(8,128)(2,1)S(1)}, bf16[1024,1024]{1,0:T(8,128)(2,1)}, u32[]{:S(2)}) %copy-start.2) | copy-done | bytes 2097176
  34.6 1.2 %copy-done.6 = bf16[1,2,512,512]{3,2,1,0:T(8,128)(2,1)S(1)} copy-done((bf16[1,2,512,512]{3,2,1,0:T(8,128)(2,1)S(1)}, bf16[1,2,512,512]{3,2,1,0:T(8,128)(2,1)}, u32[]{:S(2)}) %copy-start.6) | copy-done | bytes 1048600
  35.8 0.9 %copy-done.9 = bf16[512,256]{1,0:T(8,128)(2,1)S(1)} copy-done((bf16[512,256]{1,0:T(8,128)(2,1)S(1)}, bf16[512,256]{1,0:T(8,128)(2,1)}, u32[]{:S(2)}) %copy-start.9) | copy-done | bytes 262168
  36.7 3.9 %shard_map.144 = (bf16[1024,512]{1,0:T(8,128)(2,1)S(1)}, bf16[128,256]{1,0:T(8,128)(2,1)S(1)}) custom-call(f32[1024,512]{1,0:T(8,128)S(1)} %shard_map.143.base_ref, bf16[1024,1024]{1,0:T(8,128)(2,1)S(1)} %copy-done.2, bf16[2,64,512]{2,1,0:T(8,128)(2,1)S(1)} %copy-done.7, bf16[1,2,512,512]{3,2,1,0:T(8,128)(2,1)S(1)} %copy-done.6, ...), custom_call_target="tpu_custom_call" | custom-call | flops 1073741824 | bytes 4194304 | tf_op jit(solution)/shard_map/pallas_call | solution.py:43
  40.6 0.0 copy-start.12
  40.6 3.7 %collective-permute-start.5 = (bf16[128,256]{1,0:T(8,128)(2,1)S(1)}, bf16[128,256]{1,0:T(8,128)(2,1)S(1)}, u32[]{:S(2)}, u32[]{:S(2)}) collective-permute-start(bf16[128,256]{1,0:T(8,128)(2,1)S(1)} %get-tuple-element.17.refs_0_), channel_id=1, source_target_pairs={{3,0},{0,1},{1,2},{2,3},{7,4},{4,5},{5,6},{6,7},{11,8},{8,9},{9,10... | collective-permute-start | bytes 196616 | tf_op jit(solution)/shard_map/ppermute | solution.py:261
  44.3 1.6 %collective-permute-start.4 = (bf16[128,256]{1,0:T(8,128)(2,1)S(1)}, bf16[128,256]{1,0:T(8,128)(2,1)S(1)}, u32[]{:S(2)}, u32[]{:S(2)}) collective-permute-start(bf16[128,256]{1,0:T(8,128)(2,1)S(1)} %get-tuple-element.17.refs_0_), channel_id=1, source_target_pairs={{2,0},{3,1},{0,2},{1,3},{6,4},{7,5},{4,6},{5,7},{10,8},{11,9},{8,1... | collective-permute-start | bytes 196616 | tf_op jit(solution)/shard_map/ppermute | solution.py:261
  46.0 0.8 %collective-permute-start.3 = (bf16[128,256]{1,0:T(8,128)(2,1)S(1)}, bf16[128,256]{1,0:T(8,128)(2,1)S(1)}, u32[]{:S(2)}, u32[]{:S(2)}) collective-permute-start(bf16[128,256]{1,0:T(8,128)(2,1)S(1)} %get-tuple-element.17.refs_0_), channel_id=1, source_target_pairs={{1,0},{2,1},{3,2},{0,3},{5,4},{6,5},{7,6},{4,7},{9,8},{10,9},{11,1... | collective-permute-start | bytes 196616 | tf_op jit(solution)/shard_map/ppermute | solution.py:261
  46.8 0.8 %shard_map.145 = (f32[1024,512]{1,0:T(8,128)S(1)}, bf16[1024,256]{1,0:T(8,128)(2,1)S(1)}) custom-call(bf16[1024,512]{1,0:T(8,128)(2,1)S(1)} %get-tuple-element.19.state_ref.refs_7_, bf16[1024,512]{1,0:T(8,128)(2,1)S(1)} %copy-done, s32[2,1024]{1,0:T(2,128)S(1)} %copy-done.13), custom_call_target="tpu_custom_call" | custom-call | flops 536870912 | bytes 4194304 | tf_op jit(solution)/shard_map/pallas_call | solution.py:43
  47.5 0.9 %collective-permute-done.5.refs_3_ = bf16[128,256]{1,0:T(8,128)(2,1)S(1)} collective-permute-done((bf16[128,256]{1,0:T(8,128)(2,1)S(1)}, bf16[128,256]{1,0:T(8,128)(2,1)S(1)}, u32[]{:S(2)}, u32[]{:S(2)}) %collective-permute-start.5) | collective-permute-done | bytes 65568 | tf_op jit(solution)/shard_map/ppermute | solution.py:261
  48.4 2.2 %collective-permute-done.4.refs_2_ = bf16[128,256]{1,0:T(8,128)(2,1)S(1)} collective-permute-done((bf16[128,256]{1,0:T(8,128)(2,1)S(1)}, bf16[128,256]{1,0:T(8,128)(2,1)S(1)}, u32[]{:S(2)}, u32[]{:S(2)}) %collective-permute-start.4) | collective-permute-done | bytes 65568 | tf_op jit(solution)/shard_map/ppermute | solution.py:261
  50.7 0.4 collective-permute-done.3.refs_1_
  51.1 2.3 %shard_map.146 = (bf16[1024,512]{1,0:T(8,128)(2,1)}, bf16[32,256]{1,0:T(8,128)(2,1)}) custom-call(bf16[128,256]{1,0:T(8,128)(2,1)S(1)} %get-tuple-element.17.refs_0_, bf16[128,256]{1,0:T(8,128)(2,1)S(1)} %collective-permute-done.3.refs_1_, bf16[128,256]{1,0:T(8,128)(2,1)S(1)} %collective-permute-done.4.refs_2_, ...), custom_call_target="tpu_custom_call" | custom-call | flops 268435456 | bytes 4194304 | tf_op jit(solution)/shard_map/pallas_call | solution.py:43
  (24 shorter events, 0.0 us)
Async XLA Ops:
  0.6 19.6 %copy-start.8 = (bf16[16,64,128]{2,1,0:T(8,128)(2,1)S(1)}, bf16[16,64,128]{2,1,0:T(8,128)(2,1)}, u32[]{:S(2)}) copy-start(bf16[16,64,128]{2,1,0:T(8,128)(2,1)} %refs_1_.1) | copy-start | bytes 786436
  0.6 0.8 %copy-start.14 = (bf16[32,256]{1,0:T(8,128)(2,1)S(1)}, bf16[32,256]{1,0:T(8,128)(2,1)}, u32[]{:S(2)}) copy-start(bf16[32,256]{1,0:T(8,128)(2,1)} %atoms_ref.1) | copy-start | bytes 49156
  1.4 10.5 %copy-start.16 = (s32[16,2]{0,1:T(2,128)S(1)}, s32[16,2]{0,1:T(2,128)}, u32[]{:S(2)}) copy-start(s32[16,2]{0,1:T(2,128)} %param.17) | copy-start | bytes 388
  1.4 10.6 %copy-start.15 = (s32[1024]{0:T(1024)S(1)}, s32[1024]{0:T(1024)}, u32[]{:S(2)}) copy-start(s32[1024]{0:T(1024)} %param.15) | copy-start | bytes 12292
  4.9 22.5 %copy-start.5 = (bf16[1024,512]{1,0:T(8,128)(2,1)S(1)}, bf16[1024,512]{1,0:T(8,128)(2,1)}, u32[]{:S(2)}) copy-start(bf16[1024,512]{1,0:T(8,128)(2,1)} %edges_ref.1) | copy-start | bytes 3145732
  4.9 22.5 %copy-start.7 = (bf16[2,64,512]{2,1,0:T(8,128)(2,1)S(1)}, bf16[2,64,512]{2,1,0:T(8,128)(2,1)}, u32[]{:S(2)}) copy-start(bf16[2,64,512]{2,1,0:T(8,128)(2,1)} %up_ref.3) | copy-start | bytes 393220
  4.9 12.5 %collective-permute-start.2 = (bf16[576,128]{1,0:T(8,128)(2,1)S(1)}, bf16[576,128]{1,0:T(8,128)(2,1)S(1)}, u32[]{:S(2)}, u32[]{:S(2)}) collective-permute-start(bf16[576,128]{1,0:T(8,128)(2,1)S(1)} %shard_map.140.refs_2_), channel_id=1, source_target_pairs={{3,0},{0,1},{1,2},{2,3},{7,4},{4,5},{5,6},{6,7},{11,8},{8,9},{9,10... | collective-permute-start | bytes 442376 | tf_op jit(solution)/shard_map/ppermute | solution.py:261
  8.0 12.3 %collective-permute-start.1 = (bf16[576,128]{1,0:T(8,128)(2,1)S(1)}, bf16[576,128]{1,0:T(8,128)(2,1)S(1)}, u32[]{:S(2)}, u32[]{:S(2)}) collective-permute-start(bf16[576,128]{1,0:T(8,128)(2,1)S(1)} %shard_map.140.refs_2_), channel_id=1, source_target_pairs={{2,0},{3,1},{0,2},{1,3},{6,4},{7,5},{4,6},{5,7},{10,8},{11,9},{8,1... | collective-permute-start | bytes 442376 | tf_op jit(solution)/shard_map/ppermute | solution.py:261
  10.6 9.7 %collective-permute-start = (bf16[576,128]{1,0:T(8,128)(2,1)S(1)}, bf16[576,128]{1,0:T(8,128)(2,1)S(1)}, u32[]{:S(2)}, u32[]{:S(2)}) collective-permute-start(bf16[576,128]{1,0:T(8,128)(2,1)S(1)} %shard_map.140.refs_2_), channel_id=1, source_target_pairs={{1,0},{2,1},{3,2},{0,3},{5,4},{6,5},{7,6},{4,7},{9,8},{10,9},{11,1... | collective-permute-start | bytes 442376 | tf_op jit(solution)/shard_map/ppermute | solution.py:261
  14.7 1.3 %copy-start.1 = (bf16[1024,1024]{1,0:T(8,128)(2,1)}, bf16[1024,1024]{1,0:T(8,128)(2,1)S(1)}, u32[]{:S(2)}) copy-start(bf16[1024,1024]{1,0:T(8,128)(2,1)S(1)} %get-tuple-element.15.fetch_ref) | copy-start | bytes 6291460
  16.1 1.3 %copy-start.3 = (bf16[1024,1024]{1,0:T(8,128)(2,1)}, bf16[1024,1024]{1,0:T(8,128)(2,1)S(1)}, u32[]{:S(2)}) copy-start(bf16[1024,1024]{1,0:T(8,128)(2,1)S(1)} %get-tuple-element.14.local_ref) | copy-start | bytes 6291460
  23.0 0.7 %copy-start.10 = (bf16[1024,64]{1,0:T(8,128)(2,1)}, bf16[1024,64]{1,0:T(8,128)(2,1)S(1)}, u32[]{:S(2)}) copy-start(bf16[1024,64]{1,0:T(8,128)(2,1)S(1)} %get-tuple-element.13.trip_ref) | copy-start | bytes 393220
  23.7 9.3 %all-to-all-start = ((bf16[8,64,128]{2,1,0:T(8,128)(2,1)}), bf16[8,64,128]{2,1,0:T(8,128)(2,1)S(1)}, u32[]{:S(2)}, u32[]{:S(2)}) async-start(bf16[8,64,128]{2,1,0:T(8,128)(2,1)} %bitcast.1), calls=%async_computation | async-start | bytes 262144 | tf_op jit(solution)/shard_map/all_to_all | solution.py:325
  27.4 1.6 %copy-start.4 = (bf16[1024,1024]{1,0:T(8,128)(2,1)S(1)}, bf16[1024,1024]{1,0:T(8,128)(2,1)}, u32[]{:S(2)}) copy-start(bf16[1024,1024]{1,0:T(8,128)(2,1)} %copy-done.3) | copy-start | bytes 6291460
  29.0 0.9 %copy-start.11 = (bf16[1024,64]{1,0:T(8,128)(2,1)S(1)}, bf16[1024,64]{1,0:T(8,128)(2,1)}, u32[]{:S(2)}) copy-start(bf16[1024,64]{1,0:T(8,128)(2,1)} %copy-done.10) | copy-start | bytes 393220
  30.0 3.0 %copy-start.13 = (s32[2,1024]{1,0:T(2,128)S(1)}, s32[2,1024]{1,0:T(2,128)}, u32[]{:S(2)}) copy-start(s32[2,1024]{1,0:T(2,128)} %index_ref.3) | copy-start | bytes 24580
  33.0 1.6 %copy-start.2 = (bf16[1024,1024]{1,0:T(8,128)(2,1)S(1)}, bf16[1024,1024]{1,0:T(8,128)(2,1)}, u32[]{:S(2)}) copy-start(bf16[1024,1024]{1,0:T(8,128)(2,1)} %copy-done.1) | copy-start | bytes 6291460
  34.6 1.2 %copy-start.6 = (bf16[1,2,512,512]{3,2,1,0:T(8,128)(2,1)S(1)}, bf16[1,2,512,512]{3,2,1,0:T(8,128)(2,1)}, u32[]{:S(2)}) copy-start(bf16[1,2,512,512]{3,2,1,0:T(8,128)(2,1)} %residual_ref.1) | copy-start | bytes 3145732
  35.8 0.9 %copy-start.9 = (bf16[512,256]{1,0:T(8,128)(2,1)S(1)}, bf16[512,256]{1,0:T(8,128)(2,1)}, u32[]{:S(2)}) copy-start(bf16[512,256]{1,0:T(8,128)(2,1)} %message_ref.1) | copy-start | bytes 786436
  36.7 10.0 %copy-start = (bf16[1024,512]{1,0:T(8,128)(2,1)S(1)}, bf16[1024,512]{1,0:T(8,128)(2,1)}, u32[]{:S(2)}) copy-start(bf16[1024,512]{1,0:T(8,128)(2,1)} %refs_6_.1) | copy-start | bytes 3145732
  40.6 10.4 %copy-start.12 = (bf16[2,256,256]{2,1,0:T(8,128)(2,1)S(1)}, bf16[2,256,256]{2,1,0:T(8,128)(2,1)}, u32[]{:S(2)}) copy-start(bf16[2,256,256]{2,1,0:T(8,128)(2,1)} %refs_5_.1) | copy-start | bytes 786436
  40.6 7.8 %collective-permute-start.5 = (bf16[128,256]{1,0:T(8,128)(2,1)S(1)}, bf16[128,256]{1,0:T(8,128)(2,1)S(1)}, u32[]{:S(2)}, u32[]{:S(2)}) collective-permute-start(bf16[128,256]{1,0:T(8,128)(2,1)S(1)} %get-tuple-element.17.refs_0_), channel_id=1, source_target_pairs={{3,0},{0,1},{1,2},{2,3},{7,4},{4,5},{5,6},{6,7},{11,8},{8,9},{9,10... | collective-permute-start | bytes 196616 | tf_op jit(solution)/shard_map/ppermute | solution.py:261
  44.3 6.3 %collective-permute-start.4 = (bf16[128,256]{1,0:T(8,128)(2,1)S(1)}, bf16[128,256]{1,0:T(8,128)(2,1)S(1)}, u32[]{:S(2)}, u32[]{:S(2)}) collective-permute-start(bf16[128,256]{1,0:T(8,128)(2,1)S(1)} %get-tuple-element.17.refs_0_), channel_id=1, source_target_pairs={{2,0},{3,1},{0,2},{1,3},{6,4},{7,5},{4,6},{5,7},{10,8},{11,9},{8,1... | collective-permute-start | bytes 196616 | tf_op jit(solution)/shard_map/ppermute | solution.py:261
  46.0 5.1 %collective-permute-start.3 = (bf16[128,256]{1,0:T(8,128)(2,1)S(1)}, bf16[128,256]{1,0:T(8,128)(2,1)S(1)}, u32[]{:S(2)}, u32[]{:S(2)}) collective-permute-start(bf16[128,256]{1,0:T(8,128)(2,1)S(1)} %get-tuple-element.17.refs_0_), channel_id=1, source_target_pairs={{1,0},{2,1},{3,2},{0,3},{5,4},{6,5},{7,6},{4,7},{9,8},{10,9},{11,1... | collective-permute-start | bytes 196616 | tf_op jit(solution)/shard_map/ppermute | solution.py:261

commit v3 on v2

--- a/solution.py
+++ b/solution.py
@@ -35,7 +35,6 @@
     def space(at):
         return pltpu.SMEM if at in smem else pltpu.HBM if at in hbm else pltpu.VMEM
 
-    in_specs = [pl.BlockSpec(memory_space=space(at)) for at in range(len(args))]
     args = [
         pltpu.with_memory_space_constraint(arg, pltpu.HBM) if at in hbm else arg
         for at, arg in enumerate(args)
@@ -43,20 +42,25 @@
     return pl.pallas_call(
         kernel,
         out_shape=outs,
-        in_specs=in_specs,
-        out_specs=jax.tree.map(lambda _: pl.BlockSpec(memory_space=pltpu.VMEM), outs),
+        in_specs=[pl.BlockSpec(memory_space=space(at)) for at in range(len(args))],
+        out_specs=jax.tree.map(
+            lambda out: pl.BlockSpec(
+                memory_space=pltpu.HBM if out.memory_space == pltpu.HBM else pltpu.VMEM
+            ),
+            outs,
+        ),
         scratch_shapes=list(scratch),
         compiler_params=pltpu.CompilerParams(vmem_limit_bytes=limit * MIB),
         cost_estimate=pl.CostEstimate(flops=flops, bytes_accessed=nbytes, transcendentals=0),
     )(*args)
 
 
-def shaped(shape, dtype=jnp.bfloat16):
-    return jax.ShapeDtypeStruct(shape, dtype)
+def shaped(shape, dtype=jnp.bfloat16, space=pltpu.VMEM):
+    return space(tuple(shape), dtype)
 
 
 def narrow_kernel(
-    edges_hbm, weight_hbm, down_hbm, atoms_ref, out_ref, edges_ref, weight_ref, down_ref, sems
+    edges_hbm, weight_hbm, down_hbm, atoms_hbm, out_ref, edges_ref, weight_ref, down_ref, sems
 ):
     half = edges_hbm.shape[0] // 2
     pieces = [
@@ -71,19 +75,27 @@
         pltpu.make_async_copy(edges_hbm.at[piece], edges_ref.at[piece], sems.at[2 + at])
         for at, piece in enumerate(pieces)
     ]
-    for copy in [copies[0], copies[2], copies[1]] + copies[3:]:
+    for copy in [copies[0], copies[2], copies[3], copies[1]] + copies[4:]:
         copy.start()
-    count, wide = atoms_ref.shape
-    for at in range(wide // 128):
-        out_ref[half + at * count : half + (at + 1) * count, :] = atoms_ref[
-            :, at * 128 : (at + 1) * 128
-        ]
+    count, wide = atoms_hbm.shape
+    lanes = out_ref.shape[1]
+    atom_copies = [
+        pltpu.make_async_copy(
+            atoms_hbm.at[:, at * lanes : (at + 1) * lanes],
+            out_ref.at[half + at * count : half + (at + 1) * count, :],
+            sems.at[len(copies) + at],
+        )
+        for at in range(wide // lanes)
+    ]
+    for copy in atom_copies:
+        copy.start()
     copies[0].wait()
     copies[1].wait()
     for at, rows in enumerate(row_chunks(half)):
+        copies[2 + 2 * at].wait()
+        copies[3 + 2 * at].wait()
         sides = []
         for side in range(2):
-            copies[2 + 2 * at + side].wait()
             hidden = silu(product(edges_ref[pieces[2 * at + side], :], weight_ref[...]))
             sides.append(
                 silu(
@@ -96,9 +108,22 @@
                 )
             )
         out_ref[rows, :] = jnp.concatenate(sides, axis=1).astype(jnp.bfloat16)
-
-
-def index_kernel(domains, shards, reverse_ref, send_ref, fetch_ref, local_ref):
+    for copy in atom_copies:
+        copy.wait()
+
+
+def index_kernel(domains, shards, operands, *refs):
+    reverse_ref = refs[0]
+    sources = refs[1 : 1 + operands]
+    send_ref, fetch_ref, local_ref = refs[1 + operands : 4 + operands]
+    targets = refs[4 + operands : 4 + 2 * operands]
+    sems = refs[-1]
+    copies = [
+        pltpu.make_async_copy(source, target, sems.at[at])
+        for at, (source, target) in enumerate(zip(sources, targets))
+    ]
+    for copy in copies:
+        copy.start()
     rows = reverse_ref.shape[1]
     capacity = rows // domains
     half = capacity // 2
@@ -138,25 +163,35 @@
     local_ref[...] = (
         lax.broadcasted_iota(jnp.int32, (rows, rows), 1) == local_column
     ).astype(jnp.bfloat16)
-
-
-def mix_kernel(shards, *refs):
-    source_ref, tiles_ref = refs[:2]
-    parts = refs[2 : 2 + shards]
-    send_ref, trip_ref, out_ref, atoms_ref, held_ref = refs[2 + shards :]
+    for copy in copies:
+        copy.wait()
+
+
+def mix_kernel(count_parts, *refs):
+    source_ref, place_ref, tiles_ref = refs[:3]
+    parts = refs[3 : 3 + count_parts]
+    send_ref, trip_ref, out_ref, atoms_ref, held_ref = refs[3 + count_parts :]
     blocks, block_len, width = tiles_ref.shape
     count = width // block_len
-    lines = held_ref.shape[0] // shards
-    part_atoms, atom_wide = atoms_ref.shape
-    near_atoms = part_atoms // shards
+    lines = held_ref.shape[0] // count_parts
+    atom_wide = atoms_ref.shape[1]
+    tail = parts[0].shape[0] - lines
+    own_atoms = tail * parts[0].shape[1] // atom_wide
+    shards = atoms_ref.shape[0] // own_atoms
+    lanes = parts[0].shape[1]
     me = lax.axis_index("edge")
-    for at in range(shards):
+    for at in range(count_parts):
         held_ref[at * lines : (at + 1) * lines, :] = parts[at][:lines, :]
-        for piece in range(atom_wide // 128):
-            start = lines + piece * near_atoms
+    for by in range(shards):
+        place = place_ref[lax.rem(me + by, shards)]
+        for piece in range(atom_wide // lanes):
+            start = lines + piece * own_atoms
+            rows = parts[0][start : start + own_atoms, :]
+            for at in range(1, count_parts):
+                rows = jnp.where(place == at, parts[at][start : start + own_atoms, :], rows)
             atoms_ref[
-                at * near_atoms : (at + 1) * near_atoms, piece * 128 : (piece + 1) * 128
-            ] = parts[at][start : start + near_atoms, :]
+                by * own_atoms : (by + 1) * own_atoms, piece * lanes : (piece + 1) * lanes
+            ] = rows
     half_blocks = blocks // 2
     channels = trip_ref.shape[1]
     for block in range(blocks):
@@ -166,8 +201,7 @@
             shard = source // blocks
             within = source - shard * blocks
             upper = within // half_blocks
-            near = lax.rem(shard - me + shards, shards)
-            start = near * lines + (within - upper * half_blocks) * block_len
+            start = place_ref[shard] * lines + (within - upper * half_blocks) * block_len
             rows = held_ref[pl.ds(pl.multiple_of(start, block_len), block_len), :]
             picks.append(jnp.where(upper == 1, rows[:, channels:], rows[:, :channels]))
         mixed = product(tiles_ref[block], jnp.concatenate(picks, axis=0))
@@ -233,7 +267,7 @@
 def final_kernel(shards, scale, *refs):
     sums = refs[:shards]
     atoms_ref, weight_ref, join_ref, state_ref, side_ref, chosen_ref = refs[shards : shards + 6]
-    edges_ref, own_ref, table_ref = refs[shards + 6 :]
+    edges_hbm, own_ref, table_ref, edges_ref, sems = refs[shards + 6 :]
     part_atoms = atoms_ref.shape[0]
     count = part_atoms // shards
     total = sums[0][...].astype(jnp.float32)
@@ -250,10 +284,17 @@
         table_ref[end * part_atoms : (end + 1) * part_atoms, :] = product(
             renewed, join_ref[end * width : (end + 1) * width, :]
         ).astype(jnp.bfloat16)
-    for rows in row_chunks(state_ref.shape[0]):
+    copies = []
+    for at, rows in enumerate(row_chunks(state_ref.shape[0])):
         update = silu(product(chosen_ref[rows, :], table_ref[...]) + side_ref[rows, :])
         state = state_ref[rows, :].astype(jnp.float32)
         edges_ref[rows, :] = ((state + update) * root_half).astype(jnp.bfloat16)
+        copies.append(
+            pltpu.make_async_copy(edges_ref.at[rows], edges_hbm.at[rows], sems.at[at])
+        )
+        copies[-1].start()
+    for copy in copies:
+        copy.wait()
 
 
 def from_next(value, shards):
@@ -261,6 +302,18 @@
         lax.ppermute(value, "edge", [((at + by) % shards, at) for at in range(shards)])
         for by in range(1, shards)
     ]
+
+
+def along_edge(value, shards):
+    if shards != 4:
+        parts = [value] + from_next(value, shards)
+        return parts, [[(to - at) % shards for to in range(shards)] for at in range(shards)]
+    far = lax.ppermute(value, "edge", [(0, 2), (2, 0), (1, 3), (3, 1)])
+    middle = lax.ppermute(value, "edge", [(1, 2), (2, 1)])
+    near = lax.ppermute(value, "edge", [(0, 1), (1, 0), (2, 3), (3, 2)])
+    relayed = lax.ppermute(far, "edge", [(2, 3), (1, 0)])
+    parts = [value, near, far, middle, relayed]
+    return parts, [[0, 1, 2, 4], [1, 0, 3, 2], [2, 3, 0, 1], [4, 2, 1, 0]]
 
 
 def body(
@@ -291,34 +344,41 @@
         narrow_kernel,
         shaped((lines + count * atom_wide // packed, packed)),
         (edges, weight_edge, weight_down, atoms),
-        hbm=(0, 1, 2),
+        hbm=(0, 1, 2, 3),
         scratch=[
             pltpu.VMEM(edges.shape, jnp.bfloat16),
             pltpu.VMEM(weight_edge.shape, jnp.bfloat16),
             pltpu.VMEM(weight_down.shape, jnp.bfloat16),
-            pltpu.SemaphoreType.DMA((2 + 2 * len(row_chunks(lines)),)),
+            pltpu.SemaphoreType.DMA((2 + 2 * len(row_chunks(lines)) + atom_wide // packed,)),
         ],
         flops=2 * rows * wide * (wide + channels),
         nbytes=2 * (rows * wide + wide * wide),
     )
-    narrow_parts = [narrow] + from_next(narrow, shards)
-    send, fetch, local = call(
-        functools.partial(index_kernel, domains, shards),
-        (shaped((rows, rows)),) * 3,
-        (reverse.reshape(1, rows),),
+    narrow_parts, places = along_edge(narrow, shards)
+    place = jnp.asarray(places, jnp.int32)[lax.axis_index("edge")]
+    later = (
+        edges, tiles, weight_up, weight_residual, weight_message, weight_join, weight_atom, atom_index
+    )
+    send, fetch, local, *later = call(
+        functools.partial(index_kernel, domains, shards, len(later)),
+        (shaped((rows, rows)),) * 3 + tuple(shaped(each.shape, each.dtype) for each in later),
+        (reverse.reshape(1, rows), *later),
+        hbm=range(1, 1 + len(later)),
+        scratch=[pltpu.SemaphoreType.DMA((len(later),))],
         flops=40 * rows * rows,
         nbytes=6 * rows * rows,
     )
+    edges, tiles, weight_up, weight_residual, weight_message, weight_join, weight_atom, atom_index = later
     trip_out, outgoing, all_atoms = call(
-        functools.partial(mix_kernel, shards),
+        functools.partial(mix_kernel, len(narrow_parts)),
         (
             shaped((rows, channels)),
             shaped((lines, packed)),
             shaped((part_atoms, atom_wide)),
         ),
-        (tile_source, tiles, *narrow_parts, send),
-        smem=(0,),
-        scratch=[pltpu.VMEM((shards * lines, packed), jnp.bfloat16)],
+        (tile_source, place, tiles, *narrow_parts, send),
+        smem=(0, 1),
+        scratch=[pltpu.VMEM((len(narrow_parts) * lines, packed), jnp.bfloat16)],
         flops=2 * rows * rows * channels,
         nbytes=2 * rows * rows,
     )
@@ -348,9 +408,13 @@
     )
     return call(
         functools.partial(final_kernel, shards, (rows // count) ** -0.5),
-        (shaped((rows, wide)), shaped((count, atom_wide))),
+        (shaped((rows, wide), space=pltpu.HBM), shaped((count, atom_wide))),
         (*sums_parts, all_atoms, weight_atom, weight_join, state, side, chosen),
-        scratch=[pltpu.VMEM((2 * part_atoms, wide), jnp.bfloat16)],
+        scratch=[
+            pltpu.VMEM((2 * part_atoms, wide), jnp.bfloat16),
+            pltpu.VMEM((rows, wide), jnp.bfloat16),
+            pltpu.SemaphoreType.DMA((len(row_chunks(rows)),)),
+        ],
         flops=4 * rows * part_atoms * wide,
         nbytes=8 * rows * wide,
     )

time: 53.8 us -> 56.9 us (1.058)
  starting transfers between devices: 16.9 us -> 19.6 us
  local copies, waits for them, and re-layouts: 10.5 us -> 12.3 us
  waiting for transfers between devices: 7.79 us -> 6.84 us
  Pallas kernels: 17.4 us -> 16.8 us
    ppermute x0 -> x4, starting transfers between devices: none -> 8.93 us  [the longest x1 4.1 us: along_edge(): far = lax.ppermute(value, 'edge', [(0, 2), (2, 0), (1, 3), (3, 1)])]
    ppermute x6 -> x3, starting transfers between devices: 13.1 us -> 6.66 us  [from_next(): lax.ppermute(value, 'edge', [((at + by) % shards, at) for at in range(sha...]
    ppermute x0 -> x4, waiting for transfers between devices: none -> 4.34 us  [the longest x1 4.33 us: along_edge(): far = lax.ppermute(value, 'edge', [(0, 2), (2, 0), (1, 3), (3, 1)])]
    ppermute x6 -> x3, waiting for transfers between devices: 6.39 us -> 2.31 us  [from_next(): lax.ppermute(value, 'edge', [((at + by) % shards, at) for at in range(sha...]
    all_to_all x1, waiting for transfers between devices: 1.4 us -> 0.19 us  [body(): lax.all_to_all(outgoing, 'dom', split_axis=0, concat_axis=0, tiled=True)]
    unnamed x35 -> x34, local copies, waits for them, and re-layouts: 10.5 us -> 11.6 us
    squeeze x0 -> x1, local copies, waits for them, and re-layouts: none -> 0.74 us  [body(): place = jnp.asarray(places, jnp.int32)[lax.axis_index('edge')]]
    pallas_call x7, Pallas kernels: 17.4 us -> 16.8 us  [call(): pl.pallas_call(kernel, out_shape=outs, in_specs=[pl.BlockSpec(memory_spac...]
  transfers between devices with their start and end apart: 7 -> 8, of which waited for: 5 -> 3; matrix products, arithmetic and copies ran while one was open for 0% -> 1% of each run, Pallas kernels for 9% -> 9%
where the time goes in v3:
time: 56.9 us; the launch traced here: 56.4 us
  starting transfers between devices  19.6 us (34%)
  Pallas kernels  16.8 us (30%)
  local copies, waits for them, and re-layouts  12.3 us (22%)
  waiting for transfers between devices  6.84 us (12%)
  between operations  0.78 us (1%)
    pallas_call x7, Pallas kernels, call(): pl.pallas_call(kernel, out_shape=outs, in_specs=[pl.BlockSpec(memory_spac...  16.8 us
    unnamed x34, local copies, waits for them, and re-layouts  11.6 us
    ppermute x3, starting transfers between devices, from_next(): lax.ppermute(value, 'edge', [((at + by) % shards, at) for at in range(sha...  6.66 us
    ppermute x1, waiting for transfers between devices, along_edge(): far = lax.ppermute(value, 'edge', [(0, 2), (2, 0), (1, 3), (3, 1)])  4.33 us
    ppermute x1, starting transfers between devices, along_edge(): far = lax.ppermute(value, 'edge', [(0, 2), (2, 0), (1, 3), (3, 1)])  4.1 us
    all_to_all x1, starting transfers between devices, body(): lax.all_to_all(outgoing, 'dom', split_axis=0, concat_axis=0, tiled=True)  4.03 us
    ppermute x1, starting transfers between devices, along_edge(): near = lax.ppermute(value, 'edge', [(0, 1), (1, 0), (2, 3), (3, 2)])  2.89 us
    ppermute x3, waiting for transfers between devices, from_next(): lax.ppermute(value, 'edge', [((at + by) % shards, at) for at in range(sha...  2.31 us
  transfers between devices with their start and end apart: 8, of which 3 were waited for; matrix products, arithmetic and copies ran while one was open for 1% of the time, Pallas kernels for 9%

profile of v3, /device:TPU:0, one launch (start us, length us, event | category | flops | bytes accessed | tf_op | source)
XLA Modules:
  0.0 56.4 jit_solution(10947873908518101933)
XLA Ops:
  0.7 3.0 %shard_map.150.refs_3_ = bf16[576,128]{1,0:T(8,128)(2,1)S(1)} custom-call(bf16[1024,512]{1,0:T(8,128)(2,1)} %edges_hbm.1, bf16[512,512]{1,0:T(8,128)(2,1)} %weight_hbm.1, bf16[64,512]{1,0:T(8,128)(2,1)} %down_hbm.1, bf16[32,256]{1,0:T(8,128)(2,1)} %atoms_hbm.1), custom_call_target="tpu_custom_call" | custom-call | flops 603979776 | bytes 1572864 | tf_op jit(solution)/shard_map/pallas_call | solution.py:42
  3.7 4.1 %collective-permute-start.1 = (bf16[576,128]{1,0:T(8,128)(2,1)S(1)}, bf16[576,128]{1,0:T(8,128)(2,1)S(1)}, u32[]{:S(2)}, u32[]{:S(2)}) collective-permute-start(bf16[576,128]{1,0:T(8,128)(2,1)S(1)} %shard_map.150.refs_3_), channel_id=1, source_target_pairs={{0,2},{2,0},{1,3},{3,1},{4,6},{6,4},{5,7},{7,5},{8,10},{10,8},{9,1... | collective-permute-start | bytes 442376 | tf_op jit(solution)/shard_map/ppermute | solution.py:311
  7.8 0.7 %collective-permute-start.2 = (bf16[576,128]{1,0:T(8,128)(2,1)S(1)}, bf16[576,128]{1,0:T(8,128)(2,1)S(1)}, u32[]{:S(2)}, u32[]{:S(2)}) collective-permute-start(bf16[576,128]{1,0:T(8,128)(2,1)S(1)} %shard_map.150.refs_3_), channel_id=1, source_target_pairs={{1,2},{2,1},{5,6},{6,5},{9,10},{10,9},{13,14},{14,13},{17,18},{18,... | collective-permute-start | bytes 442376 | tf_op jit(solution)/shard_map/ppermute | solution.py:312
  8.4 2.9 %collective-permute-start = (bf16[576,128]{1,0:T(8,128)(2,1)S(1)}, bf16[576,128]{1,0:T(8,128)(2,1)S(1)}, u32[]{:S(2)}, u32[]{:S(2)}) collective-permute-start(bf16[576,128]{1,0:T(8,128)(2,1)S(1)} %shard_map.150.refs_3_), channel_id=1, source_target_pairs={{0,1},{1,0},{2,3},{3,2},{4,5},{5,4},{6,7},{7,6},{8,9},{9,8},{10,11... | collective-permute-start | bytes 442376 | tf_op jit(solution)/shard_map/ppermute | solution.py:313
  11.3 4.3 %collective-permute-done.1.refs_5_ = bf16[576,128]{1,0:T(8,128)(2,1)S(1)} collective-permute-done((bf16[576,128]{1,0:T(8,128)(2,1)S(1)}, bf16[576,128]{1,0:T(8,128)(2,1)S(1)}, u32[]{:S(2)}, u32[]{:S(2)}) %collective-permute-start.1) | collective-permute-done | bytes 147488 | tf_op jit(solution)/shard_map/ppermute | solution.py:311
  15.7 1.3 %collective-permute-start.3 = (bf16[576,128]{1,0:T(8,128)(2,1)S(1)}, bf16[576,128]{1,0:T(8,128)(2,1)S(1)}, u32[]{:S(2)}, u32[]{:S(2)}) collective-permute-start(bf16[576,128]{1,0:T(8,128)(2,1)S(1)} %collective-permute-done.1.refs_5_), channel_id=1, source_target_pairs={{2,3},{1,0},{6,7},{5,4},{10,11},{9,8},{14,15},{13,12},{18,19},{17,... | collective-permute-start | bytes 442376 | tf_op jit(solution)/shard_map/ppermute | solution.py:314
  17.0 0.1 copy.16.refs_0_
  17.1 2.8 %shard_map.149 = (bf16[1024,1024]{1,0:T(8,128)(2,1)S(1)}, bf16[1024,1024]{1,0:T(8,128)(2,1)S(1)}, bf16[1024,1024]{1,0:T(8,128)(2,1)S(1)}, bf16[1024,512]{1,0:T(8...) custom-call(s32[1,1024]{1,0:T(1,128)S(1)} %bitcast.6, ...), custom_call_target="tpu_custom_call" | custom-call | flops 41943040 | bytes 6291456 | tf_op jit(solution)/shard_map/pallas_call | solution.py:42
  19.9 1.3 %copy-done = bf16[1024,1024]{1,0:T(8,128)(2,1)} copy-done((bf16[1024,1024]{1,0:T(8,128)(2,1)}, bf16[1024,1024]{1,0:T(8,128)(2,1)S(1)}, u32[]{:S(2)}) %copy-start) | copy-done | bytes 2097176
  21.2 1.3 %copy-done.2 = bf16[1024,1024]{1,0:T(8,128)(2,1)} copy-done((bf16[1024,1024]{1,0:T(8,128)(2,1)}, bf16[1024,1024]{1,0:T(8,128)(2,1)S(1)}, u32[]{:S(2)}) %copy-start.2) | copy-done | bytes 2097176
  22.5 0.7 %dynamic-slice_bitcast_fusion.refs_1_ = s32[4]{0:T(128)S(1)} fusion(s32[4,4]{1,0:T(4,128)} %constant.10.clone, s32[]{:T(128)S(6)} %select_n.3), kind=kLoop, calls=%fused_computation | loop fusion | bytes 36 | tf_op jit(solution)/shard_map/squeeze | solution.py:358
  23.3 0.0 collective-permute-done.2.refs_6_
  23.3 0.0 collective-permute-done.refs_4_
  23.3 2.7 %shard_map.151 = (bf16[1024,64]{1,0:T(8,128)(2,1)S(1)}, bf16[512,128]{1,0:T(8,128)(2,1)}, bf16[128,256]{1,0:T(8,128)(2,1)S(1)}) custom-call(s32[16,2]{1,0:T(8,128)S(1)} %copy.16.refs_0_, s32[4]{0:T(128)S(1)} %dynamic-slice_bitcast_fusion.refs_1_, bf16[16,64,128]{2,1,0:T(8,128)(2,1)S(1)} %get-tuple-element.21.refs_2_, ...), custom_call_target="tpu_custom_call" | custom-call | flops 134217728 | bytes 2097152 | tf_op jit(solution)/shard_map/pallas_call | solution.py:42
  26.0 0.7 %copy-done.10 = bf16[1024,64]{1,0:T(8,128)(2,1)} copy-done((bf16[1024,64]{1,0:T(8,128)(2,1)}, bf16[1024,64]{1,0:T(8,128)(2,1)S(1)}, u32[]{:S(2)}) %copy-start.10) | copy-done | bytes 131096
  26.7 4.0 %all-to-all-start = ((bf16[8,64,128]{2,1,0:T(8,128)(2,1)}), bf16[8,64,128]{2,1,0:T(8,128)(2,1)S(1)}, u32[]{:S(2)}, u32[]{:S(2)}) async-start(bf16[8,64,128]{2,1,0:T(8,128)(2,1)} %bitcast.2), calls=%async_computation | async-start | bytes 262144 | tf_op jit(solution)/shard_map/all_to_all | solution.py:385
  30.7 1.6 %copy-done.3 = bf16[1024,1024]{1,0:T(8,128)(2,1)S(1)} copy-done((bf16[1024,1024]{1,0:T(8,128)(2,1)S(1)}, bf16[1024,1024]{1,0:T(8,128)(2,1)}, u32[]{:S(2)}) %copy-start.3) | copy-done | bytes 2097176
  32.3 1.2 %copy-done.7 = bf16[1024,512]{1,0:T(8,128)(2,1)S(1)} copy-done((bf16[1024,512]{1,0:T(8,128)(2,1)S(1)}, bf16[1024,512]{1,0:T(8,128)(2,1)}, u32[]{:S(2)}) %copy-start.7) | copy-done | bytes 1048600
  33.5 0.9 %copy-done.11 = bf16[1024,64]{1,0:T(8,128)(2,1)S(1)} copy-done((bf16[1024,64]{1,0:T(8,128)(2,1)S(1)}, bf16[1024,64]{1,0:T(8,128)(2,1)}, u32[]{:S(2)}) %copy-start.11) | copy-done | bytes 131096
  34.5 1.6 %shard_map.152.base_ref = f32[1024,512]{1,0:T(8,128)S(1)} custom-call(bf16[1024,512]{1,0:T(8,128)(2,1)S(1)} %copy-done.7, bf16[1024,64]{1,0:T(8,128)(2,1)S(1)} %copy-done.11, bf16[1024,1024]{1,0:T(8,128)(2,1)S(1)} %copy-done.3, bf16[2,64,512]{2,1,0:T(8,128)(2,1)S(1)} %get-tuple-element.25.up_ref), custom_call_target="tpu_custom_call" | custom-call | flops 268435456 | bytes 5242880 | tf_op jit(solution)/shard_map/pallas_call | solution.py:42
  36.1 0.2 all-to-all-done
  36.3 1.6 %copy-done.1 = bf16[1024,1024]{1,0:T(8,128)(2,1)S(1)} copy-done((bf16[1024,1024]{1,0:T(8,128)(2,1)S(1)}, bf16[1024,1024]{1,0:T(8,128)(2,1)}, u32[]{:S(2)}) %copy-start.1) | copy-done | bytes 2097176
  37.9 1.2 %copy-done.5 = bf16[1,2,512,512]{3,2,1,0:T(8,128)(2,1)S(1)} copy-done((bf16[1,2,512,512]{3,2,1,0:T(8,128)(2,1)S(1)}, bf16[1,2,512,512]{3,2,1,0:T(8,128)(2,1)}, u32[]{:S(2)}) %copy-start.5) | copy-done | bytes 1048600
  39.1 0.9 %copy-done.9 = bf16[512,256]{1,0:T(8,128)(2,1)S(1)} copy-done((bf16[512,256]{1,0:T(8,128)(2,1)S(1)}, bf16[512,256]{1,0:T(8,128)(2,1)}, u32[]{:S(2)}) %copy-start.9) | copy-done | bytes 262168
  40.0 3.9 %shard_map.153 = (bf16[1024,512]{1,0:T(8,128)(2,1)S(1)}, bf16[128,256]{1,0:T(8,128)(2,1)S(1)}) custom-call(f32[1024,512]{1,0:T(8,128)S(1)} %shard_map.152.base_ref, bf16[1024,1024]{1,0:T(8,128)(2,1)S(1)} %copy-done.1, bf16[2,64,512]{2,1,0:T(8,128)(2,1)S(1)} %get-tuple-element.25.up_ref, bf16[1,2,512,512]{3,2,1,0:T(8,128)(2,1)S(1)} %copy-done.5, ...), custom_call_target="tpu_custom_call" | custom-call | flops 1073741824 | bytes 4194304 | tf_op jit(solution)/shard_map/pallas_call | solution.py:42
  43.9 2.7 %collective-permute-start.6 = (bf16[128,256]{1,0:T(8,128)(2,1)S(1)}, bf16[128,256]{1,0:T(8,128)(2,1)S(1)}, u32[]{:S(2)}, u32[]{:S(2)}) collective-permute-start(bf16[128,256]{1,0:T(8,128)(2,1)S(1)} %get-tuple-element.31.refs_0_), channel_id=1, source_target_pairs={{3,0},{0,1},{1,2},{2,3},{7,4},{4,5},{5,6},{6,7},{11,8},{8,9},{9,10... | collective-permute-start | bytes 196616 | tf_op jit(solution)/shard_map/ppermute | solution.py:302
  46.6 1.1 %collective-permute-start.5 = (bf16[128,256]{1,0:T(8,128)(2,1)S(1)}, bf16[128,256]{1,0:T(8,128)(2,1)S(1)}, u32[]{:S(2)}, u32[]{:S(2)}) collective-permute-start(bf16[128,256]{1,0:T(8,128)(2,1)S(1)} %get-tuple-element.31.refs_0_), channel_id=1, source_target_pairs={{2,0},{3,1},{0,2},{1,3},{6,4},{7,5},{4,6},{5,7},{10,8},{11,9},{8,1... | collective-permute-start | bytes 196616 | tf_op jit(solution)/shard_map/ppermute | solution.py:302
  47.8 2.8 %collective-permute-start.4 = (bf16[128,256]{1,0:T(8,128)(2,1)S(1)}, bf16[128,256]{1,0:T(8,128)(2,1)S(1)}, u32[]{:S(2)}, u32[]{:S(2)}) collective-permute-start(bf16[128,256]{1,0:T(8,128)(2,1)S(1)} %get-tuple-element.31.refs_0_), channel_id=1, source_target_pairs={{1,0},{2,1},{3,2},{0,3},{5,4},{6,5},{7,6},{4,7},{9,8},{10,9},{11,1... | collective-permute-start | bytes 196616 | tf_op jit(solution)/shard_map/ppermute | solution.py:302
  50.6 0.8 %shard_map.154 = (f32[1024,512]{1,0:T(8,128)S(1)}, bf16[1024,256]{1,0:T(8,128)(2,1)S(1)}) custom-call(bf16[1024,512]{1,0:T(8,128)(2,1)S(1)} %get-tuple-element.35.state_ref.refs_7_, bf16[1024,512]{1,0:T(8,128)(2,1)S(1)} %get-tuple-element.34.join_ref.refs_6_, s32[2,1024]{1,0:T(2,128)S(1)} %get-tuple-element.29.index_ref), custom_call_target="tpu_custom_call" | custom-call | flops 536870912 | bytes 4194304 | tf_op jit(solution)/shard_map/pallas_call | solution.py:42
  51.4 2.3 %collective-permute-done.5.refs_2_ = bf16[128,256]{1,0:T(8,128)(2,1)S(1)} collective-permute-done((bf16[128,256]{1,0:T(8,128)(2,1)S(1)}, bf16[128,256]{1,0:T(8,128)(2,1)S(1)}, u32[]{:S(2)}, u32[]{:S(2)}) %collective-permute-start.5) | collective-permute-done | bytes 65568 | tf_op jit(solution)/shard_map/ppermute | solution.py:302
  53.7 2.1 %shard_map.155 = (bf16[1024,512]{1,0:T(8,128)(2,1)}, bf16[32,256]{1,0:T(8,128)(2,1)S(1)}) custom-call(bf16[128,256]{1,0:T(8,128)(2,1)S(1)} %get-tuple-element.31.refs_0_, bf16[128,256]{1,0:T(8,128)(2,1)S(1)} %collective-permute-done.4.refs_1_, bf16[128,256]{1,0:T(8,128)(2,1)S(1)} %collective-permute-done.5.refs_2_, ...), custom_call_target="tpu_custom_call" | custom-call | flops 268435456 | bytes 4194304 | tf_op jit(solution)/shard_map/pallas_call | solution.py:42
  55.8 0.6 %copy.17 = bf16[32,256]{1,0:T(8,128)(2,1)} copy(bf16[32,256]{1,0:T(8,128)(2,1)S(1)} %get-tuple-element.39) | data formatting | bytes 32768
  (26 shorter events, 0.1 us)
Async XLA Ops:
  0.6 16.3 %copy-start.15 = (s32[16,2]{0,1:T(2,128)S(1)}, s32[16,2]{0,1:T(2,128)}, u32[]{:S(2)}) copy-start(s32[16,2]{0,1:T(2,128)} %param.18) | copy-start | bytes 388
  0.6 16.4 %copy-start.14 = (s32[1024]{0:T(1024)S(1)}, s32[1024]{0:T(1024)}, u32[]{:S(2)}) copy-start(s32[1024]{0:T(1024)} %param.16) | copy-start | bytes 12292
  3.7 12.0 %collective-permute-start.1 = (bf16[576,128]{1,0:T(8,128)(2,1)S(1)}, bf16[576,128]{1,0:T(8,128)(2,1)S(1)}, u32[]{:S(2)}, u32[]{:S(2)}) collective-permute-start(bf16[576,128]{1,0:T(8,128)(2,1)S(1)} %shard_map.150.refs_3_), channel_id=1, source_target_pairs={{0,2},{2,0},{1,3},{3,1},{4,6},{6,4},{5,7},{7,5},{8,10},{10,8},{9,1... | collective-permute-start | bytes 442376 | tf_op jit(solution)/shard_map/ppermute | solution.py:311
  7.8 15.5 %collective-permute-start.2 = (bf16[576,128]{1,0:T(8,128)(2,1)S(1)}, bf16[576,128]{1,0:T(8,128)(2,1)S(1)}, u32[]{:S(2)}, u32[]{:S(2)}) collective-permute-start(bf16[576,128]{1,0:T(8,128)(2,1)S(1)} %shard_map.150.refs_3_), channel_id=1, source_target_pairs={{1,2},{2,1},{5,6},{6,5},{9,10},{10,9},{13,14},{14,13},{17,18},{18,... | collective-permute-start | bytes 442376 | tf_op jit(solution)/shard_map/ppermute | solution.py:312
  8.4 14.8 %collective-permute-start = (bf16[576,128]{1,0:T(8,128)(2,1)S(1)}, bf16[576,128]{1,0:T(8,128)(2,1)S(1)}, u32[]{:S(2)}, u32[]{:S(2)}) collective-permute-start(bf16[576,128]{1,0:T(8,128)(2,1)S(1)} %shard_map.150.refs_3_), channel_id=1, source_target_pairs={{0,1},{1,0},{2,3},{3,2},{4,5},{5,4},{6,7},{7,6},{8,9},{9,8},{10,11... | collective-permute-start | bytes 442376 | tf_op jit(solution)/shard_map/ppermute | solution.py:313
  15.7 7.6 %collective-permute-start.3 = (bf16[576,128]{1,0:T(8,128)(2,1)S(1)}, bf16[576,128]{1,0:T(8,128)(2,1)S(1)}, u32[]{:S(2)}, u32[]{:S(2)}) collective-permute-start(bf16[576,128]{1,0:T(8,128)(2,1)S(1)} %collective-permute-done.1.refs_5_), channel_id=1, source_target_pairs={{2,3},{1,0},{6,7},{5,4},{10,11},{9,8},{14,15},{13,12},{18,19},{17,... | collective-permute-start | bytes 442376 | tf_op jit(solution)/shard_map/ppermute | solution.py:314
  19.9 1.3 %copy-start = (bf16[1024,1024]{1,0:T(8,128)(2,1)}, bf16[1024,1024]{1,0:T(8,128)(2,1)S(1)}, u32[]{:S(2)}) copy-start(bf16[1024,1024]{1,0:T(8,128)(2,1)S(1)} %get-tuple-element.26.fetch_ref) | copy-start | bytes 6291460
  21.2 1.3 %copy-start.2 = (bf16[1024,1024]{1,0:T(8,128)(2,1)}, bf16[1024,1024]{1,0:T(8,128)(2,1)S(1)}, u32[]{:S(2)}) copy-start(bf16[1024,1024]{1,0:T(8,128)(2,1)S(1)} %get-tuple-element.24.local_ref) | copy-start | bytes 6291460
  22.5 3.5 %copy-start.4 = (bf16[1,2,512,512]{3,2,1,0:T(8,128)(2,1)}, bf16[1,2,512,512]{3,2,1,0:T(8,128)(2,1)S(1)}, u32[]{:S(2)}) copy-start(bf16[1,2,512,512]{3,2,1,0:T(8,128)(2,1)S(1)} %get-tuple-element.27.residual_ref) | copy-start | bytes 3145732
  22.5 4.2 %copy-start.6 = (bf16[1024,512]{1,0:T(8,128)(2,1)}, bf16[1024,512]{1,0:T(8,128)(2,1)S(1)}, u32[]{:S(2)}) copy-start(bf16[1024,512]{1,0:T(8,128)(2,1)S(1)} %get-tuple-element.20.edges_ref) | copy-start | bytes 3145732
  22.5 4.2 %copy-start.8 = (bf16[512,256]{1,0:T(8,128)(2,1)}, bf16[512,256]{1,0:T(8,128)(2,1)S(1)}, u32[]{:S(2)}) copy-start(bf16[512,256]{1,0:T(8,128)(2,1)S(1)} %get-tuple-element.28.message_ref) | copy-start | bytes 786436
  22.5 4.2 %copy-start.12 = (bf16[2,256,256]{2,1,0:T(8,128)(2,1)}, bf16[2,256,256]{2,1,0:T(8,128)(2,1)S(1)}, u32[]{:S(2)}) copy-start(bf16[2,256,256]{2,1,0:T(8,128)(2,1)S(1)} %get-tuple-element.33.refs_5_) | copy-start | bytes 786436
  26.0 0.7 %copy-start.10 = (bf16[1024,64]{1,0:T(8,128)(2,1)}, bf16[1024,64]{1,0:T(8,128)(2,1)S(1)}, u32[]{:S(2)}) copy-start(bf16[1024,64]{1,0:T(8,128)(2,1)S(1)} %get-tuple-element.23.trip_ref) | copy-start | bytes 393220
  26.7 9.6 %all-to-all-start = ((bf16[8,64,128]{2,1,0:T(8,128)(2,1)}), bf16[8,64,128]{2,1,0:T(8,128)(2,1)S(1)}, u32[]{:S(2)}, u32[]{:S(2)}) async-start(bf16[8,64,128]{2,1,0:T(8,128)(2,1)} %bitcast.2), calls=%async_computation | async-start | bytes 262144 | tf_op jit(solution)/shard_map/all_to_all | solution.py:385
  30.7 1.6 %copy-start.3 = (bf16[1024,1024]{1,0:T(8,128)(2,1)S(1)}, bf16[1024,1024]{1,0:T(8,128)(2,1)}, u32[]{:S(2)}) copy-start(bf16[1024,1024]{1,0:T(8,128)(2,1)} %copy-done.2) | copy-start | bytes 6291460
  32.3 1.2 %copy-start.7 = (bf16[1024,512]{1,0:T(8,128)(2,1)S(1)}, bf16[1024,512]{1,0:T(8,128)(2,1)}, u32[]{:S(2)}) copy-start(bf16[1024,512]{1,0:T(8,128)(2,1)} %copy-done.6) | copy-start | bytes 3145732
  33.5 0.9 %copy-start.11 = (bf16[1024,64]{1,0:T(8,128)(2,1)S(1)}, bf16[1024,64]{1,0:T(8,128)(2,1)}, u32[]{:S(2)}) copy-start(bf16[1024,64]{1,0:T(8,128)(2,1)} %copy-done.10) | copy-start | bytes 393220
  36.3 1.6 %copy-start.1 = (bf16[1024,1024]{1,0:T(8,128)(2,1)S(1)}, bf16[1024,1024]{1,0:T(8,128)(2,1)}, u32[]{:S(2)}) copy-start(bf16[1024,1024]{1,0:T(8,128)(2,1)} %copy-done) | copy-start | bytes 6291460
  37.8 1.2 %copy-start.5 = (bf16[1,2,512,512]{3,2,1,0:T(8,128)(2,1)S(1)}, bf16[1,2,512,512]{3,2,1,0:T(8,128)(2,1)}, u32[]{:S(2)}) copy-start(bf16[1,2,512,512]{3,2,1,0:T(8,128)(2,1)} %copy-done.4) | copy-start | bytes 3145732
  39.1 0.9 %copy-start.9 = (bf16[512,256]{1,0:T(8,128)(2,1)S(1)}, bf16[512,256]{1,0:T(8,128)(2,1)}, u32[]{:S(2)}) copy-start(bf16[512,256]{1,0:T(8,128)(2,1)} %copy-done.8) | copy-start | bytes 786436
  43.9 9.8 %copy-start.13 = (bf16[2,256,256]{2,1,0:T(8,128)(2,1)S(1)}, bf16[2,256,256]{2,1,0:T(8,128)(2,1)}, u32[]{:S(2)}) copy-start(bf16[2,256,256]{2,1,0:T(8,128)(2,1)} %copy-done.12) | copy-start | bytes 786436
  43.9 7.4 %collective-permute-start.6 = (bf16[128,256]{1,0:T(8,128)(2,1)S(1)}, bf16[128,256]{1,0:T(8,128)(2,1)S(1)}, u32[]{:S(2)}, u32[]{:S(2)}) collective-permute-start(bf16[128,256]{1,0:T(8,128)(2,1)S(1)} %get-tuple-element.31.refs_0_), channel_id=1, source_target_pairs={{3,0},{0,1},{1,2},{2,3},{7,4},{4,5},{5,6},{6,7},{11,8},{8,9},{9,10... | collective-permute-start | bytes 196616 | tf_op jit(solution)/shard_map/ppermute | solution.py:302
  46.6 7.0 %collective-permute-start.5 = (bf16[128,256]{1,0:T(8,128)(2,1)S(1)}, bf16[128,256]{1,0:T(8,128)(2,1)S(1)}, u32[]{:S(2)}, u32[]{:S(2)}) collective-permute-start(bf16[128,256]{1,0:T(8,128)(2,1)S(1)} %get-tuple-element.31.refs_0_), channel_id=1, source_target_pairs={{2,0},{3,1},{0,2},{1,3},{6,4},{7,5},{4,6},{5,7},{10,8},{11,9},{8,1... | collective-permute-start | bytes 196616 | tf_op jit(solution)/shard_map/ppermute | solution.py:302
  47.8 5.9 %collective-permute-start.4 = (bf16[128,256]{1,0:T(8,128)(2,1)S(1)}, bf16[128,256]{1,0:T(8,128)(2,1)S(1)}, u32[]{:S(2)}, u32[]{:S(2)}) collective-permute-start(bf16[128,256]{1,0:T(8,128)(2,1)S(1)} %get-tuple-element.31.refs_0_), channel_id=1, source_target_pairs={{1,0},{2,1},{3,2},{0,3},{5,4},{6,5},{7,6},{4,7},{9,8},{10,9},{11,1... | collective-permute-start | bytes 196616 | tf_op jit(solution)/shard_map/ppermute | solution.py:302

commit v4 on v3

--- a/solution.py
+++ b/solution.py
@@ -127,13 +127,14 @@
     rows = reverse_ref.shape[1]
     capacity = rows // domains
     half = capacity // 2
-    slots = domains * capacity
+    slots = (domains - 1) * capacity
     own = lax.axis_index("dom")
     reverse = reverse_ref[...]
     holder = reverse // (rows * shards)
     source_row = lax.rem(reverse, rows)
+    partner = holder ^ own
     source_column = as_column(source_row)
-    member = (lax.broadcasted_iota(jnp.int32, (domains, rows), 0) == holder).astype(jnp.bfloat16)
+    member = (lax.broadcasted_iota(jnp.int32, (domains, rows), 0) == partner).astype(jnp.bfloat16)
     before = (
         lax.broadcasted_iota(jnp.int32, (rows, rows), 0)
         < lax.broadcasted_iota(jnp.int32, (rows, rows), 1)
@@ -148,8 +149,8 @@
 
     def slot_of(at):
         part = (at >= half).astype(jnp.int32)
-        slot = part * (slots // 2) + holder * half + at - part * half
-        return jnp.where(holder == own, -1, slot)
+        slot = part * (slots // 2) + (partner - 1) * half + at - part * half
+        return jnp.where(partner == 0, -1, slot)
 
     send_slot = slot_of(place)
     send_ref[...] = (
@@ -159,7 +160,7 @@
     fetch_ref[...] = (
         lax.broadcasted_iota(jnp.int32, (rows, slots), 1) == fetch_column
     ).astype(jnp.bfloat16)
-    local_column = as_column(jnp.where(holder == own, source_row, -1))
+    local_column = as_column(jnp.where(partner == 0, source_row, -1))
     local_ref[...] = (
         lax.broadcasted_iota(jnp.int32, (rows, rows), 1) == local_column
     ).astype(jnp.bfloat16)
@@ -167,31 +168,26 @@
         copy.wait()
 
 
-def mix_kernel(count_parts, *refs):
-    source_ref, place_ref, tiles_ref = refs[:3]
-    parts = refs[3 : 3 + count_parts]
-    send_ref, trip_ref, out_ref, atoms_ref, held_ref = refs[3 + count_parts :]
+def mix_kernel(shards, *refs):
+    source_ref, tiles_ref = refs[:2]
+    parts = refs[2 : 2 + shards]
+    send_ref, trip_ref, atoms_ref = refs[2 + shards : 5 + shards]
+    out_refs = refs[5 + shards : -1]
+    held_ref = refs[-1]
     blocks, block_len, width = tiles_ref.shape
     count = width // block_len
-    lines = held_ref.shape[0] // count_parts
+    lines = held_ref.shape[0] // shards
+    own_atoms = atoms_ref.shape[0] // shards
     atom_wide = atoms_ref.shape[1]
-    tail = parts[0].shape[0] - lines
-    own_atoms = tail * parts[0].shape[1] // atom_wide
-    shards = atoms_ref.shape[0] // own_atoms
-    lanes = parts[0].shape[1]
+    lanes = held_ref.shape[1]
     me = lax.axis_index("edge")
-    for at in range(count_parts):
+    for at in range(shards):
         held_ref[at * lines : (at + 1) * lines, :] = parts[at][:lines, :]
-    for by in range(shards):
-        place = place_ref[lax.rem(me + by, shards)]
         for piece in range(atom_wide // lanes):
             start = lines + piece * own_atoms
-            rows = parts[0][start : start + own_atoms, :]
-            for at in range(1, count_parts):
-                rows = jnp.where(place == at, parts[at][start : start + own_atoms, :], rows)
             atoms_ref[
-                by * own_atoms : (by + 1) * own_atoms, piece * lanes : (piece + 1) * lanes
-            ] = rows
+                at * own_atoms : (at + 1) * own_atoms, piece * lanes : (piece + 1) * lanes
+            ] = parts[at][start : start + own_atoms, :]
     half_blocks = blocks // 2
     channels = trip_ref.shape[1]
     for block in range(blocks):
@@ -201,7 +197,8 @@
             shard = source // blocks
             within = source - shard * blocks
             upper = within // half_blocks
-            start = place_ref[shard] * lines + (within - upper * half_blocks) * block_len
+            near = lax.rem(shard - me + shards, shards)
+            start = near * lines + (within - upper * half_blocks) * block_len
             rows = held_ref[pl.ds(pl.multiple_of(start, block_len), block_len), :]
             picks.append(jnp.where(upper == 1, rows[:, channels:], rows[:, :channels]))
         mixed = product(tiles_ref[block], jnp.concatenate(picks, axis=0))
@@ -209,7 +206,10 @@
     half_slots = send_ref.shape[0] // 2
     low = product(send_ref[:half_slots, :], trip_ref[...])
     high = product(send_ref[half_slots:, :], trip_ref[...])
-    out_ref[...] = jnp.concatenate([low, high], axis=1).astype(jnp.bfloat16)
+    packed = jnp.concatenate([low, high], axis=1).astype(jnp.bfloat16)
+    each = half_slots // len(out_refs)
+    for at, out_ref in enumerate(out_refs):
+        out_ref[...] = packed[at * each : (at + 1) * each, :]
 
 
 def base_kernel(edges_ref, trip_ref, local_ref, up_ref, out_ref):
@@ -220,14 +220,16 @@
         out_ref[rows, :] = edges_ref[rows, :].astype(jnp.float32) + joined * root_half
 
 
-def state_kernel(
-    base_ref, fetch_ref, up_ref, residual_ref, message_ref, index_ref, arrived_ref,
-    state_ref, sums_ref, slots_ref,
-):
+def state_kernel(partners, *refs):
+    base_ref, fetch_ref, up_ref, residual_ref, message_ref, index_ref = refs[:6]
+    arrived = refs[6 : 6 + partners]
+    state_ref, sums_ref, slots_ref = refs[6 + partners :]
     channels = up_ref.shape[1]
-    half = arrived_ref.shape[0]
-    slots_ref[:half, :] = arrived_ref[:, :channels]
-    slots_ref[half:, :] = arrived_ref[:, channels:]
+    each = arrived[0].shape[0]
+    for at in range(partners):
+        piece = arrived[at][...]
+        slots_ref[at * each : (at + 1) * each, :] = piece[:, :channels]
+        slots_ref[(partners + at) * each : (partners + at + 1) * each, :] = piece[:, channels:]
     for rows in row_chunks(base_ref.shape[0]):
         picked = product(fetch_ref[rows, :], slots_ref[...]).astype(jnp.bfloat16)
         state = (base_ref[rows, :] + product(picked, up_ref[1]) * root_half).astype(jnp.bfloat16)
@@ -267,7 +269,7 @@
 def final_kernel(shards, scale, *refs):
     sums = refs[:shards]
     atoms_ref, weight_ref, join_ref, state_ref, side_ref, chosen_ref = refs[shards : shards + 6]
-    edges_hbm, own_ref, table_ref, edges_ref, sems = refs[shards + 6 :]
+    edges_hbm, own_hbm, table_ref, edges_ref, own_ref, sems = refs[shards + 6 :]
     part_atoms = atoms_ref.shape[0]
     count = part_atoms // shards
     total = sums[0][...].astype(jnp.float32)
@@ -279,18 +281,20 @@
     middle = silu(product(scaled, weight_ref[0])).astype(jnp.bfloat16)
     renewed = (atoms_ref[...].astype(jnp.float32) + product(middle, weight_ref[1])).astype(jnp.bfloat16)
     own_ref[...] = renewed[:count, :]
+    own_copy = pltpu.make_async_copy(own_ref, own_hbm, sems.at[0])
+    own_copy.start()
     width = renewed.shape[1]
     for end in range(2):
         table_ref[end * part_atoms : (end + 1) * part_atoms, :] = product(
             renewed, join_ref[end * width : (end + 1) * width, :]
         ).astype(jnp.bfloat16)
-    copies = []
+    copies = [own_copy]
     for at, rows in enumerate(row_chunks(state_ref.shape[0])):
         update = silu(product(chosen_ref[rows, :], table_ref[...]) + side_ref[rows, :])
         state = state_ref[rows, :].astype(jnp.float32)
         edges_ref[rows, :] = ((state + update) * root_half).astype(jnp.bfloat16)
         copies.append(
-            pltpu.make_async_copy(edges_ref.at[rows], edges_hbm.at[rows], sems.at[at])
+            pltpu.make_async_copy(edges_ref.at[rows], edges_hbm.at[rows], sems.at[1 + at])
         )
         copies[-1].start()
     for copy in copies:
@@ -302,18 +306,6 @@
         lax.ppermute(value, "edge", [((at + by) % shards, at) for at in range(shards)])
         for by in range(1, shards)
     ]
-
-
-def along_edge(value, shards):
-    if shards != 4:
-        parts = [value] + from_next(value, shards)
-        return parts, [[(to - at) % shards for to in range(shards)] for at in range(shards)]
-    far = lax.ppermute(value, "edge", [(0, 2), (2, 0), (1, 3), (3, 1)])
-    middle = lax.ppermute(value, "edge", [(1, 2), (2, 1)])
-    near = lax.ppermute(value, "edge", [(0, 1), (1, 0), (2, 3), (3, 2)])
-    relayed = lax.ppermute(far, "edge", [(2, 3), (1, 0)])
-    parts = [value, near, far, middle, relayed]
-    return parts, [[0, 1, 2, 4], [1, 0, 3, 2], [2, 3, 0, 1], [4, 2, 1, 0]]
 
 
 def body(
@@ -337,6 +329,9 @@
     shards = lax.axis_size("edge")
     count, atom_wide = atoms.shape
     part_atoms = count * shards
+    capacity = rows // domains
+    partners = domains - 1
+    slots = partners * capacity
     lines = rows // 2
     packed = 2 * channels
 
@@ -354,14 +349,14 @@
         flops=2 * rows * wide * (wide + channels),
         nbytes=2 * (rows * wide + wide * wide),
     )
-    narrow_parts, places = along_edge(narrow, shards)
-    place = jnp.asarray(places, jnp.int32)[lax.axis_index("edge")]
+    narrow_parts = [narrow] + from_next(narrow, shards)
     later = (
         edges, tiles, weight_up, weight_residual, weight_message, weight_join, weight_atom, atom_index
     )
     send, fetch, local, *later = call(
         functools.partial(index_kernel, domains, shards, len(later)),
-        (shaped((rows, rows)),) * 3 + tuple(shaped(each.shape, each.dtype) for each in later),
+        (shaped((slots, rows)), shaped((rows, slots)), shaped((rows, rows)))
+        + tuple(shaped(each.shape, each.dtype) for each in later),
         (reverse.reshape(1, rows), *later),
         hbm=range(1, 1 + len(later)),
         scratch=[pltpu.SemaphoreType.DMA((len(later),))],
@@ -369,20 +364,20 @@
         nbytes=6 * rows * rows,
     )
     edges, tiles, weight_up, weight_residual, weight_message, weight_join, weight_atom, atom_index = later
-    trip_out, outgoing, all_atoms = call(
-        functools.partial(mix_kernel, len(narrow_parts)),
-        (
-            shaped((rows, channels)),
-            shaped((lines, packed)),
-            shaped((part_atoms, atom_wide)),
-        ),
-        (tile_source, place, tiles, *narrow_parts, send),
-        smem=(0, 1),
-        scratch=[pltpu.VMEM((len(narrow_parts) * lines, packed), jnp.bfloat16)],
+    trip_out, all_atoms, *outgoing = call(
+        functools.partial(mix_kernel, shards),
+        (shaped((rows, channels)), shaped((part_atoms, atom_wide)))
+        + (shaped((capacity // 2, packed)),) * partners,
+        (tile_source, tiles, *narrow_parts, send),
+        smem=(0,),
+        scratch=[pltpu.VMEM((shards * lines, packed), jnp.bfloat16)],
         flops=2 * rows * rows * channels,
         nbytes=2 * rows * rows,
     )
-    arrived = lax.all_to_all(outgoing, "dom", split_axis=0, concat_axis=0, tiled=True)
+    arrived = [
+        lax.ppermute(outgoing[by - 1], "dom", [(at, at ^ by) for at in range(domains)])
+        for by in range(1, domains)
+    ]
     base = call(
         base_kernel,
         shaped((rows, wide), jnp.float32),
@@ -391,10 +386,10 @@
         nbytes=2 * rows * rows + 6 * rows * wide,
     )
     state, sums = call(
-        state_kernel,
+        functools.partial(state_kernel, partners),
         (shaped((rows, wide)), shaped((part_atoms, atom_wide))),
-        (base, fetch, weight_up, weight_residual, weight_message, atom_index, arrived),
-        scratch=[pltpu.VMEM((rows, channels), jnp.bfloat16)],
+        (base, fetch, weight_up, weight_residual, weight_message, atom_index, *arrived),
+        scratch=[pltpu.VMEM((slots, channels), jnp.bfloat16)],
         flops=4 * rows * wide * wide,
         nbytes=8 * rows * wide,
     )
@@ -408,12 +403,13 @@
     )
     return call(
         functools.partial(final_kernel, shards, (rows // count) ** -0.5),
-        (shaped((rows, wide), space=pltpu.HBM), shaped((count, atom_wide))),
+        (shaped((rows, wide), space=pltpu.HBM), shaped((count, atom_wide), space=pltpu.HBM)),
         (*sums_parts, all_atoms, weight_atom, weight_join, state, side, chosen),
         scratch=[
             pltpu.VMEM((2 * part_atoms, wide), jnp.bfloat16),
             pltpu.VMEM((rows, wide), jnp.bfloat16),
-            pltpu.SemaphoreType.DMA((len(row_chunks(rows)),)),
+            pltpu.VMEM((count, atom_wide), jnp.bfloat16),
+            pltpu.SemaphoreType.DMA((1 + len(row_chunks(rows)),)),
         ],
         flops=4 * rows * part_atoms * wide,
         nbytes=8 * rows * wide,

time: 56.9 us -> 47.9 us (0.84)
  local copies, waits for them, and re-layouts: 12.3 us -> 0.09 us
  waiting for transfers between devices: 6.84 us -> 11.5 us
  Pallas kernels: 16.8 us -> 16 us
    unnamed x34 -> x5, local copies, waits for them, and re-layouts: 11.6 us -> 0.09 us
    ppermute x3 -> x6, waiting for transfers between devices: 2.31 us -> 9.29 us  [from_next(): lax.ppermute(value, 'edge', [((at + by) % shards, at) for at in range(sha...]
    ppermute x3 -> x6, starting transfers between devices: 6.66 us -> 13.1 us  [from_next(): lax.ppermute(value, 'edge', [((at + by) % shards, at) for at in range(sha...]
    all_to_all x1 -> x0, starting transfers between devices: 4.03 us -> none  [body(): lax.all_to_all(outgoing, 'dom', split_axis=0, concat_axis=0, tiled=True)]
    ppermute x4 -> x7, starting transfers between devices: 8.93 us -> 6.32 us  [body(): lax.ppermute(outgoing[by - 1], 'dom', [(at, at ^ by) for at in range(doma...]
    ppermute x4 -> x7, waiting for transfers between devices: 4.34 us -> 2.21 us  [body(): lax.ppermute(outgoing[by - 1], 'dom', [(at, at ^ by) for at in range(doma...]
    pallas_call x7, Pallas kernels: 16.8 us -> 16 us  [call(): pl.pallas_call(kernel, out_shape=outs, in_specs=[pl.BlockSpec(memory_spac...]
    squeeze x1 -> x0, local copies, waits for them, and re-layouts: 0.74 us -> none  [body(): place = jnp.asarray(places, jnp.int32)[lax.axis_index('edge')]]
  transfers between devices with their start and end apart: 8 -> 13, of which waited for: 3 -> 7; matrix products, arithmetic and copies ran while one was open for 1% -> 0% of each run, Pallas kernels for 9% -> 11%
where the time goes in v4:
time: 47.9 us; the launch traced here: 47.8 us
  starting transfers between devices  19.5 us (41%)
  Pallas kernels  16 us (33%)
  waiting for transfers between devices  11.5 us (24%)
  between operations  0.73 us (2%)
    pallas_call x7, Pallas kernels, call(): pl.pallas_call(kernel, out_shape=outs, in_specs=[pl.BlockSpec(memory_spac...  16 us
    ppermute x6, starting transfers between devices, from_next(): lax.ppermute(value, 'edge', [((at + by) % shards, at) for at in range(sha...  13.1 us
    ppermute x6, waiting for transfers between devices, from_next(): lax.ppermute(value, 'edge', [((at + by) % shards, at) for at in range(sha...  9.29 us
    ppermute x7, starting transfers between devices, body(): lax.ppermute(outgoing[by - 1], 'dom', [(at, at ^ by) for at in range(doma...  6.32 us
    ppermute x7, waiting for transfers between devices, body(): lax.ppermute(outgoing[by - 1], 'dom', [(at, at ^ by) for at in range(doma...  2.21 us
  transfers between devices with their start and end apart: 13, of which 7 were waited for; matrix products, arithmetic and copies ran while one was open for 0% of the time, Pallas kernels for 11%

profile of v4, /device:TPU:0, one launch (start us, length us, event | category | flops | bytes accessed | tf_op | source)
XLA Modules:
  0.0 47.8 jit_solution(7424070934137016697)
XLA Ops:
  0.7 3.0 %shard_map.141.refs_2_ = bf16[576,128]{1,0:T(8,128)(2,1)S(1)} custom-call(bf16[1024,512]{1,0:T(8,128)(2,1)} %edges_hbm.1, bf16[512,512]{1,0:T(8,128)(2,1)} %weight_hbm.1, bf16[64,512]{1,0:T(8,128)(2,1)} %down_hbm.1, bf16[32,256]{1,0:T(8,128)(2,1)} %atoms_hbm.1), custom_call_target="tpu_custom_call" | custom-call | flops 603979776 | bytes 1572864 | tf_op jit(solution)/shard_map/pallas_call | solution.py:42
  3.7 3.1 %collective-permute-start.2 = (bf16[576,128]{1,0:T(8,128)(2,1)S(1)}, bf16[576,128]{1,0:T(8,128)(2,1)S(1)}, u32[]{:S(2)}, u32[]{:S(2)}) collective-permute-start(bf16[576,128]{1,0:T(8,128)(2,1)S(1)} %shard_map.141.refs_2_), channel_id=1, source_target_pairs={{3,0},{0,1},{1,2},{2,3},{7,4},{4,5},{5,6},{6,7},{11,8},{8,9},{9,10... | collective-permute-start | bytes 442376 | tf_op jit(solution)/shard_map/ppermute | solution.py:306
  6.8 2.6 %collective-permute-start.1 = (bf16[576,128]{1,0:T(8,128)(2,1)S(1)}, bf16[576,128]{1,0:T(8,128)(2,1)S(1)}, u32[]{:S(2)}, u32[]{:S(2)}) collective-permute-start(bf16[576,128]{1,0:T(8,128)(2,1)S(1)} %shard_map.141.refs_2_), channel_id=1, source_target_pairs={{2,0},{3,1},{0,2},{1,3},{6,4},{7,5},{4,6},{5,7},{10,8},{11,9},{8,1... | collective-permute-start | bytes 442376 | tf_op jit(solution)/shard_map/ppermute | solution.py:306
  9.3 1.3 %collective-permute-start = (bf16[576,128]{1,0:T(8,128)(2,1)S(1)}, bf16[576,128]{1,0:T(8,128)(2,1)S(1)}, u32[]{:S(2)}, u32[]{:S(2)}) collective-permute-start(bf16[576,128]{1,0:T(8,128)(2,1)S(1)} %shard_map.141.refs_2_), channel_id=1, source_target_pairs={{1,0},{2,1},{3,2},{0,3},{5,4},{6,5},{7,6},{4,7},{9,8},{10,9},{11,1... | collective-permute-start | bytes 442376 | tf_op jit(solution)/shard_map/ppermute | solution.py:306
  10.7 0.1 copy.15.refs_0_
  10.8 2.7 %shard_map.140 = (bf16[896,1024]{1,0:T(8,128)(2,1)S(1)}, bf16[1024,896]{1,0:T(8,128)(2,1)S(1)}, bf16[1024,1024]{1,0:T(8,128)(2,1)S(1)}, bf16[1024,512]{1,0:T(8,1...) custom-call(s32[1,1024]{1,0:T(1,128)S(1)} %bitcast.1, ...), custom_call_target="tpu_custom_call" | custom-call | flops 41943040 | bytes 6291456 | tf_op jit(solution)/shard_map/pallas_call | solution.py:42
  13.5 0.1 collective-permute-done.2.refs_5_
  13.6 5.5 %collective-permute-done.1.refs_4_ = bf16[576,128]{1,0:T(8,128)(2,1)S(1)} collective-permute-done((bf16[576,128]{1,0:T(8,128)(2,1)S(1)}, bf16[576,128]{1,0:T(8,128)(2,1)S(1)}, u32[]{:S(2)}, u32[]{:S(2)}) %collective-permute-start.1) | collective-permute-done | bytes 147488 | tf_op jit(solution)/shard_map/ppermute | solution.py:306
  19.0 0.0 collective-permute-done.refs_3_
  19.0 2.0 %shard_map.142 = (bf16[1024,64]{1,0:T(8,128)(2,1)S(1)}, bf16[128,256]{1,0:T(8,128)(2,1)S(1)}, bf16[64,128]{1,0:T(8,128)(2,1)S(1)}, bf16[64,128]{1,0:T(8,128)(2,1...) custom-call(s32[16,2]{1,0:T(8,128)S(1)} %copy.15.refs_0_, ...), custom_call_target="tpu_custom_call" | custom-call | flops 134217728 | bytes 2097152 | tf_op jit(solution)/shard_map/pallas_call | solution.py:42
  21.1 0.1 collective-permute-start.3
  21.1 1.6 %collective-permute-start.4 = (bf16[64,128]{1,0:T(8,128)(2,1)S(1)}, bf16[64,128]{1,0:T(8,128)(2,1)S(1)}, u32[]{:S(2)}, u32[]{:S(2)}) collective-permute-start(bf16[64,128]{1,0:T(8,128)(2,1)S(1)} %get-tuple-element.37), channel_id=1, source_target_pairs={{0,8},{4,12},{8,0},{12,4},{16,24},{20,28},{24,16},{28,20},{1,9},{5... | collective-permute-start | bytes 49160 | tf_op jit(solution)/shard_map/ppermute | solution.py:378
  22.7 0.3 collective-permute-start.5
  23.0 1.5 %collective-permute-start.6 = (bf16[64,128]{1,0:T(8,128)(2,1)S(1)}, bf16[64,128]{1,0:T(8,128)(2,1)S(1)}, u32[]{:S(2)}, u32[]{:S(2)}) collective-permute-start(bf16[64,128]{1,0:T(8,128)(2,1)S(1)} %get-tuple-element.39), channel_id=1, source_target_pairs={{0,16},{4,20},{8,24},{12,28},{16,0},{20,4},{24,8},{28,12},{1,17},{... | collective-permute-start | bytes 49160 | tf_op jit(solution)/shard_map/ppermute | solution.py:378
  24.5 0.2 collective-permute-start.7
  24.7 0.0 collective-permute-done.3.refs_6_
  24.7 2.4 %collective-permute-start.8 = (bf16[64,128]{1,0:T(8,128)(2,1)S(1)}, bf16[64,128]{1,0:T(8,128)(2,1)S(1)}, u32[]{:S(2)}, u32[]{:S(2)}) collective-permute-start(bf16[64,128]{1,0:T(8,128)(2,1)S(1)} %get-tuple-element.41), channel_id=1, source_target_pairs={{0,24},{4,28},{8,16},{12,20},{16,8},{20,12},{24,0},{28,4},{1,25},{... | collective-permute-start | bytes 49160 | tf_op jit(solution)/shard_map/ppermute | solution.py:378
  27.1 0.2 collective-permute-start.9
  27.4 1.6 %shard_map.143.refs_0_ = f32[1024,512]{1,0:T(8,128)S(1)} custom-call(bf16[1024,512]{1,0:T(8,128)(2,1)S(1)} %get-tuple-element.26.edges_ref, bf16[1024,64]{1,0:T(8,128)(2,1)S(1)} %get-tuple-element.29.trip_ref, bf16[1024,1024]{1,0:T(8,128)(2,1)S(1)} %get-tuple-element.30.local_ref, bf16[2,64,512]{2,1,0:T(8,128)(2,1)S(1)} %get-tuple-element.31.up_ref.refs_2_), custom_call_target="tpu_custom_call" | custom-call | flops 268435456 | bytes 5242880 | tf_op jit(solution)/shard_map/pallas_call | solution.py:42
  29.0 0.0 collective-permute-done.5.refs_8_
  29.0 0.0 collective-permute-done.6.refs_9_
  29.0 0.3 collective-permute-done.8.refs_11_
  29.3 1.9 %collective-permute-done.9.refs_12_ = bf16[64,128]{1,0:T(8,128)(2,1)S(1)} collective-permute-done((bf16[64,128]{1,0:T(8,128)(2,1)S(1)}, bf16[64,128]{1,0:T(8,128)(2,1)S(1)}, u32[]{:S(2)}, u32[]{:S(2)}) %collective-permute-start.9) | collective-permute-done | bytes 16416 | tf_op jit(solution)/shard_map/ppermute | solution.py:378
  31.2 3.8 %shard_map.144 = (bf16[1024,512]{1,0:T(8,128)(2,1)S(1)}, bf16[128,256]{1,0:T(8,128)(2,1)S(1)}) custom-call(f32[1024,512]{1,0:T(8,128)S(1)} %shard_map.143.refs_0_, bf16[1024,896]{1,0:T(8,128)(2,1)S(1)} %get-tuple-element.32.refs_1_, bf16[2,64,512]{2,1,0:T(8,128)(2,1)S(1)} %get-tuple-element.31.up_ref.refs_2_, ...), custom_call_target="tpu_custom_call" | custom-call | flops 1073741824 | bytes 4194304 | tf_op jit(solution)/shard_map/pallas_call | solution.py:42
  35.0 3.7 %collective-permute-start.12 = (bf16[128,256]{1,0:T(8,128)(2,1)S(1)}, bf16[128,256]{1,0:T(8,128)(2,1)S(1)}, u32[]{:S(2)}, u32[]{:S(2)}) collective-permute-start(bf16[128,256]{1,0:T(8,128)(2,1)S(1)} %get-tuple-element.43.refs_0_), channel_id=1, source_target_pairs={{3,0},{0,1},{1,2},{2,3},{7,4},{4,5},{5,6},{6,7},{11,8},{8,9},{9,10... | collective-permute-start | bytes 196616 | tf_op jit(solution)/shard_map/ppermute | solution.py:306
  38.7 1.6 %collective-permute-start.11 = (bf16[128,256]{1,0:T(8,128)(2,1)S(1)}, bf16[128,256]{1,0:T(8,128)(2,1)S(1)}, u32[]{:S(2)}, u32[]{:S(2)}) collective-permute-start(bf16[128,256]{1,0:T(8,128)(2,1)S(1)} %get-tuple-element.43.refs_0_), channel_id=1, source_target_pairs={{2,0},{3,1},{0,2},{1,3},{6,4},{7,5},{4,6},{5,7},{10,8},{11,9},{8,1... | collective-permute-start | bytes 196616 | tf_op jit(solution)/shard_map/ppermute | solution.py:306
  40.3 0.8 %collective-permute-start.10 = (bf16[128,256]{1,0:T(8,128)(2,1)S(1)}, bf16[128,256]{1,0:T(8,128)(2,1)S(1)}, u32[]{:S(2)}, u32[]{:S(2)}) collective-permute-start(bf16[128,256]{1,0:T(8,128)(2,1)S(1)} %get-tuple-element.43.refs_0_), channel_id=1, source_target_pairs={{1,0},{2,1},{3,2},{0,3},{5,4},{6,5},{7,6},{4,7},{9,8},{10,9},{11,1... | collective-permute-start | bytes 196616 | tf_op jit(solution)/shard_map/ppermute | solution.py:306
  41.2 0.8 %shard_map.145 = (f32[1024,512]{1,0:T(8,128)S(1)}, bf16[1024,256]{1,0:T(8,128)(2,1)S(1)}) custom-call(bf16[1024,512]{1,0:T(8,128)(2,1)S(1)} %get-tuple-element.47.state_ref.refs_7_, bf16[1024,512]{1,0:T(8,128)(2,1)S(1)} %get-tuple-element.46.join_ref.refs_6_, s32[2,1024]{1,0:T(2,128)S(1)} %get-tuple-element.35.refs_5_.index_ref), custom_call_target="tpu_custom_call" | custom-call | flops 536870912 | bytes 4194304 | tf_op jit(solution)/shard_map/pallas_call | solution.py:42
  41.9 0.8 %collective-permute-done.12.refs_3_ = bf16[128,256]{1,0:T(8,128)(2,1)S(1)} collective-permute-done((bf16[128,256]{1,0:T(8,128)(2,1)S(1)}, bf16[128,256]{1,0:T(8,128)(2,1)S(1)}, u32[]{:S(2)}, u32[]{:S(2)}) %collective-permute-start.12) | collective-permute-done | bytes 65568 | tf_op jit(solution)/shard_map/ppermute | solution.py:306
  42.7 2.4 %collective-permute-done.11.refs_2_ = bf16[128,256]{1,0:T(8,128)(2,1)S(1)} collective-permute-done((bf16[128,256]{1,0:T(8,128)(2,1)S(1)}, bf16[128,256]{1,0:T(8,128)(2,1)S(1)}, u32[]{:S(2)}, u32[]{:S(2)}) %collective-permute-start.11) | collective-permute-done | bytes 65568 | tf_op jit(solution)/shard_map/ppermute | solution.py:306
  45.1 0.6 %collective-permute-done.10.refs_1_ = bf16[128,256]{1,0:T(8,128)(2,1)S(1)} collective-permute-done((bf16[128,256]{1,0:T(8,128)(2,1)S(1)}, bf16[128,256]{1,0:T(8,128)(2,1)S(1)}, u32[]{:S(2)}, u32[]{:S(2)}) %collective-permute-start.10) | collective-permute-done | bytes 65568 | tf_op jit(solution)/shard_map/ppermute | solution.py:306
  45.7 2.1 %shard_map.146 = (bf16[1024,512]{1,0:T(8,128)(2,1)}, bf16[32,256]{1,0:T(8,128)(2,1)}) custom-call(bf16[128,256]{1,0:T(8,128)(2,1)S(1)} %get-tuple-element.43.refs_0_, bf16[128,256]{1,0:T(8,128)(2,1)S(1)} %collective-permute-done.10.refs_1_, bf16[128,256]{1,0:T(8,128)(2,1)S(1)} %collective-permute-done.11.refs_2_, ...), custom_call_target="tpu_custom_call" | custom-call | flops 268435456 | bytes 4194304 | tf_op jit(solution)/shard_map/pallas_call | solution.py:42
  (6 shorter events, 0.0 us)
Async XLA Ops:
  0.6 10.1 %copy-start.1 = (s32[16,2]{0,1:T(2,128)S(1)}, s32[16,2]{0,1:T(2,128)}, u32[]{:S(2)}) copy-start(s32[16,2]{0,1:T(2,128)} %param.17) | copy-start | bytes 388
  0.6 10.1 %copy-start = (s32[1024]{0:T(1024)S(1)}, s32[1024]{0:T(1024)}, u32[]{:S(2)}) copy-start(s32[1024]{0:T(1024)} %param.15) | copy-start | bytes 12292
  3.7 9.9 %collective-permute-start.2 = (bf16[576,128]{1,0:T(8,128)(2,1)S(1)}, bf16[576,128]{1,0:T(8,128)(2,1)S(1)}, u32[]{:S(2)}, u32[]{:S(2)}) collective-permute-start(bf16[576,128]{1,0:T(8,128)(2,1)S(1)} %shard_map.141.refs_2_), channel_id=1, source_target_pairs={{3,0},{0,1},{1,2},{2,3},{7,4},{4,5},{5,6},{6,7},{11,8},{8,9},{9,10... | collective-permute-start | bytes 442376 | tf_op jit(solution)/shard_map/ppermute | solution.py:306
  6.8 12.3 %collective-permute-start.1 = (bf16[576,128]{1,0:T(8,128)(2,1)S(1)}, bf16[576,128]{1,0:T(8,128)(2,1)S(1)}, u32[]{:S(2)}, u32[]{:S(2)}) collective-permute-start(bf16[576,128]{1,0:T(8,128)(2,1)S(1)} %shard_map.141.refs_2_), channel_id=1, source_target_pairs={{2,0},{3,1},{0,2},{1,3},{6,4},{7,5},{4,6},{5,7},{10,8},{11,9},{8,1... | collective-permute-start | bytes 442376 | tf_op jit(solution)/shard_map/ppermute | solution.py:306
  9.3 9.7 %collective-permute-start = (bf16[576,128]{1,0:T(8,128)(2,1)S(1)}, bf16[576,128]{1,0:T(8,128)(2,1)S(1)}, u32[]{:S(2)}, u32[]{:S(2)}) collective-permute-start(bf16[576,128]{1,0:T(8,128)(2,1)S(1)} %shard_map.141.refs_2_), channel_id=1, source_target_pairs={{1,0},{2,1},{3,2},{0,3},{5,4},{6,5},{7,6},{4,7},{9,8},{10,9},{11,1... | collective-permute-start | bytes 442376 | tf_op jit(solution)/shard_map/ppermute | solution.py:306
  21.1 3.6 %collective-permute-start.3 = (bf16[64,128]{1,0:T(8,128)(2,1)S(1)}, bf16[64,128]{1,0:T(8,128)(2,1)S(1)}, u32[]{:S(2)}, u32[]{:S(2)}) collective-permute-start(bf16[64,128]{1,0:T(8,128)(2,1)S(1)} %get-tuple-element.36), channel_id=1, source_target_pairs={{0,4},{4,0},{8,12},{12,8},{16,20},{20,16},{24,28},{28,24},{1,5},{5... | collective-permute-start | bytes 49160 | tf_op jit(solution)/shard_map/ppermute | solution.py:378
  21.1 6.0 %collective-permute-start.4 = (bf16[64,128]{1,0:T(8,128)(2,1)S(1)}, bf16[64,128]{1,0:T(8,128)(2,1)S(1)}, u32[]{:S(2)}, u32[]{:S(2)}) collective-permute-start(bf16[64,128]{1,0:T(8,128)(2,1)S(1)} %get-tuple-element.37), channel_id=1, source_target_pairs={{0,8},{4,12},{8,0},{12,4},{16,24},{20,28},{24,16},{28,20},{1,9},{5... | collective-permute-start | bytes 49160 | tf_op jit(solution)/shard_map/ppermute | solution.py:378
  22.7 6.3 %collective-permute-start.5 = (bf16[64,128]{1,0:T(8,128)(2,1)S(1)}, bf16[64,128]{1,0:T(8,128)(2,1)S(1)}, u32[]{:S(2)}, u32[]{:S(2)}) collective-permute-start(bf16[64,128]{1,0:T(8,128)(2,1)S(1)} %get-tuple-element.38), channel_id=1, source_target_pairs={{0,12},{4,8},{8,4},{12,0},{16,28},{20,24},{24,20},{28,16},{1,13},{... | collective-permute-start | bytes 49160 | tf_op jit(solution)/shard_map/ppermute | solution.py:378
  23.0 6.0 %collective-permute-start.6 = (bf16[64,128]{1,0:T(8,128)(2,1)S(1)}, bf16[64,128]{1,0:T(8,128)(2,1)S(1)}, u32[]{:S(2)}, u32[]{:S(2)}) collective-permute-start(bf16[64,128]{1,0:T(8,128)(2,1)S(1)} %get-tuple-element.39), channel_id=1, source_target_pairs={{0,16},{4,20},{8,24},{12,28},{16,0},{20,4},{24,8},{28,12},{1,17},{... | collective-permute-start | bytes 49160 | tf_op jit(solution)/shard_map/ppermute | solution.py:378
  24.5 4.5 %collective-permute-start.7 = (bf16[64,128]{1,0:T(8,128)(2,1)S(1)}, bf16[64,128]{1,0:T(8,128)(2,1)S(1)}, u32[]{:S(2)}, u32[]{:S(2)}) collective-permute-start(bf16[64,128]{1,0:T(8,128)(2,1)S(1)} %get-tuple-element.40), channel_id=1, source_target_pairs={{0,20},{4,16},{8,28},{12,24},{16,4},{20,0},{24,12},{28,8},{1,21},{... | collective-permute-start | bytes 49160 | tf_op jit(solution)/shard_map/ppermute | solution.py:378
  24.7 4.6 %collective-permute-start.8 = (bf16[64,128]{1,0:T(8,128)(2,1)S(1)}, bf16[64,128]{1,0:T(8,128)(2,1)S(1)}, u32[]{:S(2)}, u32[]{:S(2)}) collective-permute-start(bf16[64,128]{1,0:T(8,128)(2,1)S(1)} %get-tuple-element.41), channel_id=1, source_target_pairs={{0,24},{4,28},{8,16},{12,20},{16,8},{20,12},{24,0},{28,4},{1,25},{... | collective-permute-start | bytes 49160 | tf_op jit(solution)/shard_map/ppermute | solution.py:378
  27.1 4.1 %collective-permute-start.9 = (bf16[64,128]{1,0:T(8,128)(2,1)S(1)}, bf16[64,128]{1,0:T(8,128)(2,1)S(1)}, u32[]{:S(2)}, u32[]{:S(2)}) collective-permute-start(bf16[64,128]{1,0:T(8,128)(2,1)S(1)} %get-tuple-element.42), channel_id=1, source_target_pairs={{0,28},{4,24},{8,20},{12,16},{16,12},{20,8},{24,4},{28,0},{1,29},{... | collective-permute-start | bytes 49160 | tf_op jit(solution)/shard_map/ppermute | solution.py:378
  35.0 7.7 %collective-permute-start.12 = (bf16[128,256]{1,0:T(8,128)(2,1)S(1)}, bf16[128,256]{1,0:T(8,128)(2,1)S(1)}, u32[]{:S(2)}, u32[]{:S(2)}) collective-permute-start(bf16[128,256]{1,0:T(8,128)(2,1)S(1)} %get-tuple-element.43.refs_0_), channel_id=1, source_target_pairs={{3,0},{0,1},{1,2},{2,3},{7,4},{4,5},{5,6},{6,7},{11,8},{8,9},{9,10... | collective-permute-start | bytes 196616 | tf_op jit(solution)/shard_map/ppermute | solution.py:306
  38.7 6.4 %collective-permute-start.11 = (bf16[128,256]{1,0:T(8,128)(2,1)S(1)}, bf16[128,256]{1,0:T(8,128)(2,1)S(1)}, u32[]{:S(2)}, u32[]{:S(2)}) collective-permute-start(bf16[128,256]{1,0:T(8,128)(2,1)S(1)} %get-tuple-element.43.refs_0_), channel_id=1, source_target_pairs={{2,0},{3,1},{0,2},{1,3},{6,4},{7,5},{4,6},{5,7},{10,8},{11,9},{8,1... | collective-permute-start | bytes 196616 | tf_op jit(solution)/shard_map/ppermute | solution.py:306
  40.3 5.3 %collective-permute-start.10 = (bf16[128,256]{1,0:T(8,128)(2,1)S(1)}, bf16[128,256]{1,0:T(8,128)(2,1)S(1)}, u32[]{:S(2)}, u32[]{:S(2)}) collective-permute-start(bf16[128,256]{1,0:T(8,128)(2,1)S(1)} %get-tuple-element.43.refs_0_), channel_id=1, source_target_pairs={{1,0},{2,1},{3,2},{0,3},{5,4},{6,5},{7,6},{4,7},{9,8},{10,9},{11,1... | collective-permute-start | bytes 196616 | tf_op jit(solution)/shard_map/ppermute | solution.py:306

commit v5 on v4

--- a/solution.py
+++ b/solution.py
@@ -149,7 +149,7 @@
 
     def slot_of(at):
         part = (at >= half).astype(jnp.int32)
-        slot = part * (slots // 2) + (partner - 1) * half + at - part * half
+        slot = part * (slots // 2) + (domains - 1 - partner) * half + at - part * half
         return jnp.where(partner == 0, -1, slot)
 
     send_slot = slot_of(place)
@@ -181,13 +181,13 @@
     atom_wide = atoms_ref.shape[1]
     lanes = held_ref.shape[1]
     me = lax.axis_index("edge")
-    for at in range(shards):
-        held_ref[at * lines : (at + 1) * lines, :] = parts[at][:lines, :]
+    for part, at in zip(parts, distances(shards)):
+        held_ref[at * lines : (at + 1) * lines, :] = part[:lines, :]
         for piece in range(atom_wide // lanes):
             start = lines + piece * own_atoms
             atoms_ref[
                 at * own_atoms : (at + 1) * own_atoms, piece * lanes : (piece + 1) * lanes
-            ] = parts[at][start : start + own_atoms, :]
+            ] = part[start : start + own_atoms, :]
     half_blocks = blocks // 2
     channels = trip_ref.shape[1]
     for block in range(blocks):
@@ -197,8 +197,7 @@
             shard = source // blocks
             within = source - shard * blocks
             upper = within // half_blocks
-            near = lax.rem(shard - me + shards, shards)
-            start = near * lines + (within - upper * half_blocks) * block_len
+            start = (shard ^ me) * lines + (within - upper * half_blocks) * block_len
             rows = held_ref[pl.ds(pl.multiple_of(start, block_len), block_len), :]
             picks.append(jnp.where(upper == 1, rows[:, channels:], rows[:, :channels]))
         mixed = product(tiles_ref[block], jnp.concatenate(picks, axis=0))
@@ -230,28 +229,41 @@
         piece = arrived[at][...]
         slots_ref[at * each : (at + 1) * each, :] = piece[:, :channels]
         slots_ref[(partners + at) * each : (partners + at + 1) * each, :] = piece[:, channels:]
-    for rows in row_chunks(base_ref.shape[0]):
-        picked = product(fetch_ref[rows, :], slots_ref[...]).astype(jnp.bfloat16)
-        state = (base_ref[rows, :] + product(picked, up_ref[1]) * root_half).astype(jnp.bfloat16)
-        for layer in range(residual_ref.shape[0]):
-            middle = silu(product(state, residual_ref[layer, 0])).astype(jnp.bfloat16)
-            branch = silu(product(middle, residual_ref[layer, 1]))
-            state = ((state.astype(jnp.float32) + branch) * root_half).astype(jnp.bfloat16)
-        state_ref[rows, :] = state
     part_atoms = sums_ref.shape[0]
     shards = lax.axis_size("edge")
     near = near_atoms(index_ref[1:2, :], part_atoms, shards)
     chosen = (
         lax.broadcasted_iota(jnp.int32, (part_atoms, near.shape[1]), 0) == near
     ).astype(jnp.bfloat16)
-    gathered = product(chosen, state_ref[...]).astype(jnp.bfloat16)
-    sums_ref[...] = product(gathered, message_ref[...]).astype(jnp.bfloat16)
+    chunks = row_chunks(base_ref.shape[0])
+    gathered = None
+    for first in range(0, len(chunks), 2):
+        group = chunks[first : first + 2]
+        picked = [product(fetch_ref[rows, :], slots_ref[...]).astype(jnp.bfloat16) for rows in group]
+        states = [
+            (base_ref[rows, :] + product(each, up_ref[1]) * root_half).astype(jnp.bfloat16)
+            for rows, each in zip(group, picked)
+        ]
+        for layer in range(residual_ref.shape[0]):
+            middles = [
+                silu(product(each, residual_ref[layer, 0])).astype(jnp.bfloat16) for each in states
+            ]
+            branches = [silu(product(each, residual_ref[layer, 1])) for each in middles]
+            states = [
+                ((each.astype(jnp.float32) + branch) * root_half).astype(jnp.bfloat16)
+                for each, branch in zip(states, branches)
+            ]
+        for rows, each in zip(group, states):
+            state_ref[rows, :] = each
+            term = product(chosen[:, rows], each)
+            gathered = term if gathered is None else gathered + term
+    sums_ref[...] = product(gathered.astype(jnp.bfloat16), message_ref[...]).astype(jnp.bfloat16)
 
 
 def near_atoms(index, part_atoms, shards):
-    first = lax.axis_index("edge") * (part_atoms // shards)
-    shifted = index - first
-    return jnp.where(shifted < 0, shifted + part_atoms, shifted)
+    count = part_atoms // shards
+    holder = index // count
+    return (holder ^ lax.axis_index("edge")) * count + lax.rem(index, count)
 
 
 def side_kernel(shards, part_atoms, state_ref, join_ref, index_ref, out_ref, chosen_ref):
@@ -273,10 +285,9 @@
     part_atoms = atoms_ref.shape[0]
     count = part_atoms // shards
     total = sums[0][...].astype(jnp.float32)
-    for at in range(1, shards):
-        piece = sums[at][...].astype(jnp.float32)
-        cut = part_atoms - at * count
-        total = total + jnp.concatenate([piece[cut:], piece[:cut]], axis=0)
+    for by, part in list(zip(distances(shards), sums))[1:]:
+        pieces = [part[(at ^ by) * count : ((at ^ by) + 1) * count, :] for at in range(shards)]
+        total = total + jnp.concatenate(pieces, axis=0).astype(jnp.float32)
     scaled = (total * scale).astype(jnp.bfloat16)
     middle = silu(product(scaled, weight_ref[0])).astype(jnp.bfloat16)
     renewed = (atoms_ref[...].astype(jnp.float32) + product(middle, weight_ref[1])).astype(jnp.bfloat16)
@@ -301,10 +312,14 @@
         copy.wait()
 
 
-def from_next(value, shards):
-    return [
-        lax.ppermute(value, "edge", [((at + by) % shards, at) for at in range(shards)])
-        for by in range(1, shards)
+def distances(shards):
+    return [0, 1, 3, 2] if shards == 4 else list(range(shards))
+
+
+def from_others(value, shards):
+    return [value] + [
+        lax.ppermute(value, "edge", [(at, at ^ by) for at in range(shards)])
+        for by in distances(shards)[1:]
     ]
 
 
@@ -349,7 +364,7 @@
         flops=2 * rows * wide * (wide + channels),
         nbytes=2 * (rows * wide + wide * wide),
     )
-    narrow_parts = [narrow] + from_next(narrow, shards)
+    narrow_parts = from_others(narrow, shards)
     later = (
         edges, tiles, weight_up, weight_residual, weight_message, weight_join, weight_atom, atom_index
     )
@@ -375,8 +390,8 @@
         nbytes=2 * rows * rows,
     )
     arrived = [
-        lax.ppermute(outgoing[by - 1], "dom", [(at, at ^ by) for at in range(domains)])
-        for by in range(1, domains)
+        lax.ppermute(block, "dom", [(at, at ^ (partners - place)) for at in range(domains)])
+        for place, block in enumerate(outgoing)
     ]
     base = call(
         base_kernel,
@@ -393,7 +408,7 @@
         flops=4 * rows * wide * wide,
         nbytes=8 * rows * wide,
     )
-    sums_parts = [sums] + from_next(sums, shards)
+    sums_parts = from_others(sums, shards)
     side, chosen = call(
         functools.partial(side_kernel, shards, part_atoms),
         (shaped((rows, wide), jnp.float32), shaped((rows, 2 * part_atoms))),

time: 47.9 us -> 46.6 us (0.973)
  starting transfers between devices: 19.5 us -> 17.4 us
  waiting for transfers between devices: 11.5 us -> 13 us
  Pallas kernels: 16 us -> 15.2 us
    ppermute x13, starting transfers between devices: 19.5 us -> 17.4 us  [the longest x6 11.1 us: from_others(): lax.ppermute(value, 'edge', [(at, at ^ by) for at in range(shards)])]
    ppermute x13, waiting for transfers between devices: 11.5 us -> 13 us  [the longest x6 11.9 us: from_others(): lax.ppermute(value, 'edge', [(at, at ^ by) for at in range(shards)])]
    pallas_call x7, Pallas kernels: 16 us -> 15.2 us  [call(): pl.pallas_call(kernel, out_shape=outs, in_specs=[pl.BlockSpec(memory_spac...]
  transfers between devices with their start and end apart: 13 -> 13, of which waited for: 7 -> 5; matrix products, arithmetic and copies ran while one was open for 0% -> 0% of each run, Pallas kernels for 11% -> 11%
where the time goes in v5:
time: 46.6 us; the launch traced here: 46.4 us
  starting transfers between devices  17.4 us (37%)
  Pallas kernels  15.2 us (33%)
  waiting for transfers between devices  13 us (28%)
  between operations  0.73 us (2%)
    pallas_call x7, Pallas kernels, call(): pl.pallas_call(kernel, out_shape=outs, in_specs=[pl.BlockSpec(memory_spac...  15.2 us
    ppermute x6, waiting for transfers between devices, from_others(): lax.ppermute(value, 'edge', [(at, at ^ by) for at in range(shards)])  11.9 us
    ppermute x6, starting transfers between devices, from_others(): lax.ppermute(value, 'edge', [(at, at ^ by) for at in range(shards)])  11.1 us
    ppermute x7, starting transfers between devices, body(): lax.ppermute(block, 'dom', [(at, at ^ partners - place) for at in range(d...  6.31 us
    ppermute x7, waiting for transfers between devices, body(): lax.ppermute(block, 'dom', [(at, at ^ partners - place) for at in range(d...  1.13 us
  transfers between devices with their start and end apart: 13, of which 5 were waited for; matrix products, arithmetic and copies ran while one was open for 0% of the time, Pallas kernels for 11%

profile of v5, /device:TPU:0, one launch (start us, length us, event | category | flops | bytes accessed | tf_op | source)
XLA Modules:
  0.0 46.4 jit_solution(12424388693619773336)
XLA Ops:
  0.7 3.0 %shard_map.141.refs_2_ = bf16[576,128]{1,0:T(8,128)(2,1)S(1)} custom-call(bf16[1024,512]{1,0:T(8,128)(2,1)} %edges_hbm.1, bf16[512,512]{1,0:T(8,128)(2,1)} %weight_hbm.1, bf16[64,512]{1,0:T(8,128)(2,1)} %down_hbm.1, bf16[32,256]{1,0:T(8,128)(2,1)} %atoms_hbm.1), custom_call_target="tpu_custom_call" | custom-call | flops 603979776 | bytes 1572864 | tf_op jit(solution)/shard_map/pallas_call | solution.py:42
  3.7 4.1 %collective-permute-start.2 = (bf16[576,128]{1,0:T(8,128)(2,1)S(1)}, bf16[576,128]{1,0:T(8,128)(2,1)S(1)}, u32[]{:S(2)}, u32[]{:S(2)}) collective-permute-start(bf16[576,128]{1,0:T(8,128)(2,1)S(1)} %shard_map.141.refs_2_), channel_id=1, source_target_pairs={{0,2},{1,3},{2,0},{3,1},{4,6},{5,7},{6,4},{7,5},{8,10},{9,11},{10,... | collective-permute-start | bytes 442376 | tf_op jit(solution)/shard_map/ppermute | solution.py:321
  7.8 1.3 %collective-permute-start.1 = (bf16[576,128]{1,0:T(8,128)(2,1)S(1)}, bf16[576,128]{1,0:T(8,128)(2,1)S(1)}, u32[]{:S(2)}, u32[]{:S(2)}) collective-permute-start(bf16[576,128]{1,0:T(8,128)(2,1)S(1)} %shard_map.141.refs_2_), channel_id=1, source_target_pairs={{0,3},{1,2},{2,1},{3,0},{4,7},{5,6},{6,5},{7,4},{8,11},{9,10},{10,... | collective-permute-start | bytes 442376 | tf_op jit(solution)/shard_map/ppermute | solution.py:321
  9.1 0.2 collective-permute-start
  9.4 0.1 copy.15.refs_0_
  9.4 2.7 %shard_map.140 = (bf16[896,1024]{1,0:T(8,128)(2,1)S(1)}, bf16[1024,896]{1,0:T(8,128)(2,1)S(1)}, bf16[1024,1024]{1,0:T(8,128)(2,1)S(1)}, bf16[1024,512]{1,0:T(8,1...) custom-call(s32[1,1024]{1,0:T(1,128)S(1)} %bitcast.1, ...), custom_call_target="tpu_custom_call" | custom-call | flops 41943040 | bytes 6291456 | tf_op jit(solution)/shard_map/pallas_call | solution.py:42
  12.1 6.7 %collective-permute-done.2.refs_5_ = bf16[576,128]{1,0:T(8,128)(2,1)S(1)} collective-permute-done((bf16[576,128]{1,0:T(8,128)(2,1)S(1)}, bf16[576,128]{1,0:T(8,128)(2,1)S(1)}, u32[]{:S(2)}, u32[]{:S(2)}) %collective-permute-start.2) | collective-permute-done | bytes 147488 | tf_op jit(solution)/shard_map/ppermute | solution.py:321
  18.8 0.0 collective-permute-done.1.refs_4_
  18.8 0.5 %collective-permute-done.refs_3_ = bf16[576,128]{1,0:T(8,128)(2,1)S(1)} collective-permute-done((bf16[576,128]{1,0:T(8,128)(2,1)S(1)}, bf16[576,128]{1,0:T(8,128)(2,1)S(1)}, u32[]{:S(2)}, u32[]{:S(2)}) %collective-permute-start) | collective-permute-done | bytes 147488 | tf_op jit(solution)/shard_map/ppermute | solution.py:321
  19.3 1.9 %shard_map.142 = (bf16[1024,64]{1,0:T(8,128)(2,1)S(1)}, bf16[128,256]{1,0:T(8,128)(2,1)S(1)}, bf16[64,128]{1,0:T(8,128)(2,1)S(1)}, bf16[64,128]{1,0:T(8,128)(2,1...) custom-call(s32[16,2]{1,0:T(8,128)S(1)} %copy.15.refs_0_, ...), custom_call_target="tpu_custom_call" | custom-call | flops 134217728 | bytes 2097152 | tf_op jit(solution)/shard_map/pallas_call | solution.py:42
  21.3 0.1 collective-permute-start.3
  21.4 2.6 %collective-permute-start.4 = (bf16[64,128]{1,0:T(8,128)(2,1)S(1)}, bf16[64,128]{1,0:T(8,128)(2,1)S(1)}, u32[]{:S(2)}, u32[]{:S(2)}) collective-permute-start(bf16[64,128]{1,0:T(8,128)(2,1)S(1)} %get-tuple-element.37), channel_id=1, source_target_pairs={{0,24},{4,28},{8,16},{12,20},{16,8},{20,12},{24,0},{28,4},{1,25},{... | collective-permute-start | bytes 49160 | tf_op jit(solution)/shard_map/ppermute | solution.py:393
  23.9 1.4 %collective-permute-start.5 = (bf16[64,128]{1,0:T(8,128)(2,1)S(1)}, bf16[64,128]{1,0:T(8,128)(2,1)S(1)}, u32[]{:S(2)}, u32[]{:S(2)}) collective-permute-start(bf16[64,128]{1,0:T(8,128)(2,1)S(1)} %get-tuple-element.38), channel_id=1, source_target_pairs={{0,20},{4,16},{8,28},{12,24},{16,4},{20,0},{24,12},{28,8},{1,21},{... | collective-permute-start | bytes 49160 | tf_op jit(solution)/shard_map/ppermute | solution.py:393
  25.3 0.5 collective-permute-start.6
  25.7 0.8 %collective-permute-start.7 = (bf16[64,128]{1,0:T(8,128)(2,1)S(1)}, bf16[64,128]{1,0:T(8,128)(2,1)S(1)}, u32[]{:S(2)}, u32[]{:S(2)}) collective-permute-start(bf16[64,128]{1,0:T(8,128)(2,1)S(1)} %get-tuple-element.40), channel_id=1, source_target_pairs={{0,12},{4,8},{8,4},{12,0},{16,28},{20,24},{24,20},{28,16},{1,13},{... | collective-permute-start | bytes 49160 | tf_op jit(solution)/shard_map/ppermute | solution.py:393
  26.5 0.0 collective-permute-done.3.refs_6_
  26.5 0.9 %collective-permute-start.8 = (bf16[64,128]{1,0:T(8,128)(2,1)S(1)}, bf16[64,128]{1,0:T(8,128)(2,1)S(1)}, u32[]{:S(2)}, u32[]{:S(2)}) collective-permute-start(bf16[64,128]{1,0:T(8,128)(2,1)S(1)} %get-tuple-element.41), channel_id=1, source_target_pairs={{0,8},{4,12},{8,0},{12,4},{16,24},{20,28},{24,16},{28,20},{1,9},{5... | collective-permute-start | bytes 49160 | tf_op jit(solution)/shard_map/ppermute | solution.py:393
  27.4 0.2 collective-permute-start.9
  27.6 1.6 %shard_map.143.refs_0_ = f32[1024,512]{1,0:T(8,128)S(1)} custom-call(bf16[1024,512]{1,0:T(8,128)(2,1)S(1)} %get-tuple-element.26.edges_ref, bf16[1024,64]{1,0:T(8,128)(2,1)S(1)} %get-tuple-element.29.trip_ref, bf16[1024,1024]{1,0:T(8,128)(2,1)S(1)} %get-tuple-element.30.local_ref, bf16[2,64,512]{2,1,0:T(8,128)(2,1)S(1)} %get-tuple-element.31.up_ref.refs_2_), custom_call_target="tpu_custom_call" | custom-call | flops 268435456 | bytes 5242880 | tf_op jit(solution)/shard_map/pallas_call | solution.py:42
  29.2 0.0 collective-permute-done.6.refs_9_
  29.2 0.0 collective-permute-done.7.refs_10_
  29.2 1.1 %collective-permute-done.8.refs_11_ = bf16[64,128]{1,0:T(8,128)(2,1)S(1)} collective-permute-done((bf16[64,128]{1,0:T(8,128)(2,1)S(1)}, bf16[64,128]{1,0:T(8,128)(2,1)S(1)}, u32[]{:S(2)}, u32[]{:S(2)}) %collective-permute-start.8) | collective-permute-done | bytes 16416 | tf_op jit(solution)/shard_map/ppermute | solution.py:393
  30.4 0.0 collective-permute-done.9.refs_12_
  30.4 3.1 %shard_map.144 = (bf16[1024,512]{1,0:T(8,128)(2,1)S(1)}, bf16[128,256]{1,0:T(8,128)(2,1)S(1)}) custom-call(f32[1024,512]{1,0:T(8,128)S(1)} %shard_map.143.refs_0_, bf16[1024,896]{1,0:T(8,128)(2,1)S(1)} %get-tuple-element.32.refs_1_, bf16[2,64,512]{2,1,0:T(8,128)(2,1)S(1)} %get-tuple-element.31.up_ref.refs_2_, ...), custom_call_target="tpu_custom_call" | custom-call | flops 1073741824 | bytes 4194304 | tf_op jit(solution)/shard_map/pallas_call | solution.py:42
  33.5 4.8 %collective-permute-start.12 = (bf16[128,256]{1,0:T(8,128)(2,1)S(1)}, bf16[128,256]{1,0:T(8,128)(2,1)S(1)}, u32[]{:S(2)}, u32[]{:S(2)}) collective-permute-start(bf16[128,256]{1,0:T(8,128)(2,1)S(1)} %get-tuple-element.43.refs_0_), channel_id=1, source_target_pairs={{0,2},{1,3},{2,0},{3,1},{4,6},{5,7},{6,4},{7,5},{8,10},{9,11},{10,... | collective-permute-start | bytes 196616 | tf_op jit(solution)/shard_map/ppermute | solution.py:321
  38.2 0.4 collective-permute-start.11
  38.7 0.2 collective-permute-start.10
  38.9 0.8 %shard_map.145 = (f32[1024,512]{1,0:T(8,128)S(1)}, bf16[1024,256]{1,0:T(8,128)(2,1)S(1)}) custom-call(bf16[1024,512]{1,0:T(8,128)(2,1)S(1)} %get-tuple-element.47.state_ref.refs_7_, bf16[1024,512]{1,0:T(8,128)(2,1)S(1)} %get-tuple-element.46.join_ref.refs_6_, s32[2,1024]{1,0:T(2,128)S(1)} %get-tuple-element.35.refs_5_.index_ref), custom_call_target="tpu_custom_call" | custom-call | flops 536870912 | bytes 4194304 | tf_op jit(solution)/shard_map/pallas_call | solution.py:42
  39.6 2.2 %collective-permute-done.12.refs_3_ = bf16[128,256]{1,0:T(8,128)(2,1)S(1)} collective-permute-done((bf16[128,256]{1,0:T(8,128)(2,1)S(1)}, bf16[128,256]{1,0:T(8,128)(2,1)S(1)}, u32[]{:S(2)}, u32[]{:S(2)}) %collective-permute-start.12) | collective-permute-done | bytes 65568 | tf_op jit(solution)/shard_map/ppermute | solution.py:321
  41.9 2.4 %collective-permute-done.11.refs_2_ = bf16[128,256]{1,0:T(8,128)(2,1)S(1)} collective-permute-done((bf16[128,256]{1,0:T(8,128)(2,1)S(1)}, bf16[128,256]{1,0:T(8,128)(2,1)S(1)}, u32[]{:S(2)}, u32[]{:S(2)}) %collective-permute-start.11) | collective-permute-done | bytes 65568 | tf_op jit(solution)/shard_map/ppermute | solution.py:321
  44.3 0.0 collective-permute-done.10.refs_1_
  44.3 2.1 %shard_map.146 = (bf16[1024,512]{1,0:T(8,128)(2,1)}, bf16[32,256]{1,0:T(8,128)(2,1)}) custom-call(bf16[128,256]{1,0:T(8,128)(2,1)S(1)} %get-tuple-element.43.refs_0_, bf16[128,256]{1,0:T(8,128)(2,1)S(1)} %collective-permute-done.10.refs_1_, bf16[128,256]{1,0:T(8,128)(2,1)S(1)} %collective-permute-done.11.refs_2_, ...), custom_call_target="tpu_custom_call" | custom-call | flops 268435456 | bytes 4194304 | tf_op jit(solution)/shard_map/pallas_call | solution.py:42
  (6 shorter events, 0.0 us)
Async XLA Ops:
  0.6 8.7 %copy-start.1 = (s32[16,2]{0,1:T(2,128)S(1)}, s32[16,2]{0,1:T(2,128)}, u32[]{:S(2)}) copy-start(s32[16,2]{0,1:T(2,128)} %param.17) | copy-start | bytes 388
  0.6 8.8 %copy-start = (s32[1024]{0:T(1024)S(1)}, s32[1024]{0:T(1024)}, u32[]{:S(2)}) copy-start(s32[1024]{0:T(1024)} %param.15) | copy-start | bytes 12292
  3.7 15.1 %collective-permute-start.2 = (bf16[576,128]{1,0:T(8,128)(2,1)S(1)}, bf16[576,128]{1,0:T(8,128)(2,1)S(1)}, u32[]{:S(2)}, u32[]{:S(2)}) collective-permute-start(bf16[576,128]{1,0:T(8,128)(2,1)S(1)} %shard_map.141.refs_2_), channel_id=1, source_target_pairs={{0,2},{1,3},{2,0},{3,1},{4,6},{5,7},{6,4},{7,5},{8,10},{9,11},{10,... | collective-permute-start | bytes 442376 | tf_op jit(solution)/shard_map/ppermute | solution.py:321
  7.8 11.0 %collective-permute-start.1 = (bf16[576,128]{1,0:T(8,128)(2,1)S(1)}, bf16[576,128]{1,0:T(8,128)(2,1)S(1)}, u32[]{:S(2)}, u32[]{:S(2)}) collective-permute-start(bf16[576,128]{1,0:T(8,128)(2,1)S(1)} %shard_map.141.refs_2_), channel_id=1, source_target_pairs={{0,3},{1,2},{2,1},{3,0},{4,7},{5,6},{6,5},{7,4},{8,11},{9,10},{10,... | collective-permute-start | bytes 442376 | tf_op jit(solution)/shard_map/ppermute | solution.py:321
  9.1 10.2 %collective-permute-start = (bf16[576,128]{1,0:T(8,128)(2,1)S(1)}, bf16[576,128]{1,0:T(8,128)(2,1)S(1)}, u32[]{:S(2)}, u32[]{:S(2)}) collective-permute-start(bf16[576,128]{1,0:T(8,128)(2,1)S(1)} %shard_map.141.refs_2_), channel_id=1, source_target_pairs={{0,1},{1,0},{2,3},{3,2},{4,5},{5,4},{6,7},{7,6},{8,9},{9,8},{10,11... | collective-permute-start | bytes 442376 | tf_op jit(solution)/shard_map/ppermute | solution.py:321
  21.3 5.2 %collective-permute-start.3 = (bf16[64,128]{1,0:T(8,128)(2,1)S(1)}, bf16[64,128]{1,0:T(8,128)(2,1)S(1)}, u32[]{:S(2)}, u32[]{:S(2)}) collective-permute-start(bf16[64,128]{1,0:T(8,128)(2,1)S(1)} %get-tuple-element.36), channel_id=1, source_target_pairs={{0,28},{4,24},{8,20},{12,16},{16,12},{20,8},{24,4},{28,0},{1,29},{... | collective-permute-start | bytes 49160 | tf_op jit(solution)/shard_map/ppermute | solution.py:393
  21.4 6.1 %collective-permute-start.4 = (bf16[64,128]{1,0:T(8,128)(2,1)S(1)}, bf16[64,128]{1,0:T(8,128)(2,1)S(1)}, u32[]{:S(2)}, u32[]{:S(2)}) collective-permute-start(bf16[64,128]{1,0:T(8,128)(2,1)S(1)} %get-tuple-element.37), channel_id=1, source_target_pairs={{0,24},{4,28},{8,16},{12,20},{16,8},{20,12},{24,0},{28,4},{1,25},{... | collective-permute-start | bytes 49160 | tf_op jit(solution)/shard_map/ppermute | solution.py:393
  23.9 5.3 %collective-permute-start.5 = (bf16[64,128]{1,0:T(8,128)(2,1)S(1)}, bf16[64,128]{1,0:T(8,128)(2,1)S(1)}, u32[]{:S(2)}, u32[]{:S(2)}) collective-permute-start(bf16[64,128]{1,0:T(8,128)(2,1)S(1)} %get-tuple-element.38), channel_id=1, source_target_pairs={{0,20},{4,16},{8,28},{12,24},{16,4},{20,0},{24,12},{28,8},{1,21},{... | collective-permute-start | bytes 49160 | tf_op jit(solution)/shard_map/ppermute | solution.py:393
  25.3 3.9 %collective-permute-start.6 = (bf16[64,128]{1,0:T(8,128)(2,1)S(1)}, bf16[64,128]{1,0:T(8,128)(2,1)S(1)}, u32[]{:S(2)}, u32[]{:S(2)}) collective-permute-start(bf16[64,128]{1,0:T(8,128)(2,1)S(1)} %get-tuple-element.39), channel_id=1, source_target_pairs={{0,16},{4,20},{8,24},{12,28},{16,0},{20,4},{24,8},{28,12},{1,17},{... | collective-permute-start | bytes 49160 | tf_op jit(solution)/shard_map/ppermute | solution.py:393
  25.7 3.5 %collective-permute-start.7 = (bf16[64,128]{1,0:T(8,128)(2,1)S(1)}, bf16[64,128]{1,0:T(8,128)(2,1)S(1)}, u32[]{:S(2)}, u32[]{:S(2)}) collective-permute-start(bf16[64,128]{1,0:T(8,128)(2,1)S(1)} %get-tuple-element.40), channel_id=1, source_target_pairs={{0,12},{4,8},{8,4},{12,0},{16,28},{20,24},{24,20},{28,16},{1,13},{... | collective-permute-start | bytes 49160 | tf_op jit(solution)/shard_map/ppermute | solution.py:393
  26.5 3.8 %collective-permute-start.8 = (bf16[64,128]{1,0:T(8,128)(2,1)S(1)}, bf16[64,128]{1,0:T(8,128)(2,1)S(1)}, u32[]{:S(2)}, u32[]{:S(2)}) collective-permute-start(bf16[64,128]{1,0:T(8,128)(2,1)S(1)} %get-tuple-element.41), channel_id=1, source_target_pairs={{0,8},{4,12},{8,0},{12,4},{16,24},{20,28},{24,16},{28,20},{1,9},{5... | collective-permute-start | bytes 49160 | tf_op jit(solution)/shard_map/ppermute | solution.py:393
  27.4 2.9 %collective-permute-start.9 = (bf16[64,128]{1,0:T(8,128)(2,1)S(1)}, bf16[64,128]{1,0:T(8,128)(2,1)S(1)}, u32[]{:S(2)}, u32[]{:S(2)}) collective-permute-start(bf16[64,128]{1,0:T(8,128)(2,1)S(1)} %get-tuple-element.42), channel_id=1, source_target_pairs={{0,4},{4,0},{8,12},{12,8},{16,20},{20,16},{24,28},{28,24},{1,5},{5... | collective-permute-start | bytes 49160 | tf_op jit(solution)/shard_map/ppermute | solution.py:393
  33.5 8.4 %collective-permute-start.12 = (bf16[128,256]{1,0:T(8,128)(2,1)S(1)}, bf16[128,256]{1,0:T(8,128)(2,1)S(1)}, u32[]{:S(2)}, u32[]{:S(2)}) collective-permute-start(bf16[128,256]{1,0:T(8,128)(2,1)S(1)} %get-tuple-element.43.refs_0_), channel_id=1, source_target_pairs={{0,2},{1,3},{2,0},{3,1},{4,6},{5,7},{6,4},{7,5},{8,10},{9,11},{10,... | collective-permute-start | bytes 196616 | tf_op jit(solution)/shard_map/ppermute | solution.py:321
  38.2 6.1 %collective-permute-start.11 = (bf16[128,256]{1,0:T(8,128)(2,1)S(1)}, bf16[128,256]{1,0:T(8,128)(2,1)S(1)}, u32[]{:S(2)}, u32[]{:S(2)}) collective-permute-start(bf16[128,256]{1,0:T(8,128)(2,1)S(1)} %get-tuple-element.43.refs_0_), channel_id=1, source_target_pairs={{0,3},{1,2},{2,1},{3,0},{4,7},{5,6},{6,5},{7,4},{8,11},{9,10},{10,... | collective-permute-start | bytes 196616 | tf_op jit(solution)/shard_map/ppermute | solution.py:321
  38.7 5.6 %collective-permute-start.10 = (bf16[128,256]{1,0:T(8,128)(2,1)S(1)}, bf16[128,256]{1,0:T(8,128)(2,1)S(1)}, u32[]{:S(2)}, u32[]{:S(2)}) collective-permute-start(bf16[128,256]{1,0:T(8,128)(2,1)S(1)} %get-tuple-element.43.refs_0_), channel_id=1, source_target_pairs={{0,1},{1,0},{2,3},{3,2},{4,5},{5,4},{6,7},{7,6},{8,9},{9,8},{10,11... | collective-permute-start | bytes 196616 | tf_op jit(solution)/shard_map/ppermute | solution.py:321

commit v6 on v5

--- a/solution.py
+++ b/solution.py
@@ -10,6 +10,7 @@
 root_half = 0.7071067811865476
 MIB = 1 << 20
 CHUNK = 256
+GROUPS = 4
 
 
 def product(operand, weights):
@@ -94,37 +95,53 @@
     for at, rows in enumerate(row_chunks(half)):
         copies[2 + 2 * at].wait()
         copies[3 + 2 * at].wait()
-        sides = []
-        for side in range(2):
-            hidden = silu(product(edges_ref[pieces[2 * at + side], :], weight_ref[...]))
-            sides.append(
-                silu(
-                    lax.dot_general(
-                        hidden.astype(jnp.bfloat16),
-                        down_ref[...],
-                        (((1,), (1,)), ((), ())),
-                        preferred_element_type=jnp.float32,
-                    )
-                )
+        hidden = [
+            silu(product(edges_ref[piece, :], weight_ref[...])).astype(jnp.bfloat16)
+            for piece in pieces[2 * at : 2 * at + 2]
+        ]
+        sides = [
+            lax.dot_general(
+                each, down_ref[...], (((1,), (1,)), ((), ())), preferred_element_type=jnp.float32
             )
-        out_ref[rows, :] = jnp.concatenate(sides, axis=1).astype(jnp.bfloat16)
+            for each in hidden
+        ]
+        out_ref[rows, :] = silu(jnp.concatenate(sides, axis=1)).astype(jnp.bfloat16)
     for copy in atom_copies:
         copy.wait()
 
 
-def index_kernel(domains, shards, operands, *refs):
+def one_hot(shape, axis, chosen):
+    return (lax.broadcasted_iota(jnp.int32, shape, axis) == chosen).astype(jnp.bfloat16)
+
+
+def group_mask(group, channels):
+    column = lax.broadcasted_iota(jnp.int32, (group.shape[0], GROUPS * channels), 1)
+    return (column // channels == group).astype(jnp.bfloat16)
+
+
+def index_kernel(domains, shards, channels, operands, *refs):
     reverse_ref = refs[0]
     sources = refs[1 : 1 + operands]
-    send_ref, fetch_ref, local_ref = refs[1 + operands : 4 + operands]
-    targets = refs[4 + operands : 4 + 2 * operands]
+    send_ref, send_mask_ref, fetch_ref, fetch_mask_ref, local_ref, local_mask_ref, stack_ref = refs[
+        1 + operands : 8 + operands
+    ]
+    targets = refs[8 + operands : 8 + 2 * operands]
     sems = refs[-1]
     copies = [
         pltpu.make_async_copy(source, target, sems.at[at])
         for at, (source, target) in enumerate(zip(sources, targets))
+    ] + [
+        pltpu.make_async_copy(
+            sources[0].at[1],
+            stack_ref.at[at * channels : (at + 1) * channels, :],
+            sems.at[operands + at],
+        )
+        for at in range(GROUPS)
     ]
     for copy in copies:
         copy.start()
     rows = reverse_ref.shape[1]
+    each = rows // GROUPS
     capacity = rows // domains
     half = capacity // 2
     slots = (domains - 1) * capacity
@@ -133,46 +150,58 @@
     holder = reverse // (rows * shards)
     source_row = lax.rem(reverse, rows)
     partner = holder ^ own
-    source_column = as_column(source_row)
-    member = (lax.broadcasted_iota(jnp.int32, (domains, rows), 0) == partner).astype(jnp.bfloat16)
+    remote = partner != 0
+    block = domains - 1 - partner
+    member = one_hot((domains, rows), 0, partner)
     before = (
         lax.broadcasted_iota(jnp.int32, (rows, rows), 0)
         < lax.broadcasted_iota(jnp.int32, (rows, rows), 1)
     ).astype(jnp.bfloat16)
-    place = jnp.sum(
-        product(member, before) * member.astype(jnp.float32), axis=0, keepdims=True
-    ).astype(jnp.int32)
-    earlier = (source_column < source_row).astype(jnp.bfloat16)
-    far_place = jnp.sum(
-        product(member, earlier) * member.astype(jnp.float32), axis=0, keepdims=True
-    ).astype(jnp.int32)
-
-    def slot_of(at):
-        part = (at >= half).astype(jnp.int32)
-        slot = part * (slots // 2) + (domains - 1 - partner) * half + at - part * half
-        return jnp.where(partner == 0, -1, slot)
-
-    send_slot = slot_of(place)
-    send_ref[...] = (
-        lax.broadcasted_iota(jnp.int32, (slots, rows), 0) == send_slot
+    earlier = (as_column(source_row) < source_row).astype(jnp.bfloat16)
+
+    def rank(matrix):
+        counts = product(member, matrix) * member.astype(jnp.float32)
+        return jnp.sum(counts, axis=0, keepdims=True).astype(jnp.int32)
+
+    place = rank(before)
+    part = (place >= half).astype(jnp.int32)
+    send_slot = part * (slots // 2) + block * half + place - part * half
+    sent = one_hot((slots, rows), 0, jnp.where(remote, send_slot, -1))
+    owner = (
+        lax.broadcasted_iota(jnp.int32, (rows, GROUPS * channels), 0) // each
+        == lax.broadcasted_iota(jnp.int32, (rows, GROUPS * channels), 1) // channels
     ).astype(jnp.bfloat16)
-    fetch_column = as_column(slot_of(far_place))
-    fetch_ref[...] = (
-        lax.broadcasted_iota(jnp.int32, (rows, slots), 1) == fetch_column
-    ).astype(jnp.bfloat16)
-    local_column = as_column(jnp.where(partner == 0, source_row, -1))
-    local_ref[...] = (
-        lax.broadcasted_iota(jnp.int32, (rows, rows), 1) == local_column
-    ).astype(jnp.bfloat16)
+    send_mask_ref[...] = product(sent, owner).astype(jnp.bfloat16)
+    folded = sent[:, :each]
+    for at in range(1, GROUPS):
+        folded = folded + sent[:, at * each : (at + 1) * each]
+    send_ref[...] = folded
+
+    far_place = rank(earlier)
+    part = (far_place >= half).astype(jnp.int32)
+    side = (block >= domains // 2).astype(jnp.int32)
+    fetch_row = (block - side * (domains // 2)) * half + far_place - part * half
+    fetch_ref[...] = one_hot(
+        fetch_ref.shape, 1, as_column(jnp.where(remote, fetch_row, -1))
+    )
+    fetch_mask_ref[...] = group_mask(as_column(2 * side + part), channels)
+    local_group = source_row // each
+    local_row = source_row - local_group * each
+    local_ref[...] = one_hot(local_ref.shape, 1, as_column(jnp.where(remote, -1, local_row)))
+    local_mask_ref[...] = group_mask(as_column(local_group), channels)
     for copy in copies:
         copy.wait()
+
+
+def picked_rows(chosen, table, mask):
+    return product(chosen, table).astype(jnp.bfloat16) * mask
 
 
 def mix_kernel(shards, *refs):
     source_ref, tiles_ref = refs[:2]
     parts = refs[2 : 2 + shards]
-    send_ref, trip_ref, atoms_ref = refs[2 + shards : 5 + shards]
-    out_refs = refs[5 + shards : -1]
+    send_ref, mask_ref, trip_ref, atoms_ref = refs[2 + shards : 6 + shards]
+    out_refs = refs[6 + shards : -1]
     held_ref = refs[-1]
     blocks, block_len, width = tiles_ref.shape
     count = width // block_len
@@ -189,8 +218,10 @@
                 at * own_atoms : (at + 1) * own_atoms, piece * lanes : (piece + 1) * lanes
             ] = part[start : start + own_atoms, :]
     half_blocks = blocks // 2
-    channels = trip_ref.shape[1]
-    for block in range(blocks):
+    channels = trip_ref.shape[1] // GROUPS
+    per = blocks // GROUPS
+
+    def mixed(block):
         picks = []
         for tile in range(count):
             source = source_ref[block, tile]
@@ -200,35 +231,52 @@
             start = (shard ^ me) * lines + (within - upper * half_blocks) * block_len
             rows = held_ref[pl.ds(pl.multiple_of(start, block_len), block_len), :]
             picks.append(jnp.where(upper == 1, rows[:, channels:], rows[:, :channels]))
-        mixed = product(tiles_ref[block], jnp.concatenate(picks, axis=0))
-        trip_ref[block * block_len : (block + 1) * block_len, :] = mixed.astype(jnp.bfloat16)
+        return product(tiles_ref[block], jnp.concatenate(picks, axis=0))
+
+    for at in range(per):
+        for group in range(0, GROUPS, 2):
+            pair = [mixed((group + side) * per + at) for side in range(2)]
+            trip_ref[
+                at * block_len : (at + 1) * block_len, group * channels : (group + 2) * channels
+            ] = jnp.concatenate(pair, axis=1).astype(jnp.bfloat16)
     half_slots = send_ref.shape[0] // 2
-    low = product(send_ref[:half_slots, :], trip_ref[...])
-    high = product(send_ref[half_slots:, :], trip_ref[...])
-    packed = jnp.concatenate([low, high], axis=1).astype(jnp.bfloat16)
+    parts = []
+    for side in range(2):
+        rows = slice(side * half_slots, (side + 1) * half_slots)
+        found = product(send_ref[rows, :], trip_ref[...]) * mask_ref[rows, :].astype(jnp.float32)
+        both = found[:, : 2 * channels] + found[:, 2 * channels :]
+        parts.append(both + pltpu.roll(both, channels, 1))
+    lane = lax.broadcasted_iota(jnp.int32, parts[0].shape, 1)
+    packed = jnp.where(lane < channels, parts[0], parts[1]).astype(jnp.bfloat16)
     each = half_slots // len(out_refs)
     for at, out_ref in enumerate(out_refs):
         out_ref[...] = packed[at * each : (at + 1) * each, :]
 
 
-def base_kernel(edges_ref, trip_ref, local_ref, up_ref, out_ref):
-    channels = trip_ref.shape[1]
-    for rows in row_chunks(edges_ref.shape[0]):
-        picked = product(local_ref[rows, :], trip_ref[...]).astype(jnp.bfloat16)
-        joined = product(trip_ref[rows, :], up_ref[0]) + product(picked, up_ref[1])
+def base_kernel(edges_ref, trip_ref, local_ref, mask_ref, up_ref, stack_ref, out_ref):
+    each = trip_ref.shape[0]
+    channels = up_ref.shape[1]
+    for group in range(GROUPS):
+        rows = slice(group * each, (group + 1) * each)
+        picked = picked_rows(local_ref[rows, :], trip_ref[...], mask_ref[rows, :])
+        direct = trip_ref[:, group * channels : (group + 1) * channels]
+        joined = product(direct, up_ref[0]) + product(picked, stack_ref[...])
         out_ref[rows, :] = edges_ref[rows, :].astype(jnp.float32) + joined * root_half
 
 
 def state_kernel(partners, *refs):
-    base_ref, fetch_ref, up_ref, residual_ref, message_ref, index_ref = refs[:6]
-    arrived = refs[6 : 6 + partners]
-    state_ref, sums_ref, slots_ref = refs[6 + partners :]
-    channels = up_ref.shape[1]
-    each = arrived[0].shape[0]
+    base_ref, fetch_ref, mask_ref, stack_ref, residual_ref, message_ref, index_ref = refs[:7]
+    arrived = refs[7 : 7 + partners]
+    state_ref, sums_ref, slots_ref = refs[7 + partners :]
+    each, lanes = arrived[0].shape
+    column = (partners + 1) // 2
     for at in range(partners):
-        piece = arrived[at][...]
-        slots_ref[at * each : (at + 1) * each, :] = piece[:, :channels]
-        slots_ref[(partners + at) * each : (partners + at + 1) * each, :] = piece[:, channels:]
+        down, right = at % column, at // column
+        slots_ref[down * each : (down + 1) * each, right * lanes : (right + 1) * lanes] = arrived[at][...]
+    down, right = partners % column, partners // column
+    slots_ref[down * each : (down + 1) * each, right * lanes : (right + 1) * lanes] = jnp.zeros(
+        (each, lanes), slots_ref.dtype
+    )
     part_atoms = sums_ref.shape[0]
     shards = lax.axis_size("edge")
     near = near_atoms(index_ref[1:2, :], part_atoms, shards)
@@ -239,9 +287,11 @@
     gathered = None
     for first in range(0, len(chunks), 2):
         group = chunks[first : first + 2]
-        picked = [product(fetch_ref[rows, :], slots_ref[...]).astype(jnp.bfloat16) for rows in group]
+        picked = [
+            picked_rows(fetch_ref[rows, :], slots_ref[...], mask_ref[rows, :]) for rows in group
+        ]
         states = [
-            (base_ref[rows, :] + product(each, up_ref[1]) * root_half).astype(jnp.bfloat16)
+            (base_ref[rows, :] + product(each, stack_ref[...]) * root_half).astype(jnp.bfloat16)
             for rows, each in zip(group, picked)
         ]
         for layer in range(residual_ref.shape[0]):
@@ -300,14 +350,19 @@
             renewed, join_ref[end * width : (end + 1) * width, :]
         ).astype(jnp.bfloat16)
     copies = [own_copy]
-    for at, rows in enumerate(row_chunks(state_ref.shape[0])):
-        update = silu(product(chosen_ref[rows, :], table_ref[...]) + side_ref[rows, :])
-        state = state_ref[rows, :].astype(jnp.float32)
-        edges_ref[rows, :] = ((state + update) * root_half).astype(jnp.bfloat16)
-        copies.append(
-            pltpu.make_async_copy(edges_ref.at[rows], edges_hbm.at[rows], sems.at[1 + at])
-        )
-        copies[-1].start()
+    chunks = row_chunks(state_ref.shape[0])
+    for first in range(0, len(chunks), 2):
+        group = chunks[first : first + 2]
+        found = [product(chosen_ref[rows, :], table_ref[...]) + side_ref[rows, :] for rows in group]
+        for at, (rows, each) in enumerate(zip(group, found)):
+            state = state_ref[rows, :].astype(jnp.float32)
+            edges_ref[rows, :] = ((state + silu(each)) * root_half).astype(jnp.bfloat16)
+            copies.append(
+                pltpu.make_async_copy(
+                    edges_ref.at[rows], edges_hbm.at[rows], sems.at[1 + first + at]
+                )
+            )
+            copies[-1].start()
     for copy in copies:
         copy.wait()
 
@@ -366,24 +421,34 @@
     )
     narrow_parts = from_others(narrow, shards)
     later = (
-        edges, tiles, weight_up, weight_residual, weight_message, weight_join, weight_atom, atom_index
-    )
-    send, fetch, local, *later = call(
-        functools.partial(index_kernel, domains, shards, len(later)),
-        (shaped((slots, rows)), shaped((rows, slots)), shaped((rows, rows)))
+        weight_up, edges, tiles, weight_residual, weight_message, weight_join, weight_atom, atom_index
+    )
+    each, grouped = rows // GROUPS, GROUPS * channels
+    column = domains // 2 * (capacity // 2)
+    send, send_mask, fetch, fetch_mask, local, local_mask, up_stack, *later = call(
+        functools.partial(index_kernel, domains, shards, channels, len(later)),
+        (
+            shaped((slots, each)),
+            shaped((slots, grouped)),
+            shaped((rows, column)),
+            shaped((rows, grouped)),
+            shaped((rows, each)),
+            shaped((rows, grouped)),
+            shaped((grouped, wide)),
+        )
         + tuple(shaped(each.shape, each.dtype) for each in later),
         (reverse.reshape(1, rows), *later),
         hbm=range(1, 1 + len(later)),
-        scratch=[pltpu.SemaphoreType.DMA((len(later),))],
+        scratch=[pltpu.SemaphoreType.DMA((len(later) + GROUPS,))],
         flops=40 * rows * rows,
         nbytes=6 * rows * rows,
     )
-    edges, tiles, weight_up, weight_residual, weight_message, weight_join, weight_atom, atom_index = later
+    weight_up, edges, tiles, weight_residual, weight_message, weight_join, weight_atom, atom_index = later
     trip_out, all_atoms, *outgoing = call(
         functools.partial(mix_kernel, shards),
-        (shaped((rows, channels)), shaped((part_atoms, atom_wide)))
+        (shaped((each, grouped)), shaped((part_atoms, atom_wide)))
         + (shaped((capacity // 2, packed)),) * partners,
-        (tile_source, tiles, *narrow_parts, send),
+        (tile_source, tiles, *narrow_parts, send, send_mask),
         smem=(0,),
         scratch=[pltpu.VMEM((shards * lines, packed), jnp.bfloat16)],
         flops=2 * rows * rows * channels,
@@ -396,15 +461,15 @@
     base = call(
         base_kernel,
         shaped((rows, wide), jnp.float32),
-        (edges, trip_out, local, weight_up),
+        (edges, trip_out, local, local_mask, weight_up, up_stack),
         flops=2 * rows * channels * (rows + 2 * wide),
         nbytes=2 * rows * rows + 6 * rows * wide,
     )
     state, sums = call(
         functools.partial(state_kernel, partners),
         (shaped((rows, wide)), shaped((part_atoms, atom_wide))),
-        (base, fetch, weight_up, weight_residual, weight_message, atom_index, *arrived),
-        scratch=[pltpu.VMEM((slots, channels), jnp.bfloat16)],
+        (base, fetch, fetch_mask, up_stack, weight_residual, weight_message, atom_index, *arrived),
+        scratch=[pltpu.VMEM((column, grouped), jnp.bfloat16)],
         flops=4 * rows * wide * wide,
         nbytes=8 * rows * wide,
     )

time: 46.6 us -> 45.9 us (0.985)
  waiting for transfers between devices: 13 us -> 12.1 us
    ppermute x6, waiting for transfers between devices: 11.9 us -> 10.6 us  [from_others(): lax.ppermute(value, 'edge', [(at, at ^ by) for at in range(shards)])]
  transfers between devices with their start and end apart: 13 -> 13, of which waited for: 5 -> 6; matrix products, arithmetic and copies ran while one was open for 0% -> 0% of each run, Pallas kernels for 11% -> 13%
where the time goes in v6:
time: 45.9 us; the launch traced here: 45.7 us
  starting transfers between devices  17.4 us (38%)
  Pallas kernels  15.4 us (34%)
  waiting for transfers between devices  12.1 us (26%)
  between operations  0.72 us (2%)
    pallas_call x7, Pallas kernels, call(): pl.pallas_call(kernel, out_shape=outs, in_specs=[pl.BlockSpec(memory_spac...  15.4 us
    ppermute x6, starting transfers between devices, from_others(): lax.ppermute(value, 'edge', [(at, at ^ by) for at in range(shards)])  11.1 us
    ppermute x6, waiting for transfers between devices, from_others(): lax.ppermute(value, 'edge', [(at, at ^ by) for at in range(shards)])  10.6 us
    ppermute x7, starting transfers between devices, body(): lax.ppermute(block, 'dom', [(at, at ^ partners - place) for at in range(d...  6.31 us
    ppermute x7, waiting for transfers between devices, body(): lax.ppermute(block, 'dom', [(at, at ^ partners - place) for at in range(d...  1.44 us
  transfers between devices with their start and end apart: 13, of which 6 were waited for; matrix products, arithmetic and copies ran while one was open for 0% of the time, Pallas kernels for 13%

profile of v6, /device:TPU:0, one launch (start us, length us, event | category | flops | bytes accessed | tf_op | source)
XLA Modules:
  0.0 45.7 jit_solution(16447516598680630699)
XLA Ops:
  0.7 2.8 %shard_map.141.refs_2_ = bf16[576,128]{1,0:T(8,128)(2,1)S(1)} custom-call(bf16[1024,512]{1,0:T(8,128)(2,1)} %edges_hbm.1, bf16[512,512]{1,0:T(8,128)(2,1)} %weight_hbm.1, bf16[64,512]{1,0:T(8,128)(2,1)} %down_hbm.1, bf16[32,256]{1,0:T(8,128)(2,1)} %atoms_hbm.1), custom_call_target="tpu_custom_call" | custom-call | flops 603979776 | bytes 1572864 | tf_op jit(solution)/shard_map/pallas_call | solution.py:43
  3.5 4.1 %collective-permute-start.2 = (bf16[576,128]{1,0:T(8,128)(2,1)S(1)}, bf16[576,128]{1,0:T(8,128)(2,1)S(1)}, u32[]{:S(2)}, u32[]{:S(2)}) collective-permute-start(bf16[576,128]{1,0:T(8,128)(2,1)S(1)} %shard_map.141.refs_2_), channel_id=1, source_target_pairs={{0,2},{1,3},{2,0},{3,1},{4,6},{5,7},{6,4},{7,5},{8,10},{9,11},{10,... | collective-permute-start | bytes 442376 | tf_op jit(solution)/shard_map/ppermute | solution.py:376
  7.6 1.3 %collective-permute-start.1 = (bf16[576,128]{1,0:T(8,128)(2,1)S(1)}, bf16[576,128]{1,0:T(8,128)(2,1)S(1)}, u32[]{:S(2)}, u32[]{:S(2)}) collective-permute-start(bf16[576,128]{1,0:T(8,128)(2,1)S(1)} %shard_map.141.refs_2_), channel_id=1, source_target_pairs={{0,3},{1,2},{2,1},{3,0},{4,7},{5,6},{6,5},{7,4},{8,11},{9,10},{10,... | collective-permute-start | bytes 442376 | tf_op jit(solution)/shard_map/ppermute | solution.py:376
  8.9 0.2 collective-permute-start
  9.1 0.1 copy.15.refs_0_
  9.2 3.9 %shard_map.140 = (bf16[896,256]{1,0:T(8,128)(2,1)S(1)}, bf16[896,256]{1,0:T(8,128)(2,1)S(1)}, bf16[1024,256]{1,0:T(8,128)(2,1)S(1)}, bf16[1024,256]{1,0:T(8,128)...) custom-call(s32[1,1024]{1,0:T(1,128)S(1)} %bitcast.1, ...), custom_call_target="tpu_custom_call" | custom-call | flops 41943040 | bytes 6291456 | tf_op jit(solution)/shard_map/pallas_call | solution.py:43
  13.1 5.5 %collective-permute-done.2.refs_5_ = bf16[576,128]{1,0:T(8,128)(2,1)S(1)} collective-permute-done((bf16[576,128]{1,0:T(8,128)(2,1)S(1)}, bf16[576,128]{1,0:T(8,128)(2,1)S(1)}, u32[]{:S(2)}, u32[]{:S(2)}) %collective-permute-start.2) | collective-permute-done | bytes 147488 | tf_op jit(solution)/shard_map/ppermute | solution.py:376
  18.6 0.0 collective-permute-done.1.refs_4_
  18.6 0.5 %collective-permute-done.refs_3_ = bf16[576,128]{1,0:T(8,128)(2,1)S(1)} collective-permute-done((bf16[576,128]{1,0:T(8,128)(2,1)S(1)}, bf16[576,128]{1,0:T(8,128)(2,1)S(1)}, u32[]{:S(2)}, u32[]{:S(2)}) %collective-permute-start) | collective-permute-done | bytes 147488 | tf_op jit(solution)/shard_map/ppermute | solution.py:376
  19.1 1.8 %shard_map.142 = (bf16[256,256]{1,0:T(8,128)(2,1)S(1)}, bf16[128,256]{1,0:T(8,128)(2,1)S(1)}, bf16[64,128]{1,0:T(8,128)(2,1)S(1)}, bf16[64,128]{1,0:T(8,128)(2,1...) custom-call(s32[16,2]{1,0:T(8,128)S(1)} %copy.15.refs_0_, ...), custom_call_target="tpu_custom_call" | custom-call | flops 134217728 | bytes 2097152 | tf_op jit(solution)/shard_map/pallas_call | solution.py:43
  20.9 0.1 collective-permute-start.3
  21.0 2.6 %collective-permute-start.4 = (bf16[64,128]{1,0:T(8,128)(2,1)S(1)}, bf16[64,128]{1,0:T(8,128)(2,1)S(1)}, u32[]{:S(2)}, u32[]{:S(2)}) collective-permute-start(bf16[64,128]{1,0:T(8,128)(2,1)S(1)} %get-tuple-element.45), channel_id=1, source_target_pairs={{0,24},{4,28},{8,16},{12,20},{16,8},{20,12},{24,0},{28,4},{1,25},{... | collective-permute-start | bytes 49160 | tf_op jit(solution)/shard_map/ppermute | solution.py:458
  23.5 1.4 %collective-permute-start.5 = (bf16[64,128]{1,0:T(8,128)(2,1)S(1)}, bf16[64,128]{1,0:T(8,128)(2,1)S(1)}, u32[]{:S(2)}, u32[]{:S(2)}) collective-permute-start(bf16[64,128]{1,0:T(8,128)(2,1)S(1)} %get-tuple-element.46), channel_id=1, source_target_pairs={{0,20},{4,16},{8,28},{12,24},{16,4},{20,0},{24,12},{28,8},{1,21},{... | collective-permute-start | bytes 49160 | tf_op jit(solution)/shard_map/ppermute | solution.py:458
  24.9 0.4 collective-permute-start.6
  25.3 0.8 %collective-permute-start.7 = (bf16[64,128]{1,0:T(8,128)(2,1)S(1)}, bf16[64,128]{1,0:T(8,128)(2,1)S(1)}, u32[]{:S(2)}, u32[]{:S(2)}) collective-permute-start(bf16[64,128]{1,0:T(8,128)(2,1)S(1)} %get-tuple-element.48), channel_id=1, source_target_pairs={{0,12},{4,8},{8,4},{12,0},{16,28},{20,24},{24,20},{28,16},{1,13},{... | collective-permute-start | bytes 49160 | tf_op jit(solution)/shard_map/ppermute | solution.py:458
  26.1 0.0 collective-permute-done.3.refs_7_
  26.1 0.9 %collective-permute-start.8 = (bf16[64,128]{1,0:T(8,128)(2,1)S(1)}, bf16[64,128]{1,0:T(8,128)(2,1)S(1)}, u32[]{:S(2)}, u32[]{:S(2)}) collective-permute-start(bf16[64,128]{1,0:T(8,128)(2,1)S(1)} %get-tuple-element.49), channel_id=1, source_target_pairs={{0,8},{4,12},{8,0},{12,4},{16,24},{20,28},{24,16},{28,20},{1,9},{5... | collective-permute-start | bytes 49160 | tf_op jit(solution)/shard_map/ppermute | solution.py:458
  27.0 0.0 collective-permute-done.4.refs_8_
  27.0 0.2 collective-permute-start.9
  27.2 1.3 %shard_map.143.refs_0_ = f32[1024,512]{1,0:T(8,128)S(1)} custom-call(bf16[1024,512]{1,0:T(8,128)(2,1)S(1)} %get-tuple-element.30.edges_ref, bf16[256,256]{1,0:T(8,128)(2,1)S(1)} %get-tuple-element.34.trip_ref, bf16[1024,256]{1,0:T(8,128)(2,1)S(1)} %get-tuple-element.35.local_ref, bf16[1024,256]{1,0:T(8,128)(2,1)S(1)} %get-tuple-element.36.mask_ref, ...), custom_call_target="tpu_custom_call" | custom-call | flops 268435456 | bytes 5242880 | tf_op jit(solution)/shard_map/pallas_call | solution.py:43
  28.5 0.0 collective-permute-done.5.refs_9_
  28.5 0.1 collective-permute-done.6.refs_10_
  28.6 0.0 collective-permute-done.7.refs_11_
  28.6 1.3 %collective-permute-done.8.refs_12_ = bf16[64,128]{1,0:T(8,128)(2,1)S(1)} collective-permute-done((bf16[64,128]{1,0:T(8,128)(2,1)S(1)}, bf16[64,128]{1,0:T(8,128)(2,1)S(1)}, u32[]{:S(2)}, u32[]{:S(2)}) %collective-permute-start.8) | collective-permute-done | bytes 16416 | tf_op jit(solution)/shard_map/ppermute | solution.py:458
  30.0 2.8 %shard_map.144 = (bf16[1024,512]{1,0:T(8,128)(2,1)S(1)}, bf16[128,256]{1,0:T(8,128)(2,1)S(1)}) custom-call(f32[1024,512]{1,0:T(8,128)S(1)} %shard_map.143.refs_0_, bf16[1024,256]{1,0:T(8,128)(2,1)S(1)} %get-tuple-element.39.refs_1_, bf16[1024,256]{1,0:T(8,128)(2,1)S(1)} %get-tuple-element.40.refs_2_, ...), custom_call_target="tpu_custom_call" | custom-call | flops 1073741824 | bytes 4194304 | tf_op jit(solution)/shard_map/pallas_call | solution.py:43
  32.8 4.8 %collective-permute-start.12 = (bf16[128,256]{1,0:T(8,128)(2,1)S(1)}, bf16[128,256]{1,0:T(8,128)(2,1)S(1)}, u32[]{:S(2)}, u32[]{:S(2)}) collective-permute-start(bf16[128,256]{1,0:T(8,128)(2,1)S(1)} %get-tuple-element.51.refs_0_), channel_id=1, source_target_pairs={{0,2},{1,3},{2,0},{3,1},{4,6},{5,7},{6,4},{7,5},{8,10},{9,11},{10,... | collective-permute-start | bytes 196616 | tf_op jit(solution)/shard_map/ppermute | solution.py:376
  37.6 0.4 collective-permute-start.11
  38.0 0.2 collective-permute-start.10
  38.2 0.8 %shard_map.145 = (f32[1024,512]{1,0:T(8,128)S(1)}, bf16[1024,256]{1,0:T(8,128)(2,1)S(1)}) custom-call(bf16[1024,512]{1,0:T(8,128)(2,1)S(1)} %get-tuple-element.55.state_ref.refs_7_, bf16[1024,512]{1,0:T(8,128)(2,1)S(1)} %get-tuple-element.54.join_ref.refs_6_, s32[2,1024]{1,0:T(2,128)S(1)} %get-tuple-element.43.refs_6_.index_ref), custom_call_target="tpu_custom_call" | custom-call | flops 536870912 | bytes 4194304 | tf_op jit(solution)/shard_map/pallas_call | solution.py:43
  39.0 3.0 %collective-permute-done.12.refs_3_ = bf16[128,256]{1,0:T(8,128)(2,1)S(1)} collective-permute-done((bf16[128,256]{1,0:T(8,128)(2,1)S(1)}, bf16[128,256]{1,0:T(8,128)(2,1)S(1)}, u32[]{:S(2)}, u32[]{:S(2)}) %collective-permute-start.12) | collective-permute-done | bytes 65568 | tf_op jit(solution)/shard_map/ppermute | solution.py:376
  42.0 1.7 %collective-permute-done.11.refs_2_ = bf16[128,256]{1,0:T(8,128)(2,1)S(1)} collective-permute-done((bf16[128,256]{1,0:T(8,128)(2,1)S(1)}, bf16[128,256]{1,0:T(8,128)(2,1)S(1)}, u32[]{:S(2)}, u32[]{:S(2)}) %collective-permute-start.11) | collective-permute-done | bytes 65568 | tf_op jit(solution)/shard_map/ppermute | solution.py:376
  43.6 2.1 %shard_map.146 = (bf16[1024,512]{1,0:T(8,128)(2,1)}, bf16[32,256]{1,0:T(8,128)(2,1)}) custom-call(bf16[128,256]{1,0:T(8,128)(2,1)S(1)} %get-tuple-element.51.refs_0_, bf16[128,256]{1,0:T(8,128)(2,1)S(1)} %collective-permute-done.10.refs_1_, bf16[128,256]{1,0:T(8,128)(2,1)S(1)} %collective-permute-done.11.refs_2_, ...), custom_call_target="tpu_custom_call" | custom-call | flops 268435456 | bytes 4194304 | tf_op jit(solution)/shard_map/pallas_call | solution.py:43
  (6 shorter events, 0.0 us)
Async XLA Ops:
  0.6 8.5 %copy-start.1 = (s32[16,2]{0,1:T(2,128)S(1)}, s32[16,2]{0,1:T(2,128)}, u32[]{:S(2)}) copy-start(s32[16,2]{0,1:T(2,128)} %param.17) | copy-start | bytes 388
  0.6 8.6 %copy-start = (s32[1024]{0:T(1024)S(1)}, s32[1024]{0:T(1024)}, u32[]{:S(2)}) copy-start(s32[1024]{0:T(1024)} %param.15) | copy-start | bytes 12292
  3.5 15.1 %collective-permute-start.2 = (bf16[576,128]{1,0:T(8,128)(2,1)S(1)}, bf16[576,128]{1,0:T(8,128)(2,1)S(1)}, u32[]{:S(2)}, u32[]{:S(2)}) collective-permute-start(bf16[576,128]{1,0:T(8,128)(2,1)S(1)} %shard_map.141.refs_2_), channel_id=1, source_target_pairs={{0,2},{1,3},{2,0},{3,1},{4,6},{5,7},{6,4},{7,5},{8,10},{9,11},{10,... | collective-permute-start | bytes 442376 | tf_op jit(solution)/shard_map/ppermute | solution.py:376
  7.6 11.0 %collective-permute-start.1 = (bf16[576,128]{1,0:T(8,128)(2,1)S(1)}, bf16[576,128]{1,0:T(8,128)(2,1)S(1)}, u32[]{:S(2)}, u32[]{:S(2)}) collective-permute-start(bf16[576,128]{1,0:T(8,128)(2,1)S(1)} %shard_map.141.refs_2_), channel_id=1, source_target_pairs={{0,3},{1,2},{2,1},{3,0},{4,7},{5,6},{6,5},{7,4},{8,11},{9,10},{10,... | collective-permute-start | bytes 442376 | tf_op jit(solution)/shard_map/ppermute | solution.py:376
  8.9 10.2 %collective-permute-start = (bf16[576,128]{1,0:T(8,128)(2,1)S(1)}, bf16[576,128]{1,0:T(8,128)(2,1)S(1)}, u32[]{:S(2)}, u32[]{:S(2)}) collective-permute-start(bf16[576,128]{1,0:T(8,128)(2,1)S(1)} %shard_map.141.refs_2_), channel_id=1, source_target_pairs={{0,1},{1,0},{2,3},{3,2},{4,5},{5,4},{6,7},{7,6},{8,9},{9,8},{10,11... | collective-permute-start | bytes 442376 | tf_op jit(solution)/shard_map/ppermute | solution.py:376
  20.9 5.3 %collective-permute-start.3 = (bf16[64,128]{1,0:T(8,128)(2,1)S(1)}, bf16[64,128]{1,0:T(8,128)(2,1)S(1)}, u32[]{:S(2)}, u32[]{:S(2)}) collective-permute-start(bf16[64,128]{1,0:T(8,128)(2,1)S(1)} %get-tuple-element.44), channel_id=1, source_target_pairs={{0,28},{4,24},{8,20},{12,16},{16,12},{20,8},{24,4},{28,0},{1,29},{... | collective-permute-start | bytes 49160 | tf_op jit(solution)/shard_map/ppermute | solution.py:458
  21.0 6.1 %collective-permute-start.4 = (bf16[64,128]{1,0:T(8,128)(2,1)S(1)}, bf16[64,128]{1,0:T(8,128)(2,1)S(1)}, u32[]{:S(2)}, u32[]{:S(2)}) collective-permute-start(bf16[64,128]{1,0:T(8,128)(2,1)S(1)} %get-tuple-element.45), channel_id=1, source_target_pairs={{0,24},{4,28},{8,16},{12,20},{16,8},{20,12},{24,0},{28,4},{1,25},{... | collective-permute-start | bytes 49160 | tf_op jit(solution)/shard_map/ppermute | solution.py:458
  23.5 5.0 %collective-permute-start.5 = (bf16[64,128]{1,0:T(8,128)(2,1)S(1)}, bf16[64,128]{1,0:T(8,128)(2,1)S(1)}, u32[]{:S(2)}, u32[]{:S(2)}) collective-permute-start(bf16[64,128]{1,0:T(8,128)(2,1)S(1)} %get-tuple-element.46), channel_id=1, source_target_pairs={{0,20},{4,16},{8,28},{12,24},{16,4},{20,0},{24,12},{28,8},{1,21},{... | collective-permute-start | bytes 49160 | tf_op jit(solution)/shard_map/ppermute | solution.py:458
  24.9 3.7 %collective-permute-start.6 = (bf16[64,128]{1,0:T(8,128)(2,1)S(1)}, bf16[64,128]{1,0:T(8,128)(2,1)S(1)}, u32[]{:S(2)}, u32[]{:S(2)}) collective-permute-start(bf16[64,128]{1,0:T(8,128)(2,1)S(1)} %get-tuple-element.47), channel_id=1, source_target_pairs={{0,16},{4,20},{8,24},{12,28},{16,0},{20,4},{24,8},{28,12},{1,17},{... | collective-permute-start | bytes 49160 | tf_op jit(solution)/shard_map/ppermute | solution.py:458
  25.3 3.3 %collective-permute-start.7 = (bf16[64,128]{1,0:T(8,128)(2,1)S(1)}, bf16[64,128]{1,0:T(8,128)(2,1)S(1)}, u32[]{:S(2)}, u32[]{:S(2)}) collective-permute-start(bf16[64,128]{1,0:T(8,128)(2,1)S(1)} %get-tuple-element.48), channel_id=1, source_target_pairs={{0,12},{4,8},{8,4},{12,0},{16,28},{20,24},{24,20},{28,16},{1,13},{... | collective-permute-start | bytes 49160 | tf_op jit(solution)/shard_map/ppermute | solution.py:458
  26.1 3.8 %collective-permute-start.8 = (bf16[64,128]{1,0:T(8,128)(2,1)S(1)}, bf16[64,128]{1,0:T(8,128)(2,1)S(1)}, u32[]{:S(2)}, u32[]{:S(2)}) collective-permute-start(bf16[64,128]{1,0:T(8,128)(2,1)S(1)} %get-tuple-element.49), channel_id=1, source_target_pairs={{0,8},{4,12},{8,0},{12,4},{16,24},{20,28},{24,16},{28,20},{1,9},{5... | collective-permute-start | bytes 49160 | tf_op jit(solution)/shard_map/ppermute | solution.py:458
  27.0 2.9 %collective-permute-start.9 = (bf16[64,128]{1,0:T(8,128)(2,1)S(1)}, bf16[64,128]{1,0:T(8,128)(2,1)S(1)}, u32[]{:S(2)}, u32[]{:S(2)}) collective-permute-start(bf16[64,128]{1,0:T(8,128)(2,1)S(1)} %get-tuple-element.50), channel_id=1, source_target_pairs={{0,4},{4,0},{8,12},{12,8},{16,20},{20,16},{24,28},{28,24},{1,5},{5... | collective-permute-start | bytes 49160 | tf_op jit(solution)/shard_map/ppermute | solution.py:458
  32.8 9.2 %collective-permute-start.12 = (bf16[128,256]{1,0:T(8,128)(2,1)S(1)}, bf16[128,256]{1,0:T(8,128)(2,1)S(1)}, u32[]{:S(2)}, u32[]{:S(2)}) collective-permute-start(bf16[128,256]{1,0:T(8,128)(2,1)S(1)} %get-tuple-element.51.refs_0_), channel_id=1, source_target_pairs={{0,2},{1,3},{2,0},{3,1},{4,6},{5,7},{6,4},{7,5},{8,10},{9,11},{10,... | collective-permute-start | bytes 196616 | tf_op jit(solution)/shard_map/ppermute | solution.py:376
  37.6 6.1 %collective-permute-start.11 = (bf16[128,256]{1,0:T(8,128)(2,1)S(1)}, bf16[128,256]{1,0:T(8,128)(2,1)S(1)}, u32[]{:S(2)}, u32[]{:S(2)}) collective-permute-start(bf16[128,256]{1,0:T(8,128)(2,1)S(1)} %get-tuple-element.51.refs_0_), channel_id=1, source_target_pairs={{0,3},{1,2},{2,1},{3,0},{4,7},{5,6},{6,5},{7,4},{8,11},{9,10},{10,... | collective-permute-start | bytes 196616 | tf_op jit(solution)/shard_map/ppermute | solution.py:376
  38.0 5.6 %collective-permute-start.10 = (bf16[128,256]{1,0:T(8,128)(2,1)S(1)}, bf16[128,256]{1,0:T(8,128)(2,1)S(1)}, u32[]{:S(2)}, u32[]{:S(2)}) collective-permute-start(bf16[128,256]{1,0:T(8,128)(2,1)S(1)} %get-tuple-element.51.refs_0_), channel_id=1, source_target_pairs={{0,1},{1,0},{2,3},{3,2},{4,5},{5,4},{6,7},{7,6},{8,9},{9,8},{10,11... | collective-permute-start | bytes 196616 | tf_op jit(solution)/shard_map/ppermute | solution.py:376

commit v7 on v6

--- a/solution.py
+++ b/solution.py
@@ -368,7 +368,7 @@
 
 
 def distances(shards):
-    return [0, 1, 3, 2] if shards == 4 else list(range(shards))
+    return list(range(shards))
 
 
 def from_others(value, shards):

time: 45.9 us -> 45.6 us (level)
  starting transfers between devices: 17.4 us -> 16.5 us
  waiting for transfers between devices: 12.1 us -> 12.7 us
    ppermute x6, starting transfers between devices: 11.1 us -> 10.2 us  [from_others(): lax.ppermute(value, 'edge', [(at, at ^ by) for at in range(shards)])]
    ppermute x6, waiting for transfers between devices: 10.6 us -> 11.3 us  [from_others(): lax.ppermute(value, 'edge', [(at, at ^ by) for at in range(shards)])]
  transfers between devices with their start and end apart: 13 -> 13, of which waited for: 6 -> 5; matrix products, arithmetic and copies ran while one was open for 0% -> 0% of each run, Pallas kernels for 13% -> 13%
where the time goes in v7:
time: 45.6 us; the launch traced here: 45.5 us
  starting transfers between devices  16.5 us (36%)
  Pallas kernels  15.4 us (34%)
  waiting for transfers between devices  12.7 us (28%)
  between operations  0.71 us (2%)
    pallas_call x7, Pallas kernels, call(): pl.pallas_call(kernel, out_shape=outs, in_specs=[pl.BlockSpec(memory_spac...  15.4 us
    ppermute x6, waiting for transfers between devices, from_others(): lax.ppermute(value, 'edge', [(at, at ^ by) for at in range(shards)])  11.3 us
    ppermute x6, starting transfers between devices, from_others(): lax.ppermute(value, 'edge', [(at, at ^ by) for at in range(shards)])  10.2 us
    ppermute x7, starting transfers between devices, body(): lax.ppermute(block, 'dom', [(at, at ^ partners - place) for at in range(d...  6.32 us
    ppermute x7, waiting for transfers between devices, body(): lax.ppermute(block, 'dom', [(at, at ^ partners - place) for at in range(d...  1.39 us
  transfers between devices with their start and end apart: 13, of which 5 were waited for; matrix products, arithmetic and copies ran while one was open for 0% of the time, Pallas kernels for 13%

profile of v7, /device:TPU:0, one launch (start us, length us, event | category | flops | bytes accessed | tf_op | source)
XLA Modules:
  0.0 45.5 jit_solution(14019255230654370638)
XLA Ops:
  0.7 2.8 %shard_map.141.refs_2_ = bf16[576,128]{1,0:T(8,128)(2,1)S(1)} custom-call(bf16[1024,512]{1,0:T(8,128)(2,1)} %edges_hbm.1, bf16[512,512]{1,0:T(8,128)(2,1)} %weight_hbm.1, bf16[64,512]{1,0:T(8,128)(2,1)} %down_hbm.1, bf16[32,256]{1,0:T(8,128)(2,1)} %atoms_hbm.1), custom_call_target="tpu_custom_call" | custom-call | flops 603979776 | bytes 1572864 | tf_op jit(solution)/shard_map/pallas_call | solution.py:43
  3.5 5.1 %collective-permute-start.2 = (bf16[576,128]{1,0:T(8,128)(2,1)S(1)}, bf16[576,128]{1,0:T(8,128)(2,1)S(1)}, u32[]{:S(2)}, u32[]{:S(2)}) collective-permute-start(bf16[576,128]{1,0:T(8,128)(2,1)S(1)} %shard_map.141.refs_2_), channel_id=1, source_target_pairs={{0,3},{1,2},{2,1},{3,0},{4,7},{5,6},{6,5},{7,4},{8,11},{9,10},{10,... | collective-permute-start | bytes 442376 | tf_op jit(solution)/shard_map/ppermute | solution.py:376
  8.6 0.0 collective-permute-start.1
  8.6 0.6 %collective-permute-start = (bf16[576,128]{1,0:T(8,128)(2,1)S(1)}, bf16[576,128]{1,0:T(8,128)(2,1)S(1)}, u32[]{:S(2)}, u32[]{:S(2)}) collective-permute-start(bf16[576,128]{1,0:T(8,128)(2,1)S(1)} %shard_map.141.refs_2_), channel_id=1, source_target_pairs={{0,1},{1,0},{2,3},{3,2},{4,5},{5,4},{6,7},{7,6},{8,9},{9,8},{10,11... | collective-permute-start | bytes 442376 | tf_op jit(solution)/shard_map/ppermute | solution.py:376
  9.2 0.1 copy.15.refs_0_
  9.3 3.9 %shard_map.140 = (bf16[896,256]{1,0:T(8,128)(2,1)S(1)}, bf16[896,256]{1,0:T(8,128)(2,1)S(1)}, bf16[1024,256]{1,0:T(8,128)(2,1)S(1)}, bf16[1024,256]{1,0:T(8,128)...) custom-call(s32[1,1024]{1,0:T(1,128)S(1)} %bitcast.1, ...), custom_call_target="tpu_custom_call" | custom-call | flops 41943040 | bytes 6291456 | tf_op jit(solution)/shard_map/pallas_call | solution.py:43
  13.2 0.2 collective-permute-done.2.refs_5_
  13.4 7.7 %collective-permute-done.1.refs_4_ = bf16[576,128]{1,0:T(8,128)(2,1)S(1)} collective-permute-done((bf16[576,128]{1,0:T(8,128)(2,1)S(1)}, bf16[576,128]{1,0:T(8,128)(2,1)S(1)}, u32[]{:S(2)}, u32[]{:S(2)}) %collective-permute-start.1) | collective-permute-done | bytes 147488 | tf_op jit(solution)/shard_map/ppermute | solution.py:376
  21.1 0.0 collective-permute-done.refs_3_
  21.1 1.8 %shard_map.142 = (bf16[256,256]{1,0:T(8,128)(2,1)S(1)}, bf16[128,256]{1,0:T(8,128)(2,1)S(1)}, bf16[64,128]{1,0:T(8,128)(2,1)S(1)}, bf16[64,128]{1,0:T(8,128)(2,1...) custom-call(s32[16,2]{1,0:T(8,128)S(1)} %copy.15.refs_0_, ...), custom_call_target="tpu_custom_call" | custom-call | flops 134217728 | bytes 2097152 | tf_op jit(solution)/shard_map/pallas_call | solution.py:43
  22.8 1.3 %collective-permute-start.3 = (bf16[64,128]{1,0:T(8,128)(2,1)S(1)}, bf16[64,128]{1,0:T(8,128)(2,1)S(1)}, u32[]{:S(2)}, u32[]{:S(2)}) collective-permute-start(bf16[64,128]{1,0:T(8,128)(2,1)S(1)} %get-tuple-element.44), channel_id=1, source_target_pairs={{0,28},{4,24},{8,20},{12,16},{16,12},{20,8},{24,4},{28,0},{1,29},{... | collective-permute-start | bytes 49160 | tf_op jit(solution)/shard_map/ppermute | solution.py:458
  24.1 1.3 %collective-permute-start.4 = (bf16[64,128]{1,0:T(8,128)(2,1)S(1)}, bf16[64,128]{1,0:T(8,128)(2,1)S(1)}, u32[]{:S(2)}, u32[]{:S(2)}) collective-permute-start(bf16[64,128]{1,0:T(8,128)(2,1)S(1)} %get-tuple-element.45), channel_id=1, source_target_pairs={{0,24},{4,28},{8,16},{12,20},{16,8},{20,12},{24,0},{28,4},{1,25},{... | collective-permute-start | bytes 49160 | tf_op jit(solution)/shard_map/ppermute | solution.py:458
  25.4 1.3 %collective-permute-start.5 = (bf16[64,128]{1,0:T(8,128)(2,1)S(1)}, bf16[64,128]{1,0:T(8,128)(2,1)S(1)}, u32[]{:S(2)}, u32[]{:S(2)}) collective-permute-start(bf16[64,128]{1,0:T(8,128)(2,1)S(1)} %get-tuple-element.46), channel_id=1, source_target_pairs={{0,20},{4,16},{8,28},{12,24},{16,4},{20,0},{24,12},{28,8},{1,21},{... | collective-permute-start | bytes 49160 | tf_op jit(solution)/shard_map/ppermute | solution.py:458
  26.8 0.5 %collective-permute-start.6 = (bf16[64,128]{1,0:T(8,128)(2,1)S(1)}, bf16[64,128]{1,0:T(8,128)(2,1)S(1)}, u32[]{:S(2)}, u32[]{:S(2)}) collective-permute-start(bf16[64,128]{1,0:T(8,128)(2,1)S(1)} %get-tuple-element.47), channel_id=1, source_target_pairs={{0,16},{4,20},{8,24},{12,28},{16,0},{20,4},{24,8},{28,12},{1,17},{... | collective-permute-start | bytes 49160 | tf_op jit(solution)/shard_map/ppermute | solution.py:458
  27.3 0.7 %collective-permute-start.7 = (bf16[64,128]{1,0:T(8,128)(2,1)S(1)}, bf16[64,128]{1,0:T(8,128)(2,1)S(1)}, u32[]{:S(2)}, u32[]{:S(2)}) collective-permute-start(bf16[64,128]{1,0:T(8,128)(2,1)S(1)} %get-tuple-element.48), channel_id=1, source_target_pairs={{0,12},{4,8},{8,4},{12,0},{16,28},{20,24},{24,20},{28,16},{1,13},{... | collective-permute-start | bytes 49160 | tf_op jit(solution)/shard_map/ppermute | solution.py:458
  28.0 0.0 collective-permute-done.3.refs_7_
  28.0 0.9 %collective-permute-start.8 = (bf16[64,128]{1,0:T(8,128)(2,1)S(1)}, bf16[64,128]{1,0:T(8,128)(2,1)S(1)}, u32[]{:S(2)}, u32[]{:S(2)}) collective-permute-start(bf16[64,128]{1,0:T(8,128)(2,1)S(1)} %get-tuple-element.49), channel_id=1, source_target_pairs={{0,8},{4,12},{8,0},{12,4},{16,24},{20,28},{24,16},{28,20},{1,9},{5... | collective-permute-start | bytes 49160 | tf_op jit(solution)/shard_map/ppermute | solution.py:458
  28.9 0.0 collective-permute-done.4.refs_8_
  28.9 0.2 collective-permute-start.9
  29.2 1.3 %shard_map.143.refs_0_ = f32[1024,512]{1,0:T(8,128)S(1)} custom-call(bf16[1024,512]{1,0:T(8,128)(2,1)S(1)} %get-tuple-element.30.edges_ref, bf16[256,256]{1,0:T(8,128)(2,1)S(1)} %get-tuple-element.34.trip_ref, bf16[1024,256]{1,0:T(8,128)(2,1)S(1)} %get-tuple-element.35.local_ref, bf16[1024,256]{1,0:T(8,128)(2,1)S(1)} %get-tuple-element.36.mask_ref, ...), custom_call_target="tpu_custom_call" | custom-call | flops 268435456 | bytes 5242880 | tf_op jit(solution)/shard_map/pallas_call | solution.py:43
  30.5 0.0 collective-permute-done.5.refs_9_
  30.5 0.0 collective-permute-done.6.refs_10_
  30.5 1.3 %collective-permute-done.8.refs_12_ = bf16[64,128]{1,0:T(8,128)(2,1)S(1)} collective-permute-done((bf16[64,128]{1,0:T(8,128)(2,1)S(1)}, bf16[64,128]{1,0:T(8,128)(2,1)S(1)}, u32[]{:S(2)}, u32[]{:S(2)}) %collective-permute-start.8) | collective-permute-done | bytes 16416 | tf_op jit(solution)/shard_map/ppermute | solution.py:458
  31.9 0.0 collective-permute-done.9.refs_13_
  31.9 2.8 %shard_map.144 = (bf16[1024,512]{1,0:T(8,128)(2,1)S(1)}, bf16[128,256]{1,0:T(8,128)(2,1)S(1)}) custom-call(f32[1024,512]{1,0:T(8,128)S(1)} %shard_map.143.refs_0_, bf16[1024,256]{1,0:T(8,128)(2,1)S(1)} %get-tuple-element.39.refs_1_, bf16[1024,256]{1,0:T(8,128)(2,1)S(1)} %get-tuple-element.40.refs_2_, ...), custom_call_target="tpu_custom_call" | custom-call | flops 1073741824 | bytes 4194304 | tf_op jit(solution)/shard_map/pallas_call | solution.py:43
  34.7 2.6 %collective-permute-start.12 = (bf16[128,256]{1,0:T(8,128)(2,1)S(1)}, bf16[128,256]{1,0:T(8,128)(2,1)S(1)}, u32[]{:S(2)}, u32[]{:S(2)}) collective-permute-start(bf16[128,256]{1,0:T(8,128)(2,1)S(1)} %get-tuple-element.51.refs_0_), channel_id=1, source_target_pairs={{0,3},{1,2},{2,1},{3,0},{4,7},{5,6},{6,5},{7,4},{8,11},{9,10},{10,... | collective-permute-start | bytes 196616 | tf_op jit(solution)/shard_map/ppermute | solution.py:376
  37.3 0.0 collective-permute-start.11
  37.3 1.9 %collective-permute-start.10 = (bf16[128,256]{1,0:T(8,128)(2,1)S(1)}, bf16[128,256]{1,0:T(8,128)(2,1)S(1)}, u32[]{:S(2)}, u32[]{:S(2)}) collective-permute-start(bf16[128,256]{1,0:T(8,128)(2,1)S(1)} %get-tuple-element.51.refs_0_), channel_id=1, source_target_pairs={{0,1},{1,0},{2,3},{3,2},{4,5},{5,4},{6,7},{7,6},{8,9},{9,8},{10,11... | collective-permute-start | bytes 196616 | tf_op jit(solution)/shard_map/ppermute | solution.py:376
  39.1 0.8 %shard_map.145 = (f32[1024,512]{1,0:T(8,128)S(1)}, bf16[1024,256]{1,0:T(8,128)(2,1)S(1)}) custom-call(bf16[1024,512]{1,0:T(8,128)(2,1)S(1)} %get-tuple-element.55.state_ref.refs_7_, bf16[1024,512]{1,0:T(8,128)(2,1)S(1)} %get-tuple-element.54.join_ref.refs_6_, s32[2,1024]{1,0:T(2,128)S(1)} %get-tuple-element.43.refs_6_.index_ref), custom_call_target="tpu_custom_call" | custom-call | flops 536870912 | bytes 4194304 | tf_op jit(solution)/shard_map/pallas_call | solution.py:43
  39.9 1.4 %collective-permute-done.12.refs_3_ = bf16[128,256]{1,0:T(8,128)(2,1)S(1)} collective-permute-done((bf16[128,256]{1,0:T(8,128)(2,1)S(1)}, bf16[128,256]{1,0:T(8,128)(2,1)S(1)}, u32[]{:S(2)}, u32[]{:S(2)}) %collective-permute-start.12) | collective-permute-done | bytes 65568 | tf_op jit(solution)/shard_map/ppermute | solution.py:376
  41.4 2.0 %collective-permute-done.11.refs_2_ = bf16[128,256]{1,0:T(8,128)(2,1)S(1)} collective-permute-done((bf16[128,256]{1,0:T(8,128)(2,1)S(1)}, bf16[128,256]{1,0:T(8,128)(2,1)S(1)}, u32[]{:S(2)}, u32[]{:S(2)}) %collective-permute-start.11) | collective-permute-done | bytes 65568 | tf_op jit(solution)/shard_map/ppermute | solution.py:376
  43.4 2.1 %shard_map.146 = (bf16[1024,512]{1,0:T(8,128)(2,1)}, bf16[32,256]{1,0:T(8,128)(2,1)}) custom-call(bf16[128,256]{1,0:T(8,128)(2,1)S(1)} %get-tuple-element.51.refs_0_, bf16[128,256]{1,0:T(8,128)(2,1)S(1)} %collective-permute-done.10.refs_1_, bf16[128,256]{1,0:T(8,128)(2,1)S(1)} %collective-permute-done.11.refs_2_, ...), custom_call_target="tpu_custom_call" | custom-call | flops 268435456 | bytes 4194304 | tf_op jit(solution)/shard_map/pallas_call | solution.py:43
  (6 shorter events, 0.0 us)
Async XLA Ops:
  0.6 8.6 %copy-start.1 = (s32[16,2]{0,1:T(2,128)S(1)}, s32[16,2]{0,1:T(2,128)}, u32[]{:S(2)}) copy-start(s32[16,2]{0,1:T(2,128)} %param.17) | copy-start | bytes 388
  0.6 8.7 %copy-start = (s32[1024]{0:T(1024)S(1)}, s32[1024]{0:T(1024)}, u32[]{:S(2)}) copy-start(s32[1024]{0:T(1024)} %param.15) | copy-start | bytes 12292
  3.5 9.9 %collective-permute-start.2 = (bf16[576,128]{1,0:T(8,128)(2,1)S(1)}, bf16[576,128]{1,0:T(8,128)(2,1)S(1)}, u32[]{:S(2)}, u32[]{:S(2)}) collective-permute-start(bf16[576,128]{1,0:T(8,128)(2,1)S(1)} %shard_map.141.refs_2_), channel_id=1, source_target_pairs={{0,3},{1,2},{2,1},{3,0},{4,7},{5,6},{6,5},{7,4},{8,11},{9,10},{10,... | collective-permute-start | bytes 442376 | tf_op jit(solution)/shard_map/ppermute | solution.py:376
  8.6 12.5 %collective-permute-start.1 = (bf16[576,128]{1,0:T(8,128)(2,1)S(1)}, bf16[576,128]{1,0:T(8,128)(2,1)S(1)}, u32[]{:S(2)}, u32[]{:S(2)}) collective-permute-start(bf16[576,128]{1,0:T(8,128)(2,1)S(1)} %shard_map.141.refs_2_), channel_id=1, source_target_pairs={{0,2},{1,3},{2,0},{3,1},{4,6},{5,7},{6,4},{7,5},{8,10},{9,11},{10,... | collective-permute-start | bytes 442376 | tf_op jit(solution)/shard_map/ppermute | solution.py:376
  8.6 12.5 %collective-permute-start = (bf16[576,128]{1,0:T(8,128)(2,1)S(1)}, bf16[576,128]{1,0:T(8,128)(2,1)S(1)}, u32[]{:S(2)}, u32[]{:S(2)}) collective-permute-start(bf16[576,128]{1,0:T(8,128)(2,1)S(1)} %shard_map.141.refs_2_), channel_id=1, source_target_pairs={{0,1},{1,0},{2,3},{3,2},{4,5},{5,4},{6,7},{7,6},{8,9},{9,8},{10,11... | collective-permute-start | bytes 442376 | tf_op jit(solution)/shard_map/ppermute | solution.py:376
  22.8 5.2 %collective-permute-start.3 = (bf16[64,128]{1,0:T(8,128)(2,1)S(1)}, bf16[64,128]{1,0:T(8,128)(2,1)S(1)}, u32[]{:S(2)}, u32[]{:S(2)}) collective-permute-start(bf16[64,128]{1,0:T(8,128)(2,1)S(1)} %get-tuple-element.44), channel_id=1, source_target_pairs={{0,28},{4,24},{8,20},{12,16},{16,12},{20,8},{24,4},{28,0},{1,29},{... | collective-permute-start | bytes 49160 | tf_op jit(solution)/shard_map/ppermute | solution.py:458
  24.1 4.8 %collective-permute-start.4 = (bf16[64,128]{1,0:T(8,128)(2,1)S(1)}, bf16[64,128]{1,0:T(8,128)(2,1)S(1)}, u32[]{:S(2)}, u32[]{:S(2)}) collective-permute-start(bf16[64,128]{1,0:T(8,128)(2,1)S(1)} %get-tuple-element.45), channel_id=1, source_target_pairs={{0,24},{4,28},{8,16},{12,20},{16,8},{20,12},{24,0},{28,4},{1,25},{... | collective-permute-start | bytes 49160 | tf_op jit(solution)/shard_map/ppermute | solution.py:458
  25.4 5.0 %collective-permute-start.5 = (bf16[64,128]{1,0:T(8,128)(2,1)S(1)}, bf16[64,128]{1,0:T(8,128)(2,1)S(1)}, u32[]{:S(2)}, u32[]{:S(2)}) collective-permute-start(bf16[64,128]{1,0:T(8,128)(2,1)S(1)} %get-tuple-element.46), channel_id=1, source_target_pairs={{0,20},{4,16},{8,28},{12,24},{16,4},{20,0},{24,12},{28,8},{1,21},{... | collective-permute-start | bytes 49160 | tf_op jit(solution)/shard_map/ppermute | solution.py:458
  26.8 3.7 %collective-permute-start.6 = (bf16[64,128]{1,0:T(8,128)(2,1)S(1)}, bf16[64,128]{1,0:T(8,128)(2,1)S(1)}, u32[]{:S(2)}, u32[]{:S(2)}) collective-permute-start(bf16[64,128]{1,0:T(8,128)(2,1)S(1)} %get-tuple-element.47), channel_id=1, source_target_pairs={{0,16},{4,20},{8,24},{12,28},{16,0},{20,4},{24,8},{28,12},{1,17},{... | collective-permute-start | bytes 49160 | tf_op jit(solution)/shard_map/ppermute | solution.py:458
  27.3 3.2 %collective-permute-start.7 = (bf16[64,128]{1,0:T(8,128)(2,1)S(1)}, bf16[64,128]{1,0:T(8,128)(2,1)S(1)}, u32[]{:S(2)}, u32[]{:S(2)}) collective-permute-start(bf16[64,128]{1,0:T(8,128)(2,1)S(1)} %get-tuple-element.48), channel_id=1, source_target_pairs={{0,12},{4,8},{8,4},{12,0},{16,28},{20,24},{24,20},{28,16},{1,13},{... | collective-permute-start | bytes 49160 | tf_op jit(solution)/shard_map/ppermute | solution.py:458
  28.0 3.8 %collective-permute-start.8 = (bf16[64,128]{1,0:T(8,128)(2,1)S(1)}, bf16[64,128]{1,0:T(8,128)(2,1)S(1)}, u32[]{:S(2)}, u32[]{:S(2)}) collective-permute-start(bf16[64,128]{1,0:T(8,128)(2,1)S(1)} %get-tuple-element.49), channel_id=1, source_target_pairs={{0,8},{4,12},{8,0},{12,4},{16,24},{20,28},{24,16},{28,20},{1,9},{5... | collective-permute-start | bytes 49160 | tf_op jit(solution)/shard_map/ppermute | solution.py:458
  28.9 2.9 %collective-permute-start.9 = (bf16[64,128]{1,0:T(8,128)(2,1)S(1)}, bf16[64,128]{1,0:T(8,128)(2,1)S(1)}, u32[]{:S(2)}, u32[]{:S(2)}) collective-permute-start(bf16[64,128]{1,0:T(8,128)(2,1)S(1)} %get-tuple-element.50), channel_id=1, source_target_pairs={{0,4},{4,0},{8,12},{12,8},{16,20},{20,16},{24,28},{28,24},{1,5},{5... | collective-permute-start | bytes 49160 | tf_op jit(solution)/shard_map/ppermute | solution.py:458
  34.7 6.7 %collective-permute-start.12 = (bf16[128,256]{1,0:T(8,128)(2,1)S(1)}, bf16[128,256]{1,0:T(8,128)(2,1)S(1)}, u32[]{:S(2)}, u32[]{:S(2)}) collective-permute-start(bf16[128,256]{1,0:T(8,128)(2,1)S(1)} %get-tuple-element.51.refs_0_), channel_id=1, source_target_pairs={{0,3},{1,2},{2,1},{3,0},{4,7},{5,6},{6,5},{7,4},{8,11},{9,10},{10,... | collective-permute-start | bytes 196616 | tf_op jit(solution)/shard_map/ppermute | solution.py:376
  37.3 6.1 %collective-permute-start.11 = (bf16[128,256]{1,0:T(8,128)(2,1)S(1)}, bf16[128,256]{1,0:T(8,128)(2,1)S(1)}, u32[]{:S(2)}, u32[]{:S(2)}) collective-permute-start(bf16[128,256]{1,0:T(8,128)(2,1)S(1)} %get-tuple-element.51.refs_0_), channel_id=1, source_target_pairs={{0,2},{1,3},{2,0},{3,1},{4,6},{5,7},{6,4},{7,5},{8,10},{9,11},{10,... | collective-permute-start | bytes 196616 | tf_op jit(solution)/shard_map/ppermute | solution.py:376
  37.3 6.1 %collective-permute-start.10 = (bf16[128,256]{1,0:T(8,128)(2,1)S(1)}, bf16[128,256]{1,0:T(8,128)(2,1)S(1)}, u32[]{:S(2)}, u32[]{:S(2)}) collective-permute-start(bf16[128,256]{1,0:T(8,128)(2,1)S(1)} %get-tuple-element.51.refs_0_), channel_id=1, source_target_pairs={{0,1},{1,0},{2,3},{3,2},{4,5},{5,4},{6,7},{7,6},{8,9},{9,8},{10,11... | collective-permute-start | bytes 196616 | tf_op jit(solution)/shard_map/ppermute | solution.py:376

commit v8 on v7

--- a/solution.py
+++ b/solution.py
@@ -61,7 +61,7 @@
 
 
 def narrow_kernel(
-    edges_hbm, weight_hbm, down_hbm, atoms_hbm, out_ref, edges_ref, weight_ref, down_ref, sems
+    edges_hbm, weight_hbm, down_hbm, out_ref, edges_ref, weight_ref, down_ref, sems
 ):
     half = edges_hbm.shape[0] // 2
     pieces = [
@@ -77,18 +77,6 @@
         for at, piece in enumerate(pieces)
     ]
     for copy in [copies[0], copies[2], copies[3], copies[1]] + copies[4:]:
-        copy.start()
-    count, wide = atoms_hbm.shape
-    lanes = out_ref.shape[1]
-    atom_copies = [
-        pltpu.make_async_copy(
-            atoms_hbm.at[:, at * lanes : (at + 1) * lanes],
-            out_ref.at[half + at * count : half + (at + 1) * count, :],
-            sems.at[len(copies) + at],
-        )
-        for at in range(wide // lanes)
-    ]
-    for copy in atom_copies:
         copy.start()
     copies[0].wait()
     copies[1].wait()
@@ -106,8 +94,6 @@
             for each in hidden
         ]
         out_ref[rows, :] = silu(jnp.concatenate(sides, axis=1)).astype(jnp.bfloat16)
-    for copy in atom_copies:
-        copy.wait()
 
 
 def one_hot(shape, axis, chosen):
@@ -200,23 +186,15 @@
 def mix_kernel(shards, *refs):
     source_ref, tiles_ref = refs[:2]
     parts = refs[2 : 2 + shards]
-    send_ref, mask_ref, trip_ref, atoms_ref = refs[2 + shards : 6 + shards]
-    out_refs = refs[6 + shards : -1]
+    send_ref, mask_ref, trip_ref = refs[2 + shards : 5 + shards]
+    out_refs = refs[5 + shards : -1]
     held_ref = refs[-1]
     blocks, block_len, width = tiles_ref.shape
     count = width // block_len
     lines = held_ref.shape[0] // shards
-    own_atoms = atoms_ref.shape[0] // shards
-    atom_wide = atoms_ref.shape[1]
-    lanes = held_ref.shape[1]
     me = lax.axis_index("edge")
-    for part, at in zip(parts, distances(shards)):
-        held_ref[at * lines : (at + 1) * lines, :] = part[:lines, :]
-        for piece in range(atom_wide // lanes):
-            start = lines + piece * own_atoms
-            atoms_ref[
-                at * own_atoms : (at + 1) * own_atoms, piece * lanes : (piece + 1) * lanes
-            ] = part[start : start + own_atoms, :]
+    for part, at in zip(parts, orders(shards)[0]):
+        held_ref[at * lines : (at + 1) * lines, :] = part[...]
     half_blocks = blocks // 2
     channels = trip_ref.shape[1] // GROUPS
     per = blocks // GROUPS
@@ -253,7 +231,13 @@
         out_ref[...] = packed[at * each : (at + 1) * each, :]
 
 
-def base_kernel(edges_ref, trip_ref, local_ref, mask_ref, up_ref, stack_ref, out_ref):
+def base_kernel(shards, *refs):
+    edges_ref, trip_ref, local_ref, mask_ref, up_ref, stack_ref = refs[:6]
+    atoms = refs[6 : 6 + shards]
+    out_ref, atoms_ref = refs[6 + shards :]
+    count = atoms[0].shape[0]
+    for part, at in zip(atoms, orders(shards)[0]):
+        atoms_ref[at * count : (at + 1) * count, :] = part[...]
     each = trip_ref.shape[0]
     channels = up_ref.shape[1]
     for group in range(GROUPS):
@@ -335,7 +319,7 @@
     part_atoms = atoms_ref.shape[0]
     count = part_atoms // shards
     total = sums[0][...].astype(jnp.float32)
-    for by, part in list(zip(distances(shards), sums))[1:]:
+    for by, part in list(zip(orders(shards)[1], sums))[1:]:
         pieces = [part[(at ^ by) * count : ((at ^ by) + 1) * count, :] for at in range(shards)]
         total = total + jnp.concatenate(pieces, axis=0).astype(jnp.float32)
     scaled = (total * scale).astype(jnp.bfloat16)
@@ -367,14 +351,16 @@
         copy.wait()
 
 
-def distances(shards):
-    return list(range(shards))
-
-
-def from_others(value, shards):
+def orders(shards):
+    if shards == 4:
+        return [0, 1, 2, 3], [0, 1, 3, 2]
+    return list(range(shards)), list(range(shards))
+
+
+def from_others(value, order):
     return [value] + [
-        lax.ppermute(value, "edge", [(at, at ^ by) for at in range(shards)])
-        for by in distances(shards)[1:]
+        lax.ppermute(value, "edge", [(at, at ^ by) for at in range(len(order))])
+        for by in order[1:]
     ]
 
 
@@ -407,19 +393,20 @@
 
     narrow = call(
         narrow_kernel,
-        shaped((lines + count * atom_wide // packed, packed)),
-        (edges, weight_edge, weight_down, atoms),
-        hbm=(0, 1, 2, 3),
+        shaped((lines, packed)),
+        (edges, weight_edge, weight_down),
+        hbm=(0, 1, 2),
         scratch=[
             pltpu.VMEM(edges.shape, jnp.bfloat16),
             pltpu.VMEM(weight_edge.shape, jnp.bfloat16),
             pltpu.VMEM(weight_down.shape, jnp.bfloat16),
-            pltpu.SemaphoreType.DMA((2 + 2 * len(row_chunks(lines)) + atom_wide // packed,)),
+            pltpu.SemaphoreType.DMA((2 + 2 * len(row_chunks(lines)),)),
         ],
         flops=2 * rows * wide * (wide + channels),
         nbytes=2 * (rows * wide + wide * wide),
     )
-    narrow_parts = from_others(narrow, shards)
+    atom_parts = from_others(atoms, orders(shards)[0])
+    narrow_parts = from_others(narrow, orders(shards)[0])
     later = (
         weight_up, edges, tiles, weight_residual, weight_message, weight_join, weight_atom, atom_index
     )
@@ -444,10 +431,9 @@
         nbytes=6 * rows * rows,
     )
     weight_up, edges, tiles, weight_residual, weight_message, weight_join, weight_atom, atom_index = later
-    trip_out, all_atoms, *outgoing = call(
+    trip_out, *outgoing = call(
         functools.partial(mix_kernel, shards),
-        (shaped((each, grouped)), shaped((part_atoms, atom_wide)))
-        + (shaped((capacity // 2, packed)),) * partners,
+        (shaped((each, grouped)),) + (shaped((capacity // 2, packed)),) * partners,
         (tile_source, tiles, *narrow_parts, send, send_mask),
         smem=(0,),
         scratch=[pltpu.VMEM((shards * lines, packed), jnp.bfloat16)],
@@ -458,10 +444,10 @@
         lax.ppermute(block, "dom", [(at, at ^ (partners - place)) for at in range(domains)])
         for place, block in enumerate(outgoing)
     ]
-    base = call(
-        base_kernel,
-        shaped((rows, wide), jnp.float32),
-        (edges, trip_out, local, local_mask, weight_up, up_stack),
+    base, all_atoms = call(
+        functools.partial(base_kernel, shards),
+        (shaped((rows, wide), jnp.float32), shaped((part_atoms, atom_wide))),
+        (edges, trip_out, local, local_mask, weight_up, up_stack, *atom_parts),
         flops=2 * rows * channels * (rows + 2 * wide),
         nbytes=2 * rows * rows + 6 * rows * wide,
     )
@@ -473,7 +459,7 @@
         flops=4 * rows * wide * wide,
         nbytes=8 * rows * wide,
     )
-    sums_parts = from_others(sums, shards)
+    sums_parts = from_others(sums, orders(shards)[1])
     side, chosen = call(
         functools.partial(side_kernel, shards, part_atoms),
         (shaped((rows, wide), jnp.float32), shaped((rows, 2 * part_atoms))),

time: 45.6 us -> 45.2 us (level)
  waiting for transfers between devices: 12.7 us -> 8.7 us
  starting transfers between devices: 16.5 us -> 20.1 us
    ppermute x6 -> x9, waiting for transfers between devices: 11.3 us -> 7.31 us  [from_others(): lax.ppermute(value, 'edge', [(at, at ^ by) for at in range(len(order))])]
    ppermute x6 -> x9, starting transfers between devices: 10.2 us -> 13.8 us  [from_others(): lax.ppermute(value, 'edge', [(at, at ^ by) for at in range(len(order))])]
  transfers between devices with their start and end apart: 13 -> 16, of which waited for: 5 -> 5; matrix products, arithmetic and copies ran while one was open for 0% -> 0% of each run, Pallas kernels for 13% -> 17%
where the time goes in v8:
time: 45.2 us; the launch traced here: 45 us
  starting transfers between devices  20.1 us (44%)
  Pallas kernels  15.4 us (34%)
  waiting for transfers between devices  8.7 us (19%)
  between operations  0.74 us (2%)
    pallas_call x7, Pallas kernels, call(): pl.pallas_call(kernel, out_shape=outs, in_specs=[pl.BlockSpec(memory_spac...  15.4 us
    ppermute x9, starting transfers between devices, from_others(): lax.ppermute(value, 'edge', [(at, at ^ by) for at in range(len(order))])  13.8 us
    ppermute x9, waiting for transfers between devices, from_others(): lax.ppermute(value, 'edge', [(at, at ^ by) for at in range(len(order))])  7.31 us
    ppermute x7, starting transfers between devices, body(): lax.ppermute(block, 'dom', [(at, at ^ partners - place) for at in range(d...  6.32 us
    ppermute x7, waiting for transfers between devices, body(): lax.ppermute(block, 'dom', [(at, at ^ partners - place) for at in range(d...  1.39 us
  transfers between devices with their start and end apart: 16, of which 5 were waited for; matrix products, arithmetic and copies ran while one was open for 0% of the time, Pallas kernels for 17%

profile of v8, /device:TPU:0, one launch (start us, length us, event | category | flops | bytes accessed | tf_op | source)
XLA Modules:
  0.0 45.0 jit_solution(161795260007110010)
XLA Ops:
  0.7 2.8 %shard_map.141.refs_2_ = bf16[512,128]{1,0:T(8,128)(2,1)S(1)} custom-call(bf16[1024,512]{1,0:T(8,128)(2,1)} %edges_hbm.1, bf16[512,512]{1,0:T(8,128)(2,1)} %weight_hbm.1, bf16[64,512]{1,0:T(8,128)(2,1)} %down_hbm.1), custom_call_target="tpu_custom_call" | custom-call | flops 603979776 | bytes 1572864 | tf_op jit(solution)/shard_map/pallas_call | solution.py:43
  3.5 5.1 %collective-permute-start.2 = (bf16[512,128]{1,0:T(8,128)(2,1)S(1)}, bf16[512,128]{1,0:T(8,128)(2,1)S(1)}, u32[]{:S(2)}, u32[]{:S(2)}) collective-permute-start(bf16[512,128]{1,0:T(8,128)(2,1)S(1)} %shard_map.141.refs_2_), channel_id=1, source_target_pairs={{0,3},{1,2},{2,1},{3,0},{4,7},{5,6},{6,5},{7,4},{8,11},{9,10},{10,... | collective-permute-start | bytes 393224 | tf_op jit(solution)/shard_map/ppermute | solution.py:362
  8.6 0.0 collective-permute-start.1
  8.6 0.6 %collective-permute-start = (bf16[512,128]{1,0:T(8,128)(2,1)S(1)}, bf16[512,128]{1,0:T(8,128)(2,1)S(1)}, u32[]{:S(2)}, u32[]{:S(2)}) collective-permute-start(bf16[512,128]{1,0:T(8,128)(2,1)S(1)} %shard_map.141.refs_2_), channel_id=1, source_target_pairs={{0,1},{1,0},{2,3},{3,2},{4,5},{5,4},{6,7},{7,6},{8,9},{9,8},{10,11... | collective-permute-start | bytes 393224 | tf_op jit(solution)/shard_map/ppermute | solution.py:362
  9.2 2.3 %collective-permute-start.4 = (bf16[32,256]{1,0:T(8,128)(2,1)S(1)}, bf16[32,256]{1,0:T(8,128)(2,1)S(1)}, u32[]{:S(2)}, u32[]{:S(2)}) collective-permute-start(bf16[32,256]{1,0:T(8,128)(2,1)S(1)} %copy-done), channel_id=1, source_target_pairs={{0,2},{1,3},{2,0},{3,1},{4,6},{5,7},{6,4},{7,5},{8,10},{9,11},{10,... | collective-permute-start | bytes 49160 | tf_op jit(solution)/shard_map/ppermute | solution.py:362
  11.5 2.0 %collective-permute-start.3 = (bf16[32,256]{1,0:T(8,128)(2,1)S(1)}, bf16[32,256]{1,0:T(8,128)(2,1)S(1)}, u32[]{:S(2)}, u32[]{:S(2)}) collective-permute-start(bf16[32,256]{1,0:T(8,128)(2,1)S(1)} %copy-done), channel_id=1, source_target_pairs={{0,1},{1,0},{2,3},{3,2},{4,5},{5,4},{6,7},{7,6},{8,9},{9,8},{10,11... | collective-permute-start | bytes 49160 | tf_op jit(solution)/shard_map/ppermute | solution.py:362
  13.5 0.1 copy.15.refs_0_
  13.6 3.9 %shard_map.140 = (bf16[896,256]{1,0:T(8,128)(2,1)S(1)}, bf16[896,256]{1,0:T(8,128)(2,1)S(1)}, bf16[1024,256]{1,0:T(8,128)(2,1)S(1)}, bf16[1024,256]{1,0:T(8,128)...) custom-call(s32[1,1024]{1,0:T(1,128)S(1)} %bitcast.1, ...), custom_call_target="tpu_custom_call" | custom-call | flops 41943040 | bytes 6291456 | tf_op jit(solution)/shard_map/pallas_call | solution.py:43
  17.5 0.1 collective-permute-start.5
  17.6 2.7 %collective-permute-done.1.refs_4_ = bf16[512,128]{1,0:T(8,128)(2,1)S(1)} collective-permute-done((bf16[512,128]{1,0:T(8,128)(2,1)S(1)}, bf16[512,128]{1,0:T(8,128)(2,1)S(1)}, u32[]{:S(2)}, u32[]{:S(2)}) %collective-permute-start.1) | collective-permute-done | bytes 131104 | tf_op jit(solution)/shard_map/ppermute | solution.py:362
  20.3 0.0 collective-permute-done.refs_3_
  20.3 1.8 %shard_map.142 = (bf16[256,256]{1,0:T(8,128)(2,1)S(1)}, bf16[64,128]{1,0:T(8,128)(2,1)S(1)}, bf16[64,128]{1,0:T(8,128)(2,1)S(1)}, bf16[64,128]{1,0:T(8,128)(2,1)...) custom-call(s32[16,2]{1,0:T(8,128)S(1)} %copy.15.refs_0_, ...), custom_call_target="tpu_custom_call" | custom-call | flops 134217728 | bytes 2097152 | tf_op jit(solution)/shard_map/pallas_call | solution.py:43
  22.1 0.9 %collective-permute-start.6 = (bf16[64,128]{1,0:T(8,128)(2,1)S(1)}, bf16[64,128]{1,0:T(8,128)(2,1)S(1)}, u32[]{:S(2)}, u32[]{:S(2)}) collective-permute-start(bf16[64,128]{1,0:T(8,128)(2,1)S(1)} %get-tuple-element.46), channel_id=1, source_target_pairs={{0,28},{4,24},{8,20},{12,16},{16,12},{20,8},{24,4},{28,0},{1,29},{... | collective-permute-start | bytes 49160 | tf_op jit(solution)/shard_map/ppermute | solution.py:444
  23.1 1.7 %collective-permute-start.7 = (bf16[64,128]{1,0:T(8,128)(2,1)S(1)}, bf16[64,128]{1,0:T(8,128)(2,1)S(1)}, u32[]{:S(2)}, u32[]{:S(2)}) collective-permute-start(bf16[64,128]{1,0:T(8,128)(2,1)S(1)} %get-tuple-element.47), channel_id=1, source_target_pairs={{0,24},{4,28},{8,16},{12,20},{16,8},{20,12},{24,0},{28,4},{1,25},{... | collective-permute-start | bytes 49160 | tf_op jit(solution)/shard_map/ppermute | solution.py:444
  24.7 1.4 %collective-permute-start.8 = (bf16[64,128]{1,0:T(8,128)(2,1)S(1)}, bf16[64,128]{1,0:T(8,128)(2,1)S(1)}, u32[]{:S(2)}, u32[]{:S(2)}) collective-permute-start(bf16[64,128]{1,0:T(8,128)(2,1)S(1)} %get-tuple-element.48), channel_id=1, source_target_pairs={{0,20},{4,16},{8,28},{12,24},{16,4},{20,0},{24,12},{28,8},{1,21},{... | collective-permute-start | bytes 49160 | tf_op jit(solution)/shard_map/ppermute | solution.py:444
  26.1 0.0 collective-permute-done.3.refs_7_
  26.1 0.5 %collective-permute-start.9 = (bf16[64,128]{1,0:T(8,128)(2,1)S(1)}, bf16[64,128]{1,0:T(8,128)(2,1)S(1)}, u32[]{:S(2)}, u32[]{:S(2)}) collective-permute-start(bf16[64,128]{1,0:T(8,128)(2,1)S(1)} %get-tuple-element.49), channel_id=1, source_target_pairs={{0,16},{4,20},{8,24},{12,28},{16,0},{20,4},{24,8},{28,12},{1,17},{... | collective-permute-start | bytes 49160 | tf_op jit(solution)/shard_map/ppermute | solution.py:444
  26.6 0.0 collective-permute-done.5.refs_9_
  26.6 0.8 %collective-permute-start.10 = (bf16[64,128]{1,0:T(8,128)(2,1)S(1)}, bf16[64,128]{1,0:T(8,128)(2,1)S(1)}, u32[]{:S(2)}, u32[]{:S(2)}) collective-permute-start(bf16[64,128]{1,0:T(8,128)(2,1)S(1)} %get-tuple-element.50), channel_id=1, source_target_pairs={{0,12},{4,8},{8,4},{12,0},{16,28},{20,24},{24,20},{28,16},{1,13},{... | collective-permute-start | bytes 49160 | tf_op jit(solution)/shard_map/ppermute | solution.py:444
  27.4 0.9 %collective-permute-start.11 = (bf16[64,128]{1,0:T(8,128)(2,1)S(1)}, bf16[64,128]{1,0:T(8,128)(2,1)S(1)}, u32[]{:S(2)}, u32[]{:S(2)}) collective-permute-start(bf16[64,128]{1,0:T(8,128)(2,1)S(1)} %get-tuple-element.51), channel_id=1, source_target_pairs={{0,8},{4,12},{8,0},{12,4},{16,24},{20,28},{24,16},{28,20},{1,9},{5... | collective-permute-start | bytes 49160 | tf_op jit(solution)/shard_map/ppermute | solution.py:444
  28.2 0.2 collective-permute-start.12
  28.5 1.3 %shard_map.143 = (f32[1024,512]{1,0:T(8,128)S(1)}, bf16[128,256]{1,0:T(8,128)(2,1)S(1)}) custom-call(bf16[1024,512]{1,0:T(8,128)(2,1)S(1)} %get-tuple-element.31.refs_0_, bf16[256,256]{1,0:T(8,128)(2,1)S(1)} %get-tuple-element.35.refs_1_, bf16[1024,256]{1,0:T(8,128)(2,1)S(1)} %get-tuple-element.36.refs_2_, bf16[1024,256]{1,0:T(8,128)(2,1)S(1)} %get-tuple-element.37.refs_3_, ...), custom_call_target="tpu_custom_call" | custom-call | flops 268435456 | bytes 5242880 | tf_op jit(solution)/shard_map/pallas_call | solution.py:43
  29.8 0.1 collective-permute-done.9.refs_10_
  29.8 1.3 %collective-permute-done.11.refs_12_ = bf16[64,128]{1,0:T(8,128)(2,1)S(1)} collective-permute-done((bf16[64,128]{1,0:T(8,128)(2,1)S(1)}, bf16[64,128]{1,0:T(8,128)(2,1)S(1)}, u32[]{:S(2)}, u32[]{:S(2)}) %collective-permute-start.11) | collective-permute-done | bytes 16416 | tf_op jit(solution)/shard_map/ppermute | solution.py:444
  31.2 2.8 %shard_map.144 = (bf16[1024,512]{1,0:T(8,128)(2,1)S(1)}, bf16[128,256]{1,0:T(8,128)(2,1)S(1)}) custom-call(f32[1024,512]{1,0:T(8,128)S(1)} %get-tuple-element.40.refs_0_, bf16[1024,256]{1,0:T(8,128)(2,1)S(1)} %get-tuple-element.41.refs_1_, bf16[1024,256]{1,0:T(8,128)(2,1)S(1)} %get-tuple-element.42.refs_2_, ...), custom_call_target="tpu_custom_call" | custom-call | flops 1073741824 | bytes 4194304 | tf_op jit(solution)/shard_map/pallas_call | solution.py:43
  33.9 0.1 collective-permute-start.15
  34.0 2.7 %collective-permute-start.14 = (bf16[128,256]{1,0:T(8,128)(2,1)S(1)}, bf16[128,256]{1,0:T(8,128)(2,1)S(1)}, u32[]{:S(2)}, u32[]{:S(2)}) collective-permute-start(bf16[128,256]{1,0:T(8,128)(2,1)S(1)} %get-tuple-element.53.refs_0_), channel_id=1, source_target_pairs={{0,3},{1,2},{2,1},{3,0},{4,7},{5,6},{6,5},{7,4},{8,11},{9,10},{10,... | collective-permute-start | bytes 196616 | tf_op jit(solution)/shard_map/ppermute | solution.py:362
  36.7 0.8 %collective-permute-start.13 = (bf16[128,256]{1,0:T(8,128)(2,1)S(1)}, bf16[128,256]{1,0:T(8,128)(2,1)S(1)}, u32[]{:S(2)}, u32[]{:S(2)}) collective-permute-start(bf16[128,256]{1,0:T(8,128)(2,1)S(1)} %get-tuple-element.53.refs_0_), channel_id=1, source_target_pairs={{0,1},{1,0},{2,3},{3,2},{4,5},{5,4},{6,7},{7,6},{8,9},{9,8},{10,11... | collective-permute-start | bytes 196616 | tf_op jit(solution)/shard_map/ppermute | solution.py:362
  37.5 0.8 %shard_map.145 = (f32[1024,512]{1,0:T(8,128)S(1)}, bf16[1024,256]{1,0:T(8,128)(2,1)S(1)}) custom-call(bf16[1024,512]{1,0:T(8,128)(2,1)S(1)} %get-tuple-element.57.state_ref.refs_7_, bf16[1024,512]{1,0:T(8,128)(2,1)S(1)} %get-tuple-element.56.join_ref.refs_6_, s32[2,1024]{1,0:T(2,128)S(1)} %get-tuple-element.45.refs_6_.index_ref), custom_call_target="tpu_custom_call" | custom-call | flops 536870912 | bytes 4194304 | tf_op jit(solution)/shard_map/pallas_call | solution.py:43
  38.3 3.5 %collective-permute-done.15.refs_3_ = bf16[128,256]{1,0:T(8,128)(2,1)S(1)} collective-permute-done((bf16[128,256]{1,0:T(8,128)(2,1)S(1)}, bf16[128,256]{1,0:T(8,128)(2,1)S(1)}, u32[]{:S(2)}, u32[]{:S(2)}) %collective-permute-start.15) | collective-permute-done | bytes 65568 | tf_op jit(solution)/shard_map/ppermute | solution.py:362
  41.8 1.1 %collective-permute-done.13.refs_1_ = bf16[128,256]{1,0:T(8,128)(2,1)S(1)} collective-permute-done((bf16[128,256]{1,0:T(8,128)(2,1)S(1)}, bf16[128,256]{1,0:T(8,128)(2,1)S(1)}, u32[]{:S(2)}, u32[]{:S(2)}) %collective-permute-start.13) | collective-permute-done | bytes 65568 | tf_op jit(solution)/shard_map/ppermute | solution.py:362
  42.9 2.1 %shard_map.146 = (bf16[1024,512]{1,0:T(8,128)(2,1)}, bf16[32,256]{1,0:T(8,128)(2,1)}) custom-call(bf16[128,256]{1,0:T(8,128)(2,1)S(1)} %get-tuple-element.53.refs_0_, bf16[128,256]{1,0:T(8,128)(2,1)S(1)} %collective-permute-done.13.refs_1_, bf16[128,256]{1,0:T(8,128)(2,1)S(1)} %collective-permute-done.14.refs_2_, ...), custom_call_target="tpu_custom_call" | custom-call | flops 268435456 | bytes 4194304 | tf_op jit(solution)/shard_map/pallas_call | solution.py:43
  (14 shorter events, 0.0 us)
Async XLA Ops:
  0.6 8.6 %copy-start = (bf16[32,256]{1,0:T(8,128)(2,1)S(1)}, bf16[32,256]{1,0:T(8,128)(2,1)}, u32[]{:S(2)}) copy-start(bf16[32,256]{1,0:T(8,128)(2,1)} %refs_6_.3) | copy-start | bytes 49156
  0.6 12.9 %copy-start.2 = (s32[16,2]{0,1:T(2,128)S(1)}, s32[16,2]{0,1:T(2,128)}, u32[]{:S(2)}) copy-start(s32[16,2]{0,1:T(2,128)} %param.17) | copy-start | bytes 388
  0.7 13.0 %copy-start.1 = (s32[1024]{0:T(1024)S(1)}, s32[1024]{0:T(1024)}, u32[]{:S(2)}) copy-start(s32[1024]{0:T(1024)} %param.15) | copy-start | bytes 12292
  3.5 14.0 %collective-permute-start.2 = (bf16[512,128]{1,0:T(8,128)(2,1)S(1)}, bf16[512,128]{1,0:T(8,128)(2,1)S(1)}, u32[]{:S(2)}, u32[]{:S(2)}) collective-permute-start(bf16[512,128]{1,0:T(8,128)(2,1)S(1)} %shard_map.141.refs_2_), channel_id=1, source_target_pairs={{0,3},{1,2},{2,1},{3,0},{4,7},{5,6},{6,5},{7,4},{8,11},{9,10},{10,... | collective-permute-start | bytes 393224 | tf_op jit(solution)/shard_map/ppermute | solution.py:362
  8.6 11.8 %collective-permute-start.1 = (bf16[512,128]{1,0:T(8,128)(2,1)S(1)}, bf16[512,128]{1,0:T(8,128)(2,1)S(1)}, u32[]{:S(2)}, u32[]{:S(2)}) collective-permute-start(bf16[512,128]{1,0:T(8,128)(2,1)S(1)} %shard_map.141.refs_2_), channel_id=1, source_target_pairs={{0,2},{1,3},{2,0},{3,1},{4,6},{5,7},{6,4},{7,5},{8,10},{9,11},{10,... | collective-permute-start | bytes 393224 | tf_op jit(solution)/shard_map/ppermute | solution.py:362
  8.6 11.8 %collective-permute-start = (bf16[512,128]{1,0:T(8,128)(2,1)S(1)}, bf16[512,128]{1,0:T(8,128)(2,1)S(1)}, u32[]{:S(2)}, u32[]{:S(2)}) collective-permute-start(bf16[512,128]{1,0:T(8,128)(2,1)S(1)} %shard_map.141.refs_2_), channel_id=1, source_target_pairs={{0,1},{1,0},{2,3},{3,2},{4,5},{5,4},{6,7},{7,6},{8,9},{9,8},{10,11... | collective-permute-start | bytes 393224 | tf_op jit(solution)/shard_map/ppermute | solution.py:362
  9.2 15.5 %collective-permute-start.4 = (bf16[32,256]{1,0:T(8,128)(2,1)S(1)}, bf16[32,256]{1,0:T(8,128)(2,1)S(1)}, u32[]{:S(2)}, u32[]{:S(2)}) collective-permute-start(bf16[32,256]{1,0:T(8,128)(2,1)S(1)} %copy-done), channel_id=1, source_target_pairs={{0,2},{1,3},{2,0},{3,1},{4,6},{5,7},{6,4},{7,5},{8,10},{9,11},{10,... | collective-permute-start | bytes 49160 | tf_op jit(solution)/shard_map/ppermute | solution.py:362
  11.5 14.6 %collective-permute-start.3 = (bf16[32,256]{1,0:T(8,128)(2,1)S(1)}, bf16[32,256]{1,0:T(8,128)(2,1)S(1)}, u32[]{:S(2)}, u32[]{:S(2)}) collective-permute-start(bf16[32,256]{1,0:T(8,128)(2,1)S(1)} %copy-done), channel_id=1, source_target_pairs={{0,1},{1,0},{2,3},{3,2},{4,5},{5,4},{6,7},{7,6},{8,9},{9,8},{10,11... | collective-permute-start | bytes 49160 | tf_op jit(solution)/shard_map/ppermute | solution.py:362
  17.5 9.1 %collective-permute-start.5 = (bf16[32,256]{1,0:T(8,128)(2,1)S(1)}, bf16[32,256]{1,0:T(8,128)(2,1)S(1)}, u32[]{:S(2)}, u32[]{:S(2)}) collective-permute-start(bf16[32,256]{1,0:T(8,128)(2,1)S(1)} %copy-done), channel_id=1, source_target_pairs={{0,3},{1,2},{2,1},{3,0},{4,7},{5,6},{6,5},{7,4},{8,11},{9,10},{10,... | collective-permute-start | bytes 49160 | tf_op jit(solution)/shard_map/ppermute | solution.py:362
  22.1 5.2 %collective-permute-start.6 = (bf16[64,128]{1,0:T(8,128)(2,1)S(1)}, bf16[64,128]{1,0:T(8,128)(2,1)S(1)}, u32[]{:S(2)}, u32[]{:S(2)}) collective-permute-start(bf16[64,128]{1,0:T(8,128)(2,1)S(1)} %get-tuple-element.46), channel_id=1, source_target_pairs={{0,28},{4,24},{8,20},{12,16},{16,12},{20,8},{24,4},{28,0},{1,29},{... | collective-permute-start | bytes 49160 | tf_op jit(solution)/shard_map/ppermute | solution.py:444
  23.1 5.2 %collective-permute-start.7 = (bf16[64,128]{1,0:T(8,128)(2,1)S(1)}, bf16[64,128]{1,0:T(8,128)(2,1)S(1)}, u32[]{:S(2)}, u32[]{:S(2)}) collective-permute-start(bf16[64,128]{1,0:T(8,128)(2,1)S(1)} %get-tuple-element.47), channel_id=1, source_target_pairs={{0,24},{4,28},{8,16},{12,20},{16,8},{20,12},{24,0},{28,4},{1,25},{... | collective-permute-start | bytes 49160 | tf_op jit(solution)/shard_map/ppermute | solution.py:444
  24.7 5.0 %collective-permute-start.8 = (bf16[64,128]{1,0:T(8,128)(2,1)S(1)}, bf16[64,128]{1,0:T(8,128)(2,1)S(1)}, u32[]{:S(2)}, u32[]{:S(2)}) collective-permute-start(bf16[64,128]{1,0:T(8,128)(2,1)S(1)} %get-tuple-element.48), channel_id=1, source_target_pairs={{0,20},{4,16},{8,28},{12,24},{16,4},{20,0},{24,12},{28,8},{1,21},{... | collective-permute-start | bytes 49160 | tf_op jit(solution)/shard_map/ppermute | solution.py:444
  26.1 3.7 %collective-permute-start.9 = (bf16[64,128]{1,0:T(8,128)(2,1)S(1)}, bf16[64,128]{1,0:T(8,128)(2,1)S(1)}, u32[]{:S(2)}, u32[]{:S(2)}) collective-permute-start(bf16[64,128]{1,0:T(8,128)(2,1)S(1)} %get-tuple-element.49), channel_id=1, source_target_pairs={{0,16},{4,20},{8,24},{12,28},{16,0},{20,4},{24,8},{28,12},{1,17},{... | collective-permute-start | bytes 49160 | tf_op jit(solution)/shard_map/ppermute | solution.py:444
  26.6 3.2 %collective-permute-start.10 = (bf16[64,128]{1,0:T(8,128)(2,1)S(1)}, bf16[64,128]{1,0:T(8,128)(2,1)S(1)}, u32[]{:S(2)}, u32[]{:S(2)}) collective-permute-start(bf16[64,128]{1,0:T(8,128)(2,1)S(1)} %get-tuple-element.50), channel_id=1, source_target_pairs={{0,12},{4,8},{8,4},{12,0},{16,28},{20,24},{24,20},{28,16},{1,13},{... | collective-permute-start | bytes 49160 | tf_op jit(solution)/shard_map/ppermute | solution.py:444
  27.4 3.8 %collective-permute-start.11 = (bf16[64,128]{1,0:T(8,128)(2,1)S(1)}, bf16[64,128]{1,0:T(8,128)(2,1)S(1)}, u32[]{:S(2)}, u32[]{:S(2)}) collective-permute-start(bf16[64,128]{1,0:T(8,128)(2,1)S(1)} %get-tuple-element.51), channel_id=1, source_target_pairs={{0,8},{4,12},{8,0},{12,4},{16,24},{20,28},{24,16},{28,20},{1,9},{5... | collective-permute-start | bytes 49160 | tf_op jit(solution)/shard_map/ppermute | solution.py:444
  28.2 2.9 %collective-permute-start.12 = (bf16[64,128]{1,0:T(8,128)(2,1)S(1)}, bf16[64,128]{1,0:T(8,128)(2,1)S(1)}, u32[]{:S(2)}, u32[]{:S(2)}) collective-permute-start(bf16[64,128]{1,0:T(8,128)(2,1)S(1)} %get-tuple-element.52), channel_id=1, source_target_pairs={{0,4},{4,0},{8,12},{12,8},{16,20},{20,16},{24,28},{28,24},{1,5},{5... | collective-permute-start | bytes 49160 | tf_op jit(solution)/shard_map/ppermute | solution.py:444
  33.9 7.9 %collective-permute-start.15 = (bf16[128,256]{1,0:T(8,128)(2,1)S(1)}, bf16[128,256]{1,0:T(8,128)(2,1)S(1)}, u32[]{:S(2)}, u32[]{:S(2)}) collective-permute-start(bf16[128,256]{1,0:T(8,128)(2,1)S(1)} %get-tuple-element.53.refs_0_), channel_id=1, source_target_pairs={{0,2},{1,3},{2,0},{3,1},{4,6},{5,7},{6,4},{7,5},{8,10},{9,11},{10,... | collective-permute-start | bytes 196616 | tf_op jit(solution)/shard_map/ppermute | solution.py:362
  34.0 7.8 %collective-permute-start.14 = (bf16[128,256]{1,0:T(8,128)(2,1)S(1)}, bf16[128,256]{1,0:T(8,128)(2,1)S(1)}, u32[]{:S(2)}, u32[]{:S(2)}) collective-permute-start(bf16[128,256]{1,0:T(8,128)(2,1)S(1)} %get-tuple-element.53.refs_0_), channel_id=1, source_target_pairs={{0,3},{1,2},{2,1},{3,0},{4,7},{5,6},{6,5},{7,4},{8,11},{9,10},{10,... | collective-permute-start | bytes 196616 | tf_op jit(solution)/shard_map/ppermute | solution.py:362
  36.7 6.2 %collective-permute-start.13 = (bf16[128,256]{1,0:T(8,128)(2,1)S(1)}, bf16[128,256]{1,0:T(8,128)(2,1)S(1)}, u32[]{:S(2)}, u32[]{:S(2)}) collective-permute-start(bf16[128,256]{1,0:T(8,128)(2,1)S(1)} %get-tuple-element.53.refs_0_), channel_id=1, source_target_pairs={{0,1},{1,0},{2,3},{3,2},{4,5},{5,4},{6,7},{7,6},{8,9},{9,8},{10,11... | collective-permute-start | bytes 196616 | tf_op jit(solution)/shard_map/ppermute | solution.py:362

commit v9 on v8

--- a/solution.py
+++ b/solution.py
@@ -10,6 +10,7 @@
 root_half = 0.7071067811865476
 MIB = 1 << 20
 CHUNK = 256
+LONG = 512
 GROUPS = 4
 
 
@@ -27,8 +28,8 @@
     return jnp.transpose(wide)[:, :1].astype(jnp.int32)
 
 
-def row_chunks(rows):
-    step = min(CHUNK, rows)
+def row_chunks(rows, step=CHUNK):
+    step = min(step, rows)
     return [slice(at, at + step) for at in range(0, rows, step)]
 
 
@@ -66,7 +67,7 @@
     half = edges_hbm.shape[0] // 2
     pieces = [
         slice(base + rows.start, base + rows.stop)
-        for rows in row_chunks(half)
+        for rows in row_chunks(half, LONG)
         for base in (0, half)
     ]
     copies = [
@@ -80,7 +81,7 @@
         copy.start()
     copies[0].wait()
     copies[1].wait()
-    for at, rows in enumerate(row_chunks(half)):
+    for at, rows in enumerate(row_chunks(half, LONG)):
         copies[2 + 2 * at].wait()
         copies[3 + 2 * at].wait()
         hidden = [
@@ -267,7 +268,7 @@
     chosen = (
         lax.broadcasted_iota(jnp.int32, (part_atoms, near.shape[1]), 0) == near
     ).astype(jnp.bfloat16)
-    chunks = row_chunks(base_ref.shape[0])
+    chunks = row_chunks(base_ref.shape[0], LONG)
     gathered = None
     for first in range(0, len(chunks), 2):
         group = chunks[first : first + 2]
@@ -300,22 +301,30 @@
     return (holder ^ lax.axis_index("edge")) * count + lax.rem(index, count)
 
 
-def side_kernel(shards, part_atoms, state_ref, join_ref, index_ref, out_ref, chosen_ref):
-    width = join_ref.shape[0] - state_ref.shape[1]
+def side_kernel(shards, *refs):
+    state_ref, join_ref, index_ref, atoms_ref, weight_ref, out_ref, chosen_ref, fixed_ref, onward_ref = refs
+    part_atoms, width = atoms_ref.shape
     for rows in row_chunks(state_ref.shape[0]):
-        out_ref[rows, :] = product(state_ref[rows, :], join_ref[width:, :])
+        out_ref[rows, :] = product(state_ref[rows, :], join_ref[2 * width :, :])
     index = near_atoms(index_ref[...], part_atoms, shards)
     for end in range(2):
         column = as_column(index[end : end + 1, :])
         chosen_ref[:, end * part_atoms : (end + 1) * part_atoms] = (
             lax.broadcasted_iota(jnp.int32, (column.shape[0], part_atoms), 1) == column
         ).astype(jnp.bfloat16)
+        join = join_ref[end * width : (end + 1) * width, :]
+        fixed_ref[end * part_atoms : (end + 1) * part_atoms, :] = product(atoms_ref[...], join)
+        onward_ref[end * width : (end + 1) * width, :] = product(weight_ref[1], join).astype(
+            jnp.bfloat16
+        )
 
 
 def final_kernel(shards, scale, *refs):
     sums = refs[:shards]
-    atoms_ref, weight_ref, join_ref, state_ref, side_ref, chosen_ref = refs[shards : shards + 6]
-    edges_hbm, own_hbm, table_ref, edges_ref, own_ref, sems = refs[shards + 6 :]
+    atoms_ref, weight_ref, state_ref, side_ref, chosen_ref, fixed_ref, onward_ref = refs[
+        shards : shards + 7
+    ]
+    edges_hbm, own_hbm, table_ref, edges_ref, own_ref, sems = refs[shards + 7 :]
     part_atoms = atoms_ref.shape[0]
     count = part_atoms // shards
     total = sums[0][...].astype(jnp.float32)
@@ -324,15 +333,15 @@
         total = total + jnp.concatenate(pieces, axis=0).astype(jnp.float32)
     scaled = (total * scale).astype(jnp.bfloat16)
     middle = silu(product(scaled, weight_ref[0])).astype(jnp.bfloat16)
-    renewed = (atoms_ref[...].astype(jnp.float32) + product(middle, weight_ref[1])).astype(jnp.bfloat16)
-    own_ref[...] = renewed[:count, :]
+    width = middle.shape[1]
+    for end in range(2):
+        rows = slice(end * part_atoms, (end + 1) * part_atoms)
+        onward = product(middle, onward_ref[end * width : (end + 1) * width, :])
+        table_ref[rows, :] = (fixed_ref[rows, :] + onward).astype(jnp.bfloat16)
+    renewed = atoms_ref[:count, :].astype(jnp.float32) + product(middle[:count, :], weight_ref[1])
+    own_ref[...] = renewed.astype(jnp.bfloat16)
     own_copy = pltpu.make_async_copy(own_ref, own_hbm, sems.at[0])
     own_copy.start()
-    width = renewed.shape[1]
-    for end in range(2):
-        table_ref[end * part_atoms : (end + 1) * part_atoms, :] = product(
-            renewed, join_ref[end * width : (end + 1) * width, :]
-        ).astype(jnp.bfloat16)
     copies = [own_copy]
     chunks = row_chunks(state_ref.shape[0])
     for first in range(0, len(chunks), 2):
@@ -400,7 +409,7 @@
             pltpu.VMEM(edges.shape, jnp.bfloat16),
             pltpu.VMEM(weight_edge.shape, jnp.bfloat16),
             pltpu.VMEM(weight_down.shape, jnp.bfloat16),
-            pltpu.SemaphoreType.DMA((2 + 2 * len(row_chunks(lines)),)),
+            pltpu.SemaphoreType.DMA((2 + 2 * len(row_chunks(lines, LONG)),)),
         ],
         flops=2 * rows * wide * (wide + channels),
         nbytes=2 * (rows * wide + wide * wide),
@@ -460,17 +469,22 @@
         nbytes=8 * rows * wide,
     )
     sums_parts = from_others(sums, orders(shards)[1])
-    side, chosen = call(
-        functools.partial(side_kernel, shards, part_atoms),
-        (shaped((rows, wide), jnp.float32), shaped((rows, 2 * part_atoms))),
-        (state, weight_join, atom_index),
+    side, chosen, fixed, onward = call(
+        functools.partial(side_kernel, shards),
+        (
+            shaped((rows, wide), jnp.float32),
+            shaped((rows, 2 * part_atoms)),
+            shaped((2 * part_atoms, wide), jnp.float32),
+            shaped((2 * atom_wide, wide)),
+        ),
+        (state, weight_join, atom_index, all_atoms, weight_atom),
         flops=2 * rows * wide * wide,
         nbytes=8 * rows * wide,
     )
     return call(
         functools.partial(final_kernel, shards, (rows // count) ** -0.5),
         (shaped((rows, wide), space=pltpu.HBM), shaped((count, atom_wide), space=pltpu.HBM)),
-        (*sums_parts, all_atoms, weight_atom, weight_join, state, side, chosen),
+        (*sums_parts, all_atoms, weight_atom, state, side, chosen, fixed, onward),
         scratch=[
             pltpu.VMEM((2 * part_atoms, wide), jnp.bfloat16),
             pltpu.VMEM((rows, wide), jnp.bfloat16),

time: 45.2 us -> 44.6 us (0.987)
  transfers between devices with their start and end apart: 16 -> 16, of which waited for: 5 -> 5; matrix products, arithmetic and copies ran while one was open for 0% -> 0% of each run, Pallas kernels for 17% -> 18%
where the time goes in v9:
time: 44.6 us; the launch traced here: 44.4 us
  starting transfers between devices  20.1 us (45%)
  Pallas kernels  15 us (34%)
  waiting for transfers between devices  8.5 us (19%)
  between operations  0.74 us (2%)
    pallas_call x7, Pallas kernels, call(): pl.pallas_call(kernel, out_shape=outs, in_specs=[pl.BlockSpec(memory_spac...  15 us
    ppermute x9, starting transfers between devices, from_others(): lax.ppermute(value, 'edge', [(at, at ^ by) for at in range(len(order))])  13.8 us
    ppermute x9, waiting for transfers between devices, from_others(): lax.ppermute(value, 'edge', [(at, at ^ by) for at in range(len(order))])  7.11 us
    ppermute x7, starting transfers between devices, body(): lax.ppermute(block, 'dom', [(at, at ^ partners - place) for at in range(d...  6.32 us
    ppermute x7, waiting for transfers between devices, body(): lax.ppermute(block, 'dom', [(at, at ^ partners - place) for at in range(d...  1.39 us
  transfers between devices with their start and end apart: 16, of which 5 were waited for; matrix products, arithmetic and copies ran while one was open for 0% of the time, Pallas kernels for 18%

profile of v9, /device:TPU:0, one launch (start us, length us, event | category | flops | bytes accessed | tf_op | source)
XLA Modules:
  0.0 44.4 jit_solution(14986714600686730191)
XLA Ops:
  0.7 2.6 %shard_map.141.refs_2_ = bf16[512,128]{1,0:T(8,128)(2,1)S(1)} custom-call(bf16[1024,512]{1,0:T(8,128)(2,1)} %edges_hbm.1, bf16[512,512]{1,0:T(8,128)(2,1)} %weight_hbm.1, bf16[64,512]{1,0:T(8,128)(2,1)} %down_hbm.1), custom_call_target="tpu_custom_call" | custom-call | flops 603979776 | bytes 1572864 | tf_op jit(solution)/shard_map/pallas_call | solution.py:44
  3.3 5.1 %collective-permute-start.2 = (bf16[512,128]{1,0:T(8,128)(2,1)S(1)}, bf16[512,128]{1,0:T(8,128)(2,1)S(1)}, u32[]{:S(2)}, u32[]{:S(2)}) collective-permute-start(bf16[512,128]{1,0:T(8,128)(2,1)S(1)} %shard_map.141.refs_2_), channel_id=1, source_target_pairs={{0,3},{1,2},{2,1},{3,0},{4,7},{5,6},{6,5},{7,4},{8,11},{9,10},{10,... | collective-permute-start | bytes 393224 | tf_op jit(solution)/shard_map/ppermute | solution.py:371
  8.4 0.0 collective-permute-start.1
  8.4 0.6 %collective-permute-start = (bf16[512,128]{1,0:T(8,128)(2,1)S(1)}, bf16[512,128]{1,0:T(8,128)(2,1)S(1)}, u32[]{:S(2)}, u32[]{:S(2)}) collective-permute-start(bf16[512,128]{1,0:T(8,128)(2,1)S(1)} %shard_map.141.refs_2_), channel_id=1, source_target_pairs={{0,1},{1,0},{2,3},{3,2},{4,5},{5,4},{6,7},{7,6},{8,9},{9,8},{10,11... | collective-permute-start | bytes 393224 | tf_op jit(solution)/shard_map/ppermute | solution.py:371
  9.0 2.3 %collective-permute-start.4 = (bf16[32,256]{1,0:T(8,128)(2,1)S(1)}, bf16[32,256]{1,0:T(8,128)(2,1)S(1)}, u32[]{:S(2)}, u32[]{:S(2)}) collective-permute-start(bf16[32,256]{1,0:T(8,128)(2,1)S(1)} %copy-done), channel_id=1, source_target_pairs={{0,2},{1,3},{2,0},{3,1},{4,6},{5,7},{6,4},{7,5},{8,10},{9,11},{10,... | collective-permute-start | bytes 49160 | tf_op jit(solution)/shard_map/ppermute | solution.py:371
  11.3 2.0 %collective-permute-start.3 = (bf16[32,256]{1,0:T(8,128)(2,1)S(1)}, bf16[32,256]{1,0:T(8,128)(2,1)S(1)}, u32[]{:S(2)}, u32[]{:S(2)}) collective-permute-start(bf16[32,256]{1,0:T(8,128)(2,1)S(1)} %copy-done), channel_id=1, source_target_pairs={{0,1},{1,0},{2,3},{3,2},{4,5},{5,4},{6,7},{7,6},{8,9},{9,8},{10,11... | collective-permute-start | bytes 49160 | tf_op jit(solution)/shard_map/ppermute | solution.py:371
  13.3 0.1 copy.15.refs_0_
  13.4 3.9 %shard_map.140 = (bf16[896,256]{1,0:T(8,128)(2,1)S(1)}, bf16[896,256]{1,0:T(8,128)(2,1)S(1)}, bf16[1024,256]{1,0:T(8,128)(2,1)S(1)}, bf16[1024,256]{1,0:T(8,128)...) custom-call(s32[1,1024]{1,0:T(1,128)S(1)} %bitcast.1, ...), custom_call_target="tpu_custom_call" | custom-call | flops 41943040 | bytes 6291456 | tf_op jit(solution)/shard_map/pallas_call | solution.py:44
  17.3 0.1 collective-permute-start.5
  17.5 2.7 %collective-permute-done.1.refs_4_ = bf16[512,128]{1,0:T(8,128)(2,1)S(1)} collective-permute-done((bf16[512,128]{1,0:T(8,128)(2,1)S(1)}, bf16[512,128]{1,0:T(8,128)(2,1)S(1)}, u32[]{:S(2)}, u32[]{:S(2)}) %collective-permute-start.1) | collective-permute-done | bytes 131104 | tf_op jit(solution)/shard_map/ppermute | solution.py:371
  20.2 0.0 collective-permute-done.refs_3_
  20.2 1.8 %shard_map.142 = (bf16[256,256]{1,0:T(8,128)(2,1)S(1)}, bf16[64,128]{1,0:T(8,128)(2,1)S(1)}, bf16[64,128]{1,0:T(8,128)(2,1)S(1)}, bf16[64,128]{1,0:T(8,128)(2,1)...) custom-call(s32[16,2]{1,0:T(8,128)S(1)} %copy.15.refs_0_, ...), custom_call_target="tpu_custom_call" | custom-call | flops 134217728 | bytes 2097152 | tf_op jit(solution)/shard_map/pallas_call | solution.py:44
  21.9 0.9 %collective-permute-start.6 = (bf16[64,128]{1,0:T(8,128)(2,1)S(1)}, bf16[64,128]{1,0:T(8,128)(2,1)S(1)}, u32[]{:S(2)}, u32[]{:S(2)}) collective-permute-start(bf16[64,128]{1,0:T(8,128)(2,1)S(1)} %get-tuple-element.48), channel_id=1, source_target_pairs={{0,28},{4,24},{8,20},{12,16},{16,12},{20,8},{24,4},{28,0},{1,29},{... | collective-permute-start | bytes 49160 | tf_op jit(solution)/shard_map/ppermute | solution.py:453
  22.9 1.7 %collective-permute-start.7 = (bf16[64,128]{1,0:T(8,128)(2,1)S(1)}, bf16[64,128]{1,0:T(8,128)(2,1)S(1)}, u32[]{:S(2)}, u32[]{:S(2)}) collective-permute-start(bf16[64,128]{1,0:T(8,128)(2,1)S(1)} %get-tuple-element.49), channel_id=1, source_target_pairs={{0,24},{4,28},{8,16},{12,20},{16,8},{20,12},{24,0},{28,4},{1,25},{... | collective-permute-start | bytes 49160 | tf_op jit(solution)/shard_map/ppermute | solution.py:453
  24.5 1.4 %collective-permute-start.8 = (bf16[64,128]{1,0:T(8,128)(2,1)S(1)}, bf16[64,128]{1,0:T(8,128)(2,1)S(1)}, u32[]{:S(2)}, u32[]{:S(2)}) collective-permute-start(bf16[64,128]{1,0:T(8,128)(2,1)S(1)} %get-tuple-element.50), channel_id=1, source_target_pairs={{0,20},{4,16},{8,28},{12,24},{16,4},{20,0},{24,12},{28,8},{1,21},{... | collective-permute-start | bytes 49160 | tf_op jit(solution)/shard_map/ppermute | solution.py:453
  25.9 0.5 %collective-permute-start.9 = (bf16[64,128]{1,0:T(8,128)(2,1)S(1)}, bf16[64,128]{1,0:T(8,128)(2,1)S(1)}, u32[]{:S(2)}, u32[]{:S(2)}) collective-permute-start(bf16[64,128]{1,0:T(8,128)(2,1)S(1)} %get-tuple-element.51), channel_id=1, source_target_pairs={{0,16},{4,20},{8,24},{12,28},{16,0},{20,4},{24,8},{28,12},{1,17},{... | collective-permute-start | bytes 49160 | tf_op jit(solution)/shard_map/ppermute | solution.py:453
  26.4 0.8 %collective-permute-start.10 = (bf16[64,128]{1,0:T(8,128)(2,1)S(1)}, bf16[64,128]{1,0:T(8,128)(2,1)S(1)}, u32[]{:S(2)}, u32[]{:S(2)}) collective-permute-start(bf16[64,128]{1,0:T(8,128)(2,1)S(1)} %get-tuple-element.52), channel_id=1, source_target_pairs={{0,12},{4,8},{8,4},{12,0},{16,28},{20,24},{24,20},{28,16},{1,13},{... | collective-permute-start | bytes 49160 | tf_op jit(solution)/shard_map/ppermute | solution.py:453
  27.2 0.0 collective-permute-done.6.refs_7_
  27.2 0.9 %collective-permute-start.11 = (bf16[64,128]{1,0:T(8,128)(2,1)S(1)}, bf16[64,128]{1,0:T(8,128)(2,1)S(1)}, u32[]{:S(2)}, u32[]{:S(2)}) collective-permute-start(bf16[64,128]{1,0:T(8,128)(2,1)S(1)} %get-tuple-element.53), channel_id=1, source_target_pairs={{0,8},{4,12},{8,0},{12,4},{16,24},{20,28},{24,16},{28,20},{1,9},{5... | collective-permute-start | bytes 49160 | tf_op jit(solution)/shard_map/ppermute | solution.py:453
  28.0 0.2 collective-permute-start.12
  28.3 1.3 %shard_map.143 = (f32[1024,512]{1,0:T(8,128)S(1)}, bf16[128,256]{1,0:T(8,128)(2,1)S(1)}) custom-call(bf16[1024,512]{1,0:T(8,128)(2,1)S(1)} %get-tuple-element.33.refs_0_, bf16[256,256]{1,0:T(8,128)(2,1)S(1)} %get-tuple-element.37.refs_1_, bf16[1024,256]{1,0:T(8,128)(2,1)S(1)} %get-tuple-element.38.refs_2_, bf16[1024,256]{1,0:T(8,128)(2,1)S(1)} %get-tuple-element.39.refs_3_, ...), custom_call_target="tpu_custom_call" | custom-call | flops 268435456 | bytes 5242880 | tf_op jit(solution)/shard_map/pallas_call | solution.py:44
  29.6 0.1 collective-permute-done.9.refs_10_
  29.6 1.3 %collective-permute-done.11.refs_12_ = bf16[64,128]{1,0:T(8,128)(2,1)S(1)} collective-permute-done((bf16[64,128]{1,0:T(8,128)(2,1)S(1)}, bf16[64,128]{1,0:T(8,128)(2,1)S(1)}, u32[]{:S(2)}, u32[]{:S(2)}) %collective-permute-start.11) | collective-permute-done | bytes 16416 | tf_op jit(solution)/shard_map/ppermute | solution.py:453
  31.0 0.0 collective-permute-done.12.refs_13_
  31.0 2.5 %shard_map.144 = (bf16[1024,512]{1,0:T(8,128)(2,1)S(1)}, bf16[128,256]{1,0:T(8,128)(2,1)S(1)}) custom-call(f32[1024,512]{1,0:T(8,128)S(1)} %get-tuple-element.42.refs_0_, bf16[1024,256]{1,0:T(8,128)(2,1)S(1)} %get-tuple-element.43.refs_1_, bf16[1024,256]{1,0:T(8,128)(2,1)S(1)} %get-tuple-element.44.refs_2_, ...), custom_call_target="tpu_custom_call" | custom-call | flops 1073741824 | bytes 4194304 | tf_op jit(solution)/shard_map/pallas_call | solution.py:44
  33.5 0.1 collective-permute-start.15
  33.5 2.7 %collective-permute-start.14 = (bf16[128,256]{1,0:T(8,128)(2,1)S(1)}, bf16[128,256]{1,0:T(8,128)(2,1)S(1)}, u32[]{:S(2)}, u32[]{:S(2)}) collective-permute-start(bf16[128,256]{1,0:T(8,128)(2,1)S(1)} %get-tuple-element.55.refs_0_), channel_id=1, source_target_pairs={{0,3},{1,2},{2,1},{3,0},{4,7},{5,6},{6,5},{7,4},{8,11},{9,10},{10,... | collective-permute-start | bytes 196616 | tf_op jit(solution)/shard_map/ppermute | solution.py:371
  36.3 0.7 %collective-permute-start.13 = (bf16[128,256]{1,0:T(8,128)(2,1)S(1)}, bf16[128,256]{1,0:T(8,128)(2,1)S(1)}, u32[]{:S(2)}, u32[]{:S(2)}) collective-permute-start(bf16[128,256]{1,0:T(8,128)(2,1)S(1)} %get-tuple-element.55.refs_0_), channel_id=1, source_target_pairs={{0,1},{1,0},{2,3},{3,2},{4,5},{5,4},{6,7},{7,6},{8,9},{9,8},{10,11... | collective-permute-start | bytes 196616 | tf_op jit(solution)/shard_map/ppermute | solution.py:371
  37.0 1.0 %shard_map.145 = (f32[1024,512]{1,0:T(8,128)S(1)}, bf16[1024,256]{1,0:T(8,128)(2,1)S(1)}, f32[256,512]{1,0:T(8,128)S(1)}, bf16[512,512]{1,0:T(8,128)(2,1)S(1)}) custom-call(bf16[1024,512]{1,0:T(8,128)(2,1)S(1)} %get-tuple-element.58.refs_0_.refs_6_, bf16[1024,512]{1,0:T(8,128)(2,1)S(1)} %get-tuple-element.59.refs_1_, ...), custom_call_target="tpu_custom_call" | custom-call | flops 536870912 | bytes 4194304 | tf_op jit(solution)/shard_map/pallas_call | solution.py:44
  38.0 3.4 %collective-permute-done.15.refs_3_ = bf16[128,256]{1,0:T(8,128)(2,1)S(1)} collective-permute-done((bf16[128,256]{1,0:T(8,128)(2,1)S(1)}, bf16[128,256]{1,0:T(8,128)(2,1)S(1)}, u32[]{:S(2)}, u32[]{:S(2)}) %collective-permute-start.15) | collective-permute-done | bytes 65568 | tf_op jit(solution)/shard_map/ppermute | solution.py:371
  41.4 1.0 %collective-permute-done.13.refs_1_ = bf16[128,256]{1,0:T(8,128)(2,1)S(1)} collective-permute-done((bf16[128,256]{1,0:T(8,128)(2,1)S(1)}, bf16[128,256]{1,0:T(8,128)(2,1)S(1)}, u32[]{:S(2)}, u32[]{:S(2)}) %collective-permute-start.13) | collective-permute-done | bytes 65568 | tf_op jit(solution)/shard_map/ppermute | solution.py:371
  42.4 2.0 %shard_map.146 = (bf16[1024,512]{1,0:T(8,128)(2,1)}, bf16[32,256]{1,0:T(8,128)(2,1)}) custom-call(bf16[128,256]{1,0:T(8,128)(2,1)S(1)} %get-tuple-element.55.refs_0_, bf16[128,256]{1,0:T(8,128)(2,1)S(1)} %collective-permute-done.13.refs_1_, bf16[128,256]{1,0:T(8,128)(2,1)S(1)} %collective-permute-done.14.refs_2_, ...), custom_call_target="tpu_custom_call" | custom-call | flops 268435456 | bytes 4194304 | tf_op jit(solution)/shard_map/pallas_call | solution.py:44
  (14 shorter events, 0.0 us)
Async XLA Ops:
  0.6 8.4 %copy-start = (bf16[32,256]{1,0:T(8,128)(2,1)S(1)}, bf16[32,256]{1,0:T(8,128)(2,1)}, u32[]{:S(2)}) copy-start(bf16[32,256]{1,0:T(8,128)(2,1)} %refs_6_.3) | copy-start | bytes 49156
  0.6 12.7 %copy-start.2 = (s32[16,2]{0,1:T(2,128)S(1)}, s32[16,2]{0,1:T(2,128)}, u32[]{:S(2)}) copy-start(s32[16,2]{0,1:T(2,128)} %param.17) | copy-start | bytes 388
  0.7 12.8 %copy-start.1 = (s32[1024]{0:T(1024)S(1)}, s32[1024]{0:T(1024)}, u32[]{:S(2)}) copy-start(s32[1024]{0:T(1024)} %param.15) | copy-start | bytes 12292
  3.3 14.0 %collective-permute-start.2 = (bf16[512,128]{1,0:T(8,128)(2,1)S(1)}, bf16[512,128]{1,0:T(8,128)(2,1)S(1)}, u32[]{:S(2)}, u32[]{:S(2)}) collective-permute-start(bf16[512,128]{1,0:T(8,128)(2,1)S(1)} %shard_map.141.refs_2_), channel_id=1, source_target_pairs={{0,3},{1,2},{2,1},{3,0},{4,7},{5,6},{6,5},{7,4},{8,11},{9,10},{10,... | collective-permute-start | bytes 393224 | tf_op jit(solution)/shard_map/ppermute | solution.py:371
  8.4 11.8 %collective-permute-start.1 = (bf16[512,128]{1,0:T(8,128)(2,1)S(1)}, bf16[512,128]{1,0:T(8,128)(2,1)S(1)}, u32[]{:S(2)}, u32[]{:S(2)}) collective-permute-start(bf16[512,128]{1,0:T(8,128)(2,1)S(1)} %shard_map.141.refs_2_), channel_id=1, source_target_pairs={{0,2},{1,3},{2,0},{3,1},{4,6},{5,7},{6,4},{7,5},{8,10},{9,11},{10,... | collective-permute-start | bytes 393224 | tf_op jit(solution)/shard_map/ppermute | solution.py:371
  8.4 11.8 %collective-permute-start = (bf16[512,128]{1,0:T(8,128)(2,1)S(1)}, bf16[512,128]{1,0:T(8,128)(2,1)S(1)}, u32[]{:S(2)}, u32[]{:S(2)}) collective-permute-start(bf16[512,128]{1,0:T(8,128)(2,1)S(1)} %shard_map.141.refs_2_), channel_id=1, source_target_pairs={{0,1},{1,0},{2,3},{3,2},{4,5},{5,4},{6,7},{7,6},{8,9},{9,8},{10,11... | collective-permute-start | bytes 393224 | tf_op jit(solution)/shard_map/ppermute | solution.py:371
  9.0 15.5 %collective-permute-start.4 = (bf16[32,256]{1,0:T(8,128)(2,1)S(1)}, bf16[32,256]{1,0:T(8,128)(2,1)S(1)}, u32[]{:S(2)}, u32[]{:S(2)}) collective-permute-start(bf16[32,256]{1,0:T(8,128)(2,1)S(1)} %copy-done), channel_id=1, source_target_pairs={{0,2},{1,3},{2,0},{3,1},{4,6},{5,7},{6,4},{7,5},{8,10},{9,11},{10,... | collective-permute-start | bytes 49160 | tf_op jit(solution)/shard_map/ppermute | solution.py:371
  11.3 14.6 %collective-permute-start.3 = (bf16[32,256]{1,0:T(8,128)(2,1)S(1)}, bf16[32,256]{1,0:T(8,128)(2,1)S(1)}, u32[]{:S(2)}, u32[]{:S(2)}) collective-permute-start(bf16[32,256]{1,0:T(8,128)(2,1)S(1)} %copy-done), channel_id=1, source_target_pairs={{0,1},{1,0},{2,3},{3,2},{4,5},{5,4},{6,7},{7,6},{8,9},{9,8},{10,11... | collective-permute-start | bytes 49160 | tf_op jit(solution)/shard_map/ppermute | solution.py:371
  17.3 9.1 %collective-permute-start.5 = (bf16[32,256]{1,0:T(8,128)(2,1)S(1)}, bf16[32,256]{1,0:T(8,128)(2,1)S(1)}, u32[]{:S(2)}, u32[]{:S(2)}) collective-permute-start(bf16[32,256]{1,0:T(8,128)(2,1)S(1)} %copy-done), channel_id=1, source_target_pairs={{0,3},{1,2},{2,1},{3,0},{4,7},{5,6},{6,5},{7,4},{8,11},{9,10},{10,... | collective-permute-start | bytes 49160 | tf_op jit(solution)/shard_map/ppermute | solution.py:371
  21.9 5.2 %collective-permute-start.6 = (bf16[64,128]{1,0:T(8,128)(2,1)S(1)}, bf16[64,128]{1,0:T(8,128)(2,1)S(1)}, u32[]{:S(2)}, u32[]{:S(2)}) collective-permute-start(bf16[64,128]{1,0:T(8,128)(2,1)S(1)} %get-tuple-element.48), channel_id=1, source_target_pairs={{0,28},{4,24},{8,20},{12,16},{16,12},{20,8},{24,4},{28,0},{1,29},{... | collective-permute-start | bytes 49160 | tf_op jit(solution)/shard_map/ppermute | solution.py:453
  22.9 5.2 %collective-permute-start.7 = (bf16[64,128]{1,0:T(8,128)(2,1)S(1)}, bf16[64,128]{1,0:T(8,128)(2,1)S(1)}, u32[]{:S(2)}, u32[]{:S(2)}) collective-permute-start(bf16[64,128]{1,0:T(8,128)(2,1)S(1)} %get-tuple-element.49), channel_id=1, source_target_pairs={{0,24},{4,28},{8,16},{12,20},{16,8},{20,12},{24,0},{28,4},{1,25},{... | collective-permute-start | bytes 49160 | tf_op jit(solution)/shard_map/ppermute | solution.py:453
  24.5 5.0 %collective-permute-start.8 = (bf16[64,128]{1,0:T(8,128)(2,1)S(1)}, bf16[64,128]{1,0:T(8,128)(2,1)S(1)}, u32[]{:S(2)}, u32[]{:S(2)}) collective-permute-start(bf16[64,128]{1,0:T(8,128)(2,1)S(1)} %get-tuple-element.50), channel_id=1, source_target_pairs={{0,20},{4,16},{8,28},{12,24},{16,4},{20,0},{24,12},{28,8},{1,21},{... | collective-permute-start | bytes 49160 | tf_op jit(solution)/shard_map/ppermute | solution.py:453
  25.9 3.7 %collective-permute-start.9 = (bf16[64,128]{1,0:T(8,128)(2,1)S(1)}, bf16[64,128]{1,0:T(8,128)(2,1)S(1)}, u32[]{:S(2)}, u32[]{:S(2)}) collective-permute-start(bf16[64,128]{1,0:T(8,128)(2,1)S(1)} %get-tuple-element.51), channel_id=1, source_target_pairs={{0,16},{4,20},{8,24},{12,28},{16,0},{20,4},{24,8},{28,12},{1,17},{... | collective-permute-start | bytes 49160 | tf_op jit(solution)/shard_map/ppermute | solution.py:453
  26.4 3.2 %collective-permute-start.10 = (bf16[64,128]{1,0:T(8,128)(2,1)S(1)}, bf16[64,128]{1,0:T(8,128)(2,1)S(1)}, u32[]{:S(2)}, u32[]{:S(2)}) collective-permute-start(bf16[64,128]{1,0:T(8,128)(2,1)S(1)} %get-tuple-element.52), channel_id=1, source_target_pairs={{0,12},{4,8},{8,4},{12,0},{16,28},{20,24},{24,20},{28,16},{1,13},{... | collective-permute-start | bytes 49160 | tf_op jit(solution)/shard_map/ppermute | solution.py:453
  27.2 3.8 %collective-permute-start.11 = (bf16[64,128]{1,0:T(8,128)(2,1)S(1)}, bf16[64,128]{1,0:T(8,128)(2,1)S(1)}, u32[]{:S(2)}, u32[]{:S(2)}) collective-permute-start(bf16[64,128]{1,0:T(8,128)(2,1)S(1)} %get-tuple-element.53), channel_id=1, source_target_pairs={{0,8},{4,12},{8,0},{12,4},{16,24},{20,28},{24,16},{28,20},{1,9},{5... | collective-permute-start | bytes 49160 | tf_op jit(solution)/shard_map/ppermute | solution.py:453
  28.0 2.9 %collective-permute-start.12 = (bf16[64,128]{1,0:T(8,128)(2,1)S(1)}, bf16[64,128]{1,0:T(8,128)(2,1)S(1)}, u32[]{:S(2)}, u32[]{:S(2)}) collective-permute-start(bf16[64,128]{1,0:T(8,128)(2,1)S(1)} %get-tuple-element.54), channel_id=1, source_target_pairs={{0,4},{4,0},{8,12},{12,8},{16,20},{20,16},{24,28},{28,24},{1,5},{5... | collective-permute-start | bytes 49160 | tf_op jit(solution)/shard_map/ppermute | solution.py:453
  33.5 7.9 %collective-permute-start.15 = (bf16[128,256]{1,0:T(8,128)(2,1)S(1)}, bf16[128,256]{1,0:T(8,128)(2,1)S(1)}, u32[]{:S(2)}, u32[]{:S(2)}) collective-permute-start(bf16[128,256]{1,0:T(8,128)(2,1)S(1)} %get-tuple-element.55.refs_0_), channel_id=1, source_target_pairs={{0,2},{1,3},{2,0},{3,1},{4,6},{5,7},{6,4},{7,5},{8,10},{9,11},{10,... | collective-permute-start | bytes 196616 | tf_op jit(solution)/shard_map/ppermute | solution.py:371
  33.5 7.8 %collective-permute-start.14 = (bf16[128,256]{1,0:T(8,128)(2,1)S(1)}, bf16[128,256]{1,0:T(8,128)(2,1)S(1)}, u32[]{:S(2)}, u32[]{:S(2)}) collective-permute-start(bf16[128,256]{1,0:T(8,128)(2,1)S(1)} %get-tuple-element.55.refs_0_), channel_id=1, source_target_pairs={{0,3},{1,2},{2,1},{3,0},{4,7},{5,6},{6,5},{7,4},{8,11},{9,10},{10,... | collective-permute-start | bytes 196616 | tf_op jit(solution)/shard_map/ppermute | solution.py:371
  36.3 6.1 %collective-permute-start.13 = (bf16[128,256]{1,0:T(8,128)(2,1)S(1)}, bf16[128,256]{1,0:T(8,128)(2,1)S(1)}, u32[]{:S(2)}, u32[]{:S(2)}) collective-permute-start(bf16[128,256]{1,0:T(8,128)(2,1)S(1)} %get-tuple-element.55.refs_0_), channel_id=1, source_target_pairs={{0,1},{1,0},{2,3},{3,2},{4,5},{5,4},{6,7},{7,6},{8,9},{9,8},{10,11... | collective-permute-start | bytes 196616 | tf_op jit(solution)/shard_map/ppermute | solution.py:371

commit v10 on v9

--- a/solution.py
+++ b/solution.py
@@ -20,6 +20,11 @@
 
 def silu(value):
     halved = 0.5 * value
+    return halved + halved * jnp.tanh(halved)
+
+
+def narrow_silu(value):
+    halved = value.astype(jnp.bfloat16) * jnp.bfloat16(0.5)
     return halved + halved * jnp.tanh(halved)
 
 
@@ -61,40 +66,30 @@
     return space(tuple(shape), dtype)
 
 
-def narrow_kernel(
-    edges_hbm, weight_hbm, down_hbm, out_ref, edges_ref, weight_ref, down_ref, sems
-):
+def narrow_kernel(edges_hbm, weight_hbm, down_hbm, out_ref, edges_ref, weight_ref, down_ref, sems):
     half = edges_hbm.shape[0] // 2
-    pieces = [
-        slice(base + rows.start, base + rows.stop)
-        for rows in row_chunks(half, LONG)
-        for base in (0, half)
-    ]
-    copies = [
-        pltpu.make_async_copy(weight_hbm, weight_ref, sems.at[0]),
-        pltpu.make_async_copy(down_hbm, down_ref, sems.at[1]),
-    ] + [
-        pltpu.make_async_copy(edges_hbm.at[piece], edges_ref.at[piece], sems.at[2 + at])
-        for at, piece in enumerate(pieces)
-    ]
-    for copy in [copies[0], copies[2], copies[3], copies[1]] + copies[4:]:
+    cut = weight_hbm.shape[0] // 2
+    copies = [pltpu.make_async_copy(down_hbm, down_ref, sems.at[0])]
+    for at, rows in enumerate((slice(0, cut), slice(cut, 2 * cut))):
+        copies.append(pltpu.make_async_copy(weight_hbm.at[rows], weight_ref.at[rows], sems.at[1 + at]))
+    pieces = row_chunks(2 * half)
+    for at, rows in enumerate(pieces):
+        copies.append(pltpu.make_async_copy(edges_hbm.at[rows], edges_ref.at[rows], sems.at[3 + at]))
+    for copy in copies[1:] + copies[:1]:
         copy.start()
-    copies[0].wait()
-    copies[1].wait()
-    for at, rows in enumerate(row_chunks(half, LONG)):
-        copies[2 + 2 * at].wait()
-        copies[3 + 2 * at].wait()
-        hidden = [
-            silu(product(edges_ref[piece, :], weight_ref[...])).astype(jnp.bfloat16)
-            for piece in pieces[2 * at : 2 * at + 2]
-        ]
-        sides = [
-            lax.dot_general(
-                each, down_ref[...], (((1,), (1,)), ((), ())), preferred_element_type=jnp.float32
-            )
-            for each in hidden
-        ]
-        out_ref[rows, :] = silu(jnp.concatenate(sides, axis=1)).astype(jnp.bfloat16)
+    for copy in copies:
+        copy.wait()
+    hidden = [
+        narrow_silu(product(edges_ref[side * half : (side + 1) * half, :], weight_ref[...]))
+        for side in range(2)
+    ]
+    sides = [
+        lax.dot_general(
+            each, down_ref[...], (((1,), (1,)), ((), ())), preferred_element_type=jnp.float32
+        )
+        for each in hidden
+    ]
+    out_ref[...] = silu(jnp.concatenate(sides, axis=1)).astype(jnp.bfloat16)
 
 
 def one_hot(shape, axis, chosen):
@@ -280,12 +275,12 @@
             for rows, each in zip(group, picked)
         ]
         for layer in range(residual_ref.shape[0]):
-            middles = [
-                silu(product(each, residual_ref[layer, 0])).astype(jnp.bfloat16) for each in states
-            ]
-            branches = [silu(product(each, residual_ref[layer, 1])) for each in middles]
+            middles = [narrow_silu(product(each, residual_ref[layer, 0])) for each in states]
+            branches = [narrow_silu(product(each, residual_ref[layer, 1])) for each in middles]
             states = [
-                ((each.astype(jnp.float32) + branch) * root_half).astype(jnp.bfloat16)
+                (
+                    (each.astype(jnp.float32) + branch.astype(jnp.float32)) * root_half
+                ).astype(jnp.bfloat16)
                 for each, branch in zip(states, branches)
             ]
         for rows, each in zip(group, states):
@@ -349,7 +344,8 @@
         found = [product(chosen_ref[rows, :], table_ref[...]) + side_ref[rows, :] for rows in group]
         for at, (rows, each) in enumerate(zip(group, found)):
             state = state_ref[rows, :].astype(jnp.float32)
-            edges_ref[rows, :] = ((state + silu(each)) * root_half).astype(jnp.bfloat16)
+            update = narrow_silu(each).astype(jnp.float32)
+            edges_ref[rows, :] = ((state + update) * root_half).astype(jnp.bfloat16)
             copies.append(
                 pltpu.make_async_copy(
                     edges_ref.at[rows], edges_hbm.at[rows], sems.at[1 + first + at]
@@ -409,7 +405,7 @@
             pltpu.VMEM(edges.shape, jnp.bfloat16),
             pltpu.VMEM(weight_edge.shape, jnp.bfloat16),
             pltpu.VMEM(weight_down.shape, jnp.bfloat16),
-            pltpu.SemaphoreType.DMA((2 + 2 * len(row_chunks(lines, LONG)),)),
+            pltpu.SemaphoreType.DMA((3 + len(row_chunks(rows)),)),
         ],
         flops=2 * rows * wide * (wide + channels),
         nbytes=2 * (rows * wide + wide * wide),

time: 44.6 us -> 44.2 us (level)
  no operation moved by 1% of the time
where the time goes in v10:
time: 44.2 us; the launch traced here: 44 us
  starting transfers between devices  20.1 us (45%)
  Pallas kernels  14.6 us (33%)
  waiting for transfers between devices  8.51 us (19%)
  between operations  0.74 us (2%)
    pallas_call x7, Pallas kernels, call(): pl.pallas_call(kernel, out_shape=outs, in_specs=[pl.BlockSpec(memory_spac...  14.6 us
    ppermute x9, starting transfers between devices, from_others(): lax.ppermute(value, 'edge', [(at, at ^ by) for at in range(len(order))])  13.8 us
    ppermute x9, waiting for transfers between devices, from_others(): lax.ppermute(value, 'edge', [(at, at ^ by) for at in range(len(order))])  7.12 us
    ppermute x7, starting transfers between devices, body(): lax.ppermute(block, 'dom', [(at, at ^ partners - place) for at in range(d...  6.32 us
    ppermute x7, waiting for transfers between devices, body(): lax.ppermute(block, 'dom', [(at, at ^ partners - place) for at in range(d...  1.4 us
  transfers between devices with their start and end apart: 16, of which 5 were waited for; matrix products, arithmetic and copies ran while one was open for 0% of the time, Pallas kernels for 18%

profile of v10, /device:TPU:0, one launch (start us, length us, event | category | flops | bytes accessed | tf_op | source)
XLA Modules:
  0.0 44.0 jit_solution(12454179428178944457)
XLA Ops:
  0.7 2.5 %shard_map.141.refs_2_ = bf16[512,128]{1,0:T(8,128)(2,1)S(1)} custom-call(bf16[1024,512]{1,0:T(8,128)(2,1)} %edges_hbm.1, bf16[512,512]{1,0:T(8,128)(2,1)} %weight_hbm.1, bf16[64,512]{1,0:T(8,128)(2,1)} %down_hbm.1), custom_call_target="tpu_custom_call" | custom-call | flops 603979776 | bytes 1572864 | tf_op jit(solution)/shard_map/pallas_call | solution.py:49
  3.2 5.1 %collective-permute-start.2 = (bf16[512,128]{1,0:T(8,128)(2,1)S(1)}, bf16[512,128]{1,0:T(8,128)(2,1)S(1)}, u32[]{:S(2)}, u32[]{:S(2)}) collective-permute-start(bf16[512,128]{1,0:T(8,128)(2,1)S(1)} %shard_map.141.refs_2_), channel_id=1, source_target_pairs={{0,3},{1,2},{2,1},{3,0},{4,7},{5,6},{6,5},{7,4},{8,11},{9,10},{10,... | collective-permute-start | bytes 393224 | tf_op jit(solution)/shard_map/ppermute | solution.py:367
  8.3 0.0 collective-permute-start.1
  8.3 0.6 %collective-permute-start = (bf16[512,128]{1,0:T(8,128)(2,1)S(1)}, bf16[512,128]{1,0:T(8,128)(2,1)S(1)}, u32[]{:S(2)}, u32[]{:S(2)}) collective-permute-start(bf16[512,128]{1,0:T(8,128)(2,1)S(1)} %shard_map.141.refs_2_), channel_id=1, source_target_pairs={{0,1},{1,0},{2,3},{3,2},{4,5},{5,4},{6,7},{7,6},{8,9},{9,8},{10,11... | collective-permute-start | bytes 393224 | tf_op jit(solution)/shard_map/ppermute | solution.py:367
  8.9 2.3 %collective-permute-start.4 = (bf16[32,256]{1,0:T(8,128)(2,1)S(1)}, bf16[32,256]{1,0:T(8,128)(2,1)S(1)}, u32[]{:S(2)}, u32[]{:S(2)}) collective-permute-start(bf16[32,256]{1,0:T(8,128)(2,1)S(1)} %copy-done), channel_id=1, source_target_pairs={{0,2},{1,3},{2,0},{3,1},{4,6},{5,7},{6,4},{7,5},{8,10},{9,11},{10,... | collective-permute-start | bytes 49160 | tf_op jit(solution)/shard_map/ppermute | solution.py:367
  11.2 2.0 %collective-permute-start.3 = (bf16[32,256]{1,0:T(8,128)(2,1)S(1)}, bf16[32,256]{1,0:T(8,128)(2,1)S(1)}, u32[]{:S(2)}, u32[]{:S(2)}) collective-permute-start(bf16[32,256]{1,0:T(8,128)(2,1)S(1)} %copy-done), channel_id=1, source_target_pairs={{0,1},{1,0},{2,3},{3,2},{4,5},{5,4},{6,7},{7,6},{8,9},{9,8},{10,11... | collective-permute-start | bytes 49160 | tf_op jit(solution)/shard_map/ppermute | solution.py:367
  13.2 0.1 copy.15.refs_0_
  13.3 3.9 %shard_map.140 = (bf16[896,256]{1,0:T(8,128)(2,1)S(1)}, bf16[896,256]{1,0:T(8,128)(2,1)S(1)}, bf16[1024,256]{1,0:T(8,128)(2,1)S(1)}, bf16[1024,256]{1,0:T(8,128)...) custom-call(s32[1,1024]{1,0:T(1,128)S(1)} %bitcast.1, ...), custom_call_target="tpu_custom_call" | custom-call | flops 41943040 | bytes 6291456 | tf_op jit(solution)/shard_map/pallas_call | solution.py:49
  17.2 0.1 collective-permute-start.5
  17.3 2.7 %collective-permute-done.1.refs_4_ = bf16[512,128]{1,0:T(8,128)(2,1)S(1)} collective-permute-done((bf16[512,128]{1,0:T(8,128)(2,1)S(1)}, bf16[512,128]{1,0:T(8,128)(2,1)S(1)}, u32[]{:S(2)}, u32[]{:S(2)}) %collective-permute-start.1) | collective-permute-done | bytes 131104 | tf_op jit(solution)/shard_map/ppermute | solution.py:367
  20.0 0.0 collective-permute-done.refs_3_
  20.0 1.8 %shard_map.142 = (bf16[256,256]{1,0:T(8,128)(2,1)S(1)}, bf16[64,128]{1,0:T(8,128)(2,1)S(1)}, bf16[64,128]{1,0:T(8,128)(2,1)S(1)}, bf16[64,128]{1,0:T(8,128)(2,1)...) custom-call(s32[16,2]{1,0:T(8,128)S(1)} %copy.15.refs_0_, ...), custom_call_target="tpu_custom_call" | custom-call | flops 134217728 | bytes 2097152 | tf_op jit(solution)/shard_map/pallas_call | solution.py:49
  21.8 0.9 %collective-permute-start.6 = (bf16[64,128]{1,0:T(8,128)(2,1)S(1)}, bf16[64,128]{1,0:T(8,128)(2,1)S(1)}, u32[]{:S(2)}, u32[]{:S(2)}) collective-permute-start(bf16[64,128]{1,0:T(8,128)(2,1)S(1)} %get-tuple-element.48), channel_id=1, source_target_pairs={{0,28},{4,24},{8,20},{12,16},{16,12},{20,8},{24,4},{28,0},{1,29},{... | collective-permute-start | bytes 49160 | tf_op jit(solution)/shard_map/ppermute | solution.py:449
  22.8 1.7 %collective-permute-start.7 = (bf16[64,128]{1,0:T(8,128)(2,1)S(1)}, bf16[64,128]{1,0:T(8,128)(2,1)S(1)}, u32[]{:S(2)}, u32[]{:S(2)}) collective-permute-start(bf16[64,128]{1,0:T(8,128)(2,1)S(1)} %get-tuple-element.49), channel_id=1, source_target_pairs={{0,24},{4,28},{8,16},{12,20},{16,8},{20,12},{24,0},{28,4},{1,25},{... | collective-permute-start | bytes 49160 | tf_op jit(solution)/shard_map/ppermute | solution.py:449
  24.4 0.0 collective-permute-done.4.refs_8_
  24.4 1.4 %collective-permute-start.8 = (bf16[64,128]{1,0:T(8,128)(2,1)S(1)}, bf16[64,128]{1,0:T(8,128)(2,1)S(1)}, u32[]{:S(2)}, u32[]{:S(2)}) collective-permute-start(bf16[64,128]{1,0:T(8,128)(2,1)S(1)} %get-tuple-element.50), channel_id=1, source_target_pairs={{0,20},{4,16},{8,28},{12,24},{16,4},{20,0},{24,12},{28,8},{1,21},{... | collective-permute-start | bytes 49160 | tf_op jit(solution)/shard_map/ppermute | solution.py:449
  25.8 0.0 collective-permute-done.3.refs_7_
  25.8 0.5 %collective-permute-start.9 = (bf16[64,128]{1,0:T(8,128)(2,1)S(1)}, bf16[64,128]{1,0:T(8,128)(2,1)S(1)}, u32[]{:S(2)}, u32[]{:S(2)}) collective-permute-start(bf16[64,128]{1,0:T(8,128)(2,1)S(1)} %get-tuple-element.51), channel_id=1, source_target_pairs={{0,16},{4,20},{8,24},{12,28},{16,0},{20,4},{24,8},{28,12},{1,17},{... | collective-permute-start | bytes 49160 | tf_op jit(solution)/shard_map/ppermute | solution.py:449
  26.3 0.8 %collective-permute-start.10 = (bf16[64,128]{1,0:T(8,128)(2,1)S(1)}, bf16[64,128]{1,0:T(8,128)(2,1)S(1)}, u32[]{:S(2)}, u32[]{:S(2)}) collective-permute-start(bf16[64,128]{1,0:T(8,128)(2,1)S(1)} %get-tuple-element.52), channel_id=1, source_target_pairs={{0,12},{4,8},{8,4},{12,0},{16,28},{20,24},{24,20},{28,16},{1,13},{... | collective-permute-start | bytes 49160 | tf_op jit(solution)/shard_map/ppermute | solution.py:449
  27.1 0.9 %collective-permute-start.11 = (bf16[64,128]{1,0:T(8,128)(2,1)S(1)}, bf16[64,128]{1,0:T(8,128)(2,1)S(1)}, u32[]{:S(2)}, u32[]{:S(2)}) collective-permute-start(bf16[64,128]{1,0:T(8,128)(2,1)S(1)} %get-tuple-element.53), channel_id=1, source_target_pairs={{0,8},{4,12},{8,0},{12,4},{16,24},{20,28},{24,16},{28,20},{1,9},{5... | collective-permute-start | bytes 49160 | tf_op jit(solution)/shard_map/ppermute | solution.py:449
  27.9 0.2 collective-permute-start.12
  28.2 1.3 %shard_map.143 = (f32[1024,512]{1,0:T(8,128)S(1)}, bf16[128,256]{1,0:T(8,128)(2,1)S(1)}) custom-call(bf16[1024,512]{1,0:T(8,128)(2,1)S(1)} %get-tuple-element.33.refs_0_, bf16[256,256]{1,0:T(8,128)(2,1)S(1)} %get-tuple-element.37.refs_1_, bf16[1024,256]{1,0:T(8,128)(2,1)S(1)} %get-tuple-element.38.refs_2_, bf16[1024,256]{1,0:T(8,128)(2,1)S(1)} %get-tuple-element.39.refs_3_, ...), custom_call_target="tpu_custom_call" | custom-call | flops 268435456 | bytes 5242880 | tf_op jit(solution)/shard_map/pallas_call | solution.py:49
  29.5 0.1 collective-permute-done.9.refs_10_
  29.5 1.3 %collective-permute-done.11.refs_12_ = bf16[64,128]{1,0:T(8,128)(2,1)S(1)} collective-permute-done((bf16[64,128]{1,0:T(8,128)(2,1)S(1)}, bf16[64,128]{1,0:T(8,128)(2,1)S(1)}, u32[]{:S(2)}, u32[]{:S(2)}) %collective-permute-start.11) | collective-permute-done | bytes 16416 | tf_op jit(solution)/shard_map/ppermute | solution.py:449
  30.9 2.3 %shard_map.144 = (bf16[1024,512]{1,0:T(8,128)(2,1)S(1)}, bf16[128,256]{1,0:T(8,128)(2,1)S(1)}) custom-call(f32[1024,512]{1,0:T(8,128)S(1)} %get-tuple-element.42.refs_0_, bf16[1024,256]{1,0:T(8,128)(2,1)S(1)} %get-tuple-element.43.refs_1_, bf16[1024,256]{1,0:T(8,128)(2,1)S(1)} %get-tuple-element.44.refs_2_, ...), custom_call_target="tpu_custom_call" | custom-call | flops 1073741824 | bytes 4194304 | tf_op jit(solution)/shard_map/pallas_call | solution.py:49
  33.2 0.1 collective-permute-start.15
  33.3 2.7 %collective-permute-start.14 = (bf16[128,256]{1,0:T(8,128)(2,1)S(1)}, bf16[128,256]{1,0:T(8,128)(2,1)S(1)}, u32[]{:S(2)}, u32[]{:S(2)}) collective-permute-start(bf16[128,256]{1,0:T(8,128)(2,1)S(1)} %get-tuple-element.55.refs_0_), channel_id=1, source_target_pairs={{0,3},{1,2},{2,1},{3,0},{4,7},{5,6},{6,5},{7,4},{8,11},{9,10},{10,... | collective-permute-start | bytes 196616 | tf_op jit(solution)/shard_map/ppermute | solution.py:367
  36.0 0.8 %collective-permute-start.13 = (bf16[128,256]{1,0:T(8,128)(2,1)S(1)}, bf16[128,256]{1,0:T(8,128)(2,1)S(1)}, u32[]{:S(2)}, u32[]{:S(2)}) collective-permute-start(bf16[128,256]{1,0:T(8,128)(2,1)S(1)} %get-tuple-element.55.refs_0_), channel_id=1, source_target_pairs={{0,1},{1,0},{2,3},{3,2},{4,5},{5,4},{6,7},{7,6},{8,9},{9,8},{10,11... | collective-permute-start | bytes 196616 | tf_op jit(solution)/shard_map/ppermute | solution.py:367
  36.7 1.0 %shard_map.145 = (f32[1024,512]{1,0:T(8,128)S(1)}, bf16[1024,256]{1,0:T(8,128)(2,1)S(1)}, f32[256,512]{1,0:T(8,128)S(1)}, bf16[512,512]{1,0:T(8,128)(2,1)S(1)}) custom-call(bf16[1024,512]{1,0:T(8,128)(2,1)S(1)} %get-tuple-element.58.refs_0_.refs_6_, bf16[1024,512]{1,0:T(8,128)(2,1)S(1)} %get-tuple-element.59.refs_1_, ...), custom_call_target="tpu_custom_call" | custom-call | flops 536870912 | bytes 4194304 | tf_op jit(solution)/shard_map/pallas_call | solution.py:49
  37.7 3.3 %collective-permute-done.15.refs_3_ = bf16[128,256]{1,0:T(8,128)(2,1)S(1)} collective-permute-done((bf16[128,256]{1,0:T(8,128)(2,1)S(1)}, bf16[128,256]{1,0:T(8,128)(2,1)S(1)}, u32[]{:S(2)}, u32[]{:S(2)}) %collective-permute-start.15) | collective-permute-done | bytes 65568 | tf_op jit(solution)/shard_map/ppermute | solution.py:367
  41.1 1.1 %collective-permute-done.13.refs_1_ = bf16[128,256]{1,0:T(8,128)(2,1)S(1)} collective-permute-done((bf16[128,256]{1,0:T(8,128)(2,1)S(1)}, bf16[128,256]{1,0:T(8,128)(2,1)S(1)}, u32[]{:S(2)}, u32[]{:S(2)}) %collective-permute-start.13) | collective-permute-done | bytes 65568 | tf_op jit(solution)/shard_map/ppermute | solution.py:367
  42.1 1.9 %shard_map.146 = (bf16[1024,512]{1,0:T(8,128)(2,1)}, bf16[32,256]{1,0:T(8,128)(2,1)}) custom-call(bf16[128,256]{1,0:T(8,128)(2,1)S(1)} %get-tuple-element.55.refs_0_, bf16[128,256]{1,0:T(8,128)(2,1)S(1)} %collective-permute-done.13.refs_1_, bf16[128,256]{1,0:T(8,128)(2,1)S(1)} %collective-permute-done.14.refs_2_, ...), custom_call_target="tpu_custom_call" | custom-call | flops 268435456 | bytes 4194304 | tf_op jit(solution)/shard_map/pallas_call | solution.py:49
  (14 shorter events, 0.0 us)
Async XLA Ops:
  0.6 8.3 %copy-start = (bf16[32,256]{1,0:T(8,128)(2,1)S(1)}, bf16[32,256]{1,0:T(8,128)(2,1)}, u32[]{:S(2)}) copy-start(bf16[32,256]{1,0:T(8,128)(2,1)} %refs_6_.3) | copy-start | bytes 49156
  0.6 12.6 %copy-start.2 = (s32[16,2]{0,1:T(2,128)S(1)}, s32[16,2]{0,1:T(2,128)}, u32[]{:S(2)}) copy-start(s32[16,2]{0,1:T(2,128)} %param.17) | copy-start | bytes 388
  0.7 12.7 %copy-start.1 = (s32[1024]{0:T(1024)S(1)}, s32[1024]{0:T(1024)}, u32[]{:S(2)}) copy-start(s32[1024]{0:T(1024)} %param.15) | copy-start | bytes 12292
  3.2 14.0 %collective-permute-start.2 = (bf16[512,128]{1,0:T(8,128)(2,1)S(1)}, bf16[512,128]{1,0:T(8,128)(2,1)S(1)}, u32[]{:S(2)}, u32[]{:S(2)}) collective-permute-start(bf16[512,128]{1,0:T(8,128)(2,1)S(1)} %shard_map.141.refs_2_), channel_id=1, source_target_pairs={{0,3},{1,2},{2,1},{3,0},{4,7},{5,6},{6,5},{7,4},{8,11},{9,10},{10,... | collective-permute-start | bytes 393224 | tf_op jit(solution)/shard_map/ppermute | solution.py:367
  8.3 11.8 %collective-permute-start.1 = (bf16[512,128]{1,0:T(8,128)(2,1)S(1)}, bf16[512,128]{1,0:T(8,128)(2,1)S(1)}, u32[]{:S(2)}, u32[]{:S(2)}) collective-permute-start(bf16[512,128]{1,0:T(8,128)(2,1)S(1)} %shard_map.141.refs_2_), channel_id=1, source_target_pairs={{0,2},{1,3},{2,0},{3,1},{4,6},{5,7},{6,4},{7,5},{8,10},{9,11},{10,... | collective-permute-start | bytes 393224 | tf_op jit(solution)/shard_map/ppermute | solution.py:367
  8.3 11.8 %collective-permute-start = (bf16[512,128]{1,0:T(8,128)(2,1)S(1)}, bf16[512,128]{1,0:T(8,128)(2,1)S(1)}, u32[]{:S(2)}, u32[]{:S(2)}) collective-permute-start(bf16[512,128]{1,0:T(8,128)(2,1)S(1)} %shard_map.141.refs_2_), channel_id=1, source_target_pairs={{0,1},{1,0},{2,3},{3,2},{4,5},{5,4},{6,7},{7,6},{8,9},{9,8},{10,11... | collective-permute-start | bytes 393224 | tf_op jit(solution)/shard_map/ppermute | solution.py:367
  8.9 15.5 %collective-permute-start.4 = (bf16[32,256]{1,0:T(8,128)(2,1)S(1)}, bf16[32,256]{1,0:T(8,128)(2,1)S(1)}, u32[]{:S(2)}, u32[]{:S(2)}) collective-permute-start(bf16[32,256]{1,0:T(8,128)(2,1)S(1)} %copy-done), channel_id=1, source_target_pairs={{0,2},{1,3},{2,0},{3,1},{4,6},{5,7},{6,4},{7,5},{8,10},{9,11},{10,... | collective-permute-start | bytes 49160 | tf_op jit(solution)/shard_map/ppermute | solution.py:367
  11.2 14.6 %collective-permute-start.3 = (bf16[32,256]{1,0:T(8,128)(2,1)S(1)}, bf16[32,256]{1,0:T(8,128)(2,1)S(1)}, u32[]{:S(2)}, u32[]{:S(2)}) collective-permute-start(bf16[32,256]{1,0:T(8,128)(2,1)S(1)} %copy-done), channel_id=1, source_target_pairs={{0,1},{1,0},{2,3},{3,2},{4,5},{5,4},{6,7},{7,6},{8,9},{9,8},{10,11... | collective-permute-start | bytes 49160 | tf_op jit(solution)/shard_map/ppermute | solution.py:367
  17.2 9.1 %collective-permute-start.5 = (bf16[32,256]{1,0:T(8,128)(2,1)S(1)}, bf16[32,256]{1,0:T(8,128)(2,1)S(1)}, u32[]{:S(2)}, u32[]{:S(2)}) collective-permute-start(bf16[32,256]{1,0:T(8,128)(2,1)S(1)} %copy-done), channel_id=1, source_target_pairs={{0,3},{1,2},{2,1},{3,0},{4,7},{5,6},{6,5},{7,4},{8,11},{9,10},{10,... | collective-permute-start | bytes 49160 | tf_op jit(solution)/shard_map/ppermute | solution.py:367
  21.8 5.2 %collective-permute-start.6 = (bf16[64,128]{1,0:T(8,128)(2,1)S(1)}, bf16[64,128]{1,0:T(8,128)(2,1)S(1)}, u32[]{:S(2)}, u32[]{:S(2)}) collective-permute-start(bf16[64,128]{1,0:T(8,128)(2,1)S(1)} %get-tuple-element.48), channel_id=1, source_target_pairs={{0,28},{4,24},{8,20},{12,16},{16,12},{20,8},{24,4},{28,0},{1,29},{... | collective-permute-start | bytes 49160 | tf_op jit(solution)/shard_map/ppermute | solution.py:449
  22.8 5.2 %collective-permute-start.7 = (bf16[64,128]{1,0:T(8,128)(2,1)S(1)}, bf16[64,128]{1,0:T(8,128)(2,1)S(1)}, u32[]{:S(2)}, u32[]{:S(2)}) collective-permute-start(bf16[64,128]{1,0:T(8,128)(2,1)S(1)} %get-tuple-element.49), channel_id=1, source_target_pairs={{0,24},{4,28},{8,16},{12,20},{16,8},{20,12},{24,0},{28,4},{1,25},{... | collective-permute-start | bytes 49160 | tf_op jit(solution)/shard_map/ppermute | solution.py:449
  24.4 5.0 %collective-permute-start.8 = (bf16[64,128]{1,0:T(8,128)(2,1)S(1)}, bf16[64,128]{1,0:T(8,128)(2,1)S(1)}, u32[]{:S(2)}, u32[]{:S(2)}) collective-permute-start(bf16[64,128]{1,0:T(8,128)(2,1)S(1)} %get-tuple-element.50), channel_id=1, source_target_pairs={{0,20},{4,16},{8,28},{12,24},{16,4},{20,0},{24,12},{28,8},{1,21},{... | collective-permute-start | bytes 49160 | tf_op jit(solution)/shard_map/ppermute | solution.py:449
  25.8 3.7 %collective-permute-start.9 = (bf16[64,128]{1,0:T(8,128)(2,1)S(1)}, bf16[64,128]{1,0:T(8,128)(2,1)S(1)}, u32[]{:S(2)}, u32[]{:S(2)}) collective-permute-start(bf16[64,128]{1,0:T(8,128)(2,1)S(1)} %get-tuple-element.51), channel_id=1, source_target_pairs={{0,16},{4,20},{8,24},{12,28},{16,0},{20,4},{24,8},{28,12},{1,17},{... | collective-permute-start | bytes 49160 | tf_op jit(solution)/shard_map/ppermute | solution.py:449
  26.3 3.2 %collective-permute-start.10 = (bf16[64,128]{1,0:T(8,128)(2,1)S(1)}, bf16[64,128]{1,0:T(8,128)(2,1)S(1)}, u32[]{:S(2)}, u32[]{:S(2)}) collective-permute-start(bf16[64,128]{1,0:T(8,128)(2,1)S(1)} %get-tuple-element.52), channel_id=1, source_target_pairs={{0,12},{4,8},{8,4},{12,0},{16,28},{20,24},{24,20},{28,16},{1,13},{... | collective-permute-start | bytes 49160 | tf_op jit(solution)/shard_map/ppermute | solution.py:449
  27.1 3.8 %collective-permute-start.11 = (bf16[64,128]{1,0:T(8,128)(2,1)S(1)}, bf16[64,128]{1,0:T(8,128)(2,1)S(1)}, u32[]{:S(2)}, u32[]{:S(2)}) collective-permute-start(bf16[64,128]{1,0:T(8,128)(2,1)S(1)} %get-tuple-element.53), channel_id=1, source_target_pairs={{0,8},{4,12},{8,0},{12,4},{16,24},{20,28},{24,16},{28,20},{1,9},{5... | collective-permute-start | bytes 49160 | tf_op jit(solution)/shard_map/ppermute | solution.py:449
  27.9 2.9 %collective-permute-start.12 = (bf16[64,128]{1,0:T(8,128)(2,1)S(1)}, bf16[64,128]{1,0:T(8,128)(2,1)S(1)}, u32[]{:S(2)}, u32[]{:S(2)}) collective-permute-start(bf16[64,128]{1,0:T(8,128)(2,1)S(1)} %get-tuple-element.54), channel_id=1, source_target_pairs={{0,4},{4,0},{8,12},{12,8},{16,20},{20,16},{24,28},{28,24},{1,5},{5... | collective-permute-start | bytes 49160 | tf_op jit(solution)/shard_map/ppermute | solution.py:449
  33.2 7.9 %collective-permute-start.15 = (bf16[128,256]{1,0:T(8,128)(2,1)S(1)}, bf16[128,256]{1,0:T(8,128)(2,1)S(1)}, u32[]{:S(2)}, u32[]{:S(2)}) collective-permute-start(bf16[128,256]{1,0:T(8,128)(2,1)S(1)} %get-tuple-element.55.refs_0_), channel_id=1, source_target_pairs={{0,2},{1,3},{2,0},{3,1},{4,6},{5,7},{6,4},{7,5},{8,10},{9,11},{10,... | collective-permute-start | bytes 196616 | tf_op jit(solution)/shard_map/ppermute | solution.py:367
  33.3 7.8 %collective-permute-start.14 = (bf16[128,256]{1,0:T(8,128)(2,1)S(1)}, bf16[128,256]{1,0:T(8,128)(2,1)S(1)}, u32[]{:S(2)}, u32[]{:S(2)}) collective-permute-start(bf16[128,256]{1,0:T(8,128)(2,1)S(1)} %get-tuple-element.55.refs_0_), channel_id=1, source_target_pairs={{0,3},{1,2},{2,1},{3,0},{4,7},{5,6},{6,5},{7,4},{8,11},{9,10},{10,... | collective-permute-start | bytes 196616 | tf_op jit(solution)/shard_map/ppermute | solution.py:367
  36.0 6.1 %collective-permute-start.13 = (bf16[128,256]{1,0:T(8,128)(2,1)S(1)}, bf16[128,256]{1,0:T(8,128)(2,1)S(1)}, u32[]{:S(2)}, u32[]{:S(2)}) collective-permute-start(bf16[128,256]{1,0:T(8,128)(2,1)S(1)} %get-tuple-element.55.refs_0_), channel_id=1, source_target_pairs={{0,1},{1,0},{2,3},{3,2},{4,5},{5,4},{6,7},{7,6},{8,9},{9,8},{10,11... | collective-permute-start | bytes 196616 | tf_op jit(solution)/shard_map/ppermute | solution.py:367

commit v11 on v10

--- a/solution.py
+++ b/solution.py
@@ -180,31 +180,26 @@
 
 
 def mix_kernel(shards, *refs):
-    source_ref, tiles_ref = refs[:2]
-    parts = refs[2 : 2 + shards]
-    send_ref, mask_ref, trip_ref = refs[2 + shards : 5 + shards]
-    out_refs = refs[5 + shards : -1]
+    start_ref, upper_ref, tiles_ref = refs[:3]
+    parts = refs[3 : 3 + shards]
+    send_ref, mask_ref, trip_ref = refs[3 + shards : 6 + shards]
+    out_refs = refs[6 + shards : -1]
     held_ref = refs[-1]
     blocks, block_len, width = tiles_ref.shape
     count = width // block_len
     lines = held_ref.shape[0] // shards
-    me = lax.axis_index("edge")
     for part, at in zip(parts, orders(shards)[0]):
         held_ref[at * lines : (at + 1) * lines, :] = part[...]
-    half_blocks = blocks // 2
     channels = trip_ref.shape[1] // GROUPS
     per = blocks // GROUPS
 
     def mixed(block):
         picks = []
         for tile in range(count):
-            source = source_ref[block, tile]
-            shard = source // blocks
-            within = source - shard * blocks
-            upper = within // half_blocks
-            start = (shard ^ me) * lines + (within - upper * half_blocks) * block_len
-            rows = held_ref[pl.ds(pl.multiple_of(start, block_len), block_len), :]
-            picks.append(jnp.where(upper == 1, rows[:, channels:], rows[:, :channels]))
+            start = pl.multiple_of(start_ref[block * count + tile], block_len)
+            rows = held_ref[pl.ds(start, block_len), :]
+            upper = upper_ref[block * count + tile] == 1
+            picks.append(jnp.where(upper, rows[:, channels:], rows[:, :channels]))
         return product(tiles_ref[block], jnp.concatenate(picks, axis=0))
 
     for at in range(per):
@@ -436,11 +431,18 @@
         nbytes=6 * rows * rows,
     )
     weight_up, edges, tiles, weight_residual, weight_message, weight_join, weight_atom, atom_index = later
+    blocks, block_len = tiles.shape[:2]
+    source = tile_source.reshape(-1)
+    within = lax.rem(source, blocks)
+    upper = lax.div(within, blocks // 2)
+    start = (lax.div(source, blocks) ^ lax.axis_index("edge")) * lines + (
+        within - upper * (blocks // 2)
+    ) * block_len
     trip_out, *outgoing = call(
         functools.partial(mix_kernel, shards),
         (shaped((each, grouped)),) + (shaped((capacity // 2, packed)),) * partners,
-        (tile_source, tiles, *narrow_parts, send, send_mask),
-        smem=(0,),
+        (start, upper, tiles, *narrow_parts, send, send_mask),
+        smem=(0, 1),
         scratch=[pltpu.VMEM((shards * lines, packed), jnp.bfloat16)],
         flops=2 * rows * rows * channels,
         nbytes=2 * rows * rows,

time: 44.2 us -> 45.3 us (1.025)
  waiting for transfers between devices: 8.51 us -> 9.63 us
    ppermute x9, waiting for transfers between devices: 7.12 us -> 8.24 us  [from_others(): lax.ppermute(value, 'edge', [(at, at ^ by) for at in range(len(order))])]
  transfers between devices with their start and end apart: 16 -> 16, of which waited for: 5 -> 5; matrix products, arithmetic and copies ran while one was open for 0% -> 0% of each run, Pallas kernels for 18% -> 23%
where the time goes in v11:
time: 45.3 us; the launch traced here: 45.2 us
  starting transfers between devices  20.1 us (44%)
  Pallas kernels  14.4 us (32%)
  waiting for transfers between devices  9.63 us (21%)
  between operations  0.77 us (2%)
    pallas_call x7, Pallas kernels, call(): pl.pallas_call(kernel, out_shape=outs, in_specs=[pl.BlockSpec(memory_spac...  14.4 us
    ppermute x9, starting transfers between devices, from_others(): lax.ppermute(value, 'edge', [(at, at ^ by) for at in range(len(order))])  13.8 us
    ppermute x9, waiting for transfers between devices, from_others(): lax.ppermute(value, 'edge', [(at, at ^ by) for at in range(len(order))])  8.24 us
    ppermute x7, starting transfers between devices, body(): lax.ppermute(block, 'dom', [(at, at ^ partners - place) for at in range(d...  6.31 us
    ppermute x7, waiting for transfers between devices, body(): lax.ppermute(block, 'dom', [(at, at ^ partners - place) for at in range(d...  1.39 us
  transfers between devices with their start and end apart: 16, of which 5 were waited for; matrix products, arithmetic and copies ran while one was open for 0% of the time, Pallas kernels for 23%

profile of v11, /device:TPU:0, one launch (start us, length us, event | category | flops | bytes accessed | tf_op | source)
XLA Modules:
  0.0 45.2 jit_solution(2913539094767728978)
XLA Ops:
  0.7 4.1 %collective-permute-start.4 = (bf16[32,256]{1,0:T(8,128)(2,1)}, bf16[32,256]{1,0:T(8,128)(2,1)S(1)}, u32[]{:S(2)}, u32[]{:S(2)}) collective-permute-start(bf16[32,256]{1,0:T(8,128)(2,1)} %refs_6_.3), channel_id=1, source_target_pairs={{0,2},{1,3},{2,0},{3,1},{4,6},{5,7},{6,4},{7,5},{8,10},{9,11},{10,... | collective-permute-start | bytes 49160 | tf_op jit(solution)/shard_map/ppermute | solution.py:362
  4.8 1.6 %collective-permute-start.3 = (bf16[32,256]{1,0:T(8,128)(2,1)}, bf16[32,256]{1,0:T(8,128)(2,1)S(1)}, u32[]{:S(2)}, u32[]{:S(2)}) collective-permute-start(bf16[32,256]{1,0:T(8,128)(2,1)} %refs_6_.3), channel_id=1, source_target_pairs={{0,1},{1,0},{2,3},{3,2},{4,5},{5,4},{6,7},{7,6},{8,9},{9,8},{10,11... | collective-permute-start | bytes 49160 | tf_op jit(solution)/shard_map/ppermute | solution.py:362
  6.3 2.5 %shard_map.141.refs_3_ = bf16[512,128]{1,0:T(8,128)(2,1)S(1)} custom-call(bf16[1024,512]{1,0:T(8,128)(2,1)} %edges_hbm.1, bf16[512,512]{1,0:T(8,128)(2,1)} %weight_hbm.1, bf16[64,512]{1,0:T(8,128)(2,1)} %down_hbm.1), custom_call_target="tpu_custom_call" | custom-call | flops 603979776 | bytes 1572864 | tf_op jit(solution)/shard_map/pallas_call | solution.py:49
  8.8 0.0 copy-start
  8.8 0.1 collective-permute-start.2
  8.9 1.9 %collective-permute-start.1 = (bf16[512,128]{1,0:T(8,128)(2,1)S(1)}, bf16[512,128]{1,0:T(8,128)(2,1)S(1)}, u32[]{:S(2)}, u32[]{:S(2)}) collective-permute-start(bf16[512,128]{1,0:T(8,128)(2,1)S(1)} %shard_map.141.refs_3_), channel_id=1, source_target_pairs={{0,2},{1,3},{2,0},{3,1},{4,6},{5,7},{6,4},{7,5},{8,10},{9,11},{10,... | collective-permute-start | bytes 393224 | tf_op jit(solution)/shard_map/ppermute | solution.py:362
  10.8 2.5 %collective-permute-start = (bf16[512,128]{1,0:T(8,128)(2,1)S(1)}, bf16[512,128]{1,0:T(8,128)(2,1)S(1)}, u32[]{:S(2)}, u32[]{:S(2)}) collective-permute-start(bf16[512,128]{1,0:T(8,128)(2,1)S(1)} %shard_map.141.refs_3_), channel_id=1, source_target_pairs={{0,1},{1,0},{2,3},{3,2},{4,5},{5,4},{6,7},{7,6},{8,9},{9,8},{10,11... | collective-permute-start | bytes 393224 | tf_op jit(solution)/shard_map/ppermute | solution.py:362
  13.3 0.1 copy.16
  13.4 0.1 reshape.13
  13.5 3.9 %shard_map.140 = (bf16[896,256]{1,0:T(8,128)(2,1)S(1)}, bf16[896,256]{1,0:T(8,128)(2,1)S(1)}, bf16[1024,256]{1,0:T(8,128)(2,1)S(1)}, bf16[1024,256]{1,0:T(8,128)...) custom-call(s32[1,1024]{1,0:T(1,128)S(1)} %bitcast.1, ...), custom_call_target="tpu_custom_call" | custom-call | flops 41943040 | bytes 6291456 | tf_op jit(solution)/shard_map/pallas_call | solution.py:49
  17.4 0.1 collective-permute-start.5
  17.5 4.7 %collective-permute-done.1.refs_5_ = bf16[512,128]{1,0:T(8,128)(2,1)S(1)} collective-permute-done((bf16[512,128]{1,0:T(8,128)(2,1)S(1)}, bf16[512,128]{1,0:T(8,128)(2,1)S(1)}, u32[]{:S(2)}, u32[]{:S(2)}) %collective-permute-start.1) | collective-permute-done | bytes 131104 | tf_op jit(solution)/shard_map/ppermute | solution.py:362
  22.2 1.6 %shard_map.142 = (bf16[256,256]{1,0:T(8,128)(2,1)S(1)}, bf16[64,128]{1,0:T(8,128)(2,1)S(1)}, bf16[64,128]{1,0:T(8,128)(2,1)S(1)}, bf16[64,128]{1,0:T(8,128)(2,1)...) custom-call(s32[32]{0:T(128)S(1)} %get-tuple-element.64.refs_0_, ...), custom_call_target="tpu_custom_call" | custom-call | flops 134217728 | bytes 2097152 | tf_op jit(solution)/shard_map/pallas_call | solution.py:49
  23.8 0.1 collective-permute-start.6
  23.9 2.5 %collective-permute-start.7 = (bf16[64,128]{1,0:T(8,128)(2,1)S(1)}, bf16[64,128]{1,0:T(8,128)(2,1)S(1)}, u32[]{:S(2)}, u32[]{:S(2)}) collective-permute-start(bf16[64,128]{1,0:T(8,128)(2,1)S(1)} %get-tuple-element.49), channel_id=1, source_target_pairs={{0,24},{4,28},{8,16},{12,20},{16,8},{20,12},{24,0},{28,4},{1,25},{... | collective-permute-start | bytes 49160 | tf_op jit(solution)/shard_map/ppermute | solution.py:451
  26.4 0.0 collective-permute-done.4.refs_8_
  26.4 1.4 %collective-permute-start.8 = (bf16[64,128]{1,0:T(8,128)(2,1)S(1)}, bf16[64,128]{1,0:T(8,128)(2,1)S(1)}, u32[]{:S(2)}, u32[]{:S(2)}) collective-permute-start(bf16[64,128]{1,0:T(8,128)(2,1)S(1)} %get-tuple-element.50), channel_id=1, source_target_pairs={{0,20},{4,16},{8,28},{12,24},{16,4},{20,0},{24,12},{28,8},{1,21},{... | collective-permute-start | bytes 49160 | tf_op jit(solution)/shard_map/ppermute | solution.py:451
  27.8 0.5 %collective-permute-start.9 = (bf16[64,128]{1,0:T(8,128)(2,1)S(1)}, bf16[64,128]{1,0:T(8,128)(2,1)S(1)}, u32[]{:S(2)}, u32[]{:S(2)}) collective-permute-start(bf16[64,128]{1,0:T(8,128)(2,1)S(1)} %get-tuple-element.51), channel_id=1, source_target_pairs={{0,16},{4,20},{8,24},{12,28},{16,0},{20,4},{24,8},{28,12},{1,17},{... | collective-permute-start | bytes 49160 | tf_op jit(solution)/shard_map/ppermute | solution.py:451
  28.3 0.8 %collective-permute-start.10 = (bf16[64,128]{1,0:T(8,128)(2,1)S(1)}, bf16[64,128]{1,0:T(8,128)(2,1)S(1)}, u32[]{:S(2)}, u32[]{:S(2)}) collective-permute-start(bf16[64,128]{1,0:T(8,128)(2,1)S(1)} %get-tuple-element.52), channel_id=1, source_target_pairs={{0,12},{4,8},{8,4},{12,0},{16,28},{20,24},{24,20},{28,16},{1,13},{... | collective-permute-start | bytes 49160 | tf_op jit(solution)/shard_map/ppermute | solution.py:451
  29.1 0.9 %collective-permute-start.11 = (bf16[64,128]{1,0:T(8,128)(2,1)S(1)}, bf16[64,128]{1,0:T(8,128)(2,1)S(1)}, u32[]{:S(2)}, u32[]{:S(2)}) collective-permute-start(bf16[64,128]{1,0:T(8,128)(2,1)S(1)} %get-tuple-element.53), channel_id=1, source_target_pairs={{0,8},{4,12},{8,0},{12,4},{16,24},{20,28},{24,16},{28,20},{1,9},{5... | collective-permute-start | bytes 49160 | tf_op jit(solution)/shard_map/ppermute | solution.py:451
  29.9 0.2 collective-permute-start.12
  30.2 1.3 %shard_map.143 = (f32[1024,512]{1,0:T(8,128)S(1)}, bf16[128,256]{1,0:T(8,128)(2,1)S(1)}) custom-call(bf16[1024,512]{1,0:T(8,128)(2,1)S(1)} %get-tuple-element.33.refs_0_, bf16[256,256]{1,0:T(8,128)(2,1)S(1)} %get-tuple-element.37.refs_1_, bf16[1024,256]{1,0:T(8,128)(2,1)S(1)} %get-tuple-element.38.refs_2_, bf16[1024,256]{1,0:T(8,128)(2,1)S(1)} %get-tuple-element.39.refs_3_, ...), custom_call_target="tpu_custom_call" | custom-call | flops 268435456 | bytes 5242880 | tf_op jit(solution)/shard_map/pallas_call | solution.py:49
  31.5 0.1 collective-permute-done.9.refs_10_
  31.5 1.3 %collective-permute-done.11.refs_12_ = bf16[64,128]{1,0:T(8,128)(2,1)S(1)} collective-permute-done((bf16[64,128]{1,0:T(8,128)(2,1)S(1)}, bf16[64,128]{1,0:T(8,128)(2,1)S(1)}, u32[]{:S(2)}, u32[]{:S(2)}) %collective-permute-start.11) | collective-permute-done | bytes 16416 | tf_op jit(solution)/shard_map/ppermute | solution.py:451
  32.9 2.3 %shard_map.144 = (bf16[1024,512]{1,0:T(8,128)(2,1)S(1)}, bf16[128,256]{1,0:T(8,128)(2,1)S(1)}) custom-call(f32[1024,512]{1,0:T(8,128)S(1)} %get-tuple-element.42.refs_0_, bf16[1024,256]{1,0:T(8,128)(2,1)S(1)} %get-tuple-element.43.refs_1_, bf16[1024,256]{1,0:T(8,128)(2,1)S(1)} %get-tuple-element.44.refs_2_, ...), custom_call_target="tpu_custom_call" | custom-call | flops 1073741824 | bytes 4194304 | tf_op jit(solution)/shard_map/pallas_call | solution.py:49
  35.2 0.7 %collective-permute-start.15 = (bf16[128,256]{1,0:T(8,128)(2,1)S(1)}, bf16[128,256]{1,0:T(8,128)(2,1)S(1)}, u32[]{:S(2)}, u32[]{:S(2)}) collective-permute-start(bf16[128,256]{1,0:T(8,128)(2,1)S(1)} %get-tuple-element.55.refs_0_), channel_id=1, source_target_pairs={{0,2},{1,3},{2,0},{3,1},{4,6},{5,7},{6,4},{7,5},{8,10},{9,11},{10,... | collective-permute-start | bytes 196616 | tf_op jit(solution)/shard_map/ppermute | solution.py:362
  35.9 1.0 %collective-permute-start.14 = (bf16[128,256]{1,0:T(8,128)(2,1)S(1)}, bf16[128,256]{1,0:T(8,128)(2,1)S(1)}, u32[]{:S(2)}, u32[]{:S(2)}) collective-permute-start(bf16[128,256]{1,0:T(8,128)(2,1)S(1)} %get-tuple-element.55.refs_0_), channel_id=1, source_target_pairs={{0,3},{1,2},{2,1},{3,0},{4,7},{5,6},{6,5},{7,4},{8,11},{9,10},{10,... | collective-permute-start | bytes 196616 | tf_op jit(solution)/shard_map/ppermute | solution.py:362
  36.9 1.9 %collective-permute-start.13 = (bf16[128,256]{1,0:T(8,128)(2,1)S(1)}, bf16[128,256]{1,0:T(8,128)(2,1)S(1)}, u32[]{:S(2)}, u32[]{:S(2)}) collective-permute-start(bf16[128,256]{1,0:T(8,128)(2,1)S(1)} %get-tuple-element.55.refs_0_), channel_id=1, source_target_pairs={{0,1},{1,0},{2,3},{3,2},{4,5},{5,4},{6,7},{7,6},{8,9},{9,8},{10,11... | collective-permute-start | bytes 196616 | tf_op jit(solution)/shard_map/ppermute | solution.py:362
  38.7 1.0 %shard_map.145 = (f32[1024,512]{1,0:T(8,128)S(1)}, bf16[1024,256]{1,0:T(8,128)(2,1)S(1)}, f32[256,512]{1,0:T(8,128)S(1)}, bf16[512,512]{1,0:T(8,128)(2,1)S(1)}) custom-call(bf16[1024,512]{1,0:T(8,128)(2,1)S(1)} %get-tuple-element.58.refs_0_.refs_6_, bf16[1024,512]{1,0:T(8,128)(2,1)S(1)} %get-tuple-element.59.refs_1_, ...), custom_call_target="tpu_custom_call" | custom-call | flops 536870912 | bytes 4194304 | tf_op jit(solution)/shard_map/pallas_call | solution.py:49
  39.7 2.8 %collective-permute-done.15.refs_3_ = bf16[128,256]{1,0:T(8,128)(2,1)S(1)} collective-permute-done((bf16[128,256]{1,0:T(8,128)(2,1)S(1)}, bf16[128,256]{1,0:T(8,128)(2,1)S(1)}, u32[]{:S(2)}, u32[]{:S(2)}) %collective-permute-start.15) | collective-permute-done | bytes 65568 | tf_op jit(solution)/shard_map/ppermute | solution.py:362
  42.5 0.7 %collective-permute-done.13.refs_1_ = bf16[128,256]{1,0:T(8,128)(2,1)S(1)} collective-permute-done((bf16[128,256]{1,0:T(8,128)(2,1)S(1)}, bf16[128,256]{1,0:T(8,128)(2,1)S(1)}, u32[]{:S(2)}, u32[]{:S(2)}) %collective-permute-start.13) | collective-permute-done | bytes 65568 | tf_op jit(solution)/shard_map/ppermute | solution.py:362
  43.3 1.9 %shard_map.146 = (bf16[1024,512]{1,0:T(8,128)(2,1)}, bf16[32,256]{1,0:T(8,128)(2,1)}) custom-call(bf16[128,256]{1,0:T(8,128)(2,1)S(1)} %get-tuple-element.55.refs_0_, bf16[128,256]{1,0:T(8,128)(2,1)S(1)} %collective-permute-done.13.refs_1_, bf16[128,256]{1,0:T(8,128)(2,1)S(1)} %collective-permute-done.14.refs_2_, ...), custom_call_target="tpu_custom_call" | custom-call | flops 268435456 | bytes 4194304 | tf_op jit(solution)/shard_map/pallas_call | solution.py:49
  (16 shorter events, 0.1 us)
Async XLA Ops:
  0.6 12.6 %copy-start.2 = (s32[16,2]{0,1:T(2,128)S(1)}, s32[16,2]{0,1:T(2,128)}, u32[]{:S(2)}) copy-start(s32[16,2]{0,1:T(2,128)} %param.17) | copy-start | bytes 388
  0.6 12.8 %copy-start.1 = (s32[1024]{0:T(1024)S(1)}, s32[1024]{0:T(1024)}, u32[]{:S(2)}) copy-start(s32[1024]{0:T(1024)} %param.15) | copy-start | bytes 12292
  0.7 25.8 %collective-permute-start.4 = (bf16[32,256]{1,0:T(8,128)(2,1)}, bf16[32,256]{1,0:T(8,128)(2,1)S(1)}, u32[]{:S(2)}, u32[]{:S(2)}) collective-permute-start(bf16[32,256]{1,0:T(8,128)(2,1)} %refs_6_.3), channel_id=1, source_target_pairs={{0,2},{1,3},{2,0},{3,1},{4,6},{5,7},{6,4},{7,5},{8,10},{9,11},{10,... | collective-permute-start | bytes 49160 | tf_op jit(solution)/shard_map/ppermute | solution.py:362
  4.8 23.0 %collective-permute-start.3 = (bf16[32,256]{1,0:T(8,128)(2,1)}, bf16[32,256]{1,0:T(8,128)(2,1)S(1)}, u32[]{:S(2)}, u32[]{:S(2)}) collective-permute-start(bf16[32,256]{1,0:T(8,128)(2,1)} %refs_6_.3), channel_id=1, source_target_pairs={{0,1},{1,0},{2,3},{3,2},{4,5},{5,4},{6,7},{7,6},{8,9},{9,8},{10,11... | collective-permute-start | bytes 49160 | tf_op jit(solution)/shard_map/ppermute | solution.py:362
  8.8 8.6 %copy-start = (bf16[32,256]{1,0:T(8,128)(2,1)S(1)}, bf16[32,256]{1,0:T(8,128)(2,1)}, u32[]{:S(2)}) copy-start(bf16[32,256]{1,0:T(8,128)(2,1)} %refs_6_.3) | copy-start | bytes 49156
  8.8 8.5 %collective-permute-start.2 = (bf16[512,128]{1,0:T(8,128)(2,1)S(1)}, bf16[512,128]{1,0:T(8,128)(2,1)S(1)}, u32[]{:S(2)}, u32[]{:S(2)}) collective-permute-start(bf16[512,128]{1,0:T(8,128)(2,1)S(1)} %shard_map.141.refs_3_), channel_id=1, source_target_pairs={{0,3},{1,2},{2,1},{3,0},{4,7},{5,6},{6,5},{7,4},{8,11},{9,10},{10,... | collective-permute-start | bytes 393224 | tf_op jit(solution)/shard_map/ppermute | solution.py:362
  8.9 13.3 %collective-permute-start.1 = (bf16[512,128]{1,0:T(8,128)(2,1)S(1)}, bf16[512,128]{1,0:T(8,128)(2,1)S(1)}, u32[]{:S(2)}, u32[]{:S(2)}) collective-permute-start(bf16[512,128]{1,0:T(8,128)(2,1)S(1)} %shard_map.141.refs_3_), channel_id=1, source_target_pairs={{0,2},{1,3},{2,0},{3,1},{4,6},{5,7},{6,4},{7,5},{8,10},{9,11},{10,... | collective-permute-start | bytes 393224 | tf_op jit(solution)/shard_map/ppermute | solution.py:362
  10.8 11.4 %collective-permute-start = (bf16[512,128]{1,0:T(8,128)(2,1)S(1)}, bf16[512,128]{1,0:T(8,128)(2,1)S(1)}, u32[]{:S(2)}, u32[]{:S(2)}) collective-permute-start(bf16[512,128]{1,0:T(8,128)(2,1)S(1)} %shard_map.141.refs_3_), channel_id=1, source_target_pairs={{0,1},{1,0},{2,3},{3,2},{4,5},{5,4},{6,7},{7,6},{8,9},{9,8},{10,11... | collective-permute-start | bytes 393224 | tf_op jit(solution)/shard_map/ppermute | solution.py:362
  17.4 10.9 %collective-permute-start.5 = (bf16[32,256]{1,0:T(8,128)(2,1)S(1)}, bf16[32,256]{1,0:T(8,128)(2,1)S(1)}, u32[]{:S(2)}, u32[]{:S(2)}) collective-permute-start(bf16[32,256]{1,0:T(8,128)(2,1)S(1)} %copy-done), channel_id=1, source_target_pairs={{0,3},{1,2},{2,1},{3,0},{4,7},{5,6},{6,5},{7,4},{8,11},{9,10},{10,... | collective-permute-start | bytes 49160 | tf_op jit(solution)/shard_map/ppermute | solution.py:362
  23.8 5.2 %collective-permute-start.6 = (bf16[64,128]{1,0:T(8,128)(2,1)S(1)}, bf16[64,128]{1,0:T(8,128)(2,1)S(1)}, u32[]{:S(2)}, u32[]{:S(2)}) collective-permute-start(bf16[64,128]{1,0:T(8,128)(2,1)S(1)} %get-tuple-element.48), channel_id=1, source_target_pairs={{0,28},{4,24},{8,20},{12,16},{16,12},{20,8},{24,4},{28,0},{1,29},{... | collective-permute-start | bytes 49160 | tf_op jit(solution)/shard_map/ppermute | solution.py:451
  23.9 6.0 %collective-permute-start.7 = (bf16[64,128]{1,0:T(8,128)(2,1)S(1)}, bf16[64,128]{1,0:T(8,128)(2,1)S(1)}, u32[]{:S(2)}, u32[]{:S(2)}) collective-permute-start(bf16[64,128]{1,0:T(8,128)(2,1)S(1)} %get-tuple-element.49), channel_id=1, source_target_pairs={{0,24},{4,28},{8,16},{12,20},{16,8},{20,12},{24,0},{28,4},{1,25},{... | collective-permute-start | bytes 49160 | tf_op jit(solution)/shard_map/ppermute | solution.py:451
  26.4 5.0 %collective-permute-start.8 = (bf16[64,128]{1,0:T(8,128)(2,1)S(1)}, bf16[64,128]{1,0:T(8,128)(2,1)S(1)}, u32[]{:S(2)}, u32[]{:S(2)}) collective-permute-start(bf16[64,128]{1,0:T(8,128)(2,1)S(1)} %get-tuple-element.50), channel_id=1, source_target_pairs={{0,20},{4,16},{8,28},{12,24},{16,4},{20,0},{24,12},{28,8},{1,21},{... | collective-permute-start | bytes 49160 | tf_op jit(solution)/shard_map/ppermute | solution.py:451
  27.8 3.7 %collective-permute-start.9 = (bf16[64,128]{1,0:T(8,128)(2,1)S(1)}, bf16[64,128]{1,0:T(8,128)(2,1)S(1)}, u32[]{:S(2)}, u32[]{:S(2)}) collective-permute-start(bf16[64,128]{1,0:T(8,128)(2,1)S(1)} %get-tuple-element.51), channel_id=1, source_target_pairs={{0,16},{4,20},{8,24},{12,28},{16,0},{20,4},{24,8},{28,12},{1,17},{... | collective-permute-start | bytes 49160 | tf_op jit(solution)/shard_map/ppermute | solution.py:451
  28.3 3.2 %collective-permute-start.10 = (bf16[64,128]{1,0:T(8,128)(2,1)S(1)}, bf16[64,128]{1,0:T(8,128)(2,1)S(1)}, u32[]{:S(2)}, u32[]{:S(2)}) collective-permute-start(bf16[64,128]{1,0:T(8,128)(2,1)S(1)} %get-tuple-element.52), channel_id=1, source_target_pairs={{0,12},{4,8},{8,4},{12,0},{16,28},{20,24},{24,20},{28,16},{1,13},{... | collective-permute-start | bytes 49160 | tf_op jit(solution)/shard_map/ppermute | solution.py:451
  29.1 3.8 %collective-permute-start.11 = (bf16[64,128]{1,0:T(8,128)(2,1)S(1)}, bf16[64,128]{1,0:T(8,128)(2,1)S(1)}, u32[]{:S(2)}, u32[]{:S(2)}) collective-permute-start(bf16[64,128]{1,0:T(8,128)(2,1)S(1)} %get-tuple-element.53), channel_id=1, source_target_pairs={{0,8},{4,12},{8,0},{12,4},{16,24},{20,28},{24,16},{28,20},{1,9},{5... | collective-permute-start | bytes 49160 | tf_op jit(solution)/shard_map/ppermute | solution.py:451
  29.9 2.9 %collective-permute-start.12 = (bf16[64,128]{1,0:T(8,128)(2,1)S(1)}, bf16[64,128]{1,0:T(8,128)(2,1)S(1)}, u32[]{:S(2)}, u32[]{:S(2)}) collective-permute-start(bf16[64,128]{1,0:T(8,128)(2,1)S(1)} %get-tuple-element.54), channel_id=1, source_target_pairs={{0,4},{4,0},{8,12},{12,8},{16,20},{20,16},{24,28},{28,24},{1,5},{5... | collective-permute-start | bytes 49160 | tf_op jit(solution)/shard_map/ppermute | solution.py:451
  35.2 7.3 %collective-permute-start.15 = (bf16[128,256]{1,0:T(8,128)(2,1)S(1)}, bf16[128,256]{1,0:T(8,128)(2,1)S(1)}, u32[]{:S(2)}, u32[]{:S(2)}) collective-permute-start(bf16[128,256]{1,0:T(8,128)(2,1)S(1)} %get-tuple-element.55.refs_0_), channel_id=1, source_target_pairs={{0,2},{1,3},{2,0},{3,1},{4,6},{5,7},{6,4},{7,5},{8,10},{9,11},{10,... | collective-permute-start | bytes 196616 | tf_op jit(solution)/shard_map/ppermute | solution.py:362
  35.9 6.6 %collective-permute-start.14 = (bf16[128,256]{1,0:T(8,128)(2,1)S(1)}, bf16[128,256]{1,0:T(8,128)(2,1)S(1)}, u32[]{:S(2)}, u32[]{:S(2)}) collective-permute-start(bf16[128,256]{1,0:T(8,128)(2,1)S(1)} %get-tuple-element.55.refs_0_), channel_id=1, source_target_pairs={{0,3},{1,2},{2,1},{3,0},{4,7},{5,6},{6,5},{7,4},{8,11},{9,10},{10,... | collective-permute-start | bytes 196616 | tf_op jit(solution)/shard_map/ppermute | solution.py:362
  36.9 6.4 %collective-permute-start.13 = (bf16[128,256]{1,0:T(8,128)(2,1)S(1)}, bf16[128,256]{1,0:T(8,128)(2,1)S(1)}, u32[]{:S(2)}, u32[]{:S(2)}) collective-permute-start(bf16[128,256]{1,0:T(8,128)(2,1)S(1)} %get-tuple-element.55.refs_0_), channel_id=1, source_target_pairs={{0,1},{1,0},{2,3},{3,2},{4,5},{5,4},{6,7},{7,6},{8,9},{9,8},{10,11... | collective-permute-start | bytes 196616 | tf_op jit(solution)/shard_map/ppermute | solution.py:362

commit v12 on v10

--- a/solution.py
+++ b/solution.py
@@ -77,12 +77,13 @@
         copies.append(pltpu.make_async_copy(edges_hbm.at[rows], edges_ref.at[rows], sems.at[3 + at]))
     for copy in copies[1:] + copies[:1]:
         copy.start()
-    for copy in copies:
+    first = 3 + len(pieces) // 2
+    for copy in copies[1:first]:
         copy.wait()
-    hidden = [
-        narrow_silu(product(edges_ref[side * half : (side + 1) * half, :], weight_ref[...]))
-        for side in range(2)
-    ]
+    hidden = [narrow_silu(product(edges_ref[:half, :], weight_ref[...]))]
+    for copy in copies[first:] + copies[:1]:
+        copy.wait()
+    hidden.append(narrow_silu(product(edges_ref[half:, :], weight_ref[...])))
     sides = [
         lax.dot_general(
             each, down_ref[...], (((1,), (1,)), ((), ())), preferred_element_type=jnp.float32
@@ -199,9 +200,9 @@
         picks = []
         for tile in range(count):
             source = source_ref[block, tile]
-            shard = source // blocks
+            shard = lax.div(source, blocks)
             within = source - shard * blocks
-            upper = within // half_blocks
+            upper = (within >= half_blocks).astype(jnp.int32)
             start = (shard ^ me) * lines + (within - upper * half_blocks) * block_len
             rows = held_ref[pl.ds(pl.multiple_of(start, block_len), block_len), :]
             picks.append(jnp.where(upper == 1, rows[:, channels:], rows[:, :channels]))

time: 44.2 us -> 44.2 us (level)
  no operation moved by 1% of the time
where the time goes in v12:
time: 44.2 us; the launch traced here: 44 us
  starting transfers between devices  20.1 us (45%)
  Pallas kernels  14.6 us (33%)
  waiting for transfers between devices  8.5 us (19%)
  between operations  0.74 us (2%)
    pallas_call x7, Pallas kernels, call(): pl.pallas_call(kernel, out_shape=outs, in_specs=[pl.BlockSpec(memory_spac...  14.6 us
    ppermute x9, starting transfers between devices, from_others(): lax.ppermute(value, 'edge', [(at, at ^ by) for at in range(len(order))])  13.8 us
    ppermute x9, waiting for transfers between devices, from_others(): lax.ppermute(value, 'edge', [(at, at ^ by) for at in range(len(order))])  7.12 us
    ppermute x7, starting transfers between devices, body(): lax.ppermute(block, 'dom', [(at, at ^ partners - place) for at in range(d...  6.32 us
    ppermute x7, waiting for transfers between devices, body(): lax.ppermute(block, 'dom', [(at, at ^ partners - place) for at in range(d...  1.39 us
  transfers between devices with their start and end apart: 16, of which 5 were waited for; matrix products, arithmetic and copies ran while one was open for 0% of the time, Pallas kernels for 18%

profile of v12, /device:TPU:0, one launch (start us, length us, event | category | flops | bytes accessed | tf_op | source)
XLA Modules:
  0.0 44.0 jit_solution(11729589763744437726)
XLA Ops:
  0.7 2.5 %shard_map.141.refs_2_ = bf16[512,128]{1,0:T(8,128)(2,1)S(1)} custom-call(bf16[1024,512]{1,0:T(8,128)(2,1)} %edges_hbm.1, bf16[512,512]{1,0:T(8,128)(2,1)} %weight_hbm.1, bf16[64,512]{1,0:T(8,128)(2,1)} %down_hbm.1), custom_call_target="tpu_custom_call" | custom-call | flops 603979776 | bytes 1572864 | tf_op jit(solution)/shard_map/pallas_call | solution.py:49
  3.2 5.1 %collective-permute-start.2 = (bf16[512,128]{1,0:T(8,128)(2,1)S(1)}, bf16[512,128]{1,0:T(8,128)(2,1)S(1)}, u32[]{:S(2)}, u32[]{:S(2)}) collective-permute-start(bf16[512,128]{1,0:T(8,128)(2,1)S(1)} %shard_map.141.refs_2_), channel_id=1, source_target_pairs={{0,3},{1,2},{2,1},{3,0},{4,7},{5,6},{6,5},{7,4},{8,11},{9,10},{10,... | collective-permute-start | bytes 393224 | tf_op jit(solution)/shard_map/ppermute | solution.py:368
  8.3 0.6 %collective-permute-start = (bf16[512,128]{1,0:T(8,128)(2,1)S(1)}, bf16[512,128]{1,0:T(8,128)(2,1)S(1)}, u32[]{:S(2)}, u32[]{:S(2)}) collective-permute-start(bf16[512,128]{1,0:T(8,128)(2,1)S(1)} %shard_map.141.refs_2_), channel_id=1, source_target_pairs={{0,1},{1,0},{2,3},{3,2},{4,5},{5,4},{6,7},{7,6},{8,9},{9,8},{10,11... | collective-permute-start | bytes 393224 | tf_op jit(solution)/shard_map/ppermute | solution.py:368
  8.9 2.3 %collective-permute-start.4 = (bf16[32,256]{1,0:T(8,128)(2,1)S(1)}, bf16[32,256]{1,0:T(8,128)(2,1)S(1)}, u32[]{:S(2)}, u32[]{:S(2)}) collective-permute-start(bf16[32,256]{1,0:T(8,128)(2,1)S(1)} %copy-done), channel_id=1, source_target_pairs={{0,2},{1,3},{2,0},{3,1},{4,6},{5,7},{6,4},{7,5},{8,10},{9,11},{10,... | collective-permute-start | bytes 49160 | tf_op jit(solution)/shard_map/ppermute | solution.py:368
  11.2 2.0 %collective-permute-start.3 = (bf16[32,256]{1,0:T(8,128)(2,1)S(1)}, bf16[32,256]{1,0:T(8,128)(2,1)S(1)}, u32[]{:S(2)}, u32[]{:S(2)}) collective-permute-start(bf16[32,256]{1,0:T(8,128)(2,1)S(1)} %copy-done), channel_id=1, source_target_pairs={{0,1},{1,0},{2,3},{3,2},{4,5},{5,4},{6,7},{7,6},{8,9},{9,8},{10,11... | collective-permute-start | bytes 49160 | tf_op jit(solution)/shard_map/ppermute | solution.py:368
  13.2 0.1 copy.15.refs_0_
  13.3 3.9 %shard_map.140 = (bf16[896,256]{1,0:T(8,128)(2,1)S(1)}, bf16[896,256]{1,0:T(8,128)(2,1)S(1)}, bf16[1024,256]{1,0:T(8,128)(2,1)S(1)}, bf16[1024,256]{1,0:T(8,128)...) custom-call(s32[1,1024]{1,0:T(1,128)S(1)} %bitcast.1, ...), custom_call_target="tpu_custom_call" | custom-call | flops 41943040 | bytes 6291456 | tf_op jit(solution)/shard_map/pallas_call | solution.py:49
  17.2 0.0 collective-permute-done.2.refs_5_
  17.2 0.1 collective-permute-start.5
  17.4 2.7 %collective-permute-done.1.refs_4_ = bf16[512,128]{1,0:T(8,128)(2,1)S(1)} collective-permute-done((bf16[512,128]{1,0:T(8,128)(2,1)S(1)}, bf16[512,128]{1,0:T(8,128)(2,1)S(1)}, u32[]{:S(2)}, u32[]{:S(2)}) %collective-permute-start.1) | collective-permute-done | bytes 131104 | tf_op jit(solution)/shard_map/ppermute | solution.py:368
  20.1 1.7 %shard_map.142 = (bf16[256,256]{1,0:T(8,128)(2,1)S(1)}, bf16[64,128]{1,0:T(8,128)(2,1)S(1)}, bf16[64,128]{1,0:T(8,128)(2,1)S(1)}, bf16[64,128]{1,0:T(8,128)(2,1)...) custom-call(s32[16,2]{1,0:T(8,128)S(1)} %copy.15.refs_0_, ...), custom_call_target="tpu_custom_call" | custom-call | flops 134217728 | bytes 2097152 | tf_op jit(solution)/shard_map/pallas_call | solution.py:49
  21.8 0.9 %collective-permute-start.6 = (bf16[64,128]{1,0:T(8,128)(2,1)S(1)}, bf16[64,128]{1,0:T(8,128)(2,1)S(1)}, u32[]{:S(2)}, u32[]{:S(2)}) collective-permute-start(bf16[64,128]{1,0:T(8,128)(2,1)S(1)} %get-tuple-element.48), channel_id=1, source_target_pairs={{0,28},{4,24},{8,20},{12,16},{16,12},{20,8},{24,4},{28,0},{1,29},{... | collective-permute-start | bytes 49160 | tf_op jit(solution)/shard_map/ppermute | solution.py:450
  22.7 1.7 %collective-permute-start.7 = (bf16[64,128]{1,0:T(8,128)(2,1)S(1)}, bf16[64,128]{1,0:T(8,128)(2,1)S(1)}, u32[]{:S(2)}, u32[]{:S(2)}) collective-permute-start(bf16[64,128]{1,0:T(8,128)(2,1)S(1)} %get-tuple-element.49), channel_id=1, source_target_pairs={{0,24},{4,28},{8,16},{12,20},{16,8},{20,12},{24,0},{28,4},{1,25},{... | collective-permute-start | bytes 49160 | tf_op jit(solution)/shard_map/ppermute | solution.py:450
  24.4 0.0 collective-permute-done.4.refs_8_
  24.4 1.4 %collective-permute-start.8 = (bf16[64,128]{1,0:T(8,128)(2,1)S(1)}, bf16[64,128]{1,0:T(8,128)(2,1)S(1)}, u32[]{:S(2)}, u32[]{:S(2)}) collective-permute-start(bf16[64,128]{1,0:T(8,128)(2,1)S(1)} %get-tuple-element.50), channel_id=1, source_target_pairs={{0,20},{4,16},{8,28},{12,24},{16,4},{20,0},{24,12},{28,8},{1,21},{... | collective-permute-start | bytes 49160 | tf_op jit(solution)/shard_map/ppermute | solution.py:450
  25.8 0.0 collective-permute-done.3.refs_7_
  25.8 0.5 %collective-permute-start.9 = (bf16[64,128]{1,0:T(8,128)(2,1)S(1)}, bf16[64,128]{1,0:T(8,128)(2,1)S(1)}, u32[]{:S(2)}, u32[]{:S(2)}) collective-permute-start(bf16[64,128]{1,0:T(8,128)(2,1)S(1)} %get-tuple-element.51), channel_id=1, source_target_pairs={{0,16},{4,20},{8,24},{12,28},{16,0},{20,4},{24,8},{28,12},{1,17},{... | collective-permute-start | bytes 49160 | tf_op jit(solution)/shard_map/ppermute | solution.py:450
  26.3 0.8 %collective-permute-start.10 = (bf16[64,128]{1,0:T(8,128)(2,1)S(1)}, bf16[64,128]{1,0:T(8,128)(2,1)S(1)}, u32[]{:S(2)}, u32[]{:S(2)}) collective-permute-start(bf16[64,128]{1,0:T(8,128)(2,1)S(1)} %get-tuple-element.52), channel_id=1, source_target_pairs={{0,12},{4,8},{8,4},{12,0},{16,28},{20,24},{24,20},{28,16},{1,13},{... | collective-permute-start | bytes 49160 | tf_op jit(solution)/shard_map/ppermute | solution.py:450
  27.0 0.0 collective-permute-done.6.refs_7_
  27.1 0.9 %collective-permute-start.11 = (bf16[64,128]{1,0:T(8,128)(2,1)S(1)}, bf16[64,128]{1,0:T(8,128)(2,1)S(1)}, u32[]{:S(2)}, u32[]{:S(2)}) collective-permute-start(bf16[64,128]{1,0:T(8,128)(2,1)S(1)} %get-tuple-element.53), channel_id=1, source_target_pairs={{0,8},{4,12},{8,0},{12,4},{16,24},{20,28},{24,16},{28,20},{1,9},{5... | collective-permute-start | bytes 49160 | tf_op jit(solution)/shard_map/ppermute | solution.py:450
  27.9 0.2 collective-permute-start.12
  28.2 1.3 %shard_map.143 = (f32[1024,512]{1,0:T(8,128)S(1)}, bf16[128,256]{1,0:T(8,128)(2,1)S(1)}) custom-call(bf16[1024,512]{1,0:T(8,128)(2,1)S(1)} %get-tuple-element.33.refs_0_, bf16[256,256]{1,0:T(8,128)(2,1)S(1)} %get-tuple-element.37.refs_1_, bf16[1024,256]{1,0:T(8,128)(2,1)S(1)} %get-tuple-element.38.refs_2_, bf16[1024,256]{1,0:T(8,128)(2,1)S(1)} %get-tuple-element.39.refs_3_, ...), custom_call_target="tpu_custom_call" | custom-call | flops 268435456 | bytes 5242880 | tf_op jit(solution)/shard_map/pallas_call | solution.py:49
  29.5 0.1 collective-permute-done.9.refs_10_
  29.5 1.3 %collective-permute-done.11.refs_12_ = bf16[64,128]{1,0:T(8,128)(2,1)S(1)} collective-permute-done((bf16[64,128]{1,0:T(8,128)(2,1)S(1)}, bf16[64,128]{1,0:T(8,128)(2,1)S(1)}, u32[]{:S(2)}, u32[]{:S(2)}) %collective-permute-start.11) | collective-permute-done | bytes 16416 | tf_op jit(solution)/shard_map/ppermute | solution.py:450
  30.8 2.3 %shard_map.144 = (bf16[1024,512]{1,0:T(8,128)(2,1)S(1)}, bf16[128,256]{1,0:T(8,128)(2,1)S(1)}) custom-call(f32[1024,512]{1,0:T(8,128)S(1)} %get-tuple-element.42.refs_0_, bf16[1024,256]{1,0:T(8,128)(2,1)S(1)} %get-tuple-element.43.refs_1_, bf16[1024,256]{1,0:T(8,128)(2,1)S(1)} %get-tuple-element.44.refs_2_, ...), custom_call_target="tpu_custom_call" | custom-call | flops 1073741824 | bytes 4194304 | tf_op jit(solution)/shard_map/pallas_call | solution.py:49
  33.1 0.1 collective-permute-start.15
  33.2 2.7 %collective-permute-start.14 = (bf16[128,256]{1,0:T(8,128)(2,1)S(1)}, bf16[128,256]{1,0:T(8,128)(2,1)S(1)}, u32[]{:S(2)}, u32[]{:S(2)}) collective-permute-start(bf16[128,256]{1,0:T(8,128)(2,1)S(1)} %get-tuple-element.55.refs_0_), channel_id=1, source_target_pairs={{0,3},{1,2},{2,1},{3,0},{4,7},{5,6},{6,5},{7,4},{8,11},{9,10},{10,... | collective-permute-start | bytes 196616 | tf_op jit(solution)/shard_map/ppermute | solution.py:368
  36.0 0.7 %collective-permute-start.13 = (bf16[128,256]{1,0:T(8,128)(2,1)S(1)}, bf16[128,256]{1,0:T(8,128)(2,1)S(1)}, u32[]{:S(2)}, u32[]{:S(2)}) collective-permute-start(bf16[128,256]{1,0:T(8,128)(2,1)S(1)} %get-tuple-element.55.refs_0_), channel_id=1, source_target_pairs={{0,1},{1,0},{2,3},{3,2},{4,5},{5,4},{6,7},{7,6},{8,9},{9,8},{10,11... | collective-permute-start | bytes 196616 | tf_op jit(solution)/shard_map/ppermute | solution.py:368
  36.7 1.0 %shard_map.145 = (f32[1024,512]{1,0:T(8,128)S(1)}, bf16[1024,256]{1,0:T(8,128)(2,1)S(1)}, f32[256,512]{1,0:T(8,128)S(1)}, bf16[512,512]{1,0:T(8,128)(2,1)S(1)}) custom-call(bf16[1024,512]{1,0:T(8,128)(2,1)S(1)} %get-tuple-element.58.refs_0_.refs_6_, bf16[1024,512]{1,0:T(8,128)(2,1)S(1)} %get-tuple-element.59.refs_1_, ...), custom_call_target="tpu_custom_call" | custom-call | flops 536870912 | bytes 4194304 | tf_op jit(solution)/shard_map/pallas_call | solution.py:49
  37.7 3.4 %collective-permute-done.15.refs_3_ = bf16[128,256]{1,0:T(8,128)(2,1)S(1)} collective-permute-done((bf16[128,256]{1,0:T(8,128)(2,1)S(1)}, bf16[128,256]{1,0:T(8,128)(2,1)S(1)}, u32[]{:S(2)}, u32[]{:S(2)}) %collective-permute-start.15) | collective-permute-done | bytes 65568 | tf_op jit(solution)/shard_map/ppermute | solution.py:368
  41.1 1.0 %collective-permute-done.13.refs_1_ = bf16[128,256]{1,0:T(8,128)(2,1)S(1)} collective-permute-done((bf16[128,256]{1,0:T(8,128)(2,1)S(1)}, bf16[128,256]{1,0:T(8,128)(2,1)S(1)}, u32[]{:S(2)}, u32[]{:S(2)}) %collective-permute-start.13) | collective-permute-done | bytes 65568 | tf_op jit(solution)/shard_map/ppermute | solution.py:368
  42.1 1.9 %shard_map.146 = (bf16[1024,512]{1,0:T(8,128)(2,1)}, bf16[32,256]{1,0:T(8,128)(2,1)}) custom-call(bf16[128,256]{1,0:T(8,128)(2,1)S(1)} %get-tuple-element.55.refs_0_, bf16[128,256]{1,0:T(8,128)(2,1)S(1)} %collective-permute-done.13.refs_1_, bf16[128,256]{1,0:T(8,128)(2,1)S(1)} %collective-permute-done.14.refs_2_, ...), custom_call_target="tpu_custom_call" | custom-call | flops 268435456 | bytes 4194304 | tf_op jit(solution)/shard_map/pallas_call | solution.py:49
  (14 shorter events, 0.0 us)
Async XLA Ops:
  0.6 8.3 %copy-start = (bf16[32,256]{1,0:T(8,128)(2,1)S(1)}, bf16[32,256]{1,0:T(8,128)(2,1)}, u32[]{:S(2)}) copy-start(bf16[32,256]{1,0:T(8,128)(2,1)} %refs_6_.3) | copy-start | bytes 49156
  0.6 12.6 %copy-start.2 = (s32[16,2]{0,1:T(2,128)S(1)}, s32[16,2]{0,1:T(2,128)}, u32[]{:S(2)}) copy-start(s32[16,2]{0,1:T(2,128)} %param.17) | copy-start | bytes 388
  0.7 12.7 %copy-start.1 = (s32[1024]{0:T(1024)S(1)}, s32[1024]{0:T(1024)}, u32[]{:S(2)}) copy-start(s32[1024]{0:T(1024)} %param.15) | copy-start | bytes 12292
  3.2 14.0 %collective-permute-start.2 = (bf16[512,128]{1,0:T(8,128)(2,1)S(1)}, bf16[512,128]{1,0:T(8,128)(2,1)S(1)}, u32[]{:S(2)}, u32[]{:S(2)}) collective-permute-start(bf16[512,128]{1,0:T(8,128)(2,1)S(1)} %shard_map.141.refs_2_), channel_id=1, source_target_pairs={{0,3},{1,2},{2,1},{3,0},{4,7},{5,6},{6,5},{7,4},{8,11},{9,10},{10,... | collective-permute-start | bytes 393224 | tf_op jit(solution)/shard_map/ppermute | solution.py:368
  8.3 11.8 %collective-permute-start.1 = (bf16[512,128]{1,0:T(8,128)(2,1)S(1)}, bf16[512,128]{1,0:T(8,128)(2,1)S(1)}, u32[]{:S(2)}, u32[]{:S(2)}) collective-permute-start(bf16[512,128]{1,0:T(8,128)(2,1)S(1)} %shard_map.141.refs_2_), channel_id=1, source_target_pairs={{0,2},{1,3},{2,0},{3,1},{4,6},{5,7},{6,4},{7,5},{8,10},{9,11},{10,... | collective-permute-start | bytes 393224 | tf_op jit(solution)/shard_map/ppermute | solution.py:368
  8.3 11.8 %collective-permute-start = (bf16[512,128]{1,0:T(8,128)(2,1)S(1)}, bf16[512,128]{1,0:T(8,128)(2,1)S(1)}, u32[]{:S(2)}, u32[]{:S(2)}) collective-permute-start(bf16[512,128]{1,0:T(8,128)(2,1)S(1)} %shard_map.141.refs_2_), channel_id=1, source_target_pairs={{0,1},{1,0},{2,3},{3,2},{4,5},{5,4},{6,7},{7,6},{8,9},{9,8},{10,11... | collective-permute-start | bytes 393224 | tf_op jit(solution)/shard_map/ppermute | solution.py:368
  8.9 15.5 %collective-permute-start.4 = (bf16[32,256]{1,0:T(8,128)(2,1)S(1)}, bf16[32,256]{1,0:T(8,128)(2,1)S(1)}, u32[]{:S(2)}, u32[]{:S(2)}) collective-permute-start(bf16[32,256]{1,0:T(8,128)(2,1)S(1)} %copy-done), channel_id=1, source_target_pairs={{0,2},{1,3},{2,0},{3,1},{4,6},{5,7},{6,4},{7,5},{8,10},{9,11},{10,... | collective-permute-start | bytes 49160 | tf_op jit(solution)/shard_map/ppermute | solution.py:368
  11.2 14.5 %collective-permute-start.3 = (bf16[32,256]{1,0:T(8,128)(2,1)S(1)}, bf16[32,256]{1,0:T(8,128)(2,1)S(1)}, u32[]{:S(2)}, u32[]{:S(2)}) collective-permute-start(bf16[32,256]{1,0:T(8,128)(2,1)S(1)} %copy-done), channel_id=1, source_target_pairs={{0,1},{1,0},{2,3},{3,2},{4,5},{5,4},{6,7},{7,6},{8,9},{9,8},{10,11... | collective-permute-start | bytes 49160 | tf_op jit(solution)/shard_map/ppermute | solution.py:368
  17.2 9.1 %collective-permute-start.5 = (bf16[32,256]{1,0:T(8,128)(2,1)S(1)}, bf16[32,256]{1,0:T(8,128)(2,1)S(1)}, u32[]{:S(2)}, u32[]{:S(2)}) collective-permute-start(bf16[32,256]{1,0:T(8,128)(2,1)S(1)} %copy-done), channel_id=1, source_target_pairs={{0,3},{1,2},{2,1},{3,0},{4,7},{5,6},{6,5},{7,4},{8,11},{9,10},{10,... | collective-permute-start | bytes 49160 | tf_op jit(solution)/shard_map/ppermute | solution.py:368
  21.8 5.2 %collective-permute-start.6 = (bf16[64,128]{1,0:T(8,128)(2,1)S(1)}, bf16[64,128]{1,0:T(8,128)(2,1)S(1)}, u32[]{:S(2)}, u32[]{:S(2)}) collective-permute-start(bf16[64,128]{1,0:T(8,128)(2,1)S(1)} %get-tuple-element.48), channel_id=1, source_target_pairs={{0,28},{4,24},{8,20},{12,16},{16,12},{20,8},{24,4},{28,0},{1,29},{... | collective-permute-start | bytes 49160 | tf_op jit(solution)/shard_map/ppermute | solution.py:450
  22.7 5.2 %collective-permute-start.7 = (bf16[64,128]{1,0:T(8,128)(2,1)S(1)}, bf16[64,128]{1,0:T(8,128)(2,1)S(1)}, u32[]{:S(2)}, u32[]{:S(2)}) collective-permute-start(bf16[64,128]{1,0:T(8,128)(2,1)S(1)} %get-tuple-element.49), channel_id=1, source_target_pairs={{0,24},{4,28},{8,16},{12,20},{16,8},{20,12},{24,0},{28,4},{1,25},{... | collective-permute-start | bytes 49160 | tf_op jit(solution)/shard_map/ppermute | solution.py:450
  24.4 5.0 %collective-permute-start.8 = (bf16[64,128]{1,0:T(8,128)(2,1)S(1)}, bf16[64,128]{1,0:T(8,128)(2,1)S(1)}, u32[]{:S(2)}, u32[]{:S(2)}) collective-permute-start(bf16[64,128]{1,0:T(8,128)(2,1)S(1)} %get-tuple-element.50), channel_id=1, source_target_pairs={{0,20},{4,16},{8,28},{12,24},{16,4},{20,0},{24,12},{28,8},{1,21},{... | collective-permute-start | bytes 49160 | tf_op jit(solution)/shard_map/ppermute | solution.py:450
  25.8 3.7 %collective-permute-start.9 = (bf16[64,128]{1,0:T(8,128)(2,1)S(1)}, bf16[64,128]{1,0:T(8,128)(2,1)S(1)}, u32[]{:S(2)}, u32[]{:S(2)}) collective-permute-start(bf16[64,128]{1,0:T(8,128)(2,1)S(1)} %get-tuple-element.51), channel_id=1, source_target_pairs={{0,16},{4,20},{8,24},{12,28},{16,0},{20,4},{24,8},{28,12},{1,17},{... | collective-permute-start | bytes 49160 | tf_op jit(solution)/shard_map/ppermute | solution.py:450
  26.3 3.2 %collective-permute-start.10 = (bf16[64,128]{1,0:T(8,128)(2,1)S(1)}, bf16[64,128]{1,0:T(8,128)(2,1)S(1)}, u32[]{:S(2)}, u32[]{:S(2)}) collective-permute-start(bf16[64,128]{1,0:T(8,128)(2,1)S(1)} %get-tuple-element.52), channel_id=1, source_target_pairs={{0,12},{4,8},{8,4},{12,0},{16,28},{20,24},{24,20},{28,16},{1,13},{... | collective-permute-start | bytes 49160 | tf_op jit(solution)/shard_map/ppermute | solution.py:450
  27.1 3.8 %collective-permute-start.11 = (bf16[64,128]{1,0:T(8,128)(2,1)S(1)}, bf16[64,128]{1,0:T(8,128)(2,1)S(1)}, u32[]{:S(2)}, u32[]{:S(2)}) collective-permute-start(bf16[64,128]{1,0:T(8,128)(2,1)S(1)} %get-tuple-element.53), channel_id=1, source_target_pairs={{0,8},{4,12},{8,0},{12,4},{16,24},{20,28},{24,16},{28,20},{1,9},{5... | collective-permute-start | bytes 49160 | tf_op jit(solution)/shard_map/ppermute | solution.py:450
  27.9 2.9 %collective-permute-start.12 = (bf16[64,128]{1,0:T(8,128)(2,1)S(1)}, bf16[64,128]{1,0:T(8,128)(2,1)S(1)}, u32[]{:S(2)}, u32[]{:S(2)}) collective-permute-start(bf16[64,128]{1,0:T(8,128)(2,1)S(1)} %get-tuple-element.54), channel_id=1, source_target_pairs={{0,4},{4,0},{8,12},{12,8},{16,20},{20,16},{24,28},{28,24},{1,5},{5... | collective-permute-start | bytes 49160 | tf_op jit(solution)/shard_map/ppermute | solution.py:450
  33.1 7.9 %collective-permute-start.15 = (bf16[128,256]{1,0:T(8,128)(2,1)S(1)}, bf16[128,256]{1,0:T(8,128)(2,1)S(1)}, u32[]{:S(2)}, u32[]{:S(2)}) collective-permute-start(bf16[128,256]{1,0:T(8,128)(2,1)S(1)} %get-tuple-element.55.refs_0_), channel_id=1, source_target_pairs={{0,2},{1,3},{2,0},{3,1},{4,6},{5,7},{6,4},{7,5},{8,10},{9,11},{10,... | collective-permute-start | bytes 196616 | tf_op jit(solution)/shard_map/ppermute | solution.py:368
  33.2 7.8 %collective-permute-start.14 = (bf16[128,256]{1,0:T(8,128)(2,1)S(1)}, bf16[128,256]{1,0:T(8,128)(2,1)S(1)}, u32[]{:S(2)}, u32[]{:S(2)}) collective-permute-start(bf16[128,256]{1,0:T(8,128)(2,1)S(1)} %get-tuple-element.55.refs_0_), channel_id=1, source_target_pairs={{0,3},{1,2},{2,1},{3,0},{4,7},{5,6},{6,5},{7,4},{8,11},{9,10},{10,... | collective-permute-start | bytes 196616 | tf_op jit(solution)/shard_map/ppermute | solution.py:368
  36.0 6.1 %collective-permute-start.13 = (bf16[128,256]{1,0:T(8,128)(2,1)S(1)}, bf16[128,256]{1,0:T(8,128)(2,1)S(1)}, u32[]{:S(2)}, u32[]{:S(2)}) collective-permute-start(bf16[128,256]{1,0:T(8,128)(2,1)S(1)} %get-tuple-element.55.refs_0_), channel_id=1, source_target_pairs={{0,1},{1,0},{2,3},{3,2},{4,5},{5,4},{6,7},{7,6},{8,9},{9,8},{10,11... | collective-permute-start | bytes 196616 | tf_op jit(solution)/shard_map/ppermute | solution.py:368

commit v13 on v10

--- a/solution.py
+++ b/solution.py
@@ -199,9 +199,9 @@
         picks = []
         for tile in range(count):
             source = source_ref[block, tile]
-            shard = source // blocks
+            shard = lax.div(source, blocks)
             within = source - shard * blocks
-            upper = within // half_blocks
+            upper = (within >= half_blocks).astype(jnp.int32)
             start = (shard ^ me) * lines + (within - upper * half_blocks) * block_len
             rows = held_ref[pl.ds(pl.multiple_of(start, block_len), block_len), :]
             picks.append(jnp.where(upper == 1, rows[:, channels:], rows[:, :channels]))
@@ -358,7 +358,7 @@
 
 def orders(shards):
     if shards == 4:
-        return [0, 1, 2, 3], [0, 1, 3, 2]
+        return [0, 1, 3, 2], [0, 1, 3, 2]
     return list(range(shards)), list(range(shards))
 
 

time: 44.2 us -> 44 us (level)
  waiting for transfers between devices: 8.51 us -> 8 us
    ppermute x9, waiting for transfers between devices: 7.12 us -> 6.56 us  [from_others(): lax.ppermute(value, 'edge', [(at, at ^ by) for at in range(len(order))])]
  transfers between devices with their start and end apart: 16 -> 16, of which waited for: 5 -> 6; matrix products, arithmetic and copies ran while one was open for 0% -> 0% of each run, Pallas kernels for 18% -> 18%
where the time goes in v13:
time: 44 us; the launch traced here: 43.8 us
  starting transfers between devices  20.4 us (46%)
  Pallas kernels  14.6 us (33%)
  waiting for transfers between devices  8 us (18%)
  between operations  0.73 us (2%)
    pallas_call x7, Pallas kernels, call(): pl.pallas_call(kernel, out_shape=outs, in_specs=[pl.BlockSpec(memory_spac...  14.6 us
    ppermute x9, starting transfers between devices, from_others(): lax.ppermute(value, 'edge', [(at, at ^ by) for at in range(len(order))])  14.1 us
    ppermute x9, waiting for transfers between devices, from_others(): lax.ppermute(value, 'edge', [(at, at ^ by) for at in range(len(order))])  6.56 us
    ppermute x7, starting transfers between devices, body(): lax.ppermute(block, 'dom', [(at, at ^ partners - place) for at in range(d...  6.31 us
    ppermute x7, waiting for transfers between devices, body(): lax.ppermute(block, 'dom', [(at, at ^ partners - place) for at in range(d...  1.44 us
  transfers between devices with their start and end apart: 16, of which 6 were waited for; matrix products, arithmetic and copies ran while one was open for 0% of the time, Pallas kernels for 18%

profile of v13, /device:TPU:0, one launch (start us, length us, event | category | flops | bytes accessed | tf_op | source)
XLA Modules:
  0.0 43.8 jit_solution(3189396517915142238)
XLA Ops:
  0.7 2.5 %shard_map.141.refs_2_ = bf16[512,128]{1,0:T(8,128)(2,1)S(1)} custom-call(bf16[1024,512]{1,0:T(8,128)(2,1)} %edges_hbm.1, bf16[512,512]{1,0:T(8,128)(2,1)} %weight_hbm.1, bf16[64,512]{1,0:T(8,128)(2,1)} %down_hbm.1), custom_call_target="tpu_custom_call" | custom-call | flops 603979776 | bytes 1572864 | tf_op jit(solution)/shard_map/pallas_call | solution.py:49
  3.2 4.1 %collective-permute-start.2 = (bf16[512,128]{1,0:T(8,128)(2,1)S(1)}, bf16[512,128]{1,0:T(8,128)(2,1)S(1)}, u32[]{:S(2)}, u32[]{:S(2)}) collective-permute-start(bf16[512,128]{1,0:T(8,128)(2,1)S(1)} %shard_map.141.refs_2_), channel_id=1, source_target_pairs={{0,2},{1,3},{2,0},{3,1},{4,6},{5,7},{6,4},{7,5},{8,10},{9,11},{10,... | collective-permute-start | bytes 393224 | tf_op jit(solution)/shard_map/ppermute | solution.py:367
  7.3 1.3 %collective-permute-start.1 = (bf16[512,128]{1,0:T(8,128)(2,1)S(1)}, bf16[512,128]{1,0:T(8,128)(2,1)S(1)}, u32[]{:S(2)}, u32[]{:S(2)}) collective-permute-start(bf16[512,128]{1,0:T(8,128)(2,1)S(1)} %shard_map.141.refs_2_), channel_id=1, source_target_pairs={{0,3},{1,2},{2,1},{3,0},{4,7},{5,6},{6,5},{7,4},{8,11},{9,10},{10,... | collective-permute-start | bytes 393224 | tf_op jit(solution)/shard_map/ppermute | solution.py:367
  8.6 0.2 collective-permute-start
  8.8 2.9 %collective-permute-start.4 = (bf16[32,256]{1,0:T(8,128)(2,1)S(1)}, bf16[32,256]{1,0:T(8,128)(2,1)S(1)}, u32[]{:S(2)}, u32[]{:S(2)}) collective-permute-start(bf16[32,256]{1,0:T(8,128)(2,1)S(1)} %copy-done), channel_id=1, source_target_pairs={{0,3},{1,2},{2,1},{3,0},{4,7},{5,6},{6,5},{7,4},{8,11},{9,10},{10,... | collective-permute-start | bytes 49160 | tf_op jit(solution)/shard_map/ppermute | solution.py:367
  11.8 0.5 %collective-permute-start.3 = (bf16[32,256]{1,0:T(8,128)(2,1)S(1)}, bf16[32,256]{1,0:T(8,128)(2,1)S(1)}, u32[]{:S(2)}, u32[]{:S(2)}) collective-permute-start(bf16[32,256]{1,0:T(8,128)(2,1)S(1)} %copy-done), channel_id=1, source_target_pairs={{0,1},{1,0},{2,3},{3,2},{4,5},{5,4},{6,7},{7,6},{8,9},{9,8},{10,11... | collective-permute-start | bytes 49160 | tf_op jit(solution)/shard_map/ppermute | solution.py:367
  12.2 0.1 copy.15.refs_0_
  12.3 3.9 %shard_map.140 = (bf16[896,256]{1,0:T(8,128)(2,1)S(1)}, bf16[896,256]{1,0:T(8,128)(2,1)S(1)}, bf16[1024,256]{1,0:T(8,128)(2,1)S(1)}, bf16[1024,256]{1,0:T(8,128)...) custom-call(s32[1,1024]{1,0:T(1,128)S(1)} %bitcast.1, ...), custom_call_target="tpu_custom_call" | custom-call | flops 41943040 | bytes 6291456 | tf_op jit(solution)/shard_map/pallas_call | solution.py:49
  16.2 1.2 %collective-permute-done.2.refs_5_ = bf16[512,128]{1,0:T(8,128)(2,1)S(1)} collective-permute-done((bf16[512,128]{1,0:T(8,128)(2,1)S(1)}, bf16[512,128]{1,0:T(8,128)(2,1)S(1)}, u32[]{:S(2)}, u32[]{:S(2)}) %collective-permute-start.2) | collective-permute-done | bytes 131104 | tf_op jit(solution)/shard_map/ppermute | solution.py:367
  17.4 0.0 collective-permute-done.1.refs_4_
  17.4 0.9 %collective-permute-done.refs_3_ = bf16[512,128]{1,0:T(8,128)(2,1)S(1)} collective-permute-done((bf16[512,128]{1,0:T(8,128)(2,1)S(1)}, bf16[512,128]{1,0:T(8,128)(2,1)S(1)}, u32[]{:S(2)}, u32[]{:S(2)}) %collective-permute-start) | collective-permute-done | bytes 131104 | tf_op jit(solution)/shard_map/ppermute | solution.py:367
  18.3 1.7 %shard_map.142 = (bf16[256,256]{1,0:T(8,128)(2,1)S(1)}, bf16[64,128]{1,0:T(8,128)(2,1)S(1)}, bf16[64,128]{1,0:T(8,128)(2,1)S(1)}, bf16[64,128]{1,0:T(8,128)(2,1)...) custom-call(s32[16,2]{1,0:T(8,128)S(1)} %copy.15.refs_0_, ...), custom_call_target="tpu_custom_call" | custom-call | flops 134217728 | bytes 2097152 | tf_op jit(solution)/shard_map/pallas_call | solution.py:49
  20.0 0.1 collective-permute-start.6
  20.1 2.6 %collective-permute-start.7 = (bf16[64,128]{1,0:T(8,128)(2,1)S(1)}, bf16[64,128]{1,0:T(8,128)(2,1)S(1)}, u32[]{:S(2)}, u32[]{:S(2)}) collective-permute-start(bf16[64,128]{1,0:T(8,128)(2,1)S(1)} %get-tuple-element.49), channel_id=1, source_target_pairs={{0,24},{4,28},{8,16},{12,20},{16,8},{20,12},{24,0},{28,4},{1,25},{... | collective-permute-start | bytes 49160 | tf_op jit(solution)/shard_map/ppermute | solution.py:449
  22.7 1.4 %collective-permute-start.8 = (bf16[64,128]{1,0:T(8,128)(2,1)S(1)}, bf16[64,128]{1,0:T(8,128)(2,1)S(1)}, u32[]{:S(2)}, u32[]{:S(2)}) collective-permute-start(bf16[64,128]{1,0:T(8,128)(2,1)S(1)} %get-tuple-element.50), channel_id=1, source_target_pairs={{0,20},{4,16},{8,28},{12,24},{16,4},{20,0},{24,12},{28,8},{1,21},{... | collective-permute-start | bytes 49160 | tf_op jit(solution)/shard_map/ppermute | solution.py:449
  24.0 0.5 %collective-permute-start.9 = (bf16[64,128]{1,0:T(8,128)(2,1)S(1)}, bf16[64,128]{1,0:T(8,128)(2,1)S(1)}, u32[]{:S(2)}, u32[]{:S(2)}) collective-permute-start(bf16[64,128]{1,0:T(8,128)(2,1)S(1)} %get-tuple-element.51), channel_id=1, source_target_pairs={{0,16},{4,20},{8,24},{12,28},{16,0},{20,4},{24,8},{28,12},{1,17},{... | collective-permute-start | bytes 49160 | tf_op jit(solution)/shard_map/ppermute | solution.py:449
  24.5 0.0 collective-permute-done.5.refs_9_
  24.5 0.8 %collective-permute-start.10 = (bf16[64,128]{1,0:T(8,128)(2,1)S(1)}, bf16[64,128]{1,0:T(8,128)(2,1)S(1)}, u32[]{:S(2)}, u32[]{:S(2)}) collective-permute-start(bf16[64,128]{1,0:T(8,128)(2,1)S(1)} %get-tuple-element.52), channel_id=1, source_target_pairs={{0,12},{4,8},{8,4},{12,0},{16,28},{20,24},{24,20},{28,16},{1,13},{... | collective-permute-start | bytes 49160 | tf_op jit(solution)/shard_map/ppermute | solution.py:449
  25.3 0.0 collective-permute-done.6.refs_7_
  25.3 0.9 %collective-permute-start.11 = (bf16[64,128]{1,0:T(8,128)(2,1)S(1)}, bf16[64,128]{1,0:T(8,128)(2,1)S(1)}, u32[]{:S(2)}, u32[]{:S(2)}) collective-permute-start(bf16[64,128]{1,0:T(8,128)(2,1)S(1)} %get-tuple-element.53), channel_id=1, source_target_pairs={{0,8},{4,12},{8,0},{12,4},{16,24},{20,28},{24,16},{28,20},{1,9},{5... | collective-permute-start | bytes 49160 | tf_op jit(solution)/shard_map/ppermute | solution.py:449
  26.2 0.2 collective-permute-start.12
  26.4 1.3 %shard_map.143 = (f32[1024,512]{1,0:T(8,128)S(1)}, bf16[128,256]{1,0:T(8,128)(2,1)S(1)}) custom-call(bf16[1024,512]{1,0:T(8,128)(2,1)S(1)} %get-tuple-element.33.refs_0_, bf16[256,256]{1,0:T(8,128)(2,1)S(1)} %get-tuple-element.37.refs_1_, bf16[1024,256]{1,0:T(8,128)(2,1)S(1)} %get-tuple-element.38.refs_2_, bf16[1024,256]{1,0:T(8,128)(2,1)S(1)} %get-tuple-element.39.refs_3_, ...), custom_call_target="tpu_custom_call" | custom-call | flops 268435456 | bytes 5242880 | tf_op jit(solution)/shard_map/pallas_call | solution.py:49
  27.7 0.1 collective-permute-done.9.refs_10_
  27.8 1.3 %collective-permute-done.11.refs_12_ = bf16[64,128]{1,0:T(8,128)(2,1)S(1)} collective-permute-done((bf16[64,128]{1,0:T(8,128)(2,1)S(1)}, bf16[64,128]{1,0:T(8,128)(2,1)S(1)}, u32[]{:S(2)}, u32[]{:S(2)}) %collective-permute-start.11) | collective-permute-done | bytes 16416 | tf_op jit(solution)/shard_map/ppermute | solution.py:449
  29.1 2.3 %shard_map.144 = (bf16[1024,512]{1,0:T(8,128)(2,1)S(1)}, bf16[128,256]{1,0:T(8,128)(2,1)S(1)}) custom-call(f32[1024,512]{1,0:T(8,128)S(1)} %get-tuple-element.42.refs_0_, bf16[1024,256]{1,0:T(8,128)(2,1)S(1)} %get-tuple-element.43.refs_1_, bf16[1024,256]{1,0:T(8,128)(2,1)S(1)} %get-tuple-element.44.refs_2_, ...), custom_call_target="tpu_custom_call" | custom-call | flops 1073741824 | bytes 4194304 | tf_op jit(solution)/shard_map/pallas_call | solution.py:49
  31.4 4.4 %collective-permute-start.15 = (bf16[128,256]{1,0:T(8,128)(2,1)S(1)}, bf16[128,256]{1,0:T(8,128)(2,1)S(1)}, u32[]{:S(2)}, u32[]{:S(2)}) collective-permute-start(bf16[128,256]{1,0:T(8,128)(2,1)S(1)} %get-tuple-element.55.refs_0_), channel_id=1, source_target_pairs={{0,2},{1,3},{2,0},{3,1},{4,6},{5,7},{6,4},{7,5},{8,10},{9,11},{10,... | collective-permute-start | bytes 196616 | tf_op jit(solution)/shard_map/ppermute | solution.py:367
  35.8 0.5 %collective-permute-start.14 = (bf16[128,256]{1,0:T(8,128)(2,1)S(1)}, bf16[128,256]{1,0:T(8,128)(2,1)S(1)}, u32[]{:S(2)}, u32[]{:S(2)}) collective-permute-start(bf16[128,256]{1,0:T(8,128)(2,1)S(1)} %get-tuple-element.55.refs_0_), channel_id=1, source_target_pairs={{0,3},{1,2},{2,1},{3,0},{4,7},{5,6},{6,5},{7,4},{8,11},{9,10},{10,... | collective-permute-start | bytes 196616 | tf_op jit(solution)/shard_map/ppermute | solution.py:367
  36.3 0.2 collective-permute-start.13
  36.5 1.0 %shard_map.145 = (f32[1024,512]{1,0:T(8,128)S(1)}, bf16[1024,256]{1,0:T(8,128)(2,1)S(1)}, f32[256,512]{1,0:T(8,128)S(1)}, bf16[512,512]{1,0:T(8,128)(2,1)S(1)}) custom-call(bf16[1024,512]{1,0:T(8,128)(2,1)S(1)} %get-tuple-element.58.refs_0_.refs_6_, bf16[1024,512]{1,0:T(8,128)(2,1)S(1)} %get-tuple-element.59.refs_1_, ...), custom_call_target="tpu_custom_call" | custom-call | flops 536870912 | bytes 4194304 | tf_op jit(solution)/shard_map/pallas_call | solution.py:49
  37.5 3.0 %collective-permute-done.15.refs_3_ = bf16[128,256]{1,0:T(8,128)(2,1)S(1)} collective-permute-done((bf16[128,256]{1,0:T(8,128)(2,1)S(1)}, bf16[128,256]{1,0:T(8,128)(2,1)S(1)}, u32[]{:S(2)}, u32[]{:S(2)}) %collective-permute-start.15) | collective-permute-done | bytes 65568 | tf_op jit(solution)/shard_map/ppermute | solution.py:367
  40.5 1.5 %collective-permute-done.14.refs_2_ = bf16[128,256]{1,0:T(8,128)(2,1)S(1)} collective-permute-done((bf16[128,256]{1,0:T(8,128)(2,1)S(1)}, bf16[128,256]{1,0:T(8,128)(2,1)S(1)}, u32[]{:S(2)}, u32[]{:S(2)}) %collective-permute-start.14) | collective-permute-done | bytes 65568 | tf_op jit(solution)/shard_map/ppermute | solution.py:367
  41.9 1.9 %shard_map.146 = (bf16[1024,512]{1,0:T(8,128)(2,1)}, bf16[32,256]{1,0:T(8,128)(2,1)}) custom-call(bf16[128,256]{1,0:T(8,128)(2,1)S(1)} %get-tuple-element.55.refs_0_, bf16[128,256]{1,0:T(8,128)(2,1)S(1)} %collective-permute-done.13.refs_1_, bf16[128,256]{1,0:T(8,128)(2,1)S(1)} %collective-permute-done.14.refs_2_, ...), custom_call_target="tpu_custom_call" | custom-call | flops 268435456 | bytes 4194304 | tf_op jit(solution)/shard_map/pallas_call | solution.py:49
  (14 shorter events, 0.0 us)
Async XLA Ops:
  0.6 8.2 %copy-start = (bf16[32,256]{1,0:T(8,128)(2,1)S(1)}, bf16[32,256]{1,0:T(8,128)(2,1)}, u32[]{:S(2)}) copy-start(bf16[32,256]{1,0:T(8,128)(2,1)} %refs_6_.3) | copy-start | bytes 49156
  0.6 11.6 %copy-start.2 = (s32[16,2]{0,1:T(2,128)S(1)}, s32[16,2]{0,1:T(2,128)}, u32[]{:S(2)}) copy-start(s32[16,2]{0,1:T(2,128)} %param.17) | copy-start | bytes 388
  0.7 11.6 %copy-start.1 = (s32[1024]{0:T(1024)S(1)}, s32[1024]{0:T(1024)}, u32[]{:S(2)}) copy-start(s32[1024]{0:T(1024)} %param.15) | copy-start | bytes 12292
  3.2 14.3 %collective-permute-start.2 = (bf16[512,128]{1,0:T(8,128)(2,1)S(1)}, bf16[512,128]{1,0:T(8,128)(2,1)S(1)}, u32[]{:S(2)}, u32[]{:S(2)}) collective-permute-start(bf16[512,128]{1,0:T(8,128)(2,1)S(1)} %shard_map.141.refs_2_), channel_id=1, source_target_pairs={{0,2},{1,3},{2,0},{3,1},{4,6},{5,7},{6,4},{7,5},{8,10},{9,11},{10,... | collective-permute-start | bytes 393224 | tf_op jit(solution)/shard_map/ppermute | solution.py:367
  7.3 10.2 %collective-permute-start.1 = (bf16[512,128]{1,0:T(8,128)(2,1)S(1)}, bf16[512,128]{1,0:T(8,128)(2,1)S(1)}, u32[]{:S(2)}, u32[]{:S(2)}) collective-permute-start(bf16[512,128]{1,0:T(8,128)(2,1)S(1)} %shard_map.141.refs_2_), channel_id=1, source_target_pairs={{0,3},{1,2},{2,1},{3,0},{4,7},{5,6},{6,5},{7,4},{8,11},{9,10},{10,... | collective-permute-start | bytes 393224 | tf_op jit(solution)/shard_map/ppermute | solution.py:367
  8.6 9.7 %collective-permute-start = (bf16[512,128]{1,0:T(8,128)(2,1)S(1)}, bf16[512,128]{1,0:T(8,128)(2,1)S(1)}, u32[]{:S(2)}, u32[]{:S(2)}) collective-permute-start(bf16[512,128]{1,0:T(8,128)(2,1)S(1)} %shard_map.141.refs_2_), channel_id=1, source_target_pairs={{0,1},{1,0},{2,3},{3,2},{4,5},{5,4},{6,7},{7,6},{8,9},{9,8},{10,11... | collective-permute-start | bytes 393224 | tf_op jit(solution)/shard_map/ppermute | solution.py:367
  8.8 13.8 %collective-permute-start.4 = (bf16[32,256]{1,0:T(8,128)(2,1)S(1)}, bf16[32,256]{1,0:T(8,128)(2,1)S(1)}, u32[]{:S(2)}, u32[]{:S(2)}) collective-permute-start(bf16[32,256]{1,0:T(8,128)(2,1)S(1)} %copy-done), channel_id=1, source_target_pairs={{0,3},{1,2},{2,1},{3,0},{4,7},{5,6},{6,5},{7,4},{8,11},{9,10},{10,... | collective-permute-start | bytes 49160 | tf_op jit(solution)/shard_map/ppermute | solution.py:367
  11.8 12.3 %collective-permute-start.3 = (bf16[32,256]{1,0:T(8,128)(2,1)S(1)}, bf16[32,256]{1,0:T(8,128)(2,1)S(1)}, u32[]{:S(2)}, u32[]{:S(2)}) collective-permute-start(bf16[32,256]{1,0:T(8,128)(2,1)S(1)} %copy-done), channel_id=1, source_target_pairs={{0,1},{1,0},{2,3},{3,2},{4,5},{5,4},{6,7},{7,6},{8,9},{9,8},{10,11... | collective-permute-start | bytes 49160 | tf_op jit(solution)/shard_map/ppermute | solution.py:367
  17.4 7.1 %collective-permute-start.5 = (bf16[32,256]{1,0:T(8,128)(2,1)S(1)}, bf16[32,256]{1,0:T(8,128)(2,1)S(1)}, u32[]{:S(2)}, u32[]{:S(2)}) collective-permute-start(bf16[32,256]{1,0:T(8,128)(2,1)S(1)} %copy-done), channel_id=1, source_target_pairs={{0,2},{1,3},{2,0},{3,1},{4,6},{5,7},{6,4},{7,5},{8,10},{9,11},{10,... | collective-permute-start | bytes 49160 | tf_op jit(solution)/shard_map/ppermute | solution.py:367
  20.0 5.3 %collective-permute-start.6 = (bf16[64,128]{1,0:T(8,128)(2,1)S(1)}, bf16[64,128]{1,0:T(8,128)(2,1)S(1)}, u32[]{:S(2)}, u32[]{:S(2)}) collective-permute-start(bf16[64,128]{1,0:T(8,128)(2,1)S(1)} %get-tuple-element.48), channel_id=1, source_target_pairs={{0,28},{4,24},{8,20},{12,16},{16,12},{20,8},{24,4},{28,0},{1,29},{... | collective-permute-start | bytes 49160 | tf_op jit(solution)/shard_map/ppermute | solution.py:449
  20.1 6.1 %collective-permute-start.7 = (bf16[64,128]{1,0:T(8,128)(2,1)S(1)}, bf16[64,128]{1,0:T(8,128)(2,1)S(1)}, u32[]{:S(2)}, u32[]{:S(2)}) collective-permute-start(bf16[64,128]{1,0:T(8,128)(2,1)S(1)} %get-tuple-element.49), channel_id=1, source_target_pairs={{0,24},{4,28},{8,16},{12,20},{16,8},{20,12},{24,0},{28,4},{1,25},{... | collective-permute-start | bytes 49160 | tf_op jit(solution)/shard_map/ppermute | solution.py:449
  22.7 5.0 %collective-permute-start.8 = (bf16[64,128]{1,0:T(8,128)(2,1)S(1)}, bf16[64,128]{1,0:T(8,128)(2,1)S(1)}, u32[]{:S(2)}, u32[]{:S(2)}) collective-permute-start(bf16[64,128]{1,0:T(8,128)(2,1)S(1)} %get-tuple-element.50), channel_id=1, source_target_pairs={{0,20},{4,16},{8,28},{12,24},{16,4},{20,0},{24,12},{28,8},{1,21},{... | collective-permute-start | bytes 49160 | tf_op jit(solution)/shard_map/ppermute | solution.py:449
  24.0 3.7 %collective-permute-start.9 = (bf16[64,128]{1,0:T(8,128)(2,1)S(1)}, bf16[64,128]{1,0:T(8,128)(2,1)S(1)}, u32[]{:S(2)}, u32[]{:S(2)}) collective-permute-start(bf16[64,128]{1,0:T(8,128)(2,1)S(1)} %get-tuple-element.51), channel_id=1, source_target_pairs={{0,16},{4,20},{8,24},{12,28},{16,0},{20,4},{24,8},{28,12},{1,17},{... | collective-permute-start | bytes 49160 | tf_op jit(solution)/shard_map/ppermute | solution.py:449
  24.5 3.3 %collective-permute-start.10 = (bf16[64,128]{1,0:T(8,128)(2,1)S(1)}, bf16[64,128]{1,0:T(8,128)(2,1)S(1)}, u32[]{:S(2)}, u32[]{:S(2)}) collective-permute-start(bf16[64,128]{1,0:T(8,128)(2,1)S(1)} %get-tuple-element.52), channel_id=1, source_target_pairs={{0,12},{4,8},{8,4},{12,0},{16,28},{20,24},{24,20},{28,16},{1,13},{... | collective-permute-start | bytes 49160 | tf_op jit(solution)/shard_map/ppermute | solution.py:449
  25.3 3.8 %collective-permute-start.11 = (bf16[64,128]{1,0:T(8,128)(2,1)S(1)}, bf16[64,128]{1,0:T(8,128)(2,1)S(1)}, u32[]{:S(2)}, u32[]{:S(2)}) collective-permute-start(bf16[64,128]{1,0:T(8,128)(2,1)S(1)} %get-tuple-element.53), channel_id=1, source_target_pairs={{0,8},{4,12},{8,0},{12,4},{16,24},{20,28},{24,16},{28,20},{1,9},{5... | collective-permute-start | bytes 49160 | tf_op jit(solution)/shard_map/ppermute | solution.py:449
  26.2 2.9 %collective-permute-start.12 = (bf16[64,128]{1,0:T(8,128)(2,1)S(1)}, bf16[64,128]{1,0:T(8,128)(2,1)S(1)}, u32[]{:S(2)}, u32[]{:S(2)}) collective-permute-start(bf16[64,128]{1,0:T(8,128)(2,1)S(1)} %get-tuple-element.54), channel_id=1, source_target_pairs={{0,4},{4,0},{8,12},{12,8},{16,20},{20,16},{24,28},{28,24},{1,5},{5... | collective-permute-start | bytes 49160 | tf_op jit(solution)/shard_map/ppermute | solution.py:449
  31.4 9.1 %collective-permute-start.15 = (bf16[128,256]{1,0:T(8,128)(2,1)S(1)}, bf16[128,256]{1,0:T(8,128)(2,1)S(1)}, u32[]{:S(2)}, u32[]{:S(2)}) collective-permute-start(bf16[128,256]{1,0:T(8,128)(2,1)S(1)} %get-tuple-element.55.refs_0_), channel_id=1, source_target_pairs={{0,2},{1,3},{2,0},{3,1},{4,6},{5,7},{6,4},{7,5},{8,10},{9,11},{10,... | collective-permute-start | bytes 196616 | tf_op jit(solution)/shard_map/ppermute | solution.py:367
  35.8 6.1 %collective-permute-start.14 = (bf16[128,256]{1,0:T(8,128)(2,1)S(1)}, bf16[128,256]{1,0:T(8,128)(2,1)S(1)}, u32[]{:S(2)}, u32[]{:S(2)}) collective-permute-start(bf16[128,256]{1,0:T(8,128)(2,1)S(1)} %get-tuple-element.55.refs_0_), channel_id=1, source_target_pairs={{0,3},{1,2},{2,1},{3,0},{4,7},{5,6},{6,5},{7,4},{8,11},{9,10},{10,... | collective-permute-start | bytes 196616 | tf_op jit(solution)/shard_map/ppermute | solution.py:367
  36.3 5.6 %collective-permute-start.13 = (bf16[128,256]{1,0:T(8,128)(2,1)S(1)}, bf16[128,256]{1,0:T(8,128)(2,1)S(1)}, u32[]{:S(2)}, u32[]{:S(2)}) collective-permute-start(bf16[128,256]{1,0:T(8,128)(2,1)S(1)} %get-tuple-element.55.refs_0_), channel_id=1, source_target_pairs={{0,1},{1,0},{2,3},{3,2},{4,5},{5,4},{6,7},{7,6},{8,9},{9,8},{10,11... | collective-permute-start | bytes 196616 | tf_op jit(solution)/shard_map/ppermute | solution.py:367

commit v14 on v13

--- a/solution.py
+++ b/solution.py
@@ -263,10 +263,10 @@
     chosen = (
         lax.broadcasted_iota(jnp.int32, (part_atoms, near.shape[1]), 0) == near
     ).astype(jnp.bfloat16)
-    chunks = row_chunks(base_ref.shape[0], LONG)
+    chunks = row_chunks(base_ref.shape[0])
     gathered = None
-    for first in range(0, len(chunks), 2):
-        group = chunks[first : first + 2]
+    for first in range(0, len(chunks), 4):
+        group = chunks[first : first + 4]
         picked = [
             picked_rows(fetch_ref[rows, :], slots_ref[...], mask_ref[rows, :]) for rows in group
         ]
@@ -314,6 +314,12 @@
         )
 
 
+def final_chunks(rows):
+    *chunks, last = row_chunks(rows)
+    middle = (last.start + last.stop) // 2
+    return chunks + [slice(last.start, middle), slice(middle, last.stop)]
+
+
 def final_kernel(shards, scale, *refs):
     sums = refs[:shards]
     atoms_ref, weight_ref, state_ref, side_ref, chosen_ref, fixed_ref, onward_ref = refs[
@@ -338,7 +344,7 @@
     own_copy = pltpu.make_async_copy(own_ref, own_hbm, sems.at[0])
     own_copy.start()
     copies = [own_copy]
-    chunks = row_chunks(state_ref.shape[0])
+    chunks = final_chunks(state_ref.shape[0])
     for first in range(0, len(chunks), 2):
         group = chunks[first : first + 2]
         found = [product(chosen_ref[rows, :], table_ref[...]) + side_ref[rows, :] for rows in group]
@@ -485,7 +491,7 @@
             pltpu.VMEM((2 * part_atoms, wide), jnp.bfloat16),
             pltpu.VMEM((rows, wide), jnp.bfloat16),
             pltpu.VMEM((count, atom_wide), jnp.bfloat16),
-            pltpu.SemaphoreType.DMA((1 + len(row_chunks(rows)),)),
+            pltpu.SemaphoreType.DMA((1 + len(final_chunks(rows)),)),
         ],
         flops=4 * rows * part_atoms * wide,
         nbytes=8 * rows * wide,

time: 44 us -> 43.9 us (level)
  no operation moved by 1% of the time
where the time goes in v14:
time: 43.9 us; the launch traced here: 43.7 us
  starting transfers between devices  20.4 us (46%)
  Pallas kernels  14.5 us (33%)
  waiting for transfers between devices  8.01 us (18%)
  between operations  0.73 us (2%)
    pallas_call x7, Pallas kernels, call(): pl.pallas_call(kernel, out_shape=outs, in_specs=[pl.BlockSpec(memory_spac...  14.5 us
    ppermute x9, starting transfers between devices, from_others(): lax.ppermute(value, 'edge', [(at, at ^ by) for at in range(len(order))])  14.1 us
    ppermute x9, waiting for transfers between devices, from_others(): lax.ppermute(value, 'edge', [(at, at ^ by) for at in range(len(order))])  6.57 us
    ppermute x7, starting transfers between devices, body(): lax.ppermute(block, 'dom', [(at, at ^ partners - place) for at in range(d...  6.31 us
    ppermute x7, waiting for transfers between devices, body(): lax.ppermute(block, 'dom', [(at, at ^ partners - place) for at in range(d...  1.44 us
  transfers between devices with their start and end apart: 16, of which 6 were waited for; matrix products, arithmetic and copies ran while one was open for 0% of the time, Pallas kernels for 18%

profile of v14, /device:TPU:0, one launch (start us, length us, event | category | flops | bytes accessed | tf_op | source)
XLA Modules:
  0.0 43.7 jit_solution(16129363103356984209)
XLA Ops:
  0.7 2.5 %shard_map.141.refs_2_ = bf16[512,128]{1,0:T(8,128)(2,1)S(1)} custom-call(bf16[1024,512]{1,0:T(8,128)(2,1)} %edges_hbm.1, bf16[512,512]{1,0:T(8,128)(2,1)} %weight_hbm.1, bf16[64,512]{1,0:T(8,128)(2,1)} %down_hbm.1), custom_call_target="tpu_custom_call" | custom-call | flops 603979776 | bytes 1572864 | tf_op jit(solution)/shard_map/pallas_call | solution.py:49
  3.2 4.1 %collective-permute-start.2 = (bf16[512,128]{1,0:T(8,128)(2,1)S(1)}, bf16[512,128]{1,0:T(8,128)(2,1)S(1)}, u32[]{:S(2)}, u32[]{:S(2)}) collective-permute-start(bf16[512,128]{1,0:T(8,128)(2,1)S(1)} %shard_map.141.refs_2_), channel_id=1, source_target_pairs={{0,2},{1,3},{2,0},{3,1},{4,6},{5,7},{6,4},{7,5},{8,10},{9,11},{10,... | collective-permute-start | bytes 393224 | tf_op jit(solution)/shard_map/ppermute | solution.py:373
  7.3 1.3 %collective-permute-start.1 = (bf16[512,128]{1,0:T(8,128)(2,1)S(1)}, bf16[512,128]{1,0:T(8,128)(2,1)S(1)}, u32[]{:S(2)}, u32[]{:S(2)}) collective-permute-start(bf16[512,128]{1,0:T(8,128)(2,1)S(1)} %shard_map.141.refs_2_), channel_id=1, source_target_pairs={{0,3},{1,2},{2,1},{3,0},{4,7},{5,6},{6,5},{7,4},{8,11},{9,10},{10,... | collective-permute-start | bytes 393224 | tf_op jit(solution)/shard_map/ppermute | solution.py:373
  8.6 0.2 collective-permute-start
  8.8 2.9 %collective-permute-start.4 = (bf16[32,256]{1,0:T(8,128)(2,1)S(1)}, bf16[32,256]{1,0:T(8,128)(2,1)S(1)}, u32[]{:S(2)}, u32[]{:S(2)}) collective-permute-start(bf16[32,256]{1,0:T(8,128)(2,1)S(1)} %copy-done), channel_id=1, source_target_pairs={{0,3},{1,2},{2,1},{3,0},{4,7},{5,6},{6,5},{7,4},{8,11},{9,10},{10,... | collective-permute-start | bytes 49160 | tf_op jit(solution)/shard_map/ppermute | solution.py:373
  11.8 0.5 %collective-permute-start.3 = (bf16[32,256]{1,0:T(8,128)(2,1)S(1)}, bf16[32,256]{1,0:T(8,128)(2,1)S(1)}, u32[]{:S(2)}, u32[]{:S(2)}) collective-permute-start(bf16[32,256]{1,0:T(8,128)(2,1)S(1)} %copy-done), channel_id=1, source_target_pairs={{0,1},{1,0},{2,3},{3,2},{4,5},{5,4},{6,7},{7,6},{8,9},{9,8},{10,11... | collective-permute-start | bytes 49160 | tf_op jit(solution)/shard_map/ppermute | solution.py:373
  12.2 0.1 copy.15.refs_0_
  12.3 3.9 %shard_map.140 = (bf16[896,256]{1,0:T(8,128)(2,1)S(1)}, bf16[896,256]{1,0:T(8,128)(2,1)S(1)}, bf16[1024,256]{1,0:T(8,128)(2,1)S(1)}, bf16[1024,256]{1,0:T(8,128)...) custom-call(s32[1,1024]{1,0:T(1,128)S(1)} %bitcast.1, ...), custom_call_target="tpu_custom_call" | custom-call | flops 41943040 | bytes 6291456 | tf_op jit(solution)/shard_map/pallas_call | solution.py:49
  16.2 1.2 %collective-permute-done.2.refs_5_ = bf16[512,128]{1,0:T(8,128)(2,1)S(1)} collective-permute-done((bf16[512,128]{1,0:T(8,128)(2,1)S(1)}, bf16[512,128]{1,0:T(8,128)(2,1)S(1)}, u32[]{:S(2)}, u32[]{:S(2)}) %collective-permute-start.2) | collective-permute-done | bytes 131104 | tf_op jit(solution)/shard_map/ppermute | solution.py:373
  17.4 0.0 collective-permute-start.5
  17.4 0.0 collective-permute-done.1.refs_4_
  17.4 0.9 %collective-permute-done.refs_3_ = bf16[512,128]{1,0:T(8,128)(2,1)S(1)} collective-permute-done((bf16[512,128]{1,0:T(8,128)(2,1)S(1)}, bf16[512,128]{1,0:T(8,128)(2,1)S(1)}, u32[]{:S(2)}, u32[]{:S(2)}) %collective-permute-start) | collective-permute-done | bytes 131104 | tf_op jit(solution)/shard_map/ppermute | solution.py:373
  18.3 1.7 %shard_map.142 = (bf16[256,256]{1,0:T(8,128)(2,1)S(1)}, bf16[64,128]{1,0:T(8,128)(2,1)S(1)}, bf16[64,128]{1,0:T(8,128)(2,1)S(1)}, bf16[64,128]{1,0:T(8,128)(2,1)...) custom-call(s32[16,2]{1,0:T(8,128)S(1)} %copy.15.refs_0_, ...), custom_call_target="tpu_custom_call" | custom-call | flops 134217728 | bytes 2097152 | tf_op jit(solution)/shard_map/pallas_call | solution.py:49
  20.0 0.1 collective-permute-start.6
  20.1 2.6 %collective-permute-start.7 = (bf16[64,128]{1,0:T(8,128)(2,1)S(1)}, bf16[64,128]{1,0:T(8,128)(2,1)S(1)}, u32[]{:S(2)}, u32[]{:S(2)}) collective-permute-start(bf16[64,128]{1,0:T(8,128)(2,1)S(1)} %get-tuple-element.49), channel_id=1, source_target_pairs={{0,24},{4,28},{8,16},{12,20},{16,8},{20,12},{24,0},{28,4},{1,25},{... | collective-permute-start | bytes 49160 | tf_op jit(solution)/shard_map/ppermute | solution.py:455
  22.7 0.0 collective-permute-done.4.refs_8_
  22.7 1.4 %collective-permute-start.8 = (bf16[64,128]{1,0:T(8,128)(2,1)S(1)}, bf16[64,128]{1,0:T(8,128)(2,1)S(1)}, u32[]{:S(2)}, u32[]{:S(2)}) collective-permute-start(bf16[64,128]{1,0:T(8,128)(2,1)S(1)} %get-tuple-element.50), channel_id=1, source_target_pairs={{0,20},{4,16},{8,28},{12,24},{16,4},{20,0},{24,12},{28,8},{1,21},{... | collective-permute-start | bytes 49160 | tf_op jit(solution)/shard_map/ppermute | solution.py:455
  24.0 0.5 %collective-permute-start.9 = (bf16[64,128]{1,0:T(8,128)(2,1)S(1)}, bf16[64,128]{1,0:T(8,128)(2,1)S(1)}, u32[]{:S(2)}, u32[]{:S(2)}) collective-permute-start(bf16[64,128]{1,0:T(8,128)(2,1)S(1)} %get-tuple-element.51), channel_id=1, source_target_pairs={{0,16},{4,20},{8,24},{12,28},{16,0},{20,4},{24,8},{28,12},{1,17},{... | collective-permute-start | bytes 49160 | tf_op jit(solution)/shard_map/ppermute | solution.py:455
  24.5 0.8 %collective-permute-start.10 = (bf16[64,128]{1,0:T(8,128)(2,1)S(1)}, bf16[64,128]{1,0:T(8,128)(2,1)S(1)}, u32[]{:S(2)}, u32[]{:S(2)}) collective-permute-start(bf16[64,128]{1,0:T(8,128)(2,1)S(1)} %get-tuple-element.52), channel_id=1, source_target_pairs={{0,12},{4,8},{8,4},{12,0},{16,28},{20,24},{24,20},{28,16},{1,13},{... | collective-permute-start | bytes 49160 | tf_op jit(solution)/shard_map/ppermute | solution.py:455
  25.3 0.9 %collective-permute-start.11 = (bf16[64,128]{1,0:T(8,128)(2,1)S(1)}, bf16[64,128]{1,0:T(8,128)(2,1)S(1)}, u32[]{:S(2)}, u32[]{:S(2)}) collective-permute-start(bf16[64,128]{1,0:T(8,128)(2,1)S(1)} %get-tuple-element.53), channel_id=1, source_target_pairs={{0,8},{4,12},{8,0},{12,4},{16,24},{20,28},{24,16},{28,20},{1,9},{5... | collective-permute-start | bytes 49160 | tf_op jit(solution)/shard_map/ppermute | solution.py:455
  26.2 0.2 collective-permute-start.12
  26.4 1.3 %shard_map.143 = (f32[1024,512]{1,0:T(8,128)S(1)}, bf16[128,256]{1,0:T(8,128)(2,1)S(1)}) custom-call(bf16[1024,512]{1,0:T(8,128)(2,1)S(1)} %get-tuple-element.33.refs_0_, bf16[256,256]{1,0:T(8,128)(2,1)S(1)} %get-tuple-element.37.refs_1_, bf16[1024,256]{1,0:T(8,128)(2,1)S(1)} %get-tuple-element.38.refs_2_, bf16[1024,256]{1,0:T(8,128)(2,1)S(1)} %get-tuple-element.39.refs_3_, ...), custom_call_target="tpu_custom_call" | custom-call | flops 268435456 | bytes 5242880 | tf_op jit(solution)/shard_map/pallas_call | solution.py:49
  27.7 0.1 collective-permute-done.9.refs_10_
  27.8 1.3 %collective-permute-done.11.refs_12_ = bf16[64,128]{1,0:T(8,128)(2,1)S(1)} collective-permute-done((bf16[64,128]{1,0:T(8,128)(2,1)S(1)}, bf16[64,128]{1,0:T(8,128)(2,1)S(1)}, u32[]{:S(2)}, u32[]{:S(2)}) %collective-permute-start.11) | collective-permute-done | bytes 16416 | tf_op jit(solution)/shard_map/ppermute | solution.py:455
  29.1 2.3 %shard_map.144 = (bf16[1024,512]{1,0:T(8,128)(2,1)S(1)}, bf16[128,256]{1,0:T(8,128)(2,1)S(1)}) custom-call(f32[1024,512]{1,0:T(8,128)S(1)} %get-tuple-element.42.refs_0_, bf16[1024,256]{1,0:T(8,128)(2,1)S(1)} %get-tuple-element.43.refs_1_, bf16[1024,256]{1,0:T(8,128)(2,1)S(1)} %get-tuple-element.44.refs_2_, ...), custom_call_target="tpu_custom_call" | custom-call | flops 1073741824 | bytes 4194304 | tf_op jit(solution)/shard_map/pallas_call | solution.py:49
  31.4 4.4 %collective-permute-start.15 = (bf16[128,256]{1,0:T(8,128)(2,1)S(1)}, bf16[128,256]{1,0:T(8,128)(2,1)S(1)}, u32[]{:S(2)}, u32[]{:S(2)}) collective-permute-start(bf16[128,256]{1,0:T(8,128)(2,1)S(1)} %get-tuple-element.55.refs_0_), channel_id=1, source_target_pairs={{0,2},{1,3},{2,0},{3,1},{4,6},{5,7},{6,4},{7,5},{8,10},{9,11},{10,... | collective-permute-start | bytes 196616 | tf_op jit(solution)/shard_map/ppermute | solution.py:373
  35.8 0.5 %collective-permute-start.14 = (bf16[128,256]{1,0:T(8,128)(2,1)S(1)}, bf16[128,256]{1,0:T(8,128)(2,1)S(1)}, u32[]{:S(2)}, u32[]{:S(2)}) collective-permute-start(bf16[128,256]{1,0:T(8,128)(2,1)S(1)} %get-tuple-element.55.refs_0_), channel_id=1, source_target_pairs={{0,3},{1,2},{2,1},{3,0},{4,7},{5,6},{6,5},{7,4},{8,11},{9,10},{10,... | collective-permute-start | bytes 196616 | tf_op jit(solution)/shard_map/ppermute | solution.py:373
  36.3 0.2 collective-permute-start.13
  36.4 1.0 %shard_map.145 = (f32[1024,512]{1,0:T(8,128)S(1)}, bf16[1024,256]{1,0:T(8,128)(2,1)S(1)}, f32[256,512]{1,0:T(8,128)S(1)}, bf16[512,512]{1,0:T(8,128)(2,1)S(1)}) custom-call(bf16[1024,512]{1,0:T(8,128)(2,1)S(1)} %get-tuple-element.58.refs_0_.refs_6_, bf16[1024,512]{1,0:T(8,128)(2,1)S(1)} %get-tuple-element.59.refs_1_, ...), custom_call_target="tpu_custom_call" | custom-call | flops 536870912 | bytes 4194304 | tf_op jit(solution)/shard_map/pallas_call | solution.py:49
  37.4 3.0 %collective-permute-done.15.refs_3_ = bf16[128,256]{1,0:T(8,128)(2,1)S(1)} collective-permute-done((bf16[128,256]{1,0:T(8,128)(2,1)S(1)}, bf16[128,256]{1,0:T(8,128)(2,1)S(1)}, u32[]{:S(2)}, u32[]{:S(2)}) %collective-permute-start.15) | collective-permute-done | bytes 65568 | tf_op jit(solution)/shard_map/ppermute | solution.py:373
  40.4 1.5 %collective-permute-done.14.refs_2_ = bf16[128,256]{1,0:T(8,128)(2,1)S(1)} collective-permute-done((bf16[128,256]{1,0:T(8,128)(2,1)S(1)}, bf16[128,256]{1,0:T(8,128)(2,1)S(1)}, u32[]{:S(2)}, u32[]{:S(2)}) %collective-permute-start.14) | collective-permute-done | bytes 65568 | tf_op jit(solution)/shard_map/ppermute | solution.py:373
  41.9 1.9 %shard_map.146 = (bf16[1024,512]{1,0:T(8,128)(2,1)}, bf16[32,256]{1,0:T(8,128)(2,1)}) custom-call(bf16[128,256]{1,0:T(8,128)(2,1)S(1)} %get-tuple-element.55.refs_0_, bf16[128,256]{1,0:T(8,128)(2,1)S(1)} %collective-permute-done.13.refs_1_, bf16[128,256]{1,0:T(8,128)(2,1)S(1)} %collective-permute-done.14.refs_2_, ...), custom_call_target="tpu_custom_call" | custom-call | flops 268435456 | bytes 4194304 | tf_op jit(solution)/shard_map/pallas_call | solution.py:49
  (14 shorter events, 0.0 us)
Async XLA Ops:
  0.6 8.2 %copy-start = (bf16[32,256]{1,0:T(8,128)(2,1)S(1)}, bf16[32,256]{1,0:T(8,128)(2,1)}, u32[]{:S(2)}) copy-start(bf16[32,256]{1,0:T(8,128)(2,1)} %refs_6_.3) | copy-start | bytes 49156
  0.6 11.6 %copy-start.2 = (s32[16,2]{0,1:T(2,128)S(1)}, s32[16,2]{0,1:T(2,128)}, u32[]{:S(2)}) copy-start(s32[16,2]{0,1:T(2,128)} %param.17) | copy-start | bytes 388
  0.7 11.6 %copy-start.1 = (s32[1024]{0:T(1024)S(1)}, s32[1024]{0:T(1024)}, u32[]{:S(2)}) copy-start(s32[1024]{0:T(1024)} %param.15) | copy-start | bytes 12292
  3.2 14.3 %collective-permute-start.2 = (bf16[512,128]{1,0:T(8,128)(2,1)S(1)}, bf16[512,128]{1,0:T(8,128)(2,1)S(1)}, u32[]{:S(2)}, u32[]{:S(2)}) collective-permute-start(bf16[512,128]{1,0:T(8,128)(2,1)S(1)} %shard_map.141.refs_2_), channel_id=1, source_target_pairs={{0,2},{1,3},{2,0},{3,1},{4,6},{5,7},{6,4},{7,5},{8,10},{9,11},{10,... | collective-permute-start | bytes 393224 | tf_op jit(solution)/shard_map/ppermute | solution.py:373
  7.3 10.2 %collective-permute-start.1 = (bf16[512,128]{1,0:T(8,128)(2,1)S(1)}, bf16[512,128]{1,0:T(8,128)(2,1)S(1)}, u32[]{:S(2)}, u32[]{:S(2)}) collective-permute-start(bf16[512,128]{1,0:T(8,128)(2,1)S(1)} %shard_map.141.refs_2_), channel_id=1, source_target_pairs={{0,3},{1,2},{2,1},{3,0},{4,7},{5,6},{6,5},{7,4},{8,11},{9,10},{10,... | collective-permute-start | bytes 393224 | tf_op jit(solution)/shard_map/ppermute | solution.py:373
  8.6 9.7 %collective-permute-start = (bf16[512,128]{1,0:T(8,128)(2,1)S(1)}, bf16[512,128]{1,0:T(8,128)(2,1)S(1)}, u32[]{:S(2)}, u32[]{:S(2)}) collective-permute-start(bf16[512,128]{1,0:T(8,128)(2,1)S(1)} %shard_map.141.refs_2_), channel_id=1, source_target_pairs={{0,1},{1,0},{2,3},{3,2},{4,5},{5,4},{6,7},{7,6},{8,9},{9,8},{10,11... | collective-permute-start | bytes 393224 | tf_op jit(solution)/shard_map/ppermute | solution.py:373
  8.8 13.8 %collective-permute-start.4 = (bf16[32,256]{1,0:T(8,128)(2,1)S(1)}, bf16[32,256]{1,0:T(8,128)(2,1)S(1)}, u32[]{:S(2)}, u32[]{:S(2)}) collective-permute-start(bf16[32,256]{1,0:T(8,128)(2,1)S(1)} %copy-done), channel_id=1, source_target_pairs={{0,3},{1,2},{2,1},{3,0},{4,7},{5,6},{6,5},{7,4},{8,11},{9,10},{10,... | collective-permute-start | bytes 49160 | tf_op jit(solution)/shard_map/ppermute | solution.py:373
  11.8 12.3 %collective-permute-start.3 = (bf16[32,256]{1,0:T(8,128)(2,1)S(1)}, bf16[32,256]{1,0:T(8,128)(2,1)S(1)}, u32[]{:S(2)}, u32[]{:S(2)}) collective-permute-start(bf16[32,256]{1,0:T(8,128)(2,1)S(1)} %copy-done), channel_id=1, source_target_pairs={{0,1},{1,0},{2,3},{3,2},{4,5},{5,4},{6,7},{7,6},{8,9},{9,8},{10,11... | collective-permute-start | bytes 49160 | tf_op jit(solution)/shard_map/ppermute | solution.py:373
  17.4 7.1 %collective-permute-start.5 = (bf16[32,256]{1,0:T(8,128)(2,1)S(1)}, bf16[32,256]{1,0:T(8,128)(2,1)S(1)}, u32[]{:S(2)}, u32[]{:S(2)}) collective-permute-start(bf16[32,256]{1,0:T(8,128)(2,1)S(1)} %copy-done), channel_id=1, source_target_pairs={{0,2},{1,3},{2,0},{3,1},{4,6},{5,7},{6,4},{7,5},{8,10},{9,11},{10,... | collective-permute-start | bytes 49160 | tf_op jit(solution)/shard_map/ppermute | solution.py:373
  20.0 5.3 %collective-permute-start.6 = (bf16[64,128]{1,0:T(8,128)(2,1)S(1)}, bf16[64,128]{1,0:T(8,128)(2,1)S(1)}, u32[]{:S(2)}, u32[]{:S(2)}) collective-permute-start(bf16[64,128]{1,0:T(8,128)(2,1)S(1)} %get-tuple-element.48), channel_id=1, source_target_pairs={{0,28},{4,24},{8,20},{12,16},{16,12},{20,8},{24,4},{28,0},{1,29},{... | collective-permute-start | bytes 49160 | tf_op jit(solution)/shard_map/ppermute | solution.py:455
  20.1 6.1 %collective-permute-start.7 = (bf16[64,128]{1,0:T(8,128)(2,1)S(1)}, bf16[64,128]{1,0:T(8,128)(2,1)S(1)}, u32[]{:S(2)}, u32[]{:S(2)}) collective-permute-start(bf16[64,128]{1,0:T(8,128)(2,1)S(1)} %get-tuple-element.49), channel_id=1, source_target_pairs={{0,24},{4,28},{8,16},{12,20},{16,8},{20,12},{24,0},{28,4},{1,25},{... | collective-permute-start | bytes 49160 | tf_op jit(solution)/shard_map/ppermute | solution.py:455
  22.7 5.0 %collective-permute-start.8 = (bf16[64,128]{1,0:T(8,128)(2,1)S(1)}, bf16[64,128]{1,0:T(8,128)(2,1)S(1)}, u32[]{:S(2)}, u32[]{:S(2)}) collective-permute-start(bf16[64,128]{1,0:T(8,128)(2,1)S(1)} %get-tuple-element.50), channel_id=1, source_target_pairs={{0,20},{4,16},{8,28},{12,24},{16,4},{20,0},{24,12},{28,8},{1,21},{... | collective-permute-start | bytes 49160 | tf_op jit(solution)/shard_map/ppermute | solution.py:455
  24.0 3.7 %collective-permute-start.9 = (bf16[64,128]{1,0:T(8,128)(2,1)S(1)}, bf16[64,128]{1,0:T(8,128)(2,1)S(1)}, u32[]{:S(2)}, u32[]{:S(2)}) collective-permute-start(bf16[64,128]{1,0:T(8,128)(2,1)S(1)} %get-tuple-element.51), channel_id=1, source_target_pairs={{0,16},{4,20},{8,24},{12,28},{16,0},{20,4},{24,8},{28,12},{1,17},{... | collective-permute-start | bytes 49160 | tf_op jit(solution)/shard_map/ppermute | solution.py:455
  24.5 3.3 %collective-permute-start.10 = (bf16[64,128]{1,0:T(8,128)(2,1)S(1)}, bf16[64,128]{1,0:T(8,128)(2,1)S(1)}, u32[]{:S(2)}, u32[]{:S(2)}) collective-permute-start(bf16[64,128]{1,0:T(8,128)(2,1)S(1)} %get-tuple-element.52), channel_id=1, source_target_pairs={{0,12},{4,8},{8,4},{12,0},{16,28},{20,24},{24,20},{28,16},{1,13},{... | collective-permute-start | bytes 49160 | tf_op jit(solution)/shard_map/ppermute | solution.py:455
  25.3 3.8 %collective-permute-start.11 = (bf16[64,128]{1,0:T(8,128)(2,1)S(1)}, bf16[64,128]{1,0:T(8,128)(2,1)S(1)}, u32[]{:S(2)}, u32[]{:S(2)}) collective-permute-start(bf16[64,128]{1,0:T(8,128)(2,1)S(1)} %get-tuple-element.53), channel_id=1, source_target_pairs={{0,8},{4,12},{8,0},{12,4},{16,24},{20,28},{24,16},{28,20},{1,9},{5... | collective-permute-start | bytes 49160 | tf_op jit(solution)/shard_map/ppermute | solution.py:455
  26.2 2.9 %collective-permute-start.12 = (bf16[64,128]{1,0:T(8,128)(2,1)S(1)}, bf16[64,128]{1,0:T(8,128)(2,1)S(1)}, u32[]{:S(2)}, u32[]{:S(2)}) collective-permute-start(bf16[64,128]{1,0:T(8,128)(2,1)S(1)} %get-tuple-element.54), channel_id=1, source_target_pairs={{0,4},{4,0},{8,12},{12,8},{16,20},{20,16},{24,28},{28,24},{1,5},{5... | collective-permute-start | bytes 49160 | tf_op jit(solution)/shard_map/ppermute | solution.py:455
  31.4 9.0 %collective-permute-start.15 = (bf16[128,256]{1,0:T(8,128)(2,1)S(1)}, bf16[128,256]{1,0:T(8,128)(2,1)S(1)}, u32[]{:S(2)}, u32[]{:S(2)}) collective-permute-start(bf16[128,256]{1,0:T(8,128)(2,1)S(1)} %get-tuple-element.55.refs_0_), channel_id=1, source_target_pairs={{0,2},{1,3},{2,0},{3,1},{4,6},{5,7},{6,4},{7,5},{8,10},{9,11},{10,... | collective-permute-start | bytes 196616 | tf_op jit(solution)/shard_map/ppermute | solution.py:373
  35.8 6.1 %collective-permute-start.14 = (bf16[128,256]{1,0:T(8,128)(2,1)S(1)}, bf16[128,256]{1,0:T(8,128)(2,1)S(1)}, u32[]{:S(2)}, u32[]{:S(2)}) collective-permute-start(bf16[128,256]{1,0:T(8,128)(2,1)S(1)} %get-tuple-element.55.refs_0_), channel_id=1, source_target_pairs={{0,3},{1,2},{2,1},{3,0},{4,7},{5,6},{6,5},{7,4},{8,11},{9,10},{10,... | collective-permute-start | bytes 196616 | tf_op jit(solution)/shard_map/ppermute | solution.py:373
  36.3 5.6 %collective-permute-start.13 = (bf16[128,256]{1,0:T(8,128)(2,1)S(1)}, bf16[128,256]{1,0:T(8,128)(2,1)S(1)}, u32[]{:S(2)}, u32[]{:S(2)}) collective-permute-start(bf16[128,256]{1,0:T(8,128)(2,1)S(1)} %get-tuple-element.55.refs_0_), channel_id=1, source_target_pairs={{0,1},{1,0},{2,3},{3,2},{4,5},{5,4},{6,7},{7,6},{8,9},{9,8},{10,11... | collective-permute-start | bytes 196616 | tf_op jit(solution)/shard_map/ppermute | solution.py:373

commit v15 on v13

--- a/solution.py
+++ b/solution.py
@@ -52,7 +52,9 @@
         in_specs=[pl.BlockSpec(memory_space=space(at)) for at in range(len(args))],
         out_specs=jax.tree.map(
             lambda out: pl.BlockSpec(
-                memory_space=pltpu.HBM if out.memory_space == pltpu.HBM else pltpu.VMEM
+                memory_space=out.memory_space
+                if out.memory_space in (pltpu.HBM, pltpu.SMEM)
+                else pltpu.VMEM
             ),
             outs,
         ),
@@ -102,7 +104,20 @@
 
 
 def index_kernel(domains, shards, channels, operands, *refs):
-    reverse_ref = refs[0]
+    reverse_ref, source_ref = refs[:2]
+    place_ref = refs[-2]
+    refs = refs[1:]
+    blocks, tile_count = source_ref.shape
+    lines, block_len = reverse_ref.shape[1] // 2, reverse_ref.shape[1] // blocks
+    for at in range(blocks):
+        for tile in range(tile_count):
+            source = source_ref[at, tile]
+            shard = lax.div(source, blocks)
+            within = source - shard * blocks
+            upper = (within >= blocks // 2).astype(jnp.int32)
+            start = (shard ^ lax.axis_index("edge")) * lines
+            start = start + (within - upper * (blocks // 2)) * block_len
+            place_ref[at, tile] = 2 * start + upper
     sources = refs[1 : 1 + operands]
     send_ref, send_mask_ref, fetch_ref, fetch_mask_ref, local_ref, local_mask_ref, stack_ref = refs[
         1 + operands : 8 + operands
@@ -191,18 +206,15 @@
     me = lax.axis_index("edge")
     for part, at in zip(parts, orders(shards)[0]):
         held_ref[at * lines : (at + 1) * lines, :] = part[...]
-    half_blocks = blocks // 2
     channels = trip_ref.shape[1] // GROUPS
     per = blocks // GROUPS
 
     def mixed(block):
         picks = []
         for tile in range(count):
-            source = source_ref[block, tile]
-            shard = lax.div(source, blocks)
-            within = source - shard * blocks
-            upper = (within >= half_blocks).astype(jnp.int32)
-            start = (shard ^ me) * lines + (within - upper * half_blocks) * block_len
+            place = source_ref[block, tile]
+            start = lax.shift_right_logical(place, 1)
+            upper = lax.bitwise_and(place, 1)
             rows = held_ref[pl.ds(pl.multiple_of(start, block_len), block_len), :]
             picks.append(jnp.where(upper == 1, rows[:, channels:], rows[:, :channels]))
         return product(tiles_ref[block], jnp.concatenate(picks, axis=0))
@@ -417,7 +429,7 @@
     )
     each, grouped = rows // GROUPS, GROUPS * channels
     column = domains // 2 * (capacity // 2)
-    send, send_mask, fetch, fetch_mask, local, local_mask, up_stack, *later = call(
+    send, send_mask, fetch, fetch_mask, local, local_mask, up_stack, *later, places = call(
         functools.partial(index_kernel, domains, shards, channels, len(later)),
         (
             shaped((slots, each)),
@@ -428,9 +440,11 @@
             shaped((rows, grouped)),
             shaped((grouped, wide)),
         )
-        + tuple(shaped(each.shape, each.dtype) for each in later),
-        (reverse.reshape(1, rows), *later),
-        hbm=range(1, 1 + len(later)),
+        + tuple(shaped(each.shape, each.dtype) for each in later)
+        + (shaped(tile_source.shape, jnp.int32, pltpu.SMEM),),
+        (reverse.reshape(1, rows), tile_source, *later),
+        smem=(1,),
+        hbm=range(2, 2 + len(later)),
         scratch=[pltpu.SemaphoreType.DMA((len(later) + GROUPS,))],
         flops=40 * rows * rows,
         nbytes=6 * rows * rows,
@@ -439,7 +453,7 @@
     trip_out, *outgoing = call(
         functools.partial(mix_kernel, shards),
         (shaped((each, grouped)),) + (shaped((capacity // 2, packed)),) * partners,
-        (tile_source, tiles, *narrow_parts, send, send_mask),
+        (places, tiles, *narrow_parts, send, send_mask),
         smem=(0,),
         scratch=[pltpu.VMEM((shards * lines, packed), jnp.bfloat16)],
         flops=2 * rows * rows * channels,

time: 44 us -> 43.3 us (0.984)
  waiting for transfers between devices: 8 us -> 5.84 us
  Pallas kernels: 14.6 us -> 15.5 us
  starting transfers between devices: 20.4 us -> 21 us
    ppermute x9, waiting for transfers between devices: 6.56 us -> 4.45 us  [from_others(): lax.ppermute(value, 'edge', [(at, at ^ by) for at in range(len(order))])]
    pallas_call x7, Pallas kernels: 14.6 us -> 15.5 us  [call(): pl.pallas_call(kernel, out_shape=outs, in_specs=[pl.BlockSpec(memory_spac...]
    ppermute x9, starting transfers between devices: 14.1 us -> 14.6 us  [from_others(): lax.ppermute(value, 'edge', [(at, at ^ by) for at in range(len(order))])]
  transfers between devices with their start and end apart: 16 -> 16, of which waited for: 6 -> 4; matrix products, arithmetic and copies ran while one was open for 0% -> 0% of each run, Pallas kernels for 18% -> 20%
where the time goes in v15:
time: 43.3 us; the launch traced here: 43.1 us
  starting transfers between devices  21 us (48%)
  Pallas kernels  15.5 us (36%)
  waiting for transfers between devices  5.84 us (13%)
  between operations  0.73 us (2%)
    pallas_call x7, Pallas kernels, call(): pl.pallas_call(kernel, out_shape=outs, in_specs=[pl.BlockSpec(memory_spac...  15.5 us
    ppermute x9, starting transfers between devices, from_others(): lax.ppermute(value, 'edge', [(at, at ^ by) for at in range(len(order))])  14.6 us
    ppermute x7, starting transfers between devices, body(): lax.ppermute(block, 'dom', [(at, at ^ partners - place) for at in range(d...  6.32 us
    ppermute x9, waiting for transfers between devices, from_others(): lax.ppermute(value, 'edge', [(at, at ^ by) for at in range(len(order))])  4.45 us
    ppermute x7, waiting for transfers between devices, body(): lax.ppermute(block, 'dom', [(at, at ^ partners - place) for at in range(d...  1.39 us
  transfers between devices with their start and end apart: 16, of which 4 were waited for; matrix products, arithmetic and copies ran while one was open for 0% of the time, Pallas kernels for 20%

profile of v15, /device:TPU:0, one launch (start us, length us, event | category | flops | bytes accessed | tf_op | source)
XLA Modules:
  0.0 43.1 jit_solution(11005156704044428181)
XLA Ops:
  0.7 2.5 %shard_map.141.refs_2_ = bf16[512,128]{1,0:T(8,128)(2,1)S(1)} custom-call(bf16[1024,512]{1,0:T(8,128)(2,1)} %edges_hbm.1, bf16[512,512]{1,0:T(8,128)(2,1)} %weight_hbm.1, bf16[64,512]{1,0:T(8,128)(2,1)} %down_hbm.1), custom_call_target="tpu_custom_call" | custom-call | flops 603979776 | bytes 1572864 | tf_op jit(solution)/shard_map/pallas_call | solution.py:49
  3.2 4.1 %collective-permute-start.2 = (bf16[512,128]{1,0:T(8,128)(2,1)S(1)}, bf16[512,128]{1,0:T(8,128)(2,1)S(1)}, u32[]{:S(2)}, u32[]{:S(2)}) collective-permute-start(bf16[512,128]{1,0:T(8,128)(2,1)S(1)} %shard_map.141.refs_2_), channel_id=1, source_target_pairs={{0,2},{1,3},{2,0},{3,1},{4,6},{5,7},{6,4},{7,5},{8,10},{9,11},{10,... | collective-permute-start | bytes 393224 | tf_op jit(solution)/shard_map/ppermute | solution.py:379
  7.3 1.3 %collective-permute-start.1 = (bf16[512,128]{1,0:T(8,128)(2,1)S(1)}, bf16[512,128]{1,0:T(8,128)(2,1)S(1)}, u32[]{:S(2)}, u32[]{:S(2)}) collective-permute-start(bf16[512,128]{1,0:T(8,128)(2,1)S(1)} %shard_map.141.refs_2_), channel_id=1, source_target_pairs={{0,3},{1,2},{2,1},{3,0},{4,7},{5,6},{6,5},{7,4},{8,11},{9,10},{10,... | collective-permute-start | bytes 393224 | tf_op jit(solution)/shard_map/ppermute | solution.py:379
  8.6 0.2 collective-permute-start
  8.8 2.9 %collective-permute-start.4 = (bf16[32,256]{1,0:T(8,128)(2,1)S(1)}, bf16[32,256]{1,0:T(8,128)(2,1)S(1)}, u32[]{:S(2)}, u32[]{:S(2)}) collective-permute-start(bf16[32,256]{1,0:T(8,128)(2,1)S(1)} %copy-done), channel_id=1, source_target_pairs={{0,3},{1,2},{2,1},{3,0},{4,7},{5,6},{6,5},{7,4},{8,11},{9,10},{10,... | collective-permute-start | bytes 49160 | tf_op jit(solution)/shard_map/ppermute | solution.py:379
  11.8 0.5 %collective-permute-start.3 = (bf16[32,256]{1,0:T(8,128)(2,1)S(1)}, bf16[32,256]{1,0:T(8,128)(2,1)S(1)}, u32[]{:S(2)}, u32[]{:S(2)}) collective-permute-start(bf16[32,256]{1,0:T(8,128)(2,1)S(1)} %copy-done), channel_id=1, source_target_pairs={{0,1},{1,0},{2,3},{3,2},{4,5},{5,4},{6,7},{7,6},{8,9},{9,8},{10,11... | collective-permute-start | bytes 49160 | tf_op jit(solution)/shard_map/ppermute | solution.py:379
  12.2 0.1 copy.15.refs_1_
  12.3 5.5 %shard_map.140 = (bf16[896,256]{1,0:T(8,128)(2,1)S(1)}, bf16[896,256]{1,0:T(8,128)(2,1)S(1)}, bf16[1024,256]{1,0:T(8,128)(2,1)S(1)}, bf16[1024,256]{1,0:T(8,128)...) custom-call(s32[1,1024]{1,0:T(1,128)S(1)} %bitcast.1, ...), custom_call_target="tpu_custom_call" | custom-call | flops 41943040 | bytes 6291456 | tf_op jit(solution)/shard_map/pallas_call | solution.py:49
  17.8 1.1 %collective-permute-start.5 = (bf16[32,256]{1,0:T(8,128)(2,1)S(1)}, bf16[32,256]{1,0:T(8,128)(2,1)S(1)}, u32[]{:S(2)}, u32[]{:S(2)}) collective-permute-start(bf16[32,256]{1,0:T(8,128)(2,1)S(1)} %copy-done), channel_id=1, source_target_pairs={{0,2},{1,3},{2,0},{3,1},{4,6},{5,7},{6,4},{7,5},{8,10},{9,11},{10,... | collective-permute-start | bytes 49160 | tf_op jit(solution)/shard_map/ppermute | solution.py:379
  18.9 0.0 collective-permute-done.1.refs_4_
  18.9 0.0 collective-permute-done.refs_3_
  18.9 1.1 %shard_map.142 = (bf16[256,256]{1,0:T(8,128)(2,1)S(1)}, bf16[64,128]{1,0:T(8,128)(2,1)S(1)}, bf16[64,128]{1,0:T(8,128)(2,1)S(1)}, bf16[64,128]{1,0:T(8,128)(2,1)...) custom-call(s32[16,2]{1,0:T(8,128)S(4)} %get-tuple-element.35.refs_0, ...), custom_call_target="tpu_custom_call" | custom-call | flops 134217728 | bytes 2097152 | tf_op jit(solution)/shard_map/pallas_call | solution.py:49
  20.0 0.5 %collective-permute-start.6 = (bf16[64,128]{1,0:T(8,128)(2,1)S(1)}, bf16[64,128]{1,0:T(8,128)(2,1)S(1)}, u32[]{:S(2)}, u32[]{:S(2)}) collective-permute-start(bf16[64,128]{1,0:T(8,128)(2,1)S(1)} %get-tuple-element.50), channel_id=1, source_target_pairs={{0,28},{4,24},{8,20},{12,16},{16,12},{20,8},{24,4},{28,0},{1,29},{... | collective-permute-start | bytes 49160 | tf_op jit(solution)/shard_map/ppermute | solution.py:463
  20.5 2.0 %collective-permute-start.7 = (bf16[64,128]{1,0:T(8,128)(2,1)S(1)}, bf16[64,128]{1,0:T(8,128)(2,1)S(1)}, u32[]{:S(2)}, u32[]{:S(2)}) collective-permute-start(bf16[64,128]{1,0:T(8,128)(2,1)S(1)} %get-tuple-element.51), channel_id=1, source_target_pairs={{0,24},{4,28},{8,16},{12,20},{16,8},{20,12},{24,0},{28,4},{1,25},{... | collective-permute-start | bytes 49160 | tf_op jit(solution)/shard_map/ppermute | solution.py:463
  22.6 1.4 %collective-permute-start.8 = (bf16[64,128]{1,0:T(8,128)(2,1)S(1)}, bf16[64,128]{1,0:T(8,128)(2,1)S(1)}, u32[]{:S(2)}, u32[]{:S(2)}) collective-permute-start(bf16[64,128]{1,0:T(8,128)(2,1)S(1)} %get-tuple-element.52), channel_id=1, source_target_pairs={{0,20},{4,16},{8,28},{12,24},{16,4},{20,0},{24,12},{28,8},{1,21},{... | collective-permute-start | bytes 49160 | tf_op jit(solution)/shard_map/ppermute | solution.py:463
  23.9 0.0 collective-permute-done.3.refs_7_
  23.9 0.5 %collective-permute-start.9 = (bf16[64,128]{1,0:T(8,128)(2,1)S(1)}, bf16[64,128]{1,0:T(8,128)(2,1)S(1)}, u32[]{:S(2)}, u32[]{:S(2)}) collective-permute-start(bf16[64,128]{1,0:T(8,128)(2,1)S(1)} %get-tuple-element.53), channel_id=1, source_target_pairs={{0,16},{4,20},{8,24},{12,28},{16,0},{20,4},{24,8},{28,12},{1,17},{... | collective-permute-start | bytes 49160 | tf_op jit(solution)/shard_map/ppermute | solution.py:463
  24.4 0.8 %collective-permute-start.10 = (bf16[64,128]{1,0:T(8,128)(2,1)S(1)}, bf16[64,128]{1,0:T(8,128)(2,1)S(1)}, u32[]{:S(2)}, u32[]{:S(2)}) collective-permute-start(bf16[64,128]{1,0:T(8,128)(2,1)S(1)} %get-tuple-element.54), channel_id=1, source_target_pairs={{0,12},{4,8},{8,4},{12,0},{16,28},{20,24},{24,20},{28,16},{1,13},{... | collective-permute-start | bytes 49160 | tf_op jit(solution)/shard_map/ppermute | solution.py:463
  25.2 0.9 %collective-permute-start.11 = (bf16[64,128]{1,0:T(8,128)(2,1)S(1)}, bf16[64,128]{1,0:T(8,128)(2,1)S(1)}, u32[]{:S(2)}, u32[]{:S(2)}) collective-permute-start(bf16[64,128]{1,0:T(8,128)(2,1)S(1)} %get-tuple-element.55), channel_id=1, source_target_pairs={{0,8},{4,12},{8,0},{12,4},{16,24},{20,28},{24,16},{28,20},{1,9},{5... | collective-permute-start | bytes 49160 | tf_op jit(solution)/shard_map/ppermute | solution.py:463
  26.1 0.2 collective-permute-start.12
  26.3 1.3 %shard_map.143 = (f32[1024,512]{1,0:T(8,128)S(1)}, bf16[128,256]{1,0:T(8,128)(2,1)S(1)}) custom-call(bf16[1024,512]{1,0:T(8,128)(2,1)S(1)} %get-tuple-element.34.refs_0_, bf16[256,256]{1,0:T(8,128)(2,1)S(1)} %get-tuple-element.39.refs_1_, bf16[1024,256]{1,0:T(8,128)(2,1)S(1)} %get-tuple-element.40.refs_2_, bf16[1024,256]{1,0:T(8,128)(2,1)S(1)} %get-tuple-element.41.refs_3_, ...), custom_call_target="tpu_custom_call" | custom-call | flops 268435456 | bytes 5242880 | tf_op jit(solution)/shard_map/pallas_call | solution.py:49
  27.6 0.0 collective-permute-done.8.refs_9_
  27.6 0.1 collective-permute-done.9.refs_10_
  27.7 1.3 %collective-permute-done.11.refs_12_ = bf16[64,128]{1,0:T(8,128)(2,1)S(1)} collective-permute-done((bf16[64,128]{1,0:T(8,128)(2,1)S(1)}, bf16[64,128]{1,0:T(8,128)(2,1)S(1)}, u32[]{:S(2)}, u32[]{:S(2)}) %collective-permute-start.11) | collective-permute-done | bytes 16416 | tf_op jit(solution)/shard_map/ppermute | solution.py:463
  29.0 2.3 %shard_map.144 = (bf16[1024,512]{1,0:T(8,128)(2,1)S(1)}, bf16[128,256]{1,0:T(8,128)(2,1)S(1)}) custom-call(f32[1024,512]{1,0:T(8,128)S(1)} %get-tuple-element.44.refs_0_, bf16[1024,256]{1,0:T(8,128)(2,1)S(1)} %get-tuple-element.45.refs_1_, bf16[1024,256]{1,0:T(8,128)(2,1)S(1)} %get-tuple-element.46.refs_2_, ...), custom_call_target="tpu_custom_call" | custom-call | flops 1073741824 | bytes 4194304 | tf_op jit(solution)/shard_map/pallas_call | solution.py:49
  31.3 3.9 %collective-permute-start.15 = (bf16[128,256]{1,0:T(8,128)(2,1)S(1)}, bf16[128,256]{1,0:T(8,128)(2,1)S(1)}, u32[]{:S(2)}, u32[]{:S(2)}) collective-permute-start(bf16[128,256]{1,0:T(8,128)(2,1)S(1)} %get-tuple-element.57.refs_0_), channel_id=1, source_target_pairs={{0,2},{1,3},{2,0},{3,1},{4,6},{5,7},{6,4},{7,5},{8,10},{9,11},{10,... | collective-permute-start | bytes 196616 | tf_op jit(solution)/shard_map/ppermute | solution.py:379
  35.2 0.5 %collective-permute-start.14 = (bf16[128,256]{1,0:T(8,128)(2,1)S(1)}, bf16[128,256]{1,0:T(8,128)(2,1)S(1)}, u32[]{:S(2)}, u32[]{:S(2)}) collective-permute-start(bf16[128,256]{1,0:T(8,128)(2,1)S(1)} %get-tuple-element.57.refs_0_), channel_id=1, source_target_pairs={{0,3},{1,2},{2,1},{3,0},{4,7},{5,6},{6,5},{7,4},{8,11},{9,10},{10,... | collective-permute-start | bytes 196616 | tf_op jit(solution)/shard_map/ppermute | solution.py:379
  35.6 0.2 collective-permute-start.13
  35.8 1.0 %shard_map.145 = (f32[1024,512]{1,0:T(8,128)S(1)}, bf16[1024,256]{1,0:T(8,128)(2,1)S(1)}, f32[256,512]{1,0:T(8,128)S(1)}, bf16[512,512]{1,0:T(8,128)(2,1)S(1)}) custom-call(bf16[1024,512]{1,0:T(8,128)(2,1)S(1)} %get-tuple-element.60.refs_0_.refs_6_, bf16[1024,512]{1,0:T(8,128)(2,1)S(1)} %get-tuple-element.61.refs_1_, ...), custom_call_target="tpu_custom_call" | custom-call | flops 536870912 | bytes 4194304 | tf_op jit(solution)/shard_map/pallas_call | solution.py:49
  36.8 2.9 %collective-permute-done.15.refs_3_ = bf16[128,256]{1,0:T(8,128)(2,1)S(1)} collective-permute-done((bf16[128,256]{1,0:T(8,128)(2,1)S(1)}, bf16[128,256]{1,0:T(8,128)(2,1)S(1)}, u32[]{:S(2)}, u32[]{:S(2)}) %collective-permute-start.15) | collective-permute-done | bytes 65568 | tf_op jit(solution)/shard_map/ppermute | solution.py:379
  39.7 1.5 %collective-permute-done.14.refs_2_ = bf16[128,256]{1,0:T(8,128)(2,1)S(1)} collective-permute-done((bf16[128,256]{1,0:T(8,128)(2,1)S(1)}, bf16[128,256]{1,0:T(8,128)(2,1)S(1)}, u32[]{:S(2)}, u32[]{:S(2)}) %collective-permute-start.14) | collective-permute-done | bytes 65568 | tf_op jit(solution)/shard_map/ppermute | solution.py:379
  41.2 1.9 %shard_map.146 = (bf16[1024,512]{1,0:T(8,128)(2,1)}, bf16[32,256]{1,0:T(8,128)(2,1)}) custom-call(bf16[128,256]{1,0:T(8,128)(2,1)S(1)} %get-tuple-element.57.refs_0_, bf16[128,256]{1,0:T(8,128)(2,1)S(1)} %collective-permute-done.13.refs_1_, bf16[128,256]{1,0:T(8,128)(2,1)S(1)} %collective-permute-done.14.refs_2_, ...), custom_call_target="tpu_custom_call" | custom-call | flops 268435456 | bytes 4194304 | tf_op jit(solution)/shard_map/pallas_call | solution.py:49
  (14 shorter events, 0.0 us)
Async XLA Ops:
  0.6 8.2 %copy-start = (bf16[32,256]{1,0:T(8,128)(2,1)S(1)}, bf16[32,256]{1,0:T(8,128)(2,1)}, u32[]{:S(2)}) copy-start(bf16[32,256]{1,0:T(8,128)(2,1)} %refs_6_.3) | copy-start | bytes 49156
  0.6 11.6 %copy-start.2 = (s32[16,2]{0,1:T(2,128)S(1)}, s32[16,2]{0,1:T(2,128)}, u32[]{:S(2)}) copy-start(s32[16,2]{0,1:T(2,128)} %param.17) | copy-start | bytes 388
  0.7 11.6 %copy-start.1 = (s32[1024]{0:T(1024)S(1)}, s32[1024]{0:T(1024)}, u32[]{:S(2)}) copy-start(s32[1024]{0:T(1024)} %param.15) | copy-start | bytes 12292
  3.2 14.6 %collective-permute-start.2 = (bf16[512,128]{1,0:T(8,128)(2,1)S(1)}, bf16[512,128]{1,0:T(8,128)(2,1)S(1)}, u32[]{:S(2)}, u32[]{:S(2)}) collective-permute-start(bf16[512,128]{1,0:T(8,128)(2,1)S(1)} %shard_map.141.refs_2_), channel_id=1, source_target_pairs={{0,2},{1,3},{2,0},{3,1},{4,6},{5,7},{6,4},{7,5},{8,10},{9,11},{10,... | collective-permute-start | bytes 393224 | tf_op jit(solution)/shard_map/ppermute | solution.py:379
  7.3 11.6 %collective-permute-start.1 = (bf16[512,128]{1,0:T(8,128)(2,1)S(1)}, bf16[512,128]{1,0:T(8,128)(2,1)S(1)}, u32[]{:S(2)}, u32[]{:S(2)}) collective-permute-start(bf16[512,128]{1,0:T(8,128)(2,1)S(1)} %shard_map.141.refs_2_), channel_id=1, source_target_pairs={{0,3},{1,2},{2,1},{3,0},{4,7},{5,6},{6,5},{7,4},{8,11},{9,10},{10,... | collective-permute-start | bytes 393224 | tf_op jit(solution)/shard_map/ppermute | solution.py:379
  8.6 10.3 %collective-permute-start = (bf16[512,128]{1,0:T(8,128)(2,1)S(1)}, bf16[512,128]{1,0:T(8,128)(2,1)S(1)}, u32[]{:S(2)}, u32[]{:S(2)}) collective-permute-start(bf16[512,128]{1,0:T(8,128)(2,1)S(1)} %shard_map.141.refs_2_), channel_id=1, source_target_pairs={{0,1},{1,0},{2,3},{3,2},{4,5},{5,4},{6,7},{7,6},{8,9},{9,8},{10,11... | collective-permute-start | bytes 393224 | tf_op jit(solution)/shard_map/ppermute | solution.py:379
  8.8 13.7 %collective-permute-start.4 = (bf16[32,256]{1,0:T(8,128)(2,1)S(1)}, bf16[32,256]{1,0:T(8,128)(2,1)S(1)}, u32[]{:S(2)}, u32[]{:S(2)}) collective-permute-start(bf16[32,256]{1,0:T(8,128)(2,1)S(1)} %copy-done), channel_id=1, source_target_pairs={{0,3},{1,2},{2,1},{3,0},{4,7},{5,6},{6,5},{7,4},{8,11},{9,10},{10,... | collective-permute-start | bytes 49160 | tf_op jit(solution)/shard_map/ppermute | solution.py:379
  11.8 12.2 %collective-permute-start.3 = (bf16[32,256]{1,0:T(8,128)(2,1)S(1)}, bf16[32,256]{1,0:T(8,128)(2,1)S(1)}, u32[]{:S(2)}, u32[]{:S(2)}) collective-permute-start(bf16[32,256]{1,0:T(8,128)(2,1)S(1)} %copy-done), channel_id=1, source_target_pairs={{0,1},{1,0},{2,3},{3,2},{4,5},{5,4},{6,7},{7,6},{8,9},{9,8},{10,11... | collective-permute-start | bytes 49160 | tf_op jit(solution)/shard_map/ppermute | solution.py:379
  17.8 6.6 %collective-permute-start.5 = (bf16[32,256]{1,0:T(8,128)(2,1)S(1)}, bf16[32,256]{1,0:T(8,128)(2,1)S(1)}, u32[]{:S(2)}, u32[]{:S(2)}) collective-permute-start(bf16[32,256]{1,0:T(8,128)(2,1)S(1)} %copy-done), channel_id=1, source_target_pairs={{0,2},{1,3},{2,0},{3,1},{4,6},{5,7},{6,4},{7,5},{8,10},{9,11},{10,... | collective-permute-start | bytes 49160 | tf_op jit(solution)/shard_map/ppermute | solution.py:379
  20.0 5.2 %collective-permute-start.6 = (bf16[64,128]{1,0:T(8,128)(2,1)S(1)}, bf16[64,128]{1,0:T(8,128)(2,1)S(1)}, u32[]{:S(2)}, u32[]{:S(2)}) collective-permute-start(bf16[64,128]{1,0:T(8,128)(2,1)S(1)} %get-tuple-element.50), channel_id=1, source_target_pairs={{0,28},{4,24},{8,20},{12,16},{16,12},{20,8},{24,4},{28,0},{1,29},{... | collective-permute-start | bytes 49160 | tf_op jit(solution)/shard_map/ppermute | solution.py:463
  20.5 5.6 %collective-permute-start.7 = (bf16[64,128]{1,0:T(8,128)(2,1)S(1)}, bf16[64,128]{1,0:T(8,128)(2,1)S(1)}, u32[]{:S(2)}, u32[]{:S(2)}) collective-permute-start(bf16[64,128]{1,0:T(8,128)(2,1)S(1)} %get-tuple-element.51), channel_id=1, source_target_pairs={{0,24},{4,28},{8,16},{12,20},{16,8},{20,12},{24,0},{28,4},{1,25},{... | collective-permute-start | bytes 49160 | tf_op jit(solution)/shard_map/ppermute | solution.py:463
  22.6 5.0 %collective-permute-start.8 = (bf16[64,128]{1,0:T(8,128)(2,1)S(1)}, bf16[64,128]{1,0:T(8,128)(2,1)S(1)}, u32[]{:S(2)}, u32[]{:S(2)}) collective-permute-start(bf16[64,128]{1,0:T(8,128)(2,1)S(1)} %get-tuple-element.52), channel_id=1, source_target_pairs={{0,20},{4,16},{8,28},{12,24},{16,4},{20,0},{24,12},{28,8},{1,21},{... | collective-permute-start | bytes 49160 | tf_op jit(solution)/shard_map/ppermute | solution.py:463
  23.9 3.7 %collective-permute-start.9 = (bf16[64,128]{1,0:T(8,128)(2,1)S(1)}, bf16[64,128]{1,0:T(8,128)(2,1)S(1)}, u32[]{:S(2)}, u32[]{:S(2)}) collective-permute-start(bf16[64,128]{1,0:T(8,128)(2,1)S(1)} %get-tuple-element.53), channel_id=1, source_target_pairs={{0,16},{4,20},{8,24},{12,28},{16,0},{20,4},{24,8},{28,12},{1,17},{... | collective-permute-start | bytes 49160 | tf_op jit(solution)/shard_map/ppermute | solution.py:463
  24.4 3.2 %collective-permute-start.10 = (bf16[64,128]{1,0:T(8,128)(2,1)S(1)}, bf16[64,128]{1,0:T(8,128)(2,1)S(1)}, u32[]{:S(2)}, u32[]{:S(2)}) collective-permute-start(bf16[64,128]{1,0:T(8,128)(2,1)S(1)} %get-tuple-element.54), channel_id=1, source_target_pairs={{0,12},{4,8},{8,4},{12,0},{16,28},{20,24},{24,20},{28,16},{1,13},{... | collective-permute-start | bytes 49160 | tf_op jit(solution)/shard_map/ppermute | solution.py:463
  25.2 3.8 %collective-permute-start.11 = (bf16[64,128]{1,0:T(8,128)(2,1)S(1)}, bf16[64,128]{1,0:T(8,128)(2,1)S(1)}, u32[]{:S(2)}, u32[]{:S(2)}) collective-permute-start(bf16[64,128]{1,0:T(8,128)(2,1)S(1)} %get-tuple-element.55), channel_id=1, source_target_pairs={{0,8},{4,12},{8,0},{12,4},{16,24},{20,28},{24,16},{28,20},{1,9},{5... | collective-permute-start | bytes 49160 | tf_op jit(solution)/shard_map/ppermute | solution.py:463
  26.1 2.9 %collective-permute-start.12 = (bf16[64,128]{1,0:T(8,128)(2,1)S(1)}, bf16[64,128]{1,0:T(8,128)(2,1)S(1)}, u32[]{:S(2)}, u32[]{:S(2)}) collective-permute-start(bf16[64,128]{1,0:T(8,128)(2,1)S(1)} %get-tuple-element.56), channel_id=1, source_target_pairs={{0,4},{4,0},{8,12},{12,8},{16,20},{20,16},{24,28},{28,24},{1,5},{5... | collective-permute-start | bytes 49160 | tf_op jit(solution)/shard_map/ppermute | solution.py:463
  31.3 8.4 %collective-permute-start.15 = (bf16[128,256]{1,0:T(8,128)(2,1)S(1)}, bf16[128,256]{1,0:T(8,128)(2,1)S(1)}, u32[]{:S(2)}, u32[]{:S(2)}) collective-permute-start(bf16[128,256]{1,0:T(8,128)(2,1)S(1)} %get-tuple-element.57.refs_0_), channel_id=1, source_target_pairs={{0,2},{1,3},{2,0},{3,1},{4,6},{5,7},{6,4},{7,5},{8,10},{9,11},{10,... | collective-permute-start | bytes 196616 | tf_op jit(solution)/shard_map/ppermute | solution.py:379
  35.2 6.1 %collective-permute-start.14 = (bf16[128,256]{1,0:T(8,128)(2,1)S(1)}, bf16[128,256]{1,0:T(8,128)(2,1)S(1)}, u32[]{:S(2)}, u32[]{:S(2)}) collective-permute-start(bf16[128,256]{1,0:T(8,128)(2,1)S(1)} %get-tuple-element.57.refs_0_), channel_id=1, source_target_pairs={{0,3},{1,2},{2,1},{3,0},{4,7},{5,6},{6,5},{7,4},{8,11},{9,10},{10,... | collective-permute-start | bytes 196616 | tf_op jit(solution)/shard_map/ppermute | solution.py:379
  35.6 5.6 %collective-permute-start.13 = (bf16[128,256]{1,0:T(8,128)(2,1)S(1)}, bf16[128,256]{1,0:T(8,128)(2,1)S(1)}, u32[]{:S(2)}, u32[]{:S(2)}) collective-permute-start(bf16[128,256]{1,0:T(8,128)(2,1)S(1)} %get-tuple-element.57.refs_0_), channel_id=1, source_target_pairs={{0,1},{1,0},{2,3},{3,2},{4,5},{5,4},{6,7},{7,6},{8,9},{9,8},{10,11... | collective-permute-start | bytes 196616 | tf_op jit(solution)/shard_map/ppermute | solution.py:379
